TPU v7x, 32 devices: a whole 2x2x4 slice. The times are simulated.
32 devices in a mesh: grp: 2 (over core), exp: 16 (over z, y, x).
Axes of the slice: x: 2, y: 2, z: 4, core: 2. Of those that a mesh axis runs over, the one named last changes fastest.
Arguments:
- tokens: bfloat16 [4096, 7168], P('exp', 'grp'), may hold values from -6 to 6
- d_out: bfloat16 [4096, 7168], P('exp', 'grp'), may hold values from -6 to 6
- row_expert: int32 [4096], P('exp'), may hold values from 0 to 15, as said below
- w_gate_up: bfloat16 [16, 7168, 2, 1024], P('exp', 'grp'), may hold values from -0.0625 to 0.0625
- w_down: bfloat16 [16, 1024, 7168], P('exp', None, 'grp'), may hold values from -0.1875 to 0.1875
Outputs:
- token_grads: bfloat16 [4096, 7168], P('exp', 'grp')
- gate_up_grads: bfloat16 [16, 7168, 2, 1024], P('exp', 'grp')
- down_grads: bfloat16 [16, 1024, 7168], P('exp', None, 'grp')
Inputs may be any that keep to these rules, and one draw needn't show every extreme that they name: `row_expert`: in each block of 256 rows held by one index of exp, one expert, the same for every block, is named by exactly 64 rows; every other expert by at most 32 rows, and in every block some expert by exactly 32.
All inputs are finite; a program needn't handle non-finite values.
Results may differ from a plain program's by a relative error of at most 0.028.
Values may be sent and summed in bfloat16 or wider, within the bound.
No kernel may reach another device: no remote copies, remote signals or barrier semaphores. Data moves between devices by JAX's collectives and lax.ppermute only.
A program may use at most 192 MiB of HBM per device.

v0:
```python
import jax
import jax.numpy as jnp
from jax import lax
from jax.experimental.layout import Layout, with_layout_constraint
from jax.sharding import PartitionSpec as P


def rank_in_expert(row_expert):
    row_count = row_expert.shape[0]
    same = row_expert[:, None] == row_expert[None, :]
    earlier = jnp.arange(row_count)[None, :] < jnp.arange(row_count)[:, None]
    return jnp.sum((same & earlier).astype(jnp.int32), axis=1)


def one_hot(index, total):
    return (index[None, :] == jnp.arange(total, dtype=jnp.int32)[:, None]).astype(jnp.bfloat16)


def place(one_hot_rows, rows):
    return lax.dot_general(
        one_hot_rows, rows, (((1,), (0,)), ((), ())), preferred_element_type=jnp.float32
    ).astype(jnp.bfloat16)


def exchange(rows, expert_count):
    slots, width = rows.shape
    return lax.all_to_all(
        rows.reshape(expert_count, slots // expert_count, width),
        "exp",
        split_axis=0,
        concat_axis=0,
        tiled=True,
    ).reshape(slots, width)


def swap_with(rows, mask):
    total = lax.axis_size("exp")
    return lax.ppermute(rows, "exp", [(i, i ^ mask) for i in range(total)])


def by_distance(blocks):
    total = lax.axis_size("exp")
    order = lax.axis_index("exp") ^ jnp.arange(total, dtype=jnp.int32)
    return jnp.concatenate(
        [lax.dynamic_slice_in_dim(blocks, order[k], 1, axis=0) for k in range(total)], axis=0
    )


def collect(blocks):
    half = lax.axis_size("exp") // 2
    pairs = [jnp.concatenate([blocks[k], blocks[k + half]], axis=0) for k in range(half)]
    arrived = [swap_with(pairs[k], k) for k in range(1, half)]
    total = pairs[0]
    for pair in arrived:
        total = total + pair
    height = blocks.shape[1]
    return total[:height] + swap_with(total[height:], half)


def sum_over_grp(part):
    part = part.astype(jnp.bfloat16)
    if lax.axis_size("grp") == 2:
        other = lax.ppermute(part, "grp", [(0, 1), (1, 0)])
        return part.astype(jnp.float32) + other.astype(jnp.float32)
    return lax.psum(part, "grp").astype(jnp.float32)


def activate(gate_up, hidden_grads):
    hidden_width = hidden_grads.shape[1]
    gate_value = gate_up[:, :hidden_width]
    upward = gate_up[:, hidden_width:]
    sigmoid_value = jax.nn.sigmoid(gate_value)
    activated = gate_value * sigmoid_value
    gate_slope = sigmoid_value * (1.0 + gate_value * (1.0 - sigmoid_value))
    hidden = (activated * upward).astype(jnp.bfloat16)
    branch = jnp.concatenate(
        [hidden_grads * upward * gate_slope, hidden_grads * activated], axis=1
    ).astype(jnp.bfloat16)
    return hidden, branch


def row_gradients(branch, gate_up_matrix):
    return lax.dot_general(
        branch, gate_up_matrix, (((1,), (1,)), ((), ())), preferred_element_type=jnp.float32
    ).astype(jnp.bfloat16)


def outer(left, right):
    return lax.dot_general(
        left, right, (((0,), (0,)), ((), ())), preferred_element_type=jnp.float32
    ).astype(jnp.bfloat16)


def local(tokens, d_out, row_expert, w_gate_up, w_down):
    row_count, feature_share = tokens.shape
    hidden_width = w_down.shape[1]
    expert_count = lax.axis_size("exp")
    gate_up_matrix = w_gate_up.reshape(feature_share, 2 * hidden_width)
    down_matrix = w_down.reshape(hidden_width, feature_share)
    cap = 2 * row_count // expert_count
    half = cap // 2

    rank = rank_in_expert(row_expert)
    is_spill = rank >= cap
    busiest = jnp.max(jnp.where(is_spill, row_expert, -1))
    is_busiest = lax.axis_index("exp") == busiest
    spill_hot = one_hot(jnp.where(is_spill, rank - cap, -1), cap)
    chunk_hot = []
    for chunk in range(2):
        inside = (rank >= chunk * half) & (rank < (chunk + 1) * half)
        slot = row_expert * half + rank - chunk * half
        chunk_hot.append(one_hot(jnp.where(inside, slot, -1), expert_count * half))

    both = jnp.concatenate([tokens, d_out], axis=1)

    def split(both_in):
        return both_in[:, :feature_share], both_in[:, feature_share:]

    def gate_up_of(rows_in, matrix):
        return sum_over_grp(jnp.dot(rows_in, matrix, preferred_element_type=jnp.float32))

    def hidden_grads_of(grads_in, matrix):
        return sum_over_grp(
            lax.dot_general(
                grads_in, matrix, (((1,), (1,)), ((), ())), preferred_element_type=jnp.float32
            )
        )

    arrived_0 = exchange(place(chunk_hot[0], both), expert_count)
    spill_rows = lax.all_gather(place(spill_hot, tokens), "exp", tiled=True)
    sent_1 = place(chunk_hot[1], both)
    sent_grads = place(spill_hot, d_out)
    arrived_0, spill_rows, sent_1, sent_grads, gate_up_matrix = lax.optimization_barrier(
        (arrived_0, spill_rows, sent_1, sent_grads, gate_up_matrix)
    )

    arrived_1 = exchange(sent_1, expert_count)
    spill_grads = lax.all_gather(sent_grads, "exp", tiled=True)
    rows_0, grads_0 = split(arrived_0)
    hidden_0, branch_0 = activate(
        gate_up_of(rows_0, gate_up_matrix), hidden_grads_of(grads_0, down_matrix)
    )
    out_0 = row_gradients(branch_0, gate_up_matrix)
    gate_up_s = gate_up_of(spill_rows, gate_up_matrix)
    arrived_1, spill_grads, hidden_0, branch_0, out_0, gate_up_s = lax.optimization_barrier(
        (arrived_1, spill_grads, hidden_0, branch_0, out_0, gate_up_s)
    )

    back_0 = exchange(out_0, expert_count)
    rows_1, grads_1 = split(arrived_1)
    hidden_1, branch_1 = activate(
        gate_up_of(rows_1, gate_up_matrix), hidden_grads_of(grads_1, down_matrix)
    )
    out_1 = row_gradients(branch_1, gate_up_matrix)
    hidden_s, branch_s = activate(gate_up_s, hidden_grads_of(spill_grads, down_matrix))
    hidden_s = jnp.where(is_busiest, hidden_s, jnp.zeros_like(hidden_s))
    branch_s = jnp.where(is_busiest, branch_s, jnp.zeros_like(branch_s))
    turned = by_distance(branch_s.reshape(expert_count, cap, -1)).reshape(branch_s.shape)
    out_s = row_gradients(turned, gate_up_matrix)
    back_0, out_1, out_s, hidden_1, branch_1, hidden_s, branch_s = lax.optimization_barrier(
        (back_0, out_1, out_s, hidden_1, branch_1, hidden_s, branch_s)
    )

    back_1 = exchange(out_1, expert_count)
    back_s = collect(out_s.reshape(expert_count, cap, feature_share))

    all_rows = jnp.concatenate([spill_rows, rows_0, rows_1], axis=0)
    all_grads = jnp.concatenate([spill_grads, grads_0, grads_1], axis=0)
    hidden = jnp.concatenate([hidden_s, hidden_0, hidden_1], axis=0)
    branch = jnp.concatenate([branch_s, branch_0, branch_1], axis=0)
    gate_up_grads = with_layout_constraint(outer(all_rows, branch), Layout((0, 1)))
    gate_up_grads = gate_up_grads.reshape(1, feature_share, 2, hidden_width)
    down_grads = outer(hidden, all_grads).reshape(1, hidden_width, feature_share)

    pick = jnp.concatenate([spill_hot] + chunk_hot, axis=0)
    returned = jnp.concatenate([back_s, back_0, back_1], axis=0)
    token_grads = lax.dot_general(
        pick, returned, (((0,), (0,)), ((), ())), preferred_element_type=jnp.float32
    ).astype(jnp.bfloat16)
    return (token_grads, gate_up_grads, down_grads)


def solution(mesh):
    return jax.shard_map(
        local,
        mesh=mesh,
        in_specs=(
            P("exp", "grp"),
            P("exp", "grp"),
            P("exp"),
            P("exp", "grp", None, None),
            P("exp", None, "grp"),
        ),
        out_specs=(P("exp", "grp"), P("exp", "grp", None, None), P("exp", None, "grp")),
        check_vma=False,
    )
```

profile of v0, /device:TPU:0, one launch (start us, length us, event | category | flops | bytes accessed | tf_op | source)
XLA Modules:
  0.0 467.5 jit_solution(2439805573488524079)
XLA Ops:
  7.2 1.0 convert_reduce_fusion
  8.2 1.3 select_reduce_fusion
  9.5 2.6 convolution_convert_fusion.9
  12.2 0.2 constant_dynamic-update-slice_fusion.1
  12.4 1.3 copy-done.3
  13.7 0.2 constant_dynamic-update-slice_fusion
  13.9 3.0 convolution_convert_fusion.2
  16.9 8.4 %all-to-all-start = ((bf16[16,16,7168]{2,1,0:T(8,128)(2,1)}), bf16[16,16,7168]{2,1,0:T(8,128)(2,1)}, u32[]{:S(2)}, u32[]{:S(2)}) async-start(bf16[16,16,7168]{2,1,0:T(8,128)(2,1)} %bitcast.67), calls=%async_computation | async-start | bytes 7340032 | tf_op jit(solution)/shard_map/all_to_all | solution.py:27
  25.3 0.7 fusion.72
  45.7 16.2 %copy.8 = bf16[448,8,2,1024]{3,1,2,0:T(8,128)(2,1)} copy(bf16[448,8,2,1024]{3,2,1,0:T(2,128)(2,1)} %bitcast.58) | data formatting | bytes 29360128
  71.4 0.7 iota_compare_fusion
  72.1 1.1 convolution_convert_fusion.8
  73.2 5.0 %convolution_convert_fusion.1 = bf16[256,7168]{1,0:T(8,128)(2,1)} fusion(bf16[256,7168]{1,0:T(8,128)(2,1)} %copy-done.1, s32[256]{0:T(256)S(1)} %get-tuple-element.68), kind=kOutput, calls=%fused_computation.1 | convolution fusion | flops 941424640 | bytes 7341056 | tf_op jit(solution)/shard_map/dot_general | solution.py:20
  78.2 62.8 %all-gather.3.cloned.1.call-done = bf16[512,3584]{1,0:T(8,128)(2,1)} async-done(((bf16[32,3584]{1,0:T(8,128)(2,1)}), bf16[512,3584]{1,0:T(8,128)(2,1)}) %all-gather.3.cloned.1.call-update) | async-done | bytes 3670032 | tf_op jit(solution)/shard_map/all_gather | solution.py:130
  141.1 6.0 %all-to-all-start.1 = ((bf16[16,16,7168]{2,1,0:T(8,128)(2,1)}), bf16[16,16,7168]{2,1,0:T(8,128)(2,1)}, u32[]{:S(2)}, u32[]{:S(2)}) async-start(bf16[16,16,7168]{2,1,0:T(8,128)(2,1)} %bitcast.68), calls=%async_computation.1 | async-start | bytes 7340032 | tf_op jit(solution)/shard_map/all_to_all | solution.py:27
  147.1 5.9 %fusion.38 = bf16[256,1024]{1,0:T(8,128)(2,1)S(1)} fusion(bf16[1,1024,3584]{2,1,0:T(8,128)(2,1)} %param.9, bf16[256,7168]{1,0:T(8,128)(2,1)} %bitcast.1), kind=kOutput, calls=%fused_computation.57 | convolution fusion | flops 1879310336 | bytes 9699328 | tf_op jit(solution)/shard_map/dot_general | solution.py:124
  153.1 9.8 %convolution_convert_fusion.12 = bf16[256,2048]{1,0:T(8,128)(2,1)S(1)} fusion(bf16[3584,2048]{1,0:T(8,128)(2,1)} %bitcast.59, bf16[256,7168]{1,0:T(8,128)(2,1)} %bitcast.1), kind=kOutput, calls=%fused_computation.40 | convolution fusion | flops 3758620672 | bytes 17563648 | tf_op jit(solution)/shard_map/dot_general | solution.py:120
  162.9 1.2 collective-permute-start
  164.1 7.9 %convolution_convert_fusion.10 = bf16[512,2048]{1,0:T(8,128)(2,1)S(1)} fusion(bf16[512,3584]{1,0:T(8,128)(2,1)S(1)} %copy-done.23, bf16[3584,2048]{1,0:T(8,128)(2,1)S(1)} %bitcast.66), kind=kOutput, calls=%fused_computation.38 | convolution fusion | flops 7517241344 | bytes 20447232 | tf_op jit(solution)/shard_map/dot_general | solution.py:120
  172.2 4.2 fusion.69
  176.3 0.4 convert_add_fusion.3
  176.7 1.5 multiply_convert_fusion.7
  178.2 1.1 pad_maximum_fusion
  179.2 16.6 %convolution_convert_fusion.6 = bf16[256,3584]{1,0:T(8,128)(2,1)} fusion(bf16[3584,2048]{1,0:T(8,128)(2,1)} %bitcast.60, bf16[256,1024]{1,0:T(8,128)(2,1)S(1)} %get-tuple-element.64, bf16[256,1024]{1,0:T(8,128)(2,1)S(1)} %get-tuple-element.63), kind=kOutput, calls=%fused_computation.23 | convolution fusion | flops 3761111040 | bytes 17563648 | tf_op jit(solution)/shard_map/dot_general | solution.py:83
  195.8 4.4 convert_add_fusion
  200.2 63.0 %all-gather.5.cloned.1.call-done = bf16[512,3584]{1,0:T(8,128)(2,1)} async-done(((bf16[32,3584]{1,0:T(8,128)(2,1)}), bf16[512,3584]{1,0:T(8,128)(2,1)}) %all-gather.5.cloned.1.call-update) | async-done | bytes 3670032 | tf_op jit(solution)/shard_map/all_gather | solution.py:138
  263.2 5.7 %fusion.41 = bf16[256,1024]{1,0:T(8,128)(2,1)S(1)} fusion(bf16[1,1024,3584]{2,1,0:T(8,128)(2,1)} %param.9, bf16[256,7168]{1,0:T(8,128)(2,1)} %bitcast.3), kind=kOutput, calls=%fused_computation.58 | convolution fusion | flops 1879310336 | bytes 9699328 | tf_op jit(solution)/shard_map/dot_general | solution.py:124
  269.0 10.8 %convolution_convert_fusion.11 = bf16[256,2048]{1,0:T(8,128)(2,1)} fusion(bf16[3584,2048]{1,0:T(8,128)(2,1)} %bitcast.61, bf16[256,7168]{1,0:T(8,128)(2,1)} %bitcast.3), kind=kOutput, calls=%fused_computation.39 | convolution fusion | flops 3758620672 | bytes 17563648 | tf_op jit(solution)/shard_map/dot_general | solution.py:120
  279.8 4.4 all-to-all-start.2
  284.4 9.3 %fusion.35 = bf16[512,1024]{1,0:T(8,128)(2,1)} fusion(bf16[512,3584]{1,0:T(8,128)(2,1)} %all-gather.5.cloned.1.call-done, bf16[1,1024,3584]{2,1,0:T(8,128)(2,1)} %param.9), kind=kOutput, calls=%fused_computation.56 | convolution fusion | flops 3758620672 | bytes 12058624 | tf_op jit(solution)/shard_map/dot_general | solution.py:124
  293.7 0.4 collective-permute-start.4
  294.2 1.7 fusion.44
  295.9 4.2 fusion.70
  300.1 0.4 convert_add_fusion.2
  300.5 0.7 copy-done.21
  301.1 1.6 multiply_convert_fusion.5
  302.8 10.6 %convolution_convert_fusion.5 = bf16[256,3584]{1,0:T(8,128)(2,1)} fusion(bf16[3584,2048]{1,0:T(8,128)(2,1)} %bitcast.62, bf16[256,1024]{1,0:T(8,128)(2,1)} %get-tuple-element.62, bf16[256,1024]{1,0:T(8,128)(2,1)S(1)} %get-tuple-element.61), kind=kOutput, calls=%fused_computation.22 | convolution fusion | flops 3761111040 | bytes 17563648 | tf_op jit(solution)/shard_map/dot_general | solution.py:83
  313.4 2.8 multiply_convert_fusion.2
  316.2 0.5 maximum_select_fusion
  317.0 0.6 copy-done.5
  317.7 1.1 pad_maximum_fusion.1
  318.8 0.4 maximum_select_fusion.1
  319.2 12.7 %convolution_convert_fusion.4 = bf16[512,3584]{1,0:T(8,128)(2,1)} fusion(bf16[512,2048]{1,0:T(8,128)(2,1)S(1)} %bitcast.72, bf16[3584,2048]{1,0:T(8,128)(2,1)} %bitcast.63), kind=kOutput, calls=%fused_computation.21 | convolution fusion | flops 7518027776 | bytes 20447232 | tf_op jit(solution)/shard_map/dot_general | solution.py:83
  331.9 3.5 fusion.71
  335.4 6.8 %all-to-all-start.3 = ((bf16[16,16,3584]{2,1,0:T(8,128)(2,1)}), bf16[16,16,3584]{2,1,0:T(8,128)(2,1)}, u32[]{:S(2)}, u32[]{:S(2)}) async-start(bf16[16,16,3584]{2,1,0:T(8,128)(2,1)} %bitcast.71), calls=%async_computation.3 | async-start | bytes 3670016 | tf_op jit(solution)/shard_map/all_to_all | solution.py:27
  342.3 1.2 pad_maximum_fusion.2
  343.5 1.9 collective-permute-start.6
  345.4 1.2 pad_maximum_fusion.3
  346.6 1.5 collective-permute-start.7
  348.1 1.2 pad_maximum_fusion.4
  349.3 0.2 collective-permute-start.8
  349.6 1.9 collective-permute-start.9
  351.6 1.5 collective-permute-start.10
  353.2 9.2 %collective-permute-done.6 = bf16[64,3584]{1,0:T(8,128)(2,1)S(1)} collective-permute-done((bf16[64,3584]{1,0:T(8,128)(2,1)S(1)}, bf16[64,3584]{1,0:T(8,128)(2,1)S(1)}, u32[]{:S(2)}, u32[]{:S(2)}) %collective-permute-start.6) | collective-permute-done | bytes 458784 | tf_op jit(solution)/shard_map/ppermute | solution.py:38
  362.4 10.4 %collective-permute-start.11 = (bf16[64,3584]{1,0:T(8,128)(2,1)S(1)}, bf16[64,3584]{1,0:T(8,128)(2,1)S(1)}, u32[]{:S(2)}, u32[]{:S(2)}) collective-permute-start(bf16[64,3584]{1,0:T(8,128)(2,1)S(1)} %pad_maximum_fusion.7), channel_id=1, source_target_pairs={{0,6},{1,7},{2,4},{3,5},{4,2},{5,3},{6,0},{7,1},{8,14},{9,15},{10,... | collective-permute-start | bytes 1376264 | tf_op jit(solution)/shard_map/ppermute | solution.py:38
  372.8 4.6 collective-permute-done.7
  377.5 21.3 %convolution_convert_fusion = bf16[3584,2048]{1,0:T(8,128)(2,1)} fusion(bf16[256,3584]{1,0:T(8,128)(2,1)S(1)} %copy-done.9, bf16[256,3584]{1,0:T(8,128)(2,1)S(1)} %copy-done.7, bf16[512,3584]{1,0:T(8,128)(2,1)} %all-gather.3.cloned.1.call-done, bf16[256,2048]{1,0:T(8,128)(2,1)S(1)} %copy-done.11, bf16[256,2048]{1,0:T(8,128)(2,1)S(1)} %copy-done.10, ...), kind=kOutput, calls=%fused_computation | convolution fusion | flops 15074328576 | bytes 26214400 | tf_op jit(solution)/shard_map/dot_general | solution.py:89
  398.8 9.2 %collective-permute-done.11 = bf16[64,3584]{1,0:T(8,128)(2,1)S(1)} collective-permute-done((bf16[64,3584]{1,0:T(8,128)(2,1)S(1)}, bf16[64,3584]{1,0:T(8,128)(2,1)S(1)}, u32[]{:S(2)}, u32[]{:S(2)}) %collective-permute-start.11) | collective-permute-done | bytes 458784 | tf_op jit(solution)/shard_map/ppermute | solution.py:38
  408.0 8.7 %collective-permute-done.12 = bf16[64,3584]{1,0:T(8,128)(2,1)S(1)} collective-permute-done((bf16[64,3584]{1,0:T(8,128)(2,1)S(1)}, bf16[64,3584]{1,0:T(8,128)(2,1)S(1)}, u32[]{:S(2)}, u32[]{:S(2)}) %collective-permute-start.12) | collective-permute-done | bytes 458784 | tf_op jit(solution)/shard_map/ppermute | solution.py:38
  416.7 0.5 fusion.57
  417.2 2.1 collective-permute-start.13
  419.3 11.7 %fusion.16 = bf16[1,1024,3584]{2,1,0:T(8,128)(2,1)} fusion(bf16[256,3584]{1,0:T(8,128)(2,1)S(1)} %copy-done.8, bf16[256,3584]{1,0:T(8,128)(2,1)S(1)} %copy-done.6, bf16[512,3584]{1,0:T(8,128)(2,1)} %all-gather.5.cloned.1.call-done, bf16[256,1024]{1,0:T(8,128)(2,1)S(1)} %copy-done.19, bf16[256,1024]{1,0:T(8,128)(2,1)S(1)} %copy-done.18, ...), kind=kOutput, calls=%fused_computation.20 | convolution fusion | flops 7548174336 | bytes 16777216 | tf_op jit(solution)/shard_map/dot_general | solution.py:89
  431.0 24.4 %reshape.103 = bf16[1,3584,2,1024]{3,2,1,0:T(2,128)(2,1)} reshape(bf16[3584,2048]{1,0:T(8,128)(2,1)} %convolution_convert_fusion) | data formatting | bytes 29360128 | tf_op jit(solution)/shard_map/reshape | solution.py:172
  455.5 4.9 %convolution_convert_fusion.7 = bf16[256,3584]{1,0:T(8,128)(2,1)} fusion(bf16[256,3584]{1,0:T(8,128)(2,1)} %bitcast.27, bf16[256,3584]{1,0:T(8,128)(2,1)} %bitcast.6, bf16[32,3584]{1,0:T(8,128)(2,1)S(1)} %slice_add_fusion, pred[256,256]{1,0:T(32,128)(4,1)S(1)} %get-tuple-element.87, pred[256,256]{1,0:T(32,128)(4,1)S(1)} %copy-done.22, ...), kind=kOutput, calls=%fused_computation.24 | convolution fusion | flops 1011138560 | bytes 5873664 | tf_op jit(solution)/shard_map/dot_general | solution.py:177
  (101 shorter events, 1.2 us)
Async XLA Ops:
  7.2 5.0 %copy-start.2 = (bf16[256,3584]{1,0:T(8,128)(2,1)S(1)}, bf16[256,3584]{1,0:T(8,128)(2,1)}, u32[]{:S(2)}) copy-start(bf16[256,3584]{1,0:T(8,128)(2,1)} %param.5) | copy-start | bytes 5505028
  7.2 133.9 %all-gather.3.cloned.1.call-start = ((), (), s32[]{:S(2)}) async-start(), calls=%async_computation.4 | async-start | bytes 3899392 | tf_op jit(solution)/shard_map/all_gather | solution.py:130
  12.2 1.5 copy-start.3
  13.9 3.0 copy-start.1
  16.9 124.1 %all-to-all-start = ((bf16[16,16,7168]{2,1,0:T(8,128)(2,1)}), bf16[16,16,7168]{2,1,0:T(8,128)(2,1)}, u32[]{:S(2)}, u32[]{:S(2)}) async-start(bf16[16,16,7168]{2,1,0:T(8,128)(2,1)} %bitcast.67), calls=%async_computation | async-start | bytes 7340032 | tf_op jit(solution)/shard_map/all_to_all | solution.py:27
  25.3 237.9 %all-gather.5.cloned.1.call-start = ((), (), s32[]{:S(2)}) async-start(), calls=%async_computation.5 | async-start | bytes 3899392 | tf_op jit(solution)/shard_map/all_gather | solution.py:138
  45.7 26.4 %copy-start.4 = (bf16[256,3584]{1,0:T(8,128)(2,1)S(1)}, bf16[256,3584]{1,0:T(8,128)(2,1)}, u32[]{:S(2)}) copy-start(bf16[256,3584]{1,0:T(8,128)(2,1)} %param.6) | copy-start | bytes 5505028
  141.1 122.1 %all-to-all-start.1 = ((bf16[16,16,7168]{2,1,0:T(8,128)(2,1)}), bf16[16,16,7168]{2,1,0:T(8,128)(2,1)}, u32[]{:S(2)}, u32[]{:S(2)}) async-start(bf16[16,16,7168]{2,1,0:T(8,128)(2,1)} %bitcast.68), calls=%async_computation.1 | async-start | bytes 7340032 | tf_op jit(solution)/shard_map/all_to_all | solution.py:27
  147.0 17.0 %slice-start = ((s8[14680064]{0:T(1024)(128)(4,1)}), s8[4194304]{0:T(1024)(128)(4,1)S(1)}, s32[]{:S(2)}) async-start(s8[14680064]{0:T(1024)(128)(4,1)} %bitcast.64), calls=%async_computation.6 | async-start | bytes 8388608
  147.1 17.0 %slice-start.1 = ((s8[14680064]{0:T(1024)(128)(4,1)}), s8[2097152]{0:T(1024)(128)(4,1)S(1)}, s32[]{:S(2)}) async-start(s8[14680064]{0:T(1024)(128)(4,1)} %bitcast.64), calls=%async_computation.7 | async-start | bytes 4194304
  152.9 11.1 %slice-start.2 = ((s8[14680064]{0:T(1024)(128)(4,1)}), s8[4194304]{0:T(1024)(128)(4,1)S(1)}, s32[]{:S(2)}) async-start(s8[14680064]{0:T(1024)(128)(4,1)} %bitcast.64), calls=%async_computation.8 | async-start | bytes 8388608
  153.0 11.1 %slice-start.3 = ((s8[14680064]{0:T(1024)(128)(4,1)}), s8[4194304]{0:T(1024)(128)(4,1)S(1)}, s32[]{:S(2)}) async-start(s8[14680064]{0:T(1024)(128)(4,1)} %bitcast.64), calls=%async_computation.9 | async-start | bytes 8388608
  153.0 11.1 %copy-start.23 = (bf16[512,3584]{1,0:T(8,128)(2,1)S(1)}, bf16[512,3584]{1,0:T(8,128)(2,1)}, u32[]{:S(2)}) copy-start(bf16[512,3584]{1,0:T(8,128)(2,1)} %all-gather.3.cloned.1.call-done) | copy-start | bytes 11010052
  153.0 23.7 %collective-permute-start.1 = (bf16[256,1024]{1,0:T(8,128)(2,1)S(1)}, bf16[256,1024]{1,0:T(8,128)(2,1)S(1)}, u32[]{:S(2)}, u32[]{:S(2)}) collective-permute-start(bf16[256,1024]{1,0:T(8,128)(2,1)S(1)} %fusion.38), channel_id=1, source_target_pairs={{0,16},{16,0},{1,17},{17,1},{2,18},{18,2},{3,19},{19,3},{4,20},{20... | collective-permute-start | bytes 1572872 | tf_op jit(solution)/shard_map/ppermute | solution.py:63
  162.9 13.4 %collective-permute-start = (bf16[256,2048]{1,0:T(8,128)(2,1)S(1)}, bf16[256,2048]{1,0:T(8,128)(2,1)S(1)}, u32[]{:S(2)}, u32[]{:S(2)}) collective-permute-start(bf16[256,2048]{1,0:T(8,128)(2,1)S(1)} %convolution_convert_fusion.12), channel_id=1, source_target_pairs={{0,16},{16,0},{1,17},{17,1},{2,18},{18,2},{3,19},{19,3},{4,20},{20... | collective-permute-start | bytes 3145736 | tf_op jit(solution)/shard_map/ppermute | solution.py:63
  172.0 23.8 %collective-permute-start.2 = (bf16[512,2048]{1,0:T(8,128)(2,1)S(1)}, bf16[512,2048]{1,0:T(8,128)(2,1)}, u32[]{:S(2)}, u32[]{:S(2)}) collective-permute-start(bf16[512,2048]{1,0:T(8,128)(2,1)S(1)} %convolution_convert_fusion.10), channel_id=1, source_target_pairs={{0,16},{16,0},{1,17},{17,1},{2,18},{18,2},{3,19},{19,3},{4,20},{20... | collective-permute-start | bytes 6291464 | tf_op jit(solution)/shard_map/ppermute | solution.py:63
  269.0 15.3 %copy-start.20 = (bf16[256,1024]{1,0:T(8,128)(2,1)}, bf16[256,1024]{1,0:T(8,128)(2,1)S(1)}, u32[]{:S(2)}) copy-start(bf16[256,1024]{1,0:T(8,128)(2,1)S(1)} %fusion.41) | copy-start | bytes 1572868
  279.8 52.1 %all-to-all-start.2 = ((bf16[16,16,3584]{2,1,0:T(8,128)(2,1)}), bf16[16,16,3584]{2,1,0:T(8,128)(2,1)}, u32[]{:S(2)}, u32[]{:S(2)}) async-start(bf16[16,16,3584]{2,1,0:T(8,128)(2,1)} %bitcast.5), calls=%async_computation.2 | async-start | bytes 3670016 | tf_op jit(solution)/shard_map/all_to_all | solution.py:27
  284.2 9.5 %copy-start.13 = (bf16[256,2048]{1,0:T(8,128)(2,1)S(1)}, bf16[256,2048]{1,0:T(8,128)(2,1)}, u32[]{:S(2)}) copy-start(bf16[256,2048]{1,0:T(8,128)(2,1)} %convolution_convert_fusion.11) | copy-start | bytes 3145732
  284.2 16.2 %collective-permute-start.3 = (bf16[256,1024]{1,0:T(8,128)(2,1)S(1)}, bf16[256,1024]{1,0:T(8,128)(2,1)S(1)}, u32[]{:S(2)}, u32[]{:S(2)}) collective-permute-start(bf16[256,1024]{1,0:T(8,128)(2,1)S(1)} %fusion.41), channel_id=1, source_target_pairs={{0,16},{16,0},{1,17},{17,1},{2,18},{18,2},{3,19},{19,3},{4,20},{20... | collective-permute-start | bytes 1572872 | tf_op jit(solution)/shard_map/ppermute | solution.py:63
  284.4 9.8 %copy-start = (f32[512,2048]{1,0:T(8,128)S(1)}, f32[512,2048]{1,0:T(8,128)}, u32[]{:S(2)}) copy-start(f32[512,2048]{1,0:T(8,128)} %convert_add_fusion) | copy-start | bytes 12582916
  293.7 6.4 %collective-permute-start.4 = (bf16[256,2048]{1,0:T(8,128)(2,1)S(1)}, bf16[256,2048]{1,0:T(8,128)(2,1)S(1)}, u32[]{:S(2)}, u32[]{:S(2)}) collective-permute-start(bf16[256,2048]{1,0:T(8,128)(2,1)S(1)} %copy-done.13), channel_id=1, source_target_pairs={{0,16},{16,0},{1,17},{17,1},{2,18},{18,2},{3,19},{19,3},{4,20},{20... | collective-permute-start | bytes 3145736 | tf_op jit(solution)/shard_map/ppermute | solution.py:63
  294.1 19.3 %collective-permute-start.5 = (bf16[512,1024]{1,0:T(8,128)(2,1)}, bf16[512,1024]{1,0:T(8,128)(2,1)}, u32[]{:S(2)}, u32[]{:S(2)}) collective-permute-start(bf16[512,1024]{1,0:T(8,128)(2,1)} %fusion.35), channel_id=1, source_target_pairs={{0,16},{16,0},{1,17},{17,1},{2,18},{18,2},{3,19},{19,3},{4,20},{20... | collective-permute-start | bytes 3145736 | tf_op jit(solution)/shard_map/ppermute | solution.py:63
  300.1 1.0 copy-start.21
  316.6 1.0 copy-start.5
  335.4 120.1 %all-to-all-start.3 = ((bf16[16,16,3584]{2,1,0:T(8,128)(2,1)}), bf16[16,16,3584]{2,1,0:T(8,128)(2,1)}, u32[]{:S(2)}, u32[]{:S(2)}) async-start(bf16[16,16,3584]{2,1,0:T(8,128)(2,1)} %bitcast.71), calls=%async_computation.3 | async-start | bytes 3670016 | tf_op jit(solution)/shard_map/all_to_all | solution.py:27
  342.2 7.3 %copy-start.14 = (bf16[32,3584]{1,0:T(8,128)(2,1)S(1)}, bf16[32,3584]{1,0:T(8,128)(2,1)}, u32[]{:S(2)}) copy-start(bf16[32,3584]{1,0:T(8,128)(2,1)} %get-tuple-element.52) | copy-start | bytes 688132
  342.2 7.3 %copy-start.15 = (bf16[32,3584]{1,0:T(8,128)(2,1)S(1)}, bf16[32,3584]{1,0:T(8,128)(2,1)}, u32[]{:S(2)}) copy-start(bf16[32,3584]{1,0:T(8,128)(2,1)} %get-tuple-element.53) | copy-start | bytes 688132
  342.3 35.2 %copy-start.11 = (bf16[256,2048]{1,0:T(8,128)(2,1)S(1)}, bf16[256,2048]{1,0:T(8,128)(2,1)}, u32[]{:S(2)}) copy-start(bf16[256,2048]{1,0:T(8,128)(2,1)} %pad_maximum_fusion.1) | copy-start | bytes 3145732
  343.5 18.9 %collective-permute-start.6 = (bf16[64,3584]{1,0:T(8,128)(2,1)S(1)}, bf16[64,3584]{1,0:T(8,128)(2,1)S(1)}, u32[]{:S(2)}, u32[]{:S(2)}) collective-permute-start(bf16[64,3584]{1,0:T(8,128)(2,1)S(1)} %pad_maximum_fusion.2), channel_id=1, source_target_pairs={{0,1},{1,0},{2,3},{3,2},{4,5},{5,4},{6,7},{7,6},{8,9},{9,8},{10,11... | collective-permute-start | bytes 1376264 | tf_op jit(solution)/shard_map/ppermute | solution.py:38
  345.4 32.1 %copy-start.10 = (bf16[256,2048]{1,0:T(8,128)(2,1)S(1)}, bf16[256,2048]{1,0:T(8,128)(2,1)}, u32[]{:S(2)}) copy-start(bf16[256,2048]{1,0:T(8,128)(2,1)} %pad_maximum_fusion) | copy-start | bytes 3145732
  346.6 30.9 %collective-permute-start.7 = (bf16[64,3584]{1,0:T(8,128)(2,1)S(1)}, bf16[64,3584]{1,0:T(8,128)(2,1)S(1)}, u32[]{:S(2)}, u32[]{:S(2)}) collective-permute-start(bf16[64,3584]{1,0:T(8,128)(2,1)S(1)} %pad_maximum_fusion.3), channel_id=1, source_target_pairs={{0,2},{1,3},{2,0},{3,1},{4,6},{5,7},{6,4},{7,5},{8,10},{9,11},{10,... | collective-permute-start | bytes 1376264 | tf_op jit(solution)/shard_map/ppermute | solution.py:38
  348.1 29.4 %copy-start.7 = (bf16[256,3584]{1,0:T(8,128)(2,1)S(1)}, bf16[256,3584]{1,0:T(8,128)(2,1)}, u32[]{:S(2)}) copy-start(bf16[256,3584]{1,0:T(8,128)(2,1)} %get-tuple-element.42) | copy-start | bytes 5505028
  348.1 29.4 %copy-start.9 = (bf16[256,3584]{1,0:T(8,128)(2,1)S(1)}, bf16[256,3584]{1,0:T(8,128)(2,1)}, u32[]{:S(2)}) copy-start(bf16[256,3584]{1,0:T(8,128)(2,1)} %get-tuple-element.44) | copy-start | bytes 5505028
  349.3 49.5 %collective-permute-start.8 = (bf16[64,3584]{1,0:T(8,128)(2,1)S(1)}, bf16[64,3584]{1,0:T(8,128)(2,1)S(1)}, u32[]{:S(2)}, u32[]{:S(2)}) collective-permute-start(bf16[64,3584]{1,0:T(8,128)(2,1)S(1)} %pad_maximum_fusion.4), channel_id=1, source_target_pairs={{0,3},{1,2},{2,1},{3,0},{4,7},{5,6},{6,5},{7,4},{8,11},{9,10},{10,... | collective-permute-start | bytes 1376264 | tf_op jit(solution)/shard_map/ppermute | solution.py:38
  349.6 49.2 %collective-permute-start.9 = (bf16[64,3584]{1,0:T(8,128)(2,1)S(1)}, bf16[64,3584]{1,0:T(8,128)(2,1)S(1)}, u32[]{:S(2)}, u32[]{:S(2)}) collective-permute-start(bf16[64,3584]{1,0:T(8,128)(2,1)S(1)} %pad_maximum_fusion.5), channel_id=1, source_target_pairs={{0,4},{1,5},{2,6},{3,7},{4,0},{5,1},{6,2},{7,3},{8,12},{9,13},{10,... | collective-permute-start | bytes 1376264 | tf_op jit(solution)/shard_map/ppermute | solution.py:38
  351.6 47.2 %collective-permute-start.10 = (bf16[64,3584]{1,0:T(8,128)(2,1)S(1)}, bf16[64,3584]{1,0:T(8,128)(2,1)S(1)}, u32[]{:S(2)}, u32[]{:S(2)}) collective-permute-start(bf16[64,3584]{1,0:T(8,128)(2,1)S(1)} %pad_maximum_fusion.6), channel_id=1, source_target_pairs={{0,5},{1,4},{2,7},{3,6},{4,1},{5,0},{6,3},{7,2},{8,13},{9,12},{10,... | collective-permute-start | bytes 1376264 | tf_op jit(solution)/shard_map/ppermute | solution.py:38
  362.4 45.6 %collective-permute-start.11 = (bf16[64,3584]{1,0:T(8,128)(2,1)S(1)}, bf16[64,3584]{1,0:T(8,128)(2,1)S(1)}, u32[]{:S(2)}, u32[]{:S(2)}) collective-permute-start(bf16[64,3584]{1,0:T(8,128)(2,1)S(1)} %pad_maximum_fusion.7), channel_id=1, source_target_pairs={{0,6},{1,7},{2,4},{3,5},{4,2},{5,3},{6,0},{7,1},{8,14},{9,15},{10,... | collective-permute-start | bytes 1376264 | tf_op jit(solution)/shard_map/ppermute | solution.py:38
  377.4 39.2 %collective-permute-start.12 = (bf16[64,3584]{1,0:T(8,128)(2,1)S(1)}, bf16[64,3584]{1,0:T(8,128)(2,1)S(1)}, u32[]{:S(2)}, u32[]{:S(2)}) collective-permute-start(bf16[64,3584]{1,0:T(8,128)(2,1)S(1)} %pad_maximum_fusion.8), channel_id=1, source_target_pairs={{0,7},{1,6},{2,5},{3,4},{4,3},{5,2},{6,1},{7,0},{8,15},{9,14},{10,... | collective-permute-start | bytes 1376264 | tf_op jit(solution)/shard_map/ppermute | solution.py:38
  377.5 39.2 %copy-start.16 = (bf16[32,3584]{1,0:T(8,128)(2,1)S(1)}, bf16[32,3584]{1,0:T(8,128)(2,1)}, u32[]{:S(2)}) copy-start(bf16[32,3584]{1,0:T(8,128)(2,1)} %get-tuple-element.45) | copy-start | bytes 688132
  377.5 39.2 %copy-start.17 = (bf16[32,3584]{1,0:T(8,128)(2,1)S(1)}, bf16[32,3584]{1,0:T(8,128)(2,1)}, u32[]{:S(2)}) copy-start(bf16[32,3584]{1,0:T(8,128)(2,1)} %get-tuple-element.60) | copy-start | bytes 688132
  377.5 41.8 %copy-start.12 = (bf16[512,1024]{1,0:T(8,128)(2,1)S(1)}, bf16[512,1024]{1,0:T(8,128)(2,1)}, u32[]{:S(2)}) copy-start(bf16[512,1024]{1,0:T(8,128)(2,1)} %fusion.44) | copy-start | bytes 3145732
  377.5 41.8 %copy-start.19 = (bf16[256,1024]{1,0:T(8,128)(2,1)S(1)}, bf16[256,1024]{1,0:T(8,128)(2,1)}, u32[]{:S(2)}) copy-start(bf16[256,1024]{1,0:T(8,128)(2,1)} %get-tuple-element.38) | copy-start | bytes 1572868
  416.7 2.6 copy-start.6
  416.7 2.6 copy-start.8
  416.7 2.6 copy-start.18
  417.2 38.3 %collective-permute-start.13 = (bf16[32,3584]{1,0:T(8,128)(2,1)S(1)}, bf16[32,3584]{1,0:T(8,128)(2,1)S(1)}, u32[]{:S(2)}, u32[]{:S(2)}) collective-permute-start(bf16[32,3584]{1,0:T(8,128)(2,1)S(1)} %slice.197), channel_id=1, source_target_pairs={{0,8},{1,9},{2,10},{3,11},{4,12},{5,13},{6,14},{7,15},{8,0},{9,1},... | collective-permute-start | bytes 688136 | tf_op jit(solution)/shard_map/ppermute | solution.py:38
  431.0 24.5 %copy-start.22 = (pred[256,256]{1,0:T(32,128)(4,1)S(1)}, pred[256,256]{1,0:T(32,128)(4,1)}, u32[]{:S(2)}) copy-start(pred[256,256]{1,0:T(32,128)(4,1)} %get-tuple-element.88) | copy-start | bytes 196612
Sparse Core Ops, SparseCore 0:
  12.3 128.7 all-gather.2
  144.4 118.7 all-gather.4
where the time goes:
time: 474 us; the launch traced here: 467 us
  waiting for transfers between devices  158 us (33%)
  matrix products  139 us (29%)
  local copies, waits for them, and re-layouts  56.6 us (12%)
  starting transfers between devices  47.3 us (10%)
  between operations  44 us (9%)
  other arithmetic  22.9 us (5%)
    all_gather x1, waiting for transfers between devices, local(): spill_grads = lax.all_gather(sent_grads, 'exp', tiled=True)  63 us
    all_gather x1, waiting for transfers between devices, local(): spill_rows = lax.all_gather(place(spill_hot, tokens), 'exp', tiled=True)  62.8 us
    dot_general x3, matrix products, row_gradients(): lax.dot_general(branch, gate_up_matrix, (((1,), (1,)), ((), ())), preferr...  39.9 us
    dot_general x2, matrix products, outer(): lax.dot_general(left, right, (((0,), (0,)), ((), ())), preferred_element_...  33 us
    ppermute x8, waiting for transfers between devices, swap_with(): return lax.ppermute(rows, 'exp', [(i, i ^ mask) for i in range(total)])  31.7 us
    dot_general x3, matrix products, gate_up_of(): jnp.dot(rows_in, matrix, preferred_element_type=jnp.float32)  28.6 us
    all_to_all x4, starting transfers between devices, exchange(): lax.all_to_all(rows.reshape(expert_count, slots // expert_count, width),...  25.6 us
    reshape x1, local copies, waits for them, and re-layouts, local(): gate_up_grads = gate_up_grads.reshape(1, feature_share, 2, hidden_width)  24.4 us
  transfers between devices with their start and end apart: 20, of which 6 were waited for; matrix products, arithmetic and copies ran while one was open for 40% of the time, Pallas kernels for 0%

commit v1 on v0

--- a/solution.py
+++ b/solution.py
@@ -38,23 +38,34 @@
     return lax.ppermute(rows, "exp", [(i, i ^ mask) for i in range(total)])
 
 
-def by_distance(blocks):
-    total = lax.axis_size("exp")
-    order = lax.axis_index("exp") ^ jnp.arange(total, dtype=jnp.int32)
-    return jnp.concatenate(
-        [lax.dynamic_slice_in_dim(blocks, order[k], 1, axis=0) for k in range(total)], axis=0
-    )
-
-
-def collect(blocks):
-    half = lax.axis_size("exp") // 2
-    pairs = [jnp.concatenate([blocks[k], blocks[k + half]], axis=0) for k in range(half)]
-    arrived = [swap_with(pairs[k], k) for k in range(1, half)]
-    total = pairs[0]
-    for pair in arrived:
-        total = total + pair
-    height = blocks.shape[1]
-    return total[:height] + swap_with(total[height:], half)
+def inner_masks(swap):
+    masks = []
+    bit = lax.axis_size("exp") // 4
+    while bit:
+        masks.append(bit)
+        bit //= 2
+    return masks[:-2] + masks[:-3:-1] if swap else masks
+
+
+def swap_quarters(rows):
+    quarter = rows.shape[0] // 4
+    parts = [rows[i * quarter : (i + 1) * quarter] for i in (0, 2, 1, 3)]
+    return jnp.concatenate(parts, axis=0)
+
+
+def spread(rows, swap):
+    for mask in inner_masks(swap):
+        rows = jnp.concatenate([rows, swap_with(rows, mask)], axis=0)
+    return swap_quarters(rows) if swap else rows
+
+
+def collect(rows, swap):
+    if swap:
+        rows = swap_quarters(rows)
+    for mask in reversed(inner_masks(swap)):
+        half = rows.shape[0] // 2
+        rows = rows[:half] + swap_with(rows[half:], mask)
+    return rows
 
 
 def sum_over_grp(part):
@@ -126,43 +137,52 @@
             )
         )
 
-    arrived_0 = exchange(place(chunk_hot[0], both), expert_count)
-    spill_rows = lax.all_gather(place(spill_hot, tokens), "exp", tiled=True)
+    far = expert_count // 2
+    spill_both = place(spill_hot, both)
+    spill_both = jnp.concatenate([spill_both, swap_with(spill_both, far)], axis=0)
+    sent_0 = place(chunk_hot[0], both)
+    spill_both, sent_0 = lax.optimization_barrier((spill_both, sent_0))
+
+    arrived_0 = exchange(sent_0, expert_count)
+    spill_rows, spill_grads = split(spill_both)
+    spill_rows, spill_grads = spread(spill_rows, False), spread(spill_grads, True)
     sent_1 = place(chunk_hot[1], both)
-    sent_grads = place(spill_hot, d_out)
-    arrived_0, spill_rows, sent_1, sent_grads, gate_up_matrix = lax.optimization_barrier(
-        (arrived_0, spill_rows, sent_1, sent_grads, gate_up_matrix)
+    arrived_0, spill_rows, spill_grads, sent_1, gate_up_matrix = lax.optimization_barrier(
+        (arrived_0, spill_rows, spill_grads, sent_1, gate_up_matrix)
     )
 
     arrived_1 = exchange(sent_1, expert_count)
-    spill_grads = lax.all_gather(sent_grads, "exp", tiled=True)
     rows_0, grads_0 = split(arrived_0)
     hidden_0, branch_0 = activate(
         gate_up_of(rows_0, gate_up_matrix), hidden_grads_of(grads_0, down_matrix)
     )
     out_0 = row_gradients(branch_0, gate_up_matrix)
-    gate_up_s = gate_up_of(spill_rows, gate_up_matrix)
-    arrived_1, spill_grads, hidden_0, branch_0, out_0, gate_up_s = lax.optimization_barrier(
-        (arrived_1, spill_grads, hidden_0, branch_0, out_0, gate_up_s)
+    hidden_s, branch_s = activate(
+        gate_up_of(spill_rows, gate_up_matrix), hidden_grads_of(spill_grads, down_matrix)
+    )
+    hidden_s = jnp.where(is_busiest, hidden_s, jnp.zeros_like(hidden_s))
+    branch_s = jnp.where(is_busiest, branch_s, jnp.zeros_like(branch_s))
+    out_s = row_gradients(branch_s, gate_up_matrix)
+    arrived_1, hidden_0, branch_0, out_0, hidden_s, branch_s, out_s = lax.optimization_barrier(
+        (arrived_1, hidden_0, branch_0, out_0, hidden_s, branch_s, out_s)
     )
 
     back_0 = exchange(out_0, expert_count)
+    middle = feature_share // 2
+    back_s = jnp.concatenate(
+        [collect(out_s[:, :middle], False), collect(out_s[:, middle:], True)], axis=1
+    )
     rows_1, grads_1 = split(arrived_1)
     hidden_1, branch_1 = activate(
         gate_up_of(rows_1, gate_up_matrix), hidden_grads_of(grads_1, down_matrix)
     )
     out_1 = row_gradients(branch_1, gate_up_matrix)
-    hidden_s, branch_s = activate(gate_up_s, hidden_grads_of(spill_grads, down_matrix))
-    hidden_s = jnp.where(is_busiest, hidden_s, jnp.zeros_like(hidden_s))
-    branch_s = jnp.where(is_busiest, branch_s, jnp.zeros_like(branch_s))
-    turned = by_distance(branch_s.reshape(expert_count, cap, -1)).reshape(branch_s.shape)
-    out_s = row_gradients(turned, gate_up_matrix)
-    back_0, out_1, out_s, hidden_1, branch_1, hidden_s, branch_s = lax.optimization_barrier(
-        (back_0, out_1, out_s, hidden_1, branch_1, hidden_s, branch_s)
-    )
-
+    back_0, back_s, out_1, hidden_1, branch_1 = lax.optimization_barrier(
+        (back_0, back_s, out_1, hidden_1, branch_1)
+    )
+
+    back_s = back_s[:cap] + swap_with(back_s[cap:], far)
     back_1 = exchange(out_1, expert_count)
-    back_s = collect(out_s.reshape(expert_count, cap, feature_share))
 
     all_rows = jnp.concatenate([spill_rows, rows_0, rows_1], axis=0)
     all_grads = jnp.concatenate([spill_grads, grads_0, grads_1], axis=0)

time: 474 us -> 432 us (0.911)
  between operations: 44 us -> 2.14 us
  waiting for transfers between devices: 158 us -> 135 us
  starting transfers between devices: 47.3 us -> 62 us
  local copies, waits for them, and re-layouts: 56.6 us -> 63.7 us
    all_gather x2 -> x0, waiting for transfers between devices: 126 us -> none  [the longest x1 63 us: local(): spill_grads = lax.all_gather(sent_grads, 'exp', tiled=True)]
    ppermute x8 -> x14, waiting for transfers between devices: 31.7 us -> 135 us  [swap_with(): return lax.ppermute(rows, 'exp', [(i, i ^ mask) for i in range(total)])]
    all_to_all x4, starting transfers between devices: 25.6 us -> 33 us  [exchange(): lax.all_to_all(rows.reshape(expert_count, slots // expert_count, width),...]
    ppermute x8 -> x14, starting transfers between devices: 19.7 us -> 26.9 us  [swap_with(): return lax.ppermute(rows, 'exp', [(i, i ^ mask) for i in range(total)])]
    dot_general x3, matrix products: 39.9 us -> 45.1 us  [row_gradients(): lax.dot_general(branch, gate_up_matrix, (((1,), (1,)), ((), ())), preferr...]
    dot_general x4 -> x3, matrix products: 11.7 us -> 8.71 us  [place(): lax.dot_general(one_hot_rows, rows, (((1,), (0,)), ((), ())), preferred_e...]
    unnamed x73 -> x41, local copies, waits for them, and re-layouts: 19.3 us -> 22 us
  transfers between devices with their start and end apart: 20 -> 24, of which waited for: 6 -> 9; matrix products, arithmetic and copies ran while one was open for 40% -> 50% of each run, Pallas kernels for 0% -> 0%
where the time goes in v1:
time: 432 us; the launch traced here: 426 us
  matrix products  138 us (32%)
  waiting for transfers between devices  135 us (31%)
  local copies, waits for them, and re-layouts  63.7 us (15%)
  starting transfers between devices  62 us (14%)
  other arithmetic  25.8 us (6%)
    ppermute x14, waiting for transfers between devices, swap_with(): return lax.ppermute(rows, 'exp', [(i, i ^ mask) for i in range(total)])  135 us
    dot_general x3, matrix products, row_gradients(): lax.dot_general(branch, gate_up_matrix, (((1,), (1,)), ((), ())), preferr...  45.1 us
    all_to_all x4, starting transfers between devices, exchange(): lax.all_to_all(rows.reshape(expert_count, slots // expert_count, width),...  33 us
    dot_general x2, matrix products, outer(): lax.dot_general(left, right, (((0,), (0,)), ((), ())), preferred_element_...  31.9 us
    dot_general x3, matrix products, gate_up_of(): jnp.dot(rows_in, matrix, preferred_element_type=jnp.float32)  28.4 us
    ppermute x14, starting transfers between devices, swap_with(): return lax.ppermute(rows, 'exp', [(i, i ^ mask) for i in range(total)])  26.9 us
    reshape x1, local copies, waits for them, and re-layouts, local(): gate_up_grads = gate_up_grads.reshape(1, feature_share, 2, hidden_width)  24.4 us
    unnamed x41, local copies, waits for them, and re-layouts  22 us
  transfers between devices with their start and end apart: 24, of which 9 were waited for; matrix products, arithmetic and copies ran while one was open for 50% of the time, Pallas kernels for 0%

profile of v1, /device:TPU:0, one launch (start us, length us, event | category | flops | bytes accessed | tf_op | source)
XLA Modules:
  0.0 425.8 jit_solution(11436032296610084363)
XLA Ops:
  0.7 1.8 constant_dynamic-update-slice_fusion.1
  4.3 4.1 collective-permute-start
  8.4 3.1 convolution_convert_fusion.2
  11.4 17.3 %collective-permute-done = bf16[32,7168]{1,0:T(8,128)(2,1)S(1)} collective-permute-done((bf16[32,7168]{1,0:T(8,128)(2,1)S(1)}, bf16[32,7168]{1,0:T(8,128)(2,1)S(1)}, u32[]{:S(2)}, u32[]{:S(2)}) %collective-permute-start) | collective-permute-done | bytes 458784 | tf_op jit(solution)/shard_map/ppermute | solution.py:38
  28.8 0.9 fusion.64
  30.4 6.7 %all-to-all-start = ((bf16[16,16,7168]{2,1,0:T(8,128)(2,1)}), bf16[16,16,7168]{2,1,0:T(8,128)(2,1)}, u32[]{:S(2)}, u32[]{:S(2)}) async-start(bf16[16,16,7168]{2,1,0:T(8,128)(2,1)} %bitcast.48), calls=%async_computation | async-start | bytes 7340032 | tf_op jit(solution)/shard_map/all_to_all | solution.py:27
  37.1 1.9 collective-permute-start.1
  39.0 17.8 %collective-permute-done.4 = bf16[64,3584]{1,0:T(8,128)(2,1)S(1)} collective-permute-done((bf16[64,3584]{1,0:T(8,128)(2,1)S(1)}, bf16[64,3584]{1,0:T(8,128)(2,1)S(1)}, u32[]{:S(2)}, u32[]{:S(2)}) %collective-permute-start.4) | collective-permute-done | bytes 458784 | tf_op jit(solution)/shard_map/ppermute | solution.py:38
  56.9 1.5 collective-permute-start.5
  58.4 51.4 %collective-permute-done.1 = bf16[64,3584]{1,0:T(8,128)(2,1)S(1)} collective-permute-done((bf16[64,3584]{1,0:T(8,128)(2,1)S(1)}, bf16[64,3584]{1,0:T(8,128)(2,1)S(1)}, u32[]{:S(2)}, u32[]{:S(2)}) %collective-permute-start.1) | collective-permute-done | bytes 458784 | tf_op jit(solution)/shard_map/ppermute | solution.py:38
  109.8 1.0 pad_maximum_fusion.6
  110.8 2.8 collective-permute-start.2
  113.6 1.4 pad_maximum_fusion.2
  115.2 16.0 %copy.8 = bf16[448,8,2,1024]{3,1,2,0:T(8,128)(2,1)} copy(bf16[448,8,2,1024]{3,2,1,0:T(2,128)(2,1)} %bitcast.38) | data formatting | bytes 29360128
  131.9 4.9 %convolution_convert_fusion.1 = bf16[256,7168]{1,0:T(8,128)(2,1)} fusion(bf16[256,7168]{1,0:T(8,128)(2,1)} %copy-done, s32[256]{0:T(256)S(1)} %get-tuple-element.61), kind=kOutput, calls=%fused_computation.1 | convolution fusion | flops 941424640 | bytes 7341056 | tf_op jit(solution)/shard_map/dot_general | solution.py:20
  137.0 2.0 collective-permute-start.3
  139.8 33.1 %collective-permute-done.6 = bf16[256,3584]{1,0:T(8,128)(2,1)} collective-permute-done((bf16[256,3584]{1,0:T(8,128)(2,1)}, bf16[256,3584]{1,0:T(8,128)(2,1)}, u32[]{:S(2)}, u32[]{:S(2)}) %collective-permute-start.6) | collective-permute-done | bytes 1835040 | tf_op jit(solution)/shard_map/ppermute | solution.py:38
  172.9 2.2 slice_dynamic-update-slice_fusion.1
  175.1 1.0 constant_dynamic-update-slice_fusion.2
  176.1 1.7 collective-permute-done.3
  177.9 2.0 pad_maximum_fusion
  179.8 2.2 slice_dynamic-update-slice_fusion
  182.0 9.1 %all-to-all-start.1 = ((bf16[16,16,7168]{2,1,0:T(8,128)(2,1)}), bf16[16,16,7168]{2,1,0:T(8,128)(2,1)}, u32[]{:S(2)}, u32[]{:S(2)}) async-start(bf16[16,16,7168]{2,1,0:T(8,128)(2,1)} %bitcast.47), calls=%async_computation.1 | async-start | bytes 7340032 | tf_op jit(solution)/shard_map/all_to_all | solution.py:27
  191.1 5.9 %fusion.38 = bf16[256,1024]{1,0:T(8,128)(2,1)S(1)} fusion(bf16[1,1024,3584]{2,1,0:T(8,128)(2,1)} %param.9, bf16[256,7168]{1,0:T(8,128)(2,1)} %bitcast.1), kind=kOutput, calls=%fused_computation.58 | convolution fusion | flops 1879310336 | bytes 9699328 | tf_op jit(solution)/shard_map/dot_general | solution.py:135
  197.1 9.8 %convolution_convert_fusion.11 = bf16[256,2048]{1,0:T(8,128)(2,1)S(1)} fusion(bf16[3584,2048]{1,0:T(8,128)(2,1)} %bitcast.39, bf16[256,7168]{1,0:T(8,128)(2,1)} %bitcast.1), kind=kOutput, calls=%fused_computation.40 | convolution fusion | flops 3758620672 | bytes 17563648 | tf_op jit(solution)/shard_map/dot_general | solution.py:131
  206.9 1.1 collective-permute-start.7
  208.1 7.9 %convolution_convert_fusion.9 = bf16[512,2048]{1,0:T(8,128)(2,1)S(1)} fusion(bf16[512,3584]{1,0:T(8,128)(2,1)S(1)} %copy-done.3, bf16[3584,2048]{1,0:T(8,128)(2,1)S(1)} %bitcast.46), kind=kOutput, calls=%fused_computation.38 | convolution fusion | flops 7517241344 | bytes 20447232 | tf_op jit(solution)/shard_map/dot_general | solution.py:131
  216.1 8.2 %fusion.35 = bf16[512,1024]{1,0:T(8,128)(2,1)S(1)} fusion(bf16[512,3584]{1,0:T(8,128)(2,1)} %slice_dynamic-update-slice_fusion, bf16[1,1024,3584]{2,1,0:T(8,128)(2,1)} %param.9), kind=kOutput, calls=%fused_computation.57 | convolution fusion | flops 3758620672 | bytes 12058624 | tf_op jit(solution)/shard_map/dot_general | solution.py:135
  224.8 4.1 fusion.61
  229.4 1.5 multiply_convert_fusion.7
  230.8 16.3 %convolution_convert_fusion.7 = bf16[256,3584]{1,0:T(8,128)(2,1)} fusion(bf16[3584,2048]{1,0:T(8,128)(2,1)} %bitcast.40, bf16[256,1024]{1,0:T(8,128)(2,1)S(1)} %get-tuple-element.54, bf16[256,1024]{1,0:T(8,128)(2,1)S(1)} %get-tuple-element.53), kind=kOutput, calls=%fused_computation.24 | convolution fusion | flops 3761111040 | bytes 17563648 | tf_op jit(solution)/shard_map/dot_general | solution.py:94
  247.1 1.0 pad_maximum_fusion.3
  248.2 2.3 convert_add_fusion
  250.5 2.4 multiply_convert_fusion.1
  253.4 1.6 fusion.44
  255.0 12.7 %convolution_convert_fusion.5 = bf16[512,3584]{1,0:T(8,128)(2,1)} fusion(bf16[512,2048]{1,0:T(8,128)(2,1)S(1)} %maximum_select_fusion, bf16[3584,2048]{1,0:T(8,128)(2,1)} %bitcast.41), kind=kOutput, calls=%fused_computation.22 | convolution fusion | flops 7518027776 | bytes 20447232 | tf_op jit(solution)/shard_map/dot_general | solution.py:94
  267.8 1.7 fusion.63
  269.5 1.0 pad_maximum_fusion.8
  270.5 2.1 collective-permute-start.14
  272.5 10.7 %convolution_convert_fusion.10 = bf16[256,2048]{1,0:T(8,128)(2,1)} fusion(bf16[3584,2048]{1,0:T(8,128)(2,1)} %bitcast.42, bf16[256,7168]{1,0:T(8,128)(2,1)} %bitcast.3), kind=kOutput, calls=%fused_computation.39 | convolution fusion | flops 3758620672 | bytes 17563648 | tf_op jit(solution)/shard_map/dot_general | solution.py:131
  283.2 4.2 fusion.62
  287.4 2.2 slice.113
  289.6 1.5 collective-permute-start.11
  291.1 4.4 %fusion.41 = bf16[256,1024]{1,0:T(8,128)(2,1)} fusion(bf16[1,1024,3584]{2,1,0:T(8,128)(2,1)S(1)} %bitcast.52, bf16[256,7168]{1,0:T(8,128)(2,1)} %bitcast.3), kind=kOutput, calls=%fused_computation.59 | convolution fusion | flops 1879310336 | bytes 9699328 | tf_op jit(solution)/shard_map/dot_general | solution.py:135
  295.5 8.1 %all-to-all-start.2 = ((bf16[16,16,3584]{2,1,0:T(8,128)(2,1)}), bf16[16,16,3584]{2,1,0:T(8,128)(2,1)}, u32[]{:S(2)}, u32[]{:S(2)}) async-start(bf16[16,16,3584]{2,1,0:T(8,128)(2,1)} %bitcast.49), calls=%async_computation.2 | async-start | bytes 3670016 | tf_op jit(solution)/shard_map/all_to_all | solution.py:27
  303.9 1.4 maximum_add_fusion
  306.1 1.6 collective-permute-start.15
  307.8 5.4 %collective-permute-done.11 = bf16[256,1792]{1,0:T(8,128)(2,1)} collective-permute-done((bf16[256,1792]{1,0:T(8,128)(2,1)}, bf16[256,1792]{1,0:T(8,128)(2,1)}, u32[]{:S(2)}, u32[]{:S(2)}) %collective-permute-start.11) | collective-permute-done | bytes 917536 | tf_op jit(solution)/shard_map/ppermute | solution.py:38
  313.2 1.5 slice_add_fusion
  315.8 1.9 convert_add_fusion.1
  317.7 1.4 multiply_convert_fusion.5
  319.2 16.1 %convolution_convert_fusion.6 = bf16[256,3584]{1,0:T(8,128)(2,1)} fusion(bf16[3584,2048]{1,0:T(8,128)(2,1)} %bitcast.43, bf16[256,1024]{1,0:T(8,128)(2,1)S(1)} %get-tuple-element.52, bf16[256,1024]{1,0:T(8,128)(2,1)S(1)} %get-tuple-element.51), kind=kOutput, calls=%fused_computation.23 | convolution fusion | flops 3761111040 | bytes 17563648 | tf_op jit(solution)/shard_map/dot_general | solution.py:94
  335.3 1.1 pad_maximum_fusion.4
  336.5 1.1 slice_add_fusion.1
  337.6 5.5 %collective-permute-start.16 = (bf16[64,1792]{1,0:T(8,128)(2,1)S(1)}, bf16[64,1792]{1,0:T(8,128)(2,1)S(1)}, u32[]{:S(2)}, u32[]{:S(2)}) collective-permute-start(bf16[64,1792]{1,0:T(8,128)(2,1)S(1)} %slice.145), channel_id=1, source_target_pairs={{0,4},{1,5},{2,6},{3,7},{4,0},{5,1},{6,2},{7,3},{8,12},{9,13},{10,... | collective-permute-start | bytes 688136 | tf_op jit(solution)/shard_map/ppermute | solution.py:38
  343.1 1.1 slice_add_fusion.2
  344.3 5.1 %collective-permute-done.16 = bf16[64,1792]{1,0:T(8,128)(2,1)S(1)} collective-permute-done((bf16[64,1792]{1,0:T(8,128)(2,1)S(1)}, bf16[64,1792]{1,0:T(8,128)(2,1)S(1)}, u32[]{:S(2)}, u32[]{:S(2)}) %collective-permute-start.16) | collective-permute-done | bytes 229408 | tf_op jit(solution)/shard_map/ppermute | solution.py:38
  349.4 2.4 collective-permute-done.13
  351.9 9.1 %all-to-all-start.3 = ((bf16[16,16,3584]{2,1,0:T(8,128)(2,1)}), bf16[16,16,3584]{2,1,0:T(8,128)(2,1)}, u32[]{:S(2)}, u32[]{:S(2)}) async-start(bf16[16,16,3584]{2,1,0:T(8,128)(2,1)} %bitcast.50), calls=%async_computation.3 | async-start | bytes 3670016 | tf_op jit(solution)/shard_map/all_to_all | solution.py:27
  361.1 3.0 collective-permute-start.19
  364.1 20.4 %convolution_convert_fusion = bf16[3584,2048]{1,0:T(8,128)(2,1)} fusion(bf16[256,3584]{1,0:T(8,128)(2,1)} %get-tuple-element.46, bf16[256,3584]{1,0:T(8,128)(2,1)} %get-tuple-element.44, bf16[512,3584]{1,0:T(8,128)(2,1)} %pad_maximum_fusion, bf16[256,2048]{1,0:T(8,128)(2,1)} %pad_maximum_fusion.4, bf16[256,2048]{1,0:T(8,128)(2,1)} %pad_maximum_fusion.3, ...), kind=kOutput, calls=%fused_computation | convolution fusion | flops 15074328576 | bytes 26214400 | tf_op jit(solution)/shard_map/dot_general | solution.py:100
  384.5 11.5 %fusion.16 = bf16[1,1024,3584]{2,1,0:T(8,128)(2,1)} fusion(bf16[256,3584]{1,0:T(8,128)(2,1)S(1)} %copy-done.5, bf16[256,3584]{1,0:T(8,128)(2,1)S(1)} %copy-done.4, bf16[512,3584]{1,0:T(8,128)(2,1)} %slice_dynamic-update-slice_fusion, bf16[256,1024]{1,0:T(8,128)(2,1)S(1)} %copy-done.9, bf16[256,1024]{1,0:T(8,128)(2,1)S(1)} %copy-done.8, ...), kind=kOutput, calls=%fused_computation.21 | convolution fusion | flops 7548174336 | bytes 16777216 | tf_op jit(solution)/shard_map/dot_general | solution.py:100
  396.1 24.4 %reshape.61 = bf16[1,3584,2,1024]{3,2,1,0:T(2,128)(2,1)} reshape(bf16[3584,2048]{1,0:T(8,128)(2,1)} %convolution_convert_fusion) | data formatting | bytes 29360128 | tf_op jit(solution)/shard_map/reshape | solution.py:192
  420.5 4.9 %convolution_convert_fusion.8 = bf16[256,3584]{1,0:T(8,128)(2,1)} fusion(bf16[256,3584]{1,0:T(8,128)(2,1)} %bitcast.8, bf16[256,3584]{1,0:T(8,128)(2,1)} %bitcast.6, bf16[32,3584]{1,0:T(8,128)(2,1)S(1)} %slice_add_fusion.5, pred[256,256]{1,0:T(32,128)(4,1)S(1)} %get-tuple-element.64, pred[256,256]{1,0:T(32,128)(4,1)S(1)} %get-tuple-element.65, ...), kind=kOutput, calls=%fused_computation.25 | convolution fusion | flops 1011138560 | bytes 5873664 | tf_op jit(solution)/shard_map/dot_general | solution.py:197
  (84 shorter events, 8.0 us)
Async XLA Ops:
  0.6 1.9 copy-start.11
  0.6 2.7 copy-start.6
  3.6 7.9 %copy-start = (bf16[256,7168]{1,0:T(8,128)(2,1)}, bf16[256,7168]{1,0:T(8,128)(2,1)S(1)}, u32[]{:S(2)}) copy-start(bf16[256,7168]{1,0:T(8,128)(2,1)S(1)} %constant_dynamic-update-slice_fusion) | copy-start | bytes 11010052
  4.3 24.5 %collective-permute-start = (bf16[32,7168]{1,0:T(8,128)(2,1)S(1)}, bf16[32,7168]{1,0:T(8,128)(2,1)S(1)}, u32[]{:S(2)}, u32[]{:S(2)}) collective-permute-start(bf16[32,7168]{1,0:T(8,128)(2,1)S(1)} %convolution_convert_fusion.3), channel_id=1, source_target_pairs={{0,8},{1,9},{2,10},{3,11},{4,12},{5,13},{6,14},{7,15},{8,0},{9,1},... | collective-permute-start | bytes 1376264 | tf_op jit(solution)/shard_map/ppermute | solution.py:38
  29.7 27.1 %collective-permute-start.4 = (bf16[64,3584]{1,0:T(8,128)(2,1)S(1)}, bf16[64,3584]{1,0:T(8,128)(2,1)S(1)}, u32[]{:S(2)}, u32[]{:S(2)}) collective-permute-start(bf16[64,3584]{1,0:T(8,128)(2,1)S(1)} %get-tuple-element.57), channel_id=1, source_target_pairs={{0,4},{1,5},{2,6},{3,7},{4,0},{5,1},{6,2},{7,3},{8,12},{9,13},{10,... | collective-permute-start | bytes 1376264 | tf_op jit(solution)/shard_map/ppermute | solution.py:38
  30.4 151.5 %all-to-all-start = ((bf16[16,16,7168]{2,1,0:T(8,128)(2,1)}), bf16[16,16,7168]{2,1,0:T(8,128)(2,1)}, u32[]{:S(2)}, u32[]{:S(2)}) async-start(bf16[16,16,7168]{2,1,0:T(8,128)(2,1)} %bitcast.48), calls=%async_computation | async-start | bytes 7340032 | tf_op jit(solution)/shard_map/all_to_all | solution.py:27
  37.1 72.7 %collective-permute-start.1 = (bf16[64,3584]{1,0:T(8,128)(2,1)S(1)}, bf16[64,3584]{1,0:T(8,128)(2,1)S(1)}, u32[]{:S(2)}, u32[]{:S(2)}) collective-permute-start(bf16[64,3584]{1,0:T(8,128)(2,1)S(1)} %get-tuple-element.59), channel_id=1, source_target_pairs={{0,4},{1,5},{2,6},{3,7},{4,0},{5,1},{6,2},{7,3},{8,12},{9,13},{10,... | collective-permute-start | bytes 1376264 | tf_op jit(solution)/shard_map/ppermute | solution.py:38
  56.9 56.7 %collective-permute-start.5 = (bf16[128,3584]{1,0:T(8,128)(2,1)S(1)}, bf16[128,3584]{1,0:T(8,128)(2,1)S(1)}, u32[]{:S(2)}, u32[]{:S(2)}) collective-permute-start(bf16[128,3584]{1,0:T(8,128)(2,1)S(1)} %pad_maximum_fusion.7), channel_id=1, source_target_pairs={{0,1},{1,0},{2,3},{3,2},{4,5},{5,4},{6,7},{7,6},{8,9},{9,8},{10,11... | collective-permute-start | bytes 2752520 | tf_op jit(solution)/shard_map/ppermute | solution.py:38
  110.8 26.0 %collective-permute-start.2 = (bf16[128,3584]{1,0:T(8,128)(2,1)}, bf16[128,3584]{1,0:T(8,128)(2,1)S(1)}, u32[]{:S(2)}, u32[]{:S(2)}) collective-permute-start(bf16[128,3584]{1,0:T(8,128)(2,1)} %pad_maximum_fusion.6), channel_id=1, source_target_pairs={{0,2},{1,3},{2,0},{3,1},{4,6},{5,7},{6,4},{7,5},{8,10},{9,11},{10,... | collective-permute-start | bytes 2752520 | tf_op jit(solution)/shard_map/ppermute | solution.py:38
  113.6 1.5 copy-start.1
  115.2 57.8 %collective-permute-start.6 = (bf16[256,3584]{1,0:T(8,128)(2,1)}, bf16[256,3584]{1,0:T(8,128)(2,1)}, u32[]{:S(2)}, u32[]{:S(2)}) collective-permute-start(bf16[256,3584]{1,0:T(8,128)(2,1)} %pad_maximum_fusion.2), channel_id=1, source_target_pairs={{0,2},{1,3},{2,0},{3,1},{4,6},{5,7},{6,4},{7,5},{8,10},{9,11},{10,... | collective-permute-start | bytes 5505032 | tf_op jit(solution)/shard_map/ppermute | solution.py:38
  136.9 38.3 %copy-start.2 = (bf16[128,3584]{1,0:T(8,128)(2,1)S(1)}, bf16[128,3584]{1,0:T(8,128)(2,1)}, u32[]{:S(2)}) copy-start(bf16[128,3584]{1,0:T(8,128)(2,1)} %copy-done.1) | copy-start | bytes 2752516
  137.0 40.9 %collective-permute-start.3 = (bf16[256,3584]{1,0:T(8,128)(2,1)S(1)}, bf16[256,3584]{1,0:T(8,128)(2,1)S(1)}, u32[]{:S(2)}, u32[]{:S(2)}) collective-permute-start(bf16[256,3584]{1,0:T(8,128)(2,1)S(1)} %pad_maximum_fusion.1), channel_id=1, source_target_pairs={{0,1},{1,0},{2,3},{3,2},{4,5},{5,4},{6,7},{7,6},{8,9},{9,8},{10,11... | collective-permute-start | bytes 5505032 | tf_op jit(solution)/shard_map/ppermute | solution.py:38
  182.0 85.8 %all-to-all-start.1 = ((bf16[16,16,7168]{2,1,0:T(8,128)(2,1)}), bf16[16,16,7168]{2,1,0:T(8,128)(2,1)}, u32[]{:S(2)}, u32[]{:S(2)}) async-start(bf16[16,16,7168]{2,1,0:T(8,128)(2,1)} %bitcast.47), calls=%async_computation.1 | async-start | bytes 7340032 | tf_op jit(solution)/shard_map/all_to_all | solution.py:27
  191.1 17.0 %slice-start = ((s8[14680064]{0:T(1024)(128)(4,1)}), s8[4194304]{0:T(1024)(128)(4,1)S(1)}, s32[]{:S(2)}) async-start(s8[14680064]{0:T(1024)(128)(4,1)} %bitcast.44), calls=%async_computation.4 | async-start | bytes 8388608
  191.1 17.0 %slice-start.1 = ((s8[14680064]{0:T(1024)(128)(4,1)}), s8[2097152]{0:T(1024)(128)(4,1)S(1)}, s32[]{:S(2)}) async-start(s8[14680064]{0:T(1024)(128)(4,1)} %bitcast.44), calls=%async_computation.5 | async-start | bytes 4194304
  197.0 11.1 %slice-start.2 = ((s8[14680064]{0:T(1024)(128)(4,1)}), s8[4194304]{0:T(1024)(128)(4,1)S(1)}, s32[]{:S(2)}) async-start(s8[14680064]{0:T(1024)(128)(4,1)} %bitcast.44), calls=%async_computation.6 | async-start | bytes 8388608
  197.0 11.1 %slice-start.3 = ((s8[14680064]{0:T(1024)(128)(4,1)}), s8[4194304]{0:T(1024)(128)(4,1)S(1)}, s32[]{:S(2)}) async-start(s8[14680064]{0:T(1024)(128)(4,1)} %bitcast.44), calls=%async_computation.7 | async-start | bytes 8388608
  197.0 11.1 %copy-start.3 = (bf16[512,3584]{1,0:T(8,128)(2,1)S(1)}, bf16[512,3584]{1,0:T(8,128)(2,1)}, u32[]{:S(2)}) copy-start(bf16[512,3584]{1,0:T(8,128)(2,1)} %pad_maximum_fusion) | copy-start | bytes 11010052
  197.0 32.3 %collective-permute-start.8 = (bf16[256,1024]{1,0:T(8,128)(2,1)S(1)}, bf16[256,1024]{1,0:T(8,128)(2,1)S(1)}, u32[]{:S(2)}, u32[]{:S(2)}) collective-permute-start(bf16[256,1024]{1,0:T(8,128)(2,1)S(1)} %fusion.38), channel_id=1, source_target_pairs={{0,16},{16,0},{1,17},{17,1},{2,18},{18,2},{3,19},{19,3},{4,20},{20... | collective-permute-start | bytes 1572872 | tf_op jit(solution)/shard_map/ppermute | solution.py:74
  206.9 22.1 %collective-permute-start.7 = (bf16[256,2048]{1,0:T(8,128)(2,1)S(1)}, bf16[256,2048]{1,0:T(8,128)(2,1)S(1)}, u32[]{:S(2)}, u32[]{:S(2)}) collective-permute-start(bf16[256,2048]{1,0:T(8,128)(2,1)S(1)} %convolution_convert_fusion.11), channel_id=1, source_target_pairs={{0,16},{16,0},{1,17},{17,1},{2,18},{18,2},{3,19},{19,3},{4,20},{20... | collective-permute-start | bytes 3145736 | tf_op jit(solution)/shard_map/ppermute | solution.py:74
  216.0 32.2 %collective-permute-start.9 = (bf16[512,2048]{1,0:T(8,128)(2,1)S(1)}, bf16[512,2048]{1,0:T(8,128)(2,1)}, u32[]{:S(2)}, u32[]{:S(2)}) collective-permute-start(bf16[512,2048]{1,0:T(8,128)(2,1)S(1)} %convolution_convert_fusion.9), channel_id=1, source_target_pairs={{0,16},{16,0},{1,17},{17,1},{2,18},{18,2},{3,19},{19,3},{4,20},{20... | collective-permute-start | bytes 6291464 | tf_op jit(solution)/shard_map/ppermute | solution.py:74
  224.3 26.2 %collective-permute-start.10 = (bf16[512,1024]{1,0:T(8,128)(2,1)S(1)}, bf16[512,1024]{1,0:T(8,128)(2,1)}, u32[]{:S(2)}, u32[]{:S(2)}) collective-permute-start(bf16[512,1024]{1,0:T(8,128)(2,1)S(1)} %fusion.35), channel_id=1, source_target_pairs={{0,16},{16,0},{1,17},{17,1},{2,18},{18,2},{3,19},{19,3},{4,20},{20... | collective-permute-start | bytes 3145736 | tf_op jit(solution)/shard_map/ppermute | solution.py:74
  267.8 23.4 %slice-start.4 = ((s8[7340032]{0:T(1024)(128)(4,1)}), s8[4194304]{0:T(1024)(128)(4,1)S(1)}, s32[]{:S(2)}) async-start(s8[7340032]{0:T(1024)(128)(4,1)} %bitcast.51), calls=%async_computation.8 | async-start | bytes 8388608
  270.5 20.6 %slice-start.5 = ((s8[7340032]{0:T(1024)(128)(4,1)}), s8[3145728]{0:T(1024)(128)(4,1)S(1)}, s32[]{:S(2)}) async-start(s8[7340032]{0:T(1024)(128)(4,1)} %bitcast.51), calls=%async_computation.9 | async-start | bytes 6291456
  270.5 33.4 %collective-permute-start.14 = (bf16[256,1792]{1,0:T(8,128)(2,1)}, bf16[256,1792]{1,0:T(8,128)(2,1)}, u32[]{:S(2)}, u32[]{:S(2)}) collective-permute-start(bf16[256,1792]{1,0:T(8,128)(2,1)} %pad_maximum_fusion.8), channel_id=1, source_target_pairs={{0,2},{1,3},{2,0},{3,1},{4,6},{5,7},{6,4},{7,5},{8,10},{9,11},{10,... | collective-permute-start | bytes 2752520 | tf_op jit(solution)/shard_map/ppermute | solution.py:38
  289.6 23.6 %collective-permute-start.11 = (bf16[256,1792]{1,0:T(8,128)(2,1)}, bf16[256,1792]{1,0:T(8,128)(2,1)}, u32[]{:S(2)}, u32[]{:S(2)}) collective-permute-start(bf16[256,1792]{1,0:T(8,128)(2,1)} %slice.113), channel_id=1, source_target_pairs={{0,1},{1,0},{2,3},{3,2},{4,5},{5,4},{6,7},{7,6},{8,9},{9,8},{10,11... | collective-permute-start | bytes 2752520 | tf_op jit(solution)/shard_map/ppermute | solution.py:38
  291.1 24.7 %collective-permute-start.18 = (bf16[256,2048]{1,0:T(8,128)(2,1)}, bf16[256,2048]{1,0:T(8,128)(2,1)}, u32[]{:S(2)}, u32[]{:S(2)}) collective-permute-start(bf16[256,2048]{1,0:T(8,128)(2,1)} %convolution_convert_fusion.10), channel_id=1, source_target_pairs={{0,16},{16,0},{1,17},{17,1},{2,18},{18,2},{3,19},{19,3},{4,20},{20... | collective-permute-start | bytes 3145736 | tf_op jit(solution)/shard_map/ppermute | solution.py:74
  295.5 56.4 %all-to-all-start.2 = ((bf16[16,16,3584]{2,1,0:T(8,128)(2,1)}), bf16[16,16,3584]{2,1,0:T(8,128)(2,1)}, u32[]{:S(2)}, u32[]{:S(2)}) async-start(bf16[16,16,3584]{2,1,0:T(8,128)(2,1)} %bitcast.49), calls=%async_computation.2 | async-start | bytes 3670016 | tf_op jit(solution)/shard_map/all_to_all | solution.py:27
  303.6 14.1 %collective-permute-start.17 = (bf16[256,1024]{1,0:T(8,128)(2,1)}, bf16[256,1024]{1,0:T(8,128)(2,1)S(1)}, u32[]{:S(2)}, u32[]{:S(2)}) collective-permute-start(bf16[256,1024]{1,0:T(8,128)(2,1)} %fusion.41), channel_id=1, source_target_pairs={{0,16},{16,0},{1,17},{17,1},{2,18},{18,2},{3,19},{19,3},{4,20},{20... | collective-permute-start | bytes 1572872 | tf_op jit(solution)/shard_map/ppermute | solution.py:74
  306.1 11.6 %copy-start.10 = (bf16[256,1024]{1,0:T(8,128)(2,1)S(1)}, bf16[256,1024]{1,0:T(8,128)(2,1)}, u32[]{:S(2)}) copy-start(bf16[256,1024]{1,0:T(8,128)(2,1)} %fusion.41) | copy-start | bytes 1572868
  306.1 30.4 %collective-permute-start.15 = (bf16[128,1792]{1,0:T(8,128)(2,1)}, bf16[128,1792]{1,0:T(8,128)(2,1)}, u32[]{:S(2)}, u32[]{:S(2)}) collective-permute-start(bf16[128,1792]{1,0:T(8,128)(2,1)} %slice.143), channel_id=1, source_target_pairs={{0,1},{1,0},{2,3},{3,2},{4,5},{5,4},{6,7},{7,6},{8,9},{9,8},{10,11... | collective-permute-start | bytes 1376264 | tf_op jit(solution)/shard_map/ppermute | solution.py:38
  315.6 27.5 %collective-permute-start.12 = (bf16[128,1792]{1,0:T(8,128)(2,1)}, bf16[128,1792]{1,0:T(8,128)(2,1)}, u32[]{:S(2)}, u32[]{:S(2)}) collective-permute-start(bf16[128,1792]{1,0:T(8,128)(2,1)} %slice.139), channel_id=1, source_target_pairs={{0,2},{1,3},{2,0},{3,1},{4,6},{5,7},{6,4},{7,5},{8,10},{9,11},{10,... | collective-permute-start | bytes 1376264 | tf_op jit(solution)/shard_map/ppermute | solution.py:38
  337.6 11.7 %collective-permute-start.16 = (bf16[64,1792]{1,0:T(8,128)(2,1)S(1)}, bf16[64,1792]{1,0:T(8,128)(2,1)S(1)}, u32[]{:S(2)}, u32[]{:S(2)}) collective-permute-start(bf16[64,1792]{1,0:T(8,128)(2,1)S(1)} %slice.145), channel_id=1, source_target_pairs={{0,4},{1,5},{2,6},{3,7},{4,0},{5,1},{6,2},{7,3},{8,12},{9,13},{10,... | collective-permute-start | bytes 688136 | tf_op jit(solution)/shard_map/ppermute | solution.py:38
  344.2 7.6 %collective-permute-start.13 = (bf16[64,1792]{1,0:T(8,128)(2,1)S(1)}, bf16[64,1792]{1,0:T(8,128)(2,1)S(1)}, u32[]{:S(2)}, u32[]{:S(2)}) collective-permute-start(bf16[64,1792]{1,0:T(8,128)(2,1)S(1)} %slice.141), channel_id=1, source_target_pairs={{0,4},{1,5},{2,6},{3,7},{4,0},{5,1},{6,2},{7,3},{8,12},{9,13},{10,... | collective-permute-start | bytes 688136 | tf_op jit(solution)/shard_map/ppermute | solution.py:38
  351.9 68.6 %all-to-all-start.3 = ((bf16[16,16,3584]{2,1,0:T(8,128)(2,1)}), bf16[16,16,3584]{2,1,0:T(8,128)(2,1)}, u32[]{:S(2)}, u32[]{:S(2)}) async-start(bf16[16,16,3584]{2,1,0:T(8,128)(2,1)} %bitcast.50), calls=%async_computation.3 | async-start | bytes 3670016 | tf_op jit(solution)/shard_map/all_to_all | solution.py:27
  361.1 59.4 %collective-permute-start.19 = (bf16[32,3584]{1,0:T(8,128)(2,1)S(1)}, bf16[32,3584]{1,0:T(8,128)(2,1)S(1)}, u32[]{:S(2)}, u32[]{:S(2)}) collective-permute-start(bf16[32,3584]{1,0:T(8,128)(2,1)S(1)} %slice.131), channel_id=1, source_target_pairs={{0,8},{1,9},{2,10},{3,11},{4,12},{5,13},{6,14},{7,15},{8,0},{9,1},... | collective-permute-start | bytes 688136 | tf_op jit(solution)/shard_map/ppermute | solution.py:38
  364.1 20.4 %copy-start.4 = (bf16[256,3584]{1,0:T(8,128)(2,1)S(1)}, bf16[256,3584]{1,0:T(8,128)(2,1)}, u32[]{:S(2)}) copy-start(bf16[256,3584]{1,0:T(8,128)(2,1)} %get-tuple-element.43) | copy-start | bytes 5505028
  364.1 20.4 %copy-start.5 = (bf16[256,3584]{1,0:T(8,128)(2,1)S(1)}, bf16[256,3584]{1,0:T(8,128)(2,1)}, u32[]{:S(2)}) copy-start(bf16[256,3584]{1,0:T(8,128)(2,1)} %get-tuple-element.45) | copy-start | bytes 5505028
  364.1 20.4 %copy-start.7 = (bf16[512,1024]{1,0:T(8,128)(2,1)S(1)}, bf16[512,1024]{1,0:T(8,128)(2,1)}, u32[]{:S(2)}) copy-start(bf16[512,1024]{1,0:T(8,128)(2,1)} %fusion.44) | copy-start | bytes 3145732
  364.1 20.4 %copy-start.8 = (bf16[256,1024]{1,0:T(8,128)(2,1)S(1)}, bf16[256,1024]{1,0:T(8,128)(2,1)}, u32[]{:S(2)}) copy-start(bf16[256,1024]{1,0:T(8,128)(2,1)} %get-tuple-element.39) | copy-start | bytes 1572868
  364.1 20.5 %copy-start.9 = (bf16[256,1024]{1,0:T(8,128)(2,1)S(1)}, bf16[256,1024]{1,0:T(8,128)(2,1)}, u32[]{:S(2)}) copy-start(bf16[256,1024]{1,0:T(8,128)(2,1)} %get-tuple-element.40) | copy-start | bytes 1572868

commit v2 on v1

v2 whole, which is shorter than its diff:
```python
import functools

import jax
import jax.numpy as jnp
from jax import lax
from jax.experimental import pallas as pl
from jax.experimental.layout import Layout, with_layout_constraint
from jax.experimental.pallas import tpu as pltpu
from jax.sharding import PartitionSpec as P

VMEM_BYTES = 48 * 1024 * 1024


def rank_in_expert(row_expert):
    row_count = row_expert.shape[0]
    same = row_expert[:, None] == row_expert[None, :]
    earlier = jnp.arange(row_count)[None, :] < jnp.arange(row_count)[:, None]
    return jnp.sum((same & earlier).astype(jnp.int32), axis=1)


def one_hot(index, total):
    return (index[None, :] == jnp.arange(total, dtype=jnp.int32)[:, None]).astype(jnp.bfloat16)


def place(one_hot_rows, rows):
    return lax.dot_general(
        one_hot_rows, rows, (((1,), (0,)), ((), ())), preferred_element_type=jnp.float32
    ).astype(jnp.bfloat16)


def exchange(rows, expert_count):
    slots, width = rows.shape
    return lax.all_to_all(
        rows.reshape(expert_count, slots // expert_count, width),
        "exp",
        split_axis=0,
        concat_axis=0,
        tiled=True,
    ).reshape(slots, width)


def swap_with(rows, mask):
    total = lax.axis_size("exp")
    return lax.ppermute(rows, "exp", [(i, i ^ mask) for i in range(total)])


def double(rows, mask):
    return jnp.concatenate([rows, swap_with(rows, mask)], axis=0)


def halve(rows, mask):
    half = rows.shape[0] // 2
    return rows[:half] + swap_with(rows[half:], mask)


def outer_masks():
    masks = []
    bit = lax.axis_size("exp") // 2
    while bit > 2:
        masks.append(bit)
        bit //= 2
    return masks


def swap_quarters(rows):
    quarter = rows.shape[0] // 4
    parts = [rows[i * quarter : (i + 1) * quarter] for i in (0, 2, 1, 3)]
    return jnp.concatenate(parts, axis=0)


def spread(rows, swap):
    for mask in (1, 2) if swap else (2, 1):
        rows = double(rows, mask)
    return swap_quarters(rows) if swap else rows


def collect(rows, swap):
    if swap:
        rows = swap_quarters(rows)
    for mask in (2, 1) if swap else (1, 2):
        rows = halve(rows, mask)
    return rows


def block_of(extent, most):
    size = most
    while extent % size:
        size //= 2
    return size


def dot_f32(left, right, left_dim, right_dim):
    return lax.dot_general(
        left, right, (((left_dim,), (right_dim,)), ((), ())), preferred_element_type=jnp.float32
    )


def product_kernel(right_dim, left_ref, right_ref, out_ref):
    out_ref[...] = dot_f32(left_ref[...], right_ref[...], 1, right_dim).astype(out_ref.dtype)


def product(left, column_block, depth, right, transposed):
    height = left.shape[0]
    width = right.shape[0] if transposed else right.shape[1]
    step = block_of(width, 256)
    if transposed:
        right_spec = pl.BlockSpec((step, depth), lambda j: (j, 0))
    else:
        right_spec = pl.BlockSpec((depth, step), lambda j: (0, j))
    return pl.pallas_call(
        functools.partial(product_kernel, 1 if transposed else 0),
        grid=(width // step,),
        in_specs=[pl.BlockSpec((height, depth), lambda j: (0, column_block)), right_spec],
        out_specs=pl.BlockSpec((height, step), lambda j: (0, j)),
        out_shape=jax.ShapeDtypeStruct((height, width), jnp.bfloat16),
        compiler_params=pltpu.CompilerParams(vmem_limit_bytes=VMEM_BYTES),
        cost_estimate=pl.CostEstimate(
            flops=2 * height * depth * width,
            bytes_accessed=2 * (height * depth + depth * width + height * width),
            transcendentals=0,
        ),
    )(left, right)


def pair_over_grp(part):
    if lax.axis_size("grp") == 2:
        return part, lax.ppermute(part, "grp", [(0, 1), (1, 0)])
    return lax.psum(part, "grp"), jnp.zeros_like(part)


def finish_kernel(
    keep_ref, gate_a, gate_b, grad_a, grad_b, matrix_ref, out_ref, hidden_ref, branch_ref
):
    height, width = hidden_ref.shape

    @pl.when(pl.program_id(0) == 0)
    def _():
        keep = keep_ref[0] > 0
        step = block_of(height, 32)

        @pl.loop(0, height // step)
        def _(i):
            here = pl.ds(pl.multiple_of(i * step, step), step)

            def total(one, two, columns):
                return one[here, columns].astype(jnp.float32) + two[here, columns].astype(
                    jnp.float32
                )

            gate_value = total(gate_a, gate_b, pl.ds(0, width))
            upward = total(gate_a, gate_b, pl.ds(width, width))
            hidden_grads = total(grad_a, grad_b, pl.ds(0, width))
            sigmoid_value = jax.nn.sigmoid(gate_value)
            activated = gate_value * sigmoid_value
            gate_slope = sigmoid_value * (1.0 + gate_value * (1.0 - sigmoid_value))

            def put(ref, columns, value):
                ref[here, columns] = jnp.where(keep, value, 0.0).astype(ref.dtype)

            put(hidden_ref, pl.ds(0, width), activated * upward)
            put(branch_ref, pl.ds(0, width), hidden_grads * upward * gate_slope)
            put(branch_ref, pl.ds(width, width), hidden_grads * activated)

    out_ref[...] = dot_f32(branch_ref[...], matrix_ref[...], 1, 1).astype(out_ref.dtype)


def finish(keep, gate_pair, grad_pair, matrix):
    height, width = grad_pair[0].shape
    features = matrix.shape[0]
    step = block_of(features, 512)
    whole = lambda columns: pl.BlockSpec((height, columns), lambda j: (0, 0))
    shape = lambda columns: jax.ShapeDtypeStruct((height, columns), jnp.bfloat16)
    return pl.pallas_call(
        finish_kernel,
        grid=(features // step,),
        in_specs=[
            pl.BlockSpec(memory_space=pltpu.SMEM),
            whole(2 * width),
            whole(2 * width),
            whole(width),
            whole(width),
            pl.BlockSpec((step, 2 * width), lambda j: (j, 0)),
        ],
        out_specs=[
            pl.BlockSpec((height, step), lambda j: (0, j)),
            whole(width),
            whole(2 * width),
        ],
        out_shape=[shape(features), shape(width), shape(2 * width)],
        compiler_params=pltpu.CompilerParams(vmem_limit_bytes=VMEM_BYTES),
        cost_estimate=pl.CostEstimate(
            flops=4 * height * width * features,
            bytes_accessed=4 * width * features + 2 * height * (features + 9 * width),
            transcendentals=height * width,
        ),
    )(keep, *gate_pair, *grad_pair, matrix)


def outer(left, right):
    return lax.dot_general(
        left, right, (((0,), (0,)), ((), ())), preferred_element_type=jnp.float32
    ).astype(jnp.bfloat16)


def local(tokens, d_out, row_expert, w_gate_up, w_down):
    row_count, feature_share = tokens.shape
    hidden_width = w_down.shape[1]
    expert_count = lax.axis_size("exp")
    gate_up_matrix = w_gate_up.reshape(feature_share, 2 * hidden_width)
    down_matrix = w_down.reshape(hidden_width, feature_share)
    cap = 2 * row_count // expert_count
    half = cap // 2

    rank = rank_in_expert(row_expert)
    is_spill = rank >= cap
    busiest = jnp.max(jnp.where(is_spill, row_expert, -1))
    is_busiest = lax.axis_index("exp") == busiest
    spill_hot = one_hot(jnp.where(is_spill, rank - cap, -1), cap)
    chunk_hot = []
    for chunk in range(2):
        inside = (rank >= chunk * half) & (rank < (chunk + 1) * half)
        slot = row_expert * half + rank - chunk * half
        chunk_hot.append(one_hot(jnp.where(inside, slot, -1), expert_count * half))

    both = jnp.concatenate([tokens, d_out], axis=1)

    def split(both_in):
        return both_in[:, :feature_share], both_in[:, feature_share:]

    def step(keep, rows_in, rows_block, grads_in, grads_block):
        gate_pair = pair_over_grp(
            product(rows_in, rows_block, feature_share, gate_up_matrix, False)
        )
        grad_pair = pair_over_grp(
            product(grads_in, grads_block, feature_share, down_matrix, True)
        )
        return finish(keep, gate_pair, grad_pair, gate_up_matrix)

    always = jnp.ones((1,), jnp.int32)
    only_busiest = is_busiest.astype(jnp.int32).reshape(1)

    far = outer_masks()
    spill_both = place(spill_hot, both)
    for mask in far:
        spill_both = double(spill_both, mask)
    sent_0 = place(chunk_hot[0], both)
    spill_both, sent_0 = lax.optimization_barrier((spill_both, sent_0))

    arrived_0 = exchange(sent_0, expert_count)
    spill_rows, spill_grads = split(spill_both)
    spill_rows, spill_grads = spread(spill_rows, False), spread(spill_grads, True)
    sent_1 = place(chunk_hot[1], both)
    arrived_0, spill_rows, spill_grads, sent_1, gate_up_matrix = lax.optimization_barrier(
        (arrived_0, spill_rows, spill_grads, sent_1, gate_up_matrix)
    )

    arrived_1 = exchange(sent_1, expert_count)
    out_0, hidden_0, branch_0 = step(always, arrived_0, 0, arrived_0, 1)
    out_s, hidden_s, branch_s = step(only_busiest, spill_rows, 0, spill_grads, 0)
    rows_0, grads_0 = split(arrived_0)
    arrived_1, out_0, out_s = lax.optimization_barrier((arrived_1, out_0, out_s))

    back_0 = exchange(out_0, expert_count)
    middle = feature_share // 2
    back_s = jnp.concatenate(
        [collect(out_s[:, :middle], False), collect(out_s[:, middle:], True)], axis=1
    )
    out_1, hidden_1, branch_1 = step(always, arrived_1, 0, arrived_1, 1)
    rows_1, grads_1 = split(arrived_1)
    back_0, back_s, out_1 = lax.optimization_barrier((back_0, back_s, out_1))

    back_1 = exchange(out_1, expert_count)
    for mask in reversed(far):
        back_s = halve(back_s, mask)

    all_rows = jnp.concatenate([spill_rows, rows_0, rows_1], axis=0)
    all_grads = jnp.concatenate([spill_grads, grads_0, grads_1], axis=0)
    hidden = jnp.concatenate([hidden_s, hidden_0, hidden_1], axis=0)
    branch = jnp.concatenate([branch_s, branch_0, branch_1], axis=0)
    gate_up_grads = with_layout_constraint(outer(all_rows, branch), Layout((0, 1)))
    gate_up_grads = lax.optimization_barrier(
        gate_up_grads.reshape(feature_share // 8, 8, 2, hidden_width).transpose(0, 2, 1, 3)
    )
    gate_up_grads = gate_up_grads.transpose(0, 2, 1, 3).reshape(
        1, feature_share, 2, hidden_width
    )
    down_grads = outer(hidden, all_grads).reshape(1, hidden_width, feature_share)

    pick = jnp.concatenate([spill_hot] + chunk_hot, axis=0)
    returned = jnp.concatenate([back_s, back_0, back_1], axis=0)
    token_grads = lax.dot_general(
        pick, returned, (((0,), (0,)), ((), ())), preferred_element_type=jnp.float32
    ).astype(jnp.bfloat16)
    return (token_grads, gate_up_grads, down_grads)


def solution(mesh):
    return jax.shard_map(
        local,
        mesh=mesh,
        in_specs=(
            P("exp", "grp"),
            P("exp", "grp"),
            P("exp"),
            P("exp", "grp", None, None),
            P("exp", None, "grp"),
        ),
        out_specs=(P("exp", "grp"), P("exp", "grp", None, None), P("exp", None, "grp")),
        check_vma=False,
    )
```

time: 432 us -> 419 us (0.970)
  matrix products: 138 us -> 42 us
  Pallas kernels: 0 us -> 90.4 us
  other arithmetic: 25.8 us -> 8.05 us
  waiting for transfers between devices: 135 us -> 149 us
    dot_general x9 -> x0, matrix products: 92 us -> none  [the longest x3 45.1 us: row_gradients(): lax.dot_general(branch, gate_up_matrix, (((1,), (1,)), ((), ())), preferr...]
    pallas_call x0 -> x9, Pallas kernels: none -> 90.4 us  [the longest x6 51.5 us: product(): pl.pallas_call(functools.partial(product_kernel, 1 if transposed else 0),...]
    transpose x0 -> x1, local copies, waits for them, and re-layouts: none -> 27.1 us  [local(): gate_up_grads.transpose(0, 2, 1, 3)]
    reshape x1 -> x0, local copies, waits for them, and re-layouts: 24.4 us -> none  [local(): gate_up_grads = gate_up_grads.reshape(1, feature_share, 2, hidden_width)]
    ppermute x14 -> x12, waiting for transfers between devices: 135 us -> 149 us  [swap_with(): return lax.ppermute(rows, 'exp', [(i, i ^ mask) for i in range(total)])]
    add x10 -> x6, other arithmetic: 9.8 us -> 1.66 us  [halve(): return rows[:half] + swap_with(rows[half:], mask)]
    all_to_all x4, starting transfers between devices: 33 us -> 39 us  [exchange(): lax.all_to_all(rows.reshape(expert_count, slots // expert_count, width),...]
    another operation x3 -> x0, other arithmetic: 5.31 us -> none
  transfers between devices with their start and end apart: 24 -> 22, of which waited for: 9 -> 6; matrix products, arithmetic and copies ran while one was open for 50% -> 23% of each run, Pallas kernels for 0% -> 22%
where the time goes in v2:
time: 419 us; the launch traced here: 417 us
  waiting for transfers between devices  149 us (36%)
  Pallas kernels  90.4 us (22%)
  local copies, waits for them, and re-layouts  63.1 us (15%)
  starting transfers between devices  63.1 us (15%)
  matrix products  42 us (10%)
  other arithmetic  8.05 us (2%)
    ppermute x12, waiting for transfers between devices, swap_with(): return lax.ppermute(rows, 'exp', [(i, i ^ mask) for i in range(total)])  149 us
    pallas_call x6, Pallas kernels, product(): pl.pallas_call(functools.partial(product_kernel, 1 if transposed else 0),...  51.5 us
    all_to_all x4, starting transfers between devices, exchange(): lax.all_to_all(rows.reshape(expert_count, slots // expert_count, width),...  39 us
    pallas_call x3, Pallas kernels, finish(): pl.pallas_call(finish_kernel, grid=(features // step,), in_specs=[pl.Bloc...  38.9 us
    dot_general x2, matrix products, outer(): lax.dot_general(left, right, (((0,), (0,)), ((), ())), preferred_element_...  30.4 us
    transpose x1, local copies, waits for them, and re-layouts, local(): gate_up_grads.transpose(0, 2, 1, 3)  27.1 us
    ppermute x12, starting transfers between devices, swap_with(): return lax.ppermute(rows, 'exp', [(i, i ^ mask) for i in range(total)])  22.7 us
    unnamed x30, local copies, waits for them, and re-layouts  22.4 us
  transfers between devices with their start and end apart: 22, of which 6 were waited for; matrix products, arithmetic and copies ran while one was open for 23% of the time, Pallas kernels for 22%

profile of v2, /device:TPU:0, one launch (start us, length us, event | category | flops | bytes accessed | tf_op | source)
XLA Modules:
  0.0 417.0 jit_solution(4990314889946908733)
XLA Ops:
  0.7 1.8 constant_dynamic-update-slice_fusion.1
  2.5 0.2 convert_reduce_fusion
  2.7 0.6 select_reduce_fusion
  3.3 0.2 constant_dynamic-update-slice_fusion
  3.5 0.7 convolution_convert_fusion.3
  4.3 4.1 collective-permute-start
  8.4 20.3 %collective-permute-done = bf16[32,7168]{1,0:T(8,128)(2,1)S(1)} collective-permute-done((bf16[32,7168]{1,0:T(8,128)(2,1)S(1)}, bf16[32,7168]{1,0:T(8,128)(2,1)S(1)}, u32[]{:S(2)}, u32[]{:S(2)}) %collective-permute-start) | collective-permute-done | bytes 458784 | tf_op jit(solution)/shard_map/ppermute | solution.py:44
  28.8 0.8 collective-permute-start.1
  29.6 3.0 convolution_convert_fusion.2
  32.5 17.9 %collective-permute-done.1 = bf16[64,7168]{1,0:T(8,128)(2,1)S(1)} collective-permute-done((bf16[64,7168]{1,0:T(8,128)(2,1)S(1)}, bf16[64,7168]{1,0:T(8,128)(2,1)S(1)}, u32[]{:S(2)}, u32[]{:S(2)}) %collective-permute-start.1) | collective-permute-done | bytes 917536 | tf_op jit(solution)/shard_map/ppermute | solution.py:44
  50.4 0.1 pad_maximum_fusion.2
  50.5 7.6 %all-to-all-start = ((bf16[16,16,7168]{2,1,0:T(8,128)(2,1)}), bf16[16,16,7168]{2,1,0:T(8,128)(2,1)}, u32[]{:S(2)}, u32[]{:S(2)}) async-start(bf16[16,16,7168]{2,1,0:T(8,128)(2,1)} %bitcast.36), calls=%async_computation | async-start | bytes 7340032 | tf_op jit(solution)/shard_map/all_to_all | solution.py:33
  58.1 0.1 fusion.42
  58.2 1.9 collective-permute-start.2
  60.2 1.5 collective-permute-start.4
  61.6 50.0 %collective-permute-done.2 = bf16[128,3584]{1,0:T(8,128)(2,1)S(1)} collective-permute-done((bf16[128,3584]{1,0:T(8,128)(2,1)S(1)}, bf16[128,3584]{1,0:T(8,128)(2,1)S(1)}, u32[]{:S(2)}, u32[]{:S(2)}) %collective-permute-start.2) | collective-permute-done | bytes 917536 | tf_op jit(solution)/shard_map/ppermute | solution.py:44
  111.7 0.1 pad_maximum_fusion.3
  111.8 1.7 collective-permute-start.3
  113.5 0.1 pad_maximum_fusion.4
  113.6 2.5 collective-permute-start.5
  116.1 16.2 %copy.10 = bf16[448,8,2,1024]{3,1,2,0:T(8,128)(2,1)} copy(bf16[448,8,2,1024]{3,2,1,0:T(2,128)(2,1)} %bitcast.32) | data formatting | bytes 29360128
  132.3 3.0 convolution_convert_fusion.1
  135.3 27.2 %collective-permute-done.3 = bf16[256,3584]{1,0:T(8,128)(2,1)S(1)} collective-permute-done((bf16[256,3584]{1,0:T(8,128)(2,1)S(1)}, bf16[256,3584]{1,0:T(8,128)(2,1)S(1)}, u32[]{:S(2)}, u32[]{:S(2)}) %collective-permute-start.3) | collective-permute-done | bytes 1835040 | tf_op jit(solution)/shard_map/ppermute | solution.py:44
  162.5 2.0 pad_maximum_fusion.left_ref
  164.5 0.1 fusion.41
  164.7 2.0 pad_maximum_fusion.1.left_ref
  166.7 10.5 %all-to-all-start.1 = ((bf16[16,16,7168]{2,1,0:T(8,128)(2,1)}), bf16[16,16,7168]{2,1,0:T(8,128)(2,1)}, u32[]{:S(2)}, u32[]{:S(2)}) async-start(bf16[16,16,7168]{2,1,0:T(8,128)(2,1)} %bitcast.35), calls=%async_computation.1 | async-start | bytes 7340032 | tf_op jit(solution)/shard_map/all_to_all | solution.py:33
  178.0 2.0 copy-done.2
  180.0 11.9 %shard_map.79.gate_a = bf16[512,2048]{1,0:T(8,128)(2,1)S(1)} custom-call(bf16[512,3584]{1,0:T(8,128)(2,1)S(1)} %copy-done.2, bf16[3584,2048]{1,0:T(8,128)(2,1)} %bitcast.23), custom_call_target="tpu_custom_call" | custom-call | flops 7516192768 | bytes 20447232 | tf_op jit(solution)/shard_map/pallas_call | solution.py:110
  192.0 11.0 %shard_map.76.gate_a = bf16[256,2048]{1,0:T(8,128)(2,1)S(1)} custom-call(bf16[256,7168]{1,0:T(8,128)(2,1)} %bitcast.1.left_ref, bf16[3584,2048]{1,0:T(8,128)(2,1)} %bitcast.24), custom_call_target="tpu_custom_call" | custom-call | flops 3758096384 | bytes 17563648 | tf_op jit(solution)/shard_map/pallas_call | solution.py:110
  203.1 5.9 %shard_map.77.grad_a = bf16[256,1024]{1,0:T(8,128)(2,1)S(1)} custom-call(bf16[256,7168]{1,0:T(8,128)(2,1)} %bitcast.1.left_ref, bf16[1024,3584]{1,0:T(8,128)(2,1)} %bitcast.29), custom_call_target="tpu_custom_call" | custom-call | flops 1879048192 | bytes 9699328 | tf_op jit(solution)/shard_map/pallas_call | solution.py:110
  209.0 0.5 collective-permute-start.7
  209.6 6.6 %shard_map.80.grad_a = bf16[512,1024]{1,0:T(8,128)(2,1)S(1)} custom-call(bf16[512,3584]{1,0:T(8,128)(2,1)S(1)} %copy-done, bf16[1024,3584]{1,0:T(8,128)(2,1)} %bitcast.30), custom_call_target="tpu_custom_call" | custom-call | flops 3758096384 | bytes 12058624 | tf_op jit(solution)/shard_map/pallas_call | solution.py:110
  216.2 0.1 collective-permute-start.9
  216.3 4.2 %fusion.38 = (bf16[256,3584]{1,0:T(8,128)(2,1)}, bf16[256,3584]{1,0:T(8,128)(2,1)}) fusion(bf16[256,7168]{1,0:T(8,128)(2,1)} %bitcast.1.left_ref), kind=kLoop, calls=%fused_computation.69 | loop fusion | bytes 7340032 | tf_op jit(solution)/shard_map/slice | solution.py:228
  220.5 11.4 %shard_map.78 = (bf16[256,3584]{1,0:T(8,128)(2,1)}, bf16[256,1024]{1,0:T(8,128)(2,1)S(1)}, bf16[256,2048]{1,0:T(8,128)(2,1)S(1)}) custom-call(s32[1]{0:T(128)} %constant.18.clone.1.keep_ref, bf16[256,2048]{1,0:T(8,128)(2,1)S(1)} %shard_map.76.gate_a, bf16[256,2048]{1,0:T(8,128)(2,1)S(1)} %collective-permute-done.6.gate_b, ...), custom_call_target="tpu_custom_call" | custom-call | flops 3758096384 | bytes 21233664 | tf_op jit(solution)/shard_map/pallas_call | solution.py:173
  231.9 16.1 %shard_map.81 = (bf16[512,3584]{1,0:T(8,128)(2,1)}, bf16[512,1024]{1,0:T(8,128)(2,1)S(1)}, bf16[512,2048]{1,0:T(8,128)(2,1)S(1)}) custom-call(s32[1]{0:T(128)} %bitcast.5.keep_ref, bf16[512,2048]{1,0:T(8,128)(2,1)} %copy-done.3, bf16[512,2048]{1,0:T(8,128)(2,1)} %collective-permute-done.8.gate_b, bf16[512,1024]{1,0:T(8,128)(2,1)S(1)} %shard_map.80.grad_a, ...), custom_call_target="tpu_custom_call" | custom-call | flops 7516192768 | bytes 27787264 | tf_op jit(solution)/shard_map/pallas_call | solution.py:173
  248.0 1.3 copy-done.4
  249.3 1.0 copy-done.5
  250.3 1.6 fusion.40
  251.9 2.2 slice.83
  254.1 15.3 %all-to-all-start.2 = ((bf16[16,16,3584]{2,1,0:T(8,128)(2,1)}), bf16[16,16,3584]{2,1,0:T(8,128)(2,1)}, u32[]{:S(2)}, u32[]{:S(2)}) async-start(bf16[16,16,3584]{2,1,0:T(8,128)(2,1)} %bitcast.37), calls=%async_computation.2 | async-start | bytes 3670016 | tf_op jit(solution)/shard_map/all_to_all | solution.py:33
  269.4 1.9 collective-permute-start.12
  271.3 1.5 collective-permute-start.10
  272.8 4.1 fusion.39
  276.9 10.3 %shard_map.82.gate_a = bf16[256,2048]{1,0:T(8,128)(2,1)S(1)} custom-call(bf16[256,7168]{1,0:T(8,128)(2,1)} %bitcast.3.left_ref, bf16[3584,2048]{1,0:T(8,128)(2,1)} %bitcast.27), custom_call_target="tpu_custom_call" | custom-call | flops 3758096384 | bytes 17563648 | tf_op jit(solution)/shard_map/pallas_call | solution.py:110
  287.3 5.8 %shard_map.83.grad_a = bf16[256,1024]{1,0:T(8,128)(2,1)S(1)} custom-call(bf16[256,7168]{1,0:T(8,128)(2,1)} %bitcast.3.left_ref, bf16[1024,3584]{1,0:T(8,128)(2,1)} %bitcast.31), custom_call_target="tpu_custom_call" | custom-call | flops 1879048192 | bytes 9699328 | tf_op jit(solution)/shard_map/pallas_call | solution.py:110
  293.1 0.5 collective-permute-start.15
  293.7 16.4 %collective-permute-done.12 = bf16[256,1792]{1,0:T(8,128)(2,1)S(1)} collective-permute-done((bf16[256,1792]{1,0:T(8,128)(2,1)S(1)}, bf16[256,1792]{1,0:T(8,128)(2,1)S(1)}, u32[]{:S(2)}, u32[]{:S(2)}) %collective-permute-start.12) | collective-permute-done | bytes 917536 | tf_op jit(solution)/shard_map/ppermute | solution.py:44
  310.1 0.2 maximum_add_fusion
  310.4 1.5 collective-permute-start.13
  311.9 1.3 slice_add_fusion
  313.2 0.6 collective-permute-start.11
  313.8 11.4 %shard_map.84 = (bf16[256,3584]{1,0:T(8,128)(2,1)}, bf16[256,1024]{1,0:T(8,128)(2,1)S(1)}, bf16[256,2048]{1,0:T(8,128)(2,1)S(1)}) custom-call(s32[1]{0:T(128)} %constant.18.clone.1.keep_ref, bf16[256,2048]{1,0:T(8,128)(2,1)S(1)} %shard_map.82.gate_a, bf16[256,2048]{1,0:T(8,128)(2,1)S(1)} %collective-permute-done.14.gate_b, ...), custom_call_target="tpu_custom_call" | custom-call | flops 3758096384 | bytes 21233664 | tf_op jit(solution)/shard_map/pallas_call | solution.py:173
  325.3 1.0 pad_maximum_fusion.7
  326.3 5.6 %all-to-all-start.3 = ((bf16[16,16,3584]{2,1,0:T(8,128)(2,1)}), bf16[16,16,3584]{2,1,0:T(8,128)(2,1)}, u32[]{:S(2)}, u32[]{:S(2)}) async-start(bf16[16,16,3584]{2,1,0:T(8,128)(2,1)} %bitcast.38), calls=%async_computation.3 | async-start | bytes 3670016 | tf_op jit(solution)/shard_map/all_to_all | solution.py:33
  331.9 1.1 slice.93
  333.0 1.9 collective-permute-start.16
  335.0 20.3 %convolution_convert_fusion = bf16[3584,2048]{1,0:T(8,128)(2,1)} fusion(bf16[256,3584]{1,0:T(8,128)(2,1)} %get-tuple-element.50, bf16[256,3584]{1,0:T(8,128)(2,1)} %get-tuple-element.48, bf16[512,3584]{1,0:T(8,128)(2,1)} %pad_maximum_fusion.left_ref, bf16[256,2048]{1,0:T(8,128)(2,1)S(1)} %get-tuple-element.43, bf16[256,2048]{1,0:T(8,128)(2,1)S(1)} %get-tuple-element.42, ...), kind=kOutput, calls=%fused_computation | convolution fusion | flops 15074328576 | bytes 26214400 | tf_op jit(solution)/shard_map/dot_general | solution.py:200
  355.3 16.9 %collective-permute-done.16 = bf16[64,3584]{1,0:T(8,128)(2,1)S(1)} collective-permute-done((bf16[64,3584]{1,0:T(8,128)(2,1)S(1)}, bf16[64,3584]{1,0:T(8,128)(2,1)S(1)}, u32[]{:S(2)}, u32[]{:S(2)}) %collective-permute-start.16) | collective-permute-done | bytes 458784 | tf_op jit(solution)/shard_map/ppermute | solution.py:44
  372.2 2.7 collective-permute-start.17
  374.9 10.0 %fusion.10 = bf16[1,1024,3584]{2,1,0:T(8,128)(2,1)} fusion(bf16[256,3584]{1,0:T(8,128)(2,1)S(1)} %copy-done.11, bf16[256,3584]{1,0:T(8,128)(2,1)S(1)} %copy-done.10, bf16[512,3584]{1,0:T(8,128)(2,1)S(1)} %copy-done.1, bf16[256,1024]{1,0:T(8,128)(2,1)S(1)} %get-tuple-element.46, bf16[256,1024]{1,0:T(8,128)(2,1)S(1)} %get-tuple-element.45, ...), kind=kOutput, calls=%fused_computation.15 | convolution fusion | flops 7548174336 | bytes 16777216 | tf_op jit(solution)/shard_map/dot_general | solution.py:200
  385.0 27.1 %copy.9 = bf16[448,8,2,1024]{3,2,1,0:T(2,128)(2,1)} copy(bf16[448,8,2,1024]{3,1,2,0:T(8,128)(2,1)} %bitcast.33) | data formatting | bytes 29360128 | tf_op jit(solution)/shard_map/transpose | solution.py:284
  412.1 4.9 %convolution_convert_fusion.5 = bf16[256,3584]{1,0:T(8,128)(2,1)} fusion(bf16[256,3584]{1,0:T(8,128)(2,1)} %bitcast.9, bf16[256,3584]{1,0:T(8,128)(2,1)} %bitcast.7, bf16[32,3584]{1,0:T(8,128)(2,1)S(1)} %slice_add_fusion.4, pred[256,256]{1,0:T(32,128)(4,1)S(1)} %get-tuple-element.63, pred[256,256]{1,0:T(32,128)(4,1)S(1)} %get-tuple-element.64, ...), kind=kOutput, calls=%fused_computation.16 | convolution fusion | flops 1011138560 | bytes 5873664 | tf_op jit(solution)/shard_map/dot_general | solution.py:291
  (55 shorter events, 0.8 us)
Async XLA Ops:
  0.6 1.9 copy-start.13
  0.6 2.7 copy-start.12
  3.5 29.0 %copy-start.7 = (bf16[256,7168]{1,0:T(8,128)(2,1)}, bf16[256,7168]{1,0:T(8,128)(2,1)S(1)}, u32[]{:S(2)}) copy-start(bf16[256,7168]{1,0:T(8,128)(2,1)S(1)} %constant_dynamic-update-slice_fusion) | copy-start | bytes 11010052
  4.3 24.5 %collective-permute-start = (bf16[32,7168]{1,0:T(8,128)(2,1)S(1)}, bf16[32,7168]{1,0:T(8,128)(2,1)S(1)}, u32[]{:S(2)}, u32[]{:S(2)}) collective-permute-start(bf16[32,7168]{1,0:T(8,128)(2,1)S(1)} %convolution_convert_fusion.3), channel_id=1, source_target_pairs={{0,8},{1,9},{2,10},{3,11},{4,12},{5,13},{6,14},{7,15},{8,0},{9,1},... | collective-permute-start | bytes 1376264 | tf_op jit(solution)/shard_map/ppermute | solution.py:44
  28.8 21.6 %collective-permute-start.1 = (bf16[64,7168]{1,0:T(8,128)(2,1)S(1)}, bf16[64,7168]{1,0:T(8,128)(2,1)S(1)}, u32[]{:S(2)}, u32[]{:S(2)}) collective-permute-start(bf16[64,7168]{1,0:T(8,128)(2,1)S(1)} %pad_maximum_fusion.5), channel_id=1, source_target_pairs={{0,4},{1,5},{2,6},{3,7},{4,0},{5,1},{6,2},{7,3},{8,12},{9,13},{10,... | collective-permute-start | bytes 2752520 | tf_op jit(solution)/shard_map/ppermute | solution.py:44
  50.5 116.1 %all-to-all-start = ((bf16[16,16,7168]{2,1,0:T(8,128)(2,1)}), bf16[16,16,7168]{2,1,0:T(8,128)(2,1)}, u32[]{:S(2)}, u32[]{:S(2)}) async-start(bf16[16,16,7168]{2,1,0:T(8,128)(2,1)} %bitcast.36), calls=%async_computation | async-start | bytes 7340032 | tf_op jit(solution)/shard_map/all_to_all | solution.py:33
  58.2 53.4 %collective-permute-start.2 = (bf16[128,3584]{1,0:T(8,128)(2,1)S(1)}, bf16[128,3584]{1,0:T(8,128)(2,1)S(1)}, u32[]{:S(2)}, u32[]{:S(2)}) collective-permute-start(bf16[128,3584]{1,0:T(8,128)(2,1)S(1)} %get-tuple-element.58), channel_id=1, source_target_pairs={{0,2},{1,3},{2,0},{3,1},{4,6},{5,7},{6,4},{7,5},{8,10},{9,11},{10,... | collective-permute-start | bytes 2752520 | tf_op jit(solution)/shard_map/ppermute | solution.py:44
  60.2 53.3 %collective-permute-start.4 = (bf16[128,3584]{1,0:T(8,128)(2,1)S(1)}, bf16[128,3584]{1,0:T(8,128)(2,1)S(1)}, u32[]{:S(2)}, u32[]{:S(2)}) collective-permute-start(bf16[128,3584]{1,0:T(8,128)(2,1)S(1)} %get-tuple-element.57), channel_id=1, source_target_pairs={{0,1},{1,0},{2,3},{3,2},{4,5},{5,4},{6,7},{7,6},{8,9},{9,8},{10,11... | collective-permute-start | bytes 2752520 | tf_op jit(solution)/shard_map/ppermute | solution.py:44
  111.8 50.7 %collective-permute-start.3 = (bf16[256,3584]{1,0:T(8,128)(2,1)S(1)}, bf16[256,3584]{1,0:T(8,128)(2,1)S(1)}, u32[]{:S(2)}, u32[]{:S(2)}) collective-permute-start(bf16[256,3584]{1,0:T(8,128)(2,1)S(1)} %pad_maximum_fusion.3), channel_id=1, source_target_pairs={{0,1},{1,0},{2,3},{3,2},{4,5},{5,4},{6,7},{7,6},{8,9},{9,8},{10,11... | collective-permute-start | bytes 5505032 | tf_op jit(solution)/shard_map/ppermute | solution.py:44
  113.6 50.9 %collective-permute-start.5 = (bf16[256,3584]{1,0:T(8,128)(2,1)S(1)}, bf16[256,3584]{1,0:T(8,128)(2,1)S(1)}, u32[]{:S(2)}, u32[]{:S(2)}) collective-permute-start(bf16[256,3584]{1,0:T(8,128)(2,1)S(1)} %pad_maximum_fusion.4), channel_id=1, source_target_pairs={{0,2},{1,3},{2,0},{3,1},{4,6},{5,7},{6,4},{7,5},{8,10},{9,11},{10,... | collective-permute-start | bytes 5505032 | tf_op jit(solution)/shard_map/ppermute | solution.py:44
  116.1 16.2 %copy-start.8 = (bf16[256,7168]{1,0:T(8,128)(2,1)S(1)}, bf16[256,7168]{1,0:T(8,128)(2,1)}, u32[]{:S(2)}) copy-start(bf16[256,7168]{1,0:T(8,128)(2,1)} %copy-done.7) | copy-start | bytes 11010052
  166.7 83.7 %all-to-all-start.1 = ((bf16[16,16,7168]{2,1,0:T(8,128)(2,1)}), bf16[16,16,7168]{2,1,0:T(8,128)(2,1)}, u32[]{:S(2)}, u32[]{:S(2)}) async-start(bf16[16,16,7168]{2,1,0:T(8,128)(2,1)} %bitcast.35), calls=%async_computation.1 | async-start | bytes 7340032 | tf_op jit(solution)/shard_map/all_to_all | solution.py:33
  178.0 2.0 copy-start.2
  191.9 11.1 %copy-start.3 = (bf16[512,2048]{1,0:T(8,128)(2,1)}, bf16[512,2048]{1,0:T(8,128)(2,1)S(1)}, u32[]{:S(2)}) copy-start(bf16[512,2048]{1,0:T(8,128)(2,1)S(1)} %shard_map.79.gate_a) | copy-start | bytes 6291460
  191.9 40.0 %collective-permute-start.8 = (bf16[512,2048]{1,0:T(8,128)(2,1)S(1)}, bf16[512,2048]{1,0:T(8,128)(2,1)}, u32[]{:S(2)}, u32[]{:S(2)}) collective-permute-start(bf16[512,2048]{1,0:T(8,128)(2,1)S(1)} %shard_map.79.gate_a), channel_id=1, source_target_pairs={{0,16},{16,0},{1,17},{17,1},{2,18},{18,2},{3,19},{19,3},{4,20},{20... | collective-permute-start | bytes 6291464 | tf_op jit(solution)/shard_map/ppermute | solution.py:127
  203.0 17.5 %collective-permute-start.6 = (bf16[256,2048]{1,0:T(8,128)(2,1)S(1)}, bf16[256,2048]{1,0:T(8,128)(2,1)S(1)}, u32[]{:S(2)}, u32[]{:S(2)}) collective-permute-start(bf16[256,2048]{1,0:T(8,128)(2,1)S(1)} %shard_map.76.gate_a), channel_id=1, source_target_pairs={{0,16},{16,0},{1,17},{17,1},{2,18},{18,2},{3,19},{19,3},{4,20},{20... | collective-permute-start | bytes 3145736 | tf_op jit(solution)/shard_map/ppermute | solution.py:127
  203.1 6.5 %copy-start = (bf16[512,3584]{1,0:T(8,128)(2,1)S(1)}, bf16[512,3584]{1,0:T(8,128)(2,1)}, u32[]{:S(2)}) copy-start(bf16[512,3584]{1,0:T(8,128)(2,1)} %pad_maximum_fusion.1.left_ref) | copy-start | bytes 11010052
  209.0 11.4 %collective-permute-start.7 = (bf16[256,1024]{1,0:T(8,128)(2,1)S(1)}, bf16[256,1024]{1,0:T(8,128)(2,1)S(1)}, u32[]{:S(2)}, u32[]{:S(2)}) collective-permute-start(bf16[256,1024]{1,0:T(8,128)(2,1)S(1)} %shard_map.77.grad_a), channel_id=1, source_target_pairs={{0,16},{16,0},{1,17},{17,1},{2,18},{18,2},{3,19},{19,3},{4,20},{20... | collective-permute-start | bytes 1572872 | tf_op jit(solution)/shard_map/ppermute | solution.py:127
  216.2 15.7 %collective-permute-start.9 = (bf16[512,1024]{1,0:T(8,128)(2,1)S(1)}, bf16[512,1024]{1,0:T(8,128)(2,1)S(1)}, u32[]{:S(2)}, u32[]{:S(2)}) collective-permute-start(bf16[512,1024]{1,0:T(8,128)(2,1)S(1)} %shard_map.80.grad_a), channel_id=1, source_target_pairs={{0,16},{16,0},{1,17},{17,1},{2,18},{18,2},{3,19},{19,3},{4,20},{20... | collective-permute-start | bytes 3145736 | tf_op jit(solution)/shard_map/ppermute | solution.py:127
  248.0 1.3 copy-start.4
  249.3 1.0 copy-start.5
  254.1 72.3 %all-to-all-start.2 = ((bf16[16,16,3584]{2,1,0:T(8,128)(2,1)}), bf16[16,16,3584]{2,1,0:T(8,128)(2,1)}, u32[]{:S(2)}, u32[]{:S(2)}) async-start(bf16[16,16,3584]{2,1,0:T(8,128)(2,1)} %bitcast.37), calls=%async_computation.2 | async-start | bytes 3670016 | tf_op jit(solution)/shard_map/all_to_all | solution.py:33
  269.4 40.7 %collective-permute-start.12 = (bf16[256,1792]{1,0:T(8,128)(2,1)S(1)}, bf16[256,1792]{1,0:T(8,128)(2,1)S(1)}, u32[]{:S(2)}, u32[]{:S(2)}) collective-permute-start(bf16[256,1792]{1,0:T(8,128)(2,1)S(1)} %pad_maximum_fusion.6), channel_id=1, source_target_pairs={{0,2},{1,3},{2,0},{3,1},{4,6},{5,7},{6,4},{7,5},{8,10},{9,11},{10,... | collective-permute-start | bytes 2752520 | tf_op jit(solution)/shard_map/ppermute | solution.py:44
  271.3 40.6 %collective-permute-start.10 = (bf16[256,1792]{1,0:T(8,128)(2,1)}, bf16[256,1792]{1,0:T(8,128)(2,1)S(1)}, u32[]{:S(2)}, u32[]{:S(2)}) collective-permute-start(bf16[256,1792]{1,0:T(8,128)(2,1)} %slice.83), channel_id=1, source_target_pairs={{0,1},{1,0},{2,3},{3,2},{4,5},{5,4},{6,7},{7,6},{8,9},{9,8},{10,11... | collective-permute-start | bytes 2752520 | tf_op jit(solution)/shard_map/ppermute | solution.py:44
  287.3 26.6 %collective-permute-start.14 = (bf16[256,2048]{1,0:T(8,128)(2,1)S(1)}, bf16[256,2048]{1,0:T(8,128)(2,1)S(1)}, u32[]{:S(2)}, u32[]{:S(2)}) collective-permute-start(bf16[256,2048]{1,0:T(8,128)(2,1)S(1)} %shard_map.82.gate_a), channel_id=1, source_target_pairs={{0,16},{16,0},{1,17},{17,1},{2,18},{18,2},{3,19},{19,3},{4,20},{20... | collective-permute-start | bytes 3145736 | tf_op jit(solution)/shard_map/ppermute | solution.py:127
  293.1 20.7 %collective-permute-start.15 = (bf16[256,1024]{1,0:T(8,128)(2,1)S(1)}, bf16[256,1024]{1,0:T(8,128)(2,1)S(1)}, u32[]{:S(2)}, u32[]{:S(2)}) collective-permute-start(bf16[256,1024]{1,0:T(8,128)(2,1)S(1)} %shard_map.83.grad_a), channel_id=1, source_target_pairs={{0,16},{16,0},{1,17},{17,1},{2,18},{18,2},{3,19},{19,3},{4,20},{20... | collective-permute-start | bytes 1572872 | tf_op jit(solution)/shard_map/ppermute | solution.py:127
  310.4 14.9 %collective-permute-start.13 = (bf16[128,1792]{1,0:T(8,128)(2,1)S(1)}, bf16[128,1792]{1,0:T(8,128)(2,1)S(1)}, u32[]{:S(2)}, u32[]{:S(2)}) collective-permute-start(bf16[128,1792]{1,0:T(8,128)(2,1)S(1)} %slice.105), channel_id=1, source_target_pairs={{0,1},{1,0},{2,3},{3,2},{4,5},{5,4},{6,7},{7,6},{8,9},{9,8},{10,11... | collective-permute-start | bytes 1376264 | tf_op jit(solution)/shard_map/ppermute | solution.py:44
  313.2 12.1 %collective-permute-start.11 = (bf16[128,1792]{1,0:T(8,128)(2,1)S(1)}, bf16[128,1792]{1,0:T(8,128)(2,1)S(1)}, u32[]{:S(2)}, u32[]{:S(2)}) collective-permute-start(bf16[128,1792]{1,0:T(8,128)(2,1)S(1)} %slice.103), channel_id=1, source_target_pairs={{0,2},{1,3},{2,0},{3,1},{4,6},{5,7},{6,4},{7,5},{8,10},{9,11},{10,... | collective-permute-start | bytes 1376264 | tf_op jit(solution)/shard_map/ppermute | solution.py:44
  326.3 85.8 %all-to-all-start.3 = ((bf16[16,16,3584]{2,1,0:T(8,128)(2,1)}), bf16[16,16,3584]{2,1,0:T(8,128)(2,1)}, u32[]{:S(2)}, u32[]{:S(2)}) async-start(bf16[16,16,3584]{2,1,0:T(8,128)(2,1)} %bitcast.38), calls=%async_computation.3 | async-start | bytes 3670016 | tf_op jit(solution)/shard_map/all_to_all | solution.py:33
  333.0 39.2 %collective-permute-start.16 = (bf16[64,3584]{1,0:T(8,128)(2,1)S(1)}, bf16[64,3584]{1,0:T(8,128)(2,1)S(1)}, u32[]{:S(2)}, u32[]{:S(2)}) collective-permute-start(bf16[64,3584]{1,0:T(8,128)(2,1)S(1)} %slice.93), channel_id=1, source_target_pairs={{0,4},{1,5},{2,6},{3,7},{4,0},{5,1},{6,2},{7,3},{8,12},{9,13},{10,... | collective-permute-start | bytes 1376264 | tf_op jit(solution)/shard_map/ppermute | solution.py:44
  334.9 37.2 %copy-start.9 = (bf16[128,3584]{1,0:T(8,128)(2,1)S(1)}, bf16[128,3584]{1,0:T(8,128)(2,1)}, u32[]{:S(2)}) copy-start(bf16[128,3584]{1,0:T(8,128)(2,1)} %pad_maximum_fusion.7) | copy-start | bytes 2752516
  334.9 40.0 %copy-start.1 = (bf16[512,3584]{1,0:T(8,128)(2,1)S(1)}, bf16[512,3584]{1,0:T(8,128)(2,1)}, u32[]{:S(2)}) copy-start(bf16[512,3584]{1,0:T(8,128)(2,1)} %pad_maximum_fusion.1.left_ref) | copy-start | bytes 11010052
  334.9 40.0 %copy-start.6 = (bf16[512,1024]{1,0:T(8,128)(2,1)S(1)}, bf16[512,1024]{1,0:T(8,128)(2,1)}, u32[]{:S(2)}) copy-start(bf16[512,1024]{1,0:T(8,128)(2,1)} %copy-done.5) | copy-start | bytes 3145732
  334.9 40.0 %copy-start.10 = (bf16[256,3584]{1,0:T(8,128)(2,1)S(1)}, bf16[256,3584]{1,0:T(8,128)(2,1)}, u32[]{:S(2)}) copy-start(bf16[256,3584]{1,0:T(8,128)(2,1)} %get-tuple-element.47) | copy-start | bytes 5505028
  334.9 40.0 %copy-start.11 = (bf16[256,3584]{1,0:T(8,128)(2,1)S(1)}, bf16[256,3584]{1,0:T(8,128)(2,1)}, u32[]{:S(2)}) copy-start(bf16[256,3584]{1,0:T(8,128)(2,1)} %get-tuple-element.49) | copy-start | bytes 5505028
  372.2 39.8 %collective-permute-start.17 = (bf16[32,3584]{1,0:T(8,128)(2,1)S(1)}, bf16[32,3584]{1,0:T(8,128)(2,1)S(1)}, u32[]{:S(2)}, u32[]{:S(2)}) collective-permute-start(bf16[32,3584]{1,0:T(8,128)(2,1)S(1)} %slice.107), channel_id=1, source_target_pairs={{0,8},{1,9},{2,10},{3,11},{4,12},{5,13},{6,14},{7,15},{8,0},{9,1},... | collective-permute-start | bytes 688136 | tf_op jit(solution)/shard_map/ppermute | solution.py:44

commit v3 on v2

--- a/solution.py
+++ b/solution.py
@@ -48,9 +48,14 @@
     return jnp.concatenate([rows, swap_with(rows, mask)], axis=0)
 
 
+def halves(rows):
+    half = rows.shape[0] // 2
+    return rows[:half], rows[half:]
+
+
 def halve(rows, mask):
-    half = rows.shape[0] // 2
-    return rows[:half] + swap_with(rows[half:], mask)
+    kept, sent = halves(rows)
+    return kept + swap_with(sent, mask)
 
 
 def outer_masks():
@@ -66,20 +71,6 @@
     quarter = rows.shape[0] // 4
     parts = [rows[i * quarter : (i + 1) * quarter] for i in (0, 2, 1, 3)]
     return jnp.concatenate(parts, axis=0)
-
-
-def spread(rows, swap):
-    for mask in (1, 2) if swap else (2, 1):
-        rows = double(rows, mask)
-    return swap_quarters(rows) if swap else rows
-
-
-def collect(rows, swap):
-    if swap:
-        rows = swap_quarters(rows)
-    for mask in (2, 1) if swap else (1, 2):
-        rows = halve(rows, mask)
-    return rows
 
 
 def block_of(extent, most):
@@ -240,38 +231,43 @@
     only_busiest = is_busiest.astype(jnp.int32).reshape(1)
 
     far = outer_masks()
-    spill_both = place(spill_hot, both)
-    for mask in far:
+    spill_both = double(place(spill_hot, both), far[0])
+    spill_both, hot_0 = lax.optimization_barrier((spill_both, chunk_hot[0]))
+
+    arrived_0 = exchange(place(hot_0, both), expert_count)
+    for mask in far[1:]:
         spill_both = double(spill_both, mask)
-    sent_0 = place(chunk_hot[0], both)
-    spill_both, sent_0 = lax.optimization_barrier((spill_both, sent_0))
-
-    arrived_0 = exchange(sent_0, expert_count)
     spill_rows, spill_grads = split(spill_both)
-    spill_rows, spill_grads = spread(spill_rows, False), spread(spill_grads, True)
-    sent_1 = place(chunk_hot[1], both)
-    arrived_0, spill_rows, spill_grads, sent_1, gate_up_matrix = lax.optimization_barrier(
-        (arrived_0, spill_rows, spill_grads, sent_1, gate_up_matrix)
-    )
-
-    arrived_1 = exchange(sent_1, expert_count)
+    spill_rows, spill_grads = double(spill_rows, 2), double(spill_grads, 1)
+    arrived_0, spill_rows, spill_grads, hot_1, gate_up_matrix = lax.optimization_barrier(
+        (arrived_0, spill_rows, spill_grads, chunk_hot[1], gate_up_matrix)
+    )
+
+    arrived_1 = exchange(place(hot_1, both), expert_count)
+    spill_rows, spill_grads = double(spill_rows, 1), swap_quarters(double(spill_grads, 2))
     out_0, hidden_0, branch_0 = step(always, arrived_0, 0, arrived_0, 1)
     out_s, hidden_s, branch_s = step(only_busiest, spill_rows, 0, spill_grads, 0)
     rows_0, grads_0 = split(arrived_0)
-    arrived_1, out_0, out_s = lax.optimization_barrier((arrived_1, out_0, out_s))
+    middle = feature_share // 2
+    kept_a, sent_a = halves(out_s[:, :middle])
+    kept_b, sent_b = halves(swap_quarters(out_s[:, middle:]))
+    arrived_1, out_0, kept_a, sent_a, kept_b, sent_b = lax.optimization_barrier(
+        (arrived_1, out_0, kept_a, sent_a, kept_b, sent_b)
+    )
 
     back_0 = exchange(out_0, expert_count)
-    middle = feature_share // 2
-    back_s = jnp.concatenate(
-        [collect(out_s[:, :middle], False), collect(out_s[:, middle:], True)], axis=1
-    )
+    back_a = kept_a + swap_with(sent_a, 1)
+    back_b = kept_b + swap_with(sent_b, 2)
     out_1, hidden_1, branch_1 = step(always, arrived_1, 0, arrived_1, 1)
+    back_0, back_a, back_b, out_1, arrived_1 = lax.optimization_barrier(
+        (back_0, back_a, back_b, out_1, arrived_1)
+    )
+
+    back_1 = exchange(out_1, expert_count)
+    back_s = jnp.concatenate([halve(back_a, 2), halve(back_b, 1)], axis=1)
+    for mask in reversed(far[1:]):
+        back_s = halve(back_s, mask)
     rows_1, grads_1 = split(arrived_1)
-    back_0, back_s, out_1 = lax.optimization_barrier((back_0, back_s, out_1))
-
-    back_1 = exchange(out_1, expert_count)
-    for mask in reversed(far):
-        back_s = halve(back_s, mask)
 
     all_rows = jnp.concatenate([spill_rows, rows_0, rows_1], axis=0)
     all_grads = jnp.concatenate([spill_grads, grads_0, grads_1], axis=0)
@@ -285,6 +281,11 @@
         1, feature_share, 2, hidden_width
     )
     down_grads = outer(hidden, all_grads).reshape(1, hidden_width, feature_share)
+
+    back_s, gate_up_grads, down_grads = lax.optimization_barrier(
+        (back_s, gate_up_grads, down_grads)
+    )
+    back_s = halve(back_s, far[0])
 
     pick = jnp.concatenate([spill_hot] + chunk_hot, axis=0)
     returned = jnp.concatenate([back_s, back_0, back_1], axis=0)

time: 419 us -> 431 us (1.029)
  waiting for transfers between devices: 149 us -> 170 us
  starting transfers between devices: 63.1 us -> 50.1 us
  local copies, waits for them, and re-layouts: 63.1 us -> 56.8 us
  other arithmetic: 8.05 us -> 13.7 us
    ppermute x12, waiting for transfers between devices: 149 us -> 169 us  [swap_with(): return lax.ppermute(rows, 'exp', [(i, i ^ mask) for i in range(total)])]
    transpose x1, local copies, waits for them, and re-layouts: 27.1 us -> 13.8 us  [local(): gate_up_grads.transpose(0, 2, 1, 3)]
    all_to_all x4, starting transfers between devices: 39 us -> 26.1 us  [exchange(): lax.all_to_all(rows.reshape(expert_count, slots // expert_count, width),...]
    unnamed x30 -> x52, local copies, waits for them, and re-layouts: 22.4 us -> 32.2 us
    slice x3 -> x1, local copies, waits for them, and re-layouts: 8.45 us -> 0.12 us  [split(): return (both_in[:, :feature_share], both_in[:, feature_share:])]
    concatenate x0 -> x2, local copies, waits for them, and re-layouts: none -> 4.32 us  [the longest x1 4.26 us: local(): all_grads = jnp.concatenate([spill_grads, grads_0, grads_1], axis=0)]
  transfers between devices with their start and end apart: 22 -> 22, of which waited for: 6 -> 10; matrix products, arithmetic and copies ran while one was open for 23% -> 23% of each run, Pallas kernels for 22% -> 21%
where the time goes in v3:
time: 431 us; the launch traced here: 429 us
  waiting for transfers between devices  170 us (39%)
  Pallas kernels  92.1 us (21%)
  local copies, waits for them, and re-layouts  56.8 us (13%)
  starting transfers between devices  50.1 us (12%)
  matrix products  45.5 us (11%)
  other arithmetic  13.7 us (3%)
    ppermute x12, waiting for transfers between devices, swap_with(): return lax.ppermute(rows, 'exp', [(i, i ^ mask) for i in range(total)])  169 us
    pallas_call x6, Pallas kernels, product(): pl.pallas_call(functools.partial(product_kernel, 1 if transposed else 0),...  52.6 us
    pallas_call x3, Pallas kernels, finish(): pl.pallas_call(finish_kernel, grid=(features // step,), in_specs=[pl.Bloc...  39.5 us
    dot_general x2, matrix products, outer(): lax.dot_general(left, right, (((0,), (0,)), ((), ())), preferred_element_...  34 us
    unnamed x52, local copies, waits for them, and re-layouts  32.2 us
    all_to_all x4, starting transfers between devices, exchange(): lax.all_to_all(rows.reshape(expert_count, slots // expert_count, width),...  26.1 us
    ppermute x12, starting transfers between devices, swap_with(): return lax.ppermute(rows, 'exp', [(i, i ^ mask) for i in range(total)])  22.8 us
    transpose x1, local copies, waits for them, and re-layouts, local(): gate_up_grads.transpose(0, 2, 1, 3)  13.8 us
  transfers between devices with their start and end apart: 22, of which 10 were waited for; matrix products, arithmetic and copies ran while one was open for 23% of the time, Pallas kernels for 21%

profile of v3, /device:TPU:0, one launch (start us, length us, event | category | flops | bytes accessed | tf_op | source)
XLA Modules:
  0.0 429.4 jit_solution(7329034210410882517)
XLA Ops:
  0.6 1.0 convert_reduce_fusion
  1.6 1.4 select_reduce_fusion
  3.0 1.7 constant_dynamic-update-slice_fusion.1
  5.0 0.7 convolution_convert_fusion.3
  5.7 4.1 collective-permute-start
  9.8 20.3 %collective-permute-done = bf16[32,7168]{1,0:T(8,128)(2,1)S(1)} collective-permute-done((bf16[32,7168]{1,0:T(8,128)(2,1)S(1)}, bf16[32,7168]{1,0:T(8,128)(2,1)S(1)}, u32[]{:S(2)}, u32[]{:S(2)}) %collective-permute-start) | collective-permute-done | bytes 458784 | tf_op jit(solution)/shard_map/ppermute | solution.py:44
  30.2 2.9 convolution_convert_fusion.2
  33.1 6.8 %all-to-all-start = ((bf16[16,16,7168]{2,1,0:T(8,128)(2,1)}), bf16[16,16,7168]{2,1,0:T(8,128)(2,1)}, u32[]{:S(2)}, u32[]{:S(2)}) async-start(bf16[16,16,7168]{2,1,0:T(8,128)(2,1)} %bitcast.36), calls=%async_computation | async-start | bytes 7340032 | tf_op jit(solution)/shard_map/all_to_all | solution.py:33
  40.0 1.9 collective-permute-start.1
  41.9 79.1 %collective-permute-done.1 = bf16[64,7168]{1,0:T(8,128)(2,1)S(1)} collective-permute-done((bf16[64,7168]{1,0:T(8,128)(2,1)S(1)}, bf16[64,7168]{1,0:T(8,128)(2,1)S(1)}, u32[]{:S(2)}, u32[]{:S(2)}) %collective-permute-start.1) | collective-permute-done | bytes 917536 | tf_op jit(solution)/shard_map/ppermute | solution.py:44
  121.2 1.5 collective-permute-start.3
  122.7 3.5 collective-permute-start.2
  126.2 16.0 %copy.10 = bf16[448,8,2,1024]{3,1,2,0:T(8,128)(2,1)} copy(bf16[448,8,2,1024]{3,2,1,0:T(2,128)(2,1)} %bitcast.37) | data formatting | bytes 29360128
  142.6 1.3 pad_maximum_fusion.3
  143.9 1.6 collective-permute-done.2
  145.6 1.4 pad_maximum_fusion.2
  147.3 3.0 collective-permute-start.8
  150.3 10.3 %shard_map.76.gate_a = bf16[256,2048]{1,0:T(8,128)(2,1)S(1)} custom-call(bf16[256,7168]{1,0:T(8,128)(2,1)} %bitcast.1.left_ref, bf16[3584,2048]{1,0:T(8,128)(2,1)} %bitcast.26), custom_call_target="tpu_custom_call" | custom-call | flops 3758096384 | bytes 17563648 | tf_op jit(solution)/shard_map/pallas_call | solution.py:101
  160.7 3.0 convolution_convert_fusion.1
  163.7 4.5 %all-to-all-start.1 = ((bf16[16,16,7168]{2,1,0:T(8,128)(2,1)}), bf16[16,16,7168]{2,1,0:T(8,128)(2,1)}, u32[]{:S(2)}, u32[]{:S(2)}) async-start(bf16[16,16,7168]{2,1,0:T(8,128)(2,1)} %bitcast.35), calls=%async_computation.1 | async-start | bytes 7340032 | tf_op jit(solution)/shard_map/all_to_all | solution.py:33
  168.2 1.2 constant_dynamic-update-slice_fusion.7
  169.5 20.7 %collective-permute-done.6 = bf16[256,3584]{1,0:T(8,128)(2,1)} collective-permute-done((bf16[256,3584]{1,0:T(8,128)(2,1)}, bf16[256,3584]{1,0:T(8,128)(2,1)}, u32[]{:S(2)}, u32[]{:S(2)}) %collective-permute-start.6) | collective-permute-done | bytes 1835040 | tf_op jit(solution)/shard_map/ppermute | solution.py:44
  190.2 2.3 pad_maximum_fusion.left_ref
  192.5 12.9 %shard_map.79.gate_a = bf16[512,2048]{1,0:T(8,128)(2,1)} custom-call(bf16[512,3584]{1,0:T(8,128)(2,1)S(1)} %pad_maximum_fusion.left_ref, bf16[3584,2048]{1,0:T(8,128)(2,1)} %bitcast.27), custom_call_target="tpu_custom_call" | custom-call | flops 7516192768 | bytes 20447232 | tf_op jit(solution)/shard_map/pallas_call | solution.py:101
  205.4 10.3 %collective-permute-done.8 = bf16[256,3584]{1,0:T(8,128)(2,1)} collective-permute-done((bf16[256,3584]{1,0:T(8,128)(2,1)}, bf16[256,3584]{1,0:T(8,128)(2,1)}, u32[]{:S(2)}, u32[]{:S(2)}) %collective-permute-start.8) | collective-permute-done | bytes 1835040 | tf_op jit(solution)/shard_map/ppermute | solution.py:44
  215.7 1.2 constant_dynamic-update-slice_fusion.6
  217.0 1.7 constant_dynamic-update-slice_fusion.5
  218.7 1.7 constant_dynamic-update-slice_fusion.4
  220.7 2.6 copy-done.17
  223.2 7.4 %shard_map.80.grad_a = bf16[512,1024]{1,0:T(8,128)(2,1)} custom-call(bf16[512,3584]{1,0:T(8,128)(2,1)S(1)} %pad_maximum_fusion.1.left_ref, bf16[1024,3584]{1,0:T(8,128)(2,1)} %bitcast.32), custom_call_target="tpu_custom_call" | custom-call | flops 3758096384 | bytes 12058624 | tf_op jit(solution)/shard_map/pallas_call | solution.py:101
  230.6 5.8 %shard_map.77.grad_a = bf16[256,1024]{1,0:T(8,128)(2,1)S(1)} custom-call(bf16[256,7168]{1,0:T(8,128)(2,1)} %bitcast.1.left_ref, bf16[1024,3584]{1,0:T(8,128)(2,1)} %bitcast.33), custom_call_target="tpu_custom_call" | custom-call | flops 1879048192 | bytes 9699328 | tf_op jit(solution)/shard_map/pallas_call | solution.py:101
  237.6 0.9 collective-permute-done.5.grad_b
  238.5 11.4 %shard_map.78 = (bf16[256,3584]{1,0:T(8,128)(2,1)}, bf16[256,1024]{1,0:T(8,128)(2,1)S(1)}, bf16[256,2048]{1,0:T(8,128)(2,1)S(1)}) custom-call(s32[1]{0:T(128)} %constant.18.clone.1.keep_ref, bf16[256,2048]{1,0:T(8,128)(2,1)S(1)} %shard_map.76.gate_a, bf16[256,2048]{1,0:T(8,128)(2,1)S(1)} %collective-permute-done.4.gate_b, ...), custom_call_target="tpu_custom_call" | custom-call | flops 3758096384 | bytes 21233664 | tf_op jit(solution)/shard_map/pallas_call | solution.py:164
  249.9 1.0 copy-done
  250.9 0.8 copy-done.2
  251.7 16.7 %shard_map.81 = (bf16[512,3584]{1,0:T(8,128)(2,1)}, bf16[512,1024]{1,0:T(8,128)(2,1)S(1)}, bf16[512,2048]{1,0:T(8,128)(2,1)S(1)}) custom-call(s32[1]{0:T(128)} %bitcast.5.keep_ref, bf16[512,2048]{1,0:T(8,128)(2,1)} %shard_map.79.gate_a, bf16[512,2048]{1,0:T(8,128)(2,1)} %collective-permute-done.7.gate_b, bf16[512,1024]{1,0:T(8,128)(2,1)} %shard_map.80.grad_a, ...), custom_call_target="tpu_custom_call" | custom-call | flops 7516192768 | bytes 27787264 | tf_op jit(solution)/shard_map/pallas_call | solution.py:164
  268.4 2.4 fusion.38
  270.8 1.0 pad_maximum_fusion.5
  271.8 1.1 fusion.39
  272.9 5.7 %all-to-all-start.2 = ((bf16[16,16,3584]{2,1,0:T(8,128)(2,1)}), bf16[16,16,3584]{2,1,0:T(8,128)(2,1)}, u32[]{:S(2)}, u32[]{:S(2)}) async-start(bf16[16,16,3584]{2,1,0:T(8,128)(2,1)} %bitcast.42), calls=%async_computation.2 | async-start | bytes 3670016 | tf_op jit(solution)/shard_map/all_to_all | solution.py:33
  278.6 10.3 %shard_map.82.gate_a = bf16[256,2048]{1,0:T(8,128)(2,1)S(1)} custom-call(bf16[256,7168]{1,0:T(8,128)(2,1)} %bitcast.3.left_ref, bf16[3584,2048]{1,0:T(8,128)(2,1)} %bitcast.30), custom_call_target="tpu_custom_call" | custom-call | flops 3758096384 | bytes 17563648 | tf_op jit(solution)/shard_map/pallas_call | solution.py:101
  289.0 5.9 %shard_map.83.grad_a = bf16[256,1024]{1,0:T(8,128)(2,1)S(1)} custom-call(bf16[256,7168]{1,0:T(8,128)(2,1)} %bitcast.3.left_ref, bf16[1024,3584]{1,0:T(8,128)(2,1)} %bitcast.34), custom_call_target="tpu_custom_call" | custom-call | flops 1879048192 | bytes 9699328 | tf_op jit(solution)/shard_map/pallas_call | solution.py:101
  295.4 1.9 collective-permute-start.11
  297.2 1.5 collective-permute-start.10
  298.7 4.1 slice_dynamic-update-slice_fusion.1
  302.8 22.3 %collective-permute-done.11 = bf16[256,1792]{1,0:T(8,128)(2,1)S(1)} collective-permute-done((bf16[256,1792]{1,0:T(8,128)(2,1)S(1)}, bf16[256,1792]{1,0:T(8,128)(2,1)S(1)}, u32[]{:S(2)}, u32[]{:S(2)}) %collective-permute-start.11) | collective-permute-done | bytes 917536 | tf_op jit(solution)/shard_map/ppermute | solution.py:44
  325.2 1.2 add.30
  326.3 4.8 %collective-permute-done.10 = bf16[256,1792]{1,0:T(8,128)(2,1)S(1)} collective-permute-done((bf16[256,1792]{1,0:T(8,128)(2,1)S(1)}, bf16[256,1792]{1,0:T(8,128)(2,1)S(1)}, u32[]{:S(2)}, u32[]{:S(2)}) %collective-permute-start.10) | collective-permute-done | bytes 917536 | tf_op jit(solution)/shard_map/ppermute | solution.py:44
  331.1 1.2 add.29
  332.3 11.5 %shard_map.84 = (bf16[256,3584]{1,0:T(8,128)(2,1)}, bf16[256,1024]{1,0:T(8,128)(2,1)S(1)}, bf16[256,2048]{1,0:T(8,128)(2,1)S(1)}) custom-call(s32[1]{0:T(128)} %constant.18.clone.1.keep_ref, bf16[256,2048]{1,0:T(8,128)(2,1)S(1)} %shard_map.82.gate_a, bf16[256,2048]{1,0:T(8,128)(2,1)S(1)} %collective-permute-done.12.gate_b, ...), custom_call_target="tpu_custom_call" | custom-call | flops 3758096384 | bytes 21233664 | tf_op jit(solution)/shard_map/pallas_call | solution.py:164
  343.8 1.8 slice.97
  345.6 0.8 slice.99
  346.4 0.7 collective-permute-start.15
  347.1 9.0 %all-to-all-start.3 = ((bf16[16,16,3584]{2,1,0:T(8,128)(2,1)}), bf16[16,16,3584]{2,1,0:T(8,128)(2,1)}, u32[]{:S(2)}, u32[]{:S(2)}) async-start(bf16[16,16,3584]{2,1,0:T(8,128)(2,1)} %bitcast.43), calls=%async_computation.3 | async-start | bytes 3670016 | tf_op jit(solution)/shard_map/all_to_all | solution.py:33
  356.1 4.3 slice_dynamic-update-slice_fusion
  360.4 20.9 %convolution_convert_fusion = bf16[3584,2048]{1,0:T(8,128)(2,1)} fusion(bf16[256,3584]{1,0:T(8,128)(2,1)} %get-tuple-element.64, bf16[256,3584]{1,0:T(8,128)(2,1)} %get-tuple-element.66, bf16[256,3584]{1,0:T(8,128)(2,1)} %collective-permute-done.6, bf16[256,3584]{1,0:T(8,128)(2,1)} %pad_maximum_fusion.2, bf16[256,2048]{1,0:T(8,128)(2,1)S(1)} %get-tuple-element.54, ...), kind=kOutput, calls=%fused_computation | convolution fusion | flops 15081668608 | bytes 26214400 | tf_op jit(solution)/shard_map/dot_general | solution.py:191
  381.3 1.3 slice_add_fusion.1
  382.5 1.1 slice_add_fusion
  383.7 1.9 collective-permute-start.16
  385.6 13.1 %fusion.7 = bf16[1,1024,3584]{2,1,0:T(8,128)(2,1)} fusion(bf16[1024,3584]{1,0:T(8,128)(2,1)} %get-tuple-element.63, bf16[256,1024]{1,0:T(8,128)(2,1)S(1)} %get-tuple-element.57, bf16[256,1024]{1,0:T(8,128)(2,1)S(1)} %copy-done.3, bf16[512,1024]{1,0:T(8,128)(2,1)S(1)} %get-tuple-element.55), kind=kOutput, calls=%fused_computation.12 | convolution fusion | flops 7526154240 | bytes 16777216 | tf_op jit(solution)/shard_map/dot_general | solution.py:191
  398.8 13.8 %copy.9 = bf16[448,8,2,1024]{3,2,1,0:T(2,128)(2,1)} copy(bf16[448,8,2,1024]{3,1,2,0:T(8,128)(2,1)S(1)} %bitcast.41) | data formatting | bytes 29360128 | tf_op jit(solution)/shard_map/transpose | solution.py:280
  412.7 2.4 collective-permute-start.17
  415.2 9.2 %collective-permute-done.17 = bf16[32,3584]{1,0:T(8,128)(2,1)S(1)} collective-permute-done((bf16[32,3584]{1,0:T(8,128)(2,1)S(1)}, bf16[32,3584]{1,0:T(8,128)(2,1)S(1)}, u32[]{:S(2)}, u32[]{:S(2)}) %collective-permute-start.17) | collective-permute-done | bytes 229408 | tf_op jit(solution)/shard_map/ppermute | solution.py:44
  424.5 4.9 %convolution_convert_fusion.5 = bf16[256,3584]{1,0:T(8,128)(2,1)} fusion(bf16[256,3584]{1,0:T(8,128)(2,1)} %bitcast.14, bf16[256,3584]{1,0:T(8,128)(2,1)} %bitcast.7, bf16[32,3584]{1,0:T(8,128)(2,1)S(1)} %slice_add_fusion.2, bf16[256,256]{1,0:T(8,128)(2,1)S(1)} %copy-done.16, bf16[256,256]{1,0:T(8,128)(2,1)S(1)} %copy-done.14, bf16[32,256]{1,0:T(8,128)(2,1)S(1)} %fusion.33), kind=kOutput, calls=%fused_computation.13 | convolution fusion | flops 1011695616 | bytes 6012928 | tf_op jit(solution)/shard_map/dot_general | solution.py:292
  (76 shorter events, 3.0 us)
Async XLA Ops:
  0.6 4.1 copy-start.10
  5.0 28.1 %copy-start.6 = (bf16[256,7168]{1,0:T(8,128)(2,1)}, bf16[256,7168]{1,0:T(8,128)(2,1)S(1)}, u32[]{:S(2)}) copy-start(bf16[256,7168]{1,0:T(8,128)(2,1)S(1)} %constant_dynamic-update-slice_fusion) | copy-start | bytes 11010052
  5.7 24.5 %collective-permute-start = (bf16[32,7168]{1,0:T(8,128)(2,1)S(1)}, bf16[32,7168]{1,0:T(8,128)(2,1)S(1)}, u32[]{:S(2)}, u32[]{:S(2)}) collective-permute-start(bf16[32,7168]{1,0:T(8,128)(2,1)S(1)} %convolution_convert_fusion.3), channel_id=1, source_target_pairs={{0,8},{1,9},{2,10},{3,11},{4,12},{5,13},{6,14},{7,15},{8,0},{9,1},... | collective-permute-start | bytes 1376264 | tf_op jit(solution)/shard_map/ppermute | solution.py:44
  9.8 23.3 %copy-start.13 = (bf16[256,256]{1,0:T(8,128)(2,1)}, bf16[256,256]{1,0:T(8,128)(2,1)S(1)}, u32[]{:S(2)}) copy-start(bf16[256,256]{1,0:T(8,128)(2,1)S(1)} %fusion.31) | copy-start | bytes 393220
  33.1 113.8 %all-to-all-start = ((bf16[16,16,7168]{2,1,0:T(8,128)(2,1)}), bf16[16,16,7168]{2,1,0:T(8,128)(2,1)}, u32[]{:S(2)}, u32[]{:S(2)}) async-start(bf16[16,16,7168]{2,1,0:T(8,128)(2,1)} %bitcast.36), calls=%async_computation | async-start | bytes 7340032 | tf_op jit(solution)/shard_map/all_to_all | solution.py:33
  40.0 81.0 %collective-permute-start.1 = (bf16[64,7168]{1,0:T(8,128)(2,1)S(1)}, bf16[64,7168]{1,0:T(8,128)(2,1)S(1)}, u32[]{:S(2)}, u32[]{:S(2)}) collective-permute-start(bf16[64,7168]{1,0:T(8,128)(2,1)S(1)} %pad_maximum_fusion.4), channel_id=1, source_target_pairs={{0,4},{1,5},{2,6},{3,7},{4,0},{5,1},{6,2},{7,3},{8,12},{9,13},{10,... | collective-permute-start | bytes 2752520 | tf_op jit(solution)/shard_map/ppermute | solution.py:44
  121.2 21.4 %collective-permute-start.3 = (bf16[128,3584]{1,0:T(8,128)(2,1)S(1)}, bf16[128,3584]{1,0:T(8,128)(2,1)S(1)}, u32[]{:S(2)}, u32[]{:S(2)}) collective-permute-start(bf16[128,3584]{1,0:T(8,128)(2,1)S(1)} %get-tuple-element.79), channel_id=1, source_target_pairs={{0,1},{1,0},{2,3},{3,2},{4,5},{5,4},{6,7},{7,6},{8,9},{9,8},{10,11... | collective-permute-start | bytes 2752520 | tf_op jit(solution)/shard_map/ppermute | solution.py:44
  122.7 22.8 %collective-permute-start.2 = (bf16[128,3584]{1,0:T(8,128)(2,1)S(1)}, bf16[128,3584]{1,0:T(8,128)(2,1)S(1)}, u32[]{:S(2)}, u32[]{:S(2)}) collective-permute-start(bf16[128,3584]{1,0:T(8,128)(2,1)S(1)} %get-tuple-element.80), channel_id=1, source_target_pairs={{0,2},{1,3},{2,0},{3,1},{4,6},{5,7},{6,4},{7,5},{8,10},{9,11},{10,... | collective-permute-start | bytes 2752520 | tf_op jit(solution)/shard_map/ppermute | solution.py:44
  142.3 18.4 %copy-start.15 = (bf16[256,256]{1,0:T(8,128)(2,1)}, bf16[256,256]{1,0:T(8,128)(2,1)S(1)}, u32[]{:S(2)}) copy-start(bf16[256,256]{1,0:T(8,128)(2,1)S(1)} %fusion.32) | copy-start | bytes 393220
  146.9 13.8 %copy-start.7 = (bf16[256,7168]{1,0:T(8,128)(2,1)S(1)}, bf16[256,7168]{1,0:T(8,128)(2,1)}, u32[]{:S(2)}) copy-start(bf16[256,7168]{1,0:T(8,128)(2,1)} %copy-done.6) | copy-start | bytes 11010052
  146.9 43.3 %collective-permute-start.6 = (bf16[256,3584]{1,0:T(8,128)(2,1)}, bf16[256,3584]{1,0:T(8,128)(2,1)}, u32[]{:S(2)}, u32[]{:S(2)}) collective-permute-start(bf16[256,3584]{1,0:T(8,128)(2,1)} %pad_maximum_fusion.2), channel_id=1, source_target_pairs={{0,1},{1,0},{2,3},{3,2},{4,5},{5,4},{6,7},{7,6},{8,9},{9,8},{10,11... | collective-permute-start | bytes 5505032 | tf_op jit(solution)/shard_map/ppermute | solution.py:44
  147.3 68.4 %collective-permute-start.8 = (bf16[256,3584]{1,0:T(8,128)(2,1)}, bf16[256,3584]{1,0:T(8,128)(2,1)}, u32[]{:S(2)}, u32[]{:S(2)}) collective-permute-start(bf16[256,3584]{1,0:T(8,128)(2,1)} %pad_maximum_fusion.3), channel_id=1, source_target_pairs={{0,2},{1,3},{2,0},{3,1},{4,6},{5,7},{6,4},{7,5},{8,10},{9,11},{10,... | collective-permute-start | bytes 5505032 | tf_op jit(solution)/shard_map/ppermute | solution.py:44
  160.6 77.9 %collective-permute-start.4 = (bf16[256,2048]{1,0:T(8,128)(2,1)S(1)}, bf16[256,2048]{1,0:T(8,128)(2,1)S(1)}, u32[]{:S(2)}, u32[]{:S(2)}) collective-permute-start(bf16[256,2048]{1,0:T(8,128)(2,1)S(1)} %shard_map.76.gate_a), channel_id=1, source_target_pairs={{0,16},{16,0},{1,17},{17,1},{2,18},{18,2},{3,19},{19,3},{4,20},{20... | collective-permute-start | bytes 3145736 | tf_op jit(solution)/shard_map/ppermute | solution.py:118
  163.7 109.2 %all-to-all-start.1 = ((bf16[16,16,7168]{2,1,0:T(8,128)(2,1)}), bf16[16,16,7168]{2,1,0:T(8,128)(2,1)}, u32[]{:S(2)}, u32[]{:S(2)}) async-start(bf16[16,16,7168]{2,1,0:T(8,128)(2,1)} %bitcast.35), calls=%async_computation.1 | async-start | bytes 7340032 | tf_op jit(solution)/shard_map/all_to_all | solution.py:33
  205.4 46.3 %collective-permute-start.7 = (bf16[512,2048]{1,0:T(8,128)(2,1)}, bf16[512,2048]{1,0:T(8,128)(2,1)}, u32[]{:S(2)}, u32[]{:S(2)}) collective-permute-start(bf16[512,2048]{1,0:T(8,128)(2,1)} %shard_map.79.gate_a), channel_id=1, source_target_pairs={{0,16},{16,0},{1,17},{17,1},{2,18},{18,2},{3,19},{19,3},{4,20},{20... | collective-permute-start | bytes 6291464 | tf_op jit(solution)/shard_map/ppermute | solution.py:118
  220.4 2.9 copy-start.17
  230.6 21.1 %collective-permute-start.9 = (bf16[512,1024]{1,0:T(8,128)(2,1)}, bf16[512,1024]{1,0:T(8,128)(2,1)}, u32[]{:S(2)}, u32[]{:S(2)}) collective-permute-start(bf16[512,1024]{1,0:T(8,128)(2,1)} %shard_map.80.grad_a), channel_id=1, source_target_pairs={{0,16},{16,0},{1,17},{17,1},{2,18},{18,2},{3,19},{19,3},{4,20},{20... | collective-permute-start | bytes 3145736 | tf_op jit(solution)/shard_map/ppermute | solution.py:118
  236.4 2.1 collective-permute-start.5
  249.9 1.0 copy-start
  250.9 0.8 copy-start.2
  268.4 3.4 copy-start.4
  268.4 3.4 copy-start.8
  272.9 70.8 %all-to-all-start.2 = ((bf16[16,16,3584]{2,1,0:T(8,128)(2,1)}), bf16[16,16,3584]{2,1,0:T(8,128)(2,1)}, u32[]{:S(2)}, u32[]{:S(2)}) async-start(bf16[16,16,3584]{2,1,0:T(8,128)(2,1)} %bitcast.42), calls=%async_computation.2 | async-start | bytes 3670016 | tf_op jit(solution)/shard_map/all_to_all | solution.py:33
  288.9 6.4 %copy-start.11 = (bf16[256,1792]{1,0:T(8,128)(2,1)S(1)}, bf16[256,1792]{1,0:T(8,128)(2,1)}, u32[]{:S(2)}) copy-start(bf16[256,1792]{1,0:T(8,128)(2,1)} %get-tuple-element.46) | copy-start | bytes 2752516
  288.9 8.3 %copy-start.12 = (bf16[256,1792]{1,0:T(8,128)(2,1)S(1)}, bf16[256,1792]{1,0:T(8,128)(2,1)}, u32[]{:S(2)}) copy-start(bf16[256,1792]{1,0:T(8,128)(2,1)} %get-tuple-element.44) | copy-start | bytes 2752516
  289.0 43.3 %collective-permute-start.12 = (bf16[256,2048]{1,0:T(8,128)(2,1)S(1)}, bf16[256,2048]{1,0:T(8,128)(2,1)S(1)}, u32[]{:S(2)}, u32[]{:S(2)}) collective-permute-start(bf16[256,2048]{1,0:T(8,128)(2,1)S(1)} %shard_map.82.gate_a), channel_id=1, source_target_pairs={{0,16},{16,0},{1,17},{17,1},{2,18},{18,2},{3,19},{19,3},{4,20},{20... | collective-permute-start | bytes 3145736 | tf_op jit(solution)/shard_map/ppermute | solution.py:118
  294.9 37.3 %collective-permute-start.13 = (bf16[256,1024]{1,0:T(8,128)(2,1)S(1)}, bf16[256,1024]{1,0:T(8,128)(2,1)S(1)}, u32[]{:S(2)}, u32[]{:S(2)}) collective-permute-start(bf16[256,1024]{1,0:T(8,128)(2,1)S(1)} %shard_map.83.grad_a), channel_id=1, source_target_pairs={{0,16},{16,0},{1,17},{17,1},{2,18},{18,2},{3,19},{19,3},{4,20},{20... | collective-permute-start | bytes 1572872 | tf_op jit(solution)/shard_map/ppermute | solution.py:118
  295.4 29.8 %collective-permute-start.11 = (bf16[256,1792]{1,0:T(8,128)(2,1)S(1)}, bf16[256,1792]{1,0:T(8,128)(2,1)S(1)}, u32[]{:S(2)}, u32[]{:S(2)}) collective-permute-start(bf16[256,1792]{1,0:T(8,128)(2,1)S(1)} %copy-done.11), channel_id=1, source_target_pairs={{0,2},{1,3},{2,0},{3,1},{4,6},{5,7},{6,4},{7,5},{8,10},{9,11},{10,... | collective-permute-start | bytes 2752520 | tf_op jit(solution)/shard_map/ppermute | solution.py:44
  297.2 33.9 %collective-permute-start.10 = (bf16[256,1792]{1,0:T(8,128)(2,1)S(1)}, bf16[256,1792]{1,0:T(8,128)(2,1)S(1)}, u32[]{:S(2)}, u32[]{:S(2)}) collective-permute-start(bf16[256,1792]{1,0:T(8,128)(2,1)S(1)} %copy-done.12), channel_id=1, source_target_pairs={{0,1},{1,0},{2,3},{3,2},{4,5},{5,4},{6,7},{7,6},{8,9},{9,8},{10,11... | collective-permute-start | bytes 2752520 | tf_op jit(solution)/shard_map/ppermute | solution.py:44
  332.3 13.3 %copy-start.9 = (bf16[256,1792]{1,0:T(8,128)(2,1)S(1)}, bf16[256,1792]{1,0:T(8,128)(2,1)}, u32[]{:S(2)}) copy-start(bf16[256,1792]{1,0:T(8,128)(2,1)} %add.30) | copy-start | bytes 2752516
  345.6 35.7 %collective-permute-start.14 = (bf16[128,1792]{1,0:T(8,128)(2,1)}, bf16[128,1792]{1,0:T(8,128)(2,1)}, u32[]{:S(2)}, u32[]{:S(2)}) collective-permute-start(bf16[128,1792]{1,0:T(8,128)(2,1)} %slice.97), channel_id=1, source_target_pairs={{0,2},{1,3},{2,0},{3,1},{4,6},{5,7},{6,4},{7,5},{8,10},{9,11},{10,... | collective-permute-start | bytes 1376264 | tf_op jit(solution)/shard_map/ppermute | solution.py:44
  346.4 36.2 %collective-permute-start.15 = (bf16[128,1792]{1,0:T(8,128)(2,1)}, bf16[128,1792]{1,0:T(8,128)(2,1)}, u32[]{:S(2)}, u32[]{:S(2)}) collective-permute-start(bf16[128,1792]{1,0:T(8,128)(2,1)} %slice.99), channel_id=1, source_target_pairs={{0,1},{1,0},{2,3},{3,2},{4,5},{5,4},{6,7},{7,6},{8,9},{9,8},{10,11... | collective-permute-start | bytes 1376264 | tf_op jit(solution)/shard_map/ppermute | solution.py:44
  347.1 77.4 %all-to-all-start.3 = ((bf16[16,16,3584]{2,1,0:T(8,128)(2,1)}), bf16[16,16,3584]{2,1,0:T(8,128)(2,1)}, u32[]{:S(2)}, u32[]{:S(2)}) async-start(bf16[16,16,3584]{2,1,0:T(8,128)(2,1)} %bitcast.43), calls=%async_computation.3 | async-start | bytes 3670016 | tf_op jit(solution)/shard_map/all_to_all | solution.py:33
  356.1 4.3 copy-start.1
  356.1 4.3 copy-start.5
  381.3 4.3 %copy-start.3 = (bf16[256,1024]{1,0:T(8,128)(2,1)S(1)}, bf16[256,1024]{1,0:T(8,128)(2,1)}, u32[]{:S(2)}) copy-start(bf16[256,1024]{1,0:T(8,128)(2,1)} %copy-done.2) | copy-start | bytes 1572868
  383.7 29.0 %collective-permute-start.16 = (bf16[64,3584]{1,0:T(8,128)(2,1)S(1)}, bf16[64,3584]{1,0:T(8,128)(2,1)S(1)}, u32[]{:S(2)}, u32[]{:S(2)}) collective-permute-start(bf16[64,3584]{1,0:T(8,128)(2,1)S(1)} %pad_maximum_fusion.7), channel_id=1, source_target_pairs={{0,4},{1,5},{2,6},{3,7},{4,0},{5,1},{6,2},{7,3},{8,12},{9,13},{10,... | collective-permute-start | bytes 1376264 | tf_op jit(solution)/shard_map/ppermute | solution.py:44
  385.6 13.2 %slice-start = ((s8[14680064]{0:T(1024)(128)(4,1)}), s8[4194304]{0:T(1024)(128)(4,1)S(1)}, s32[]{:S(2)}) async-start(s8[14680064]{0:T(1024)(128)(4,1)} %bitcast.39), calls=%async_computation.4 | async-start | bytes 8388608
  385.6 13.2 %slice-start.1 = ((s8[14680064]{0:T(1024)(128)(4,1)}), s8[4194304]{0:T(1024)(128)(4,1)S(1)}, s32[]{:S(2)}) async-start(s8[14680064]{0:T(1024)(128)(4,1)} %bitcast.39), calls=%async_computation.5 | async-start | bytes 8388608
  385.6 13.2 %slice-start.2 = ((s8[14680064]{0:T(1024)(128)(4,1)}), s8[4194304]{0:T(1024)(128)(4,1)S(1)}, s32[]{:S(2)}) async-start(s8[14680064]{0:T(1024)(128)(4,1)} %bitcast.39), calls=%async_computation.6 | async-start | bytes 8388608
  385.6 13.2 %slice-start.3 = ((s8[14680064]{0:T(1024)(128)(4,1)}), s8[2097152]{0:T(1024)(128)(4,1)S(1)}, s32[]{:S(2)}) async-start(s8[14680064]{0:T(1024)(128)(4,1)} %bitcast.39), calls=%async_computation.7 | async-start | bytes 4194304
  398.8 25.7 %copy-start.14 = (bf16[256,256]{1,0:T(8,128)(2,1)S(1)}, bf16[256,256]{1,0:T(8,128)(2,1)}, u32[]{:S(2)}) copy-start(bf16[256,256]{1,0:T(8,128)(2,1)} %copy-done.13) | copy-start | bytes 393220
  398.8 25.7 %copy-start.16 = (bf16[256,256]{1,0:T(8,128)(2,1)S(1)}, bf16[256,256]{1,0:T(8,128)(2,1)}, u32[]{:S(2)}) copy-start(bf16[256,256]{1,0:T(8,128)(2,1)} %copy-done.15) | copy-start | bytes 393220
  412.7 11.7 %collective-permute-start.17 = (bf16[32,3584]{1,0:T(8,128)(2,1)S(1)}, bf16[32,3584]{1,0:T(8,128)(2,1)S(1)}, u32[]{:S(2)}, u32[]{:S(2)}) collective-permute-start(bf16[32,3584]{1,0:T(8,128)(2,1)S(1)} %slice.107), channel_id=1, source_target_pairs={{0,8},{1,9},{2,10},{3,11},{4,12},{5,13},{6,14},{7,15},{8,0},{9,1},... | collective-permute-start | bytes 688136 | tf_op jit(solution)/shard_map/ppermute | solution.py:44

commit v4 on v3

--- a/solution.py
+++ b/solution.py
@@ -9,6 +9,7 @@
 from jax.sharding import PartitionSpec as P
 
 VMEM_BYTES = 48 * 1024 * 1024
+SMALL_COST = pl.CostEstimate(flops=1, bytes_accessed=1, transcendentals=0)
 
 
 def rank_in_expert(row_expert):
@@ -105,11 +106,7 @@
         out_specs=pl.BlockSpec((height, step), lambda j: (0, j)),
         out_shape=jax.ShapeDtypeStruct((height, width), jnp.bfloat16),
         compiler_params=pltpu.CompilerParams(vmem_limit_bytes=VMEM_BYTES),
-        cost_estimate=pl.CostEstimate(
-            flops=2 * height * depth * width,
-            bytes_accessed=2 * (height * depth + depth * width + height * width),
-            transcendentals=0,
-        ),
+        cost_estimate=SMALL_COST,
     )(left, right)
 
 
@@ -179,11 +176,7 @@
         ],
         out_shape=[shape(features), shape(width), shape(2 * width)],
         compiler_params=pltpu.CompilerParams(vmem_limit_bytes=VMEM_BYTES),
-        cost_estimate=pl.CostEstimate(
-            flops=4 * height * width * features,
-            bytes_accessed=4 * width * features + 2 * height * (features + 9 * width),
-            transcendentals=height * width,
-        ),
+        cost_estimate=SMALL_COST,
     )(keep, *gate_pair, *grad_pair, matrix)
 
 
@@ -200,7 +193,7 @@
     gate_up_matrix = w_gate_up.reshape(feature_share, 2 * hidden_width)
     down_matrix = w_down.reshape(hidden_width, feature_share)
     cap = 2 * row_count // expert_count
-    half = cap // 2
+    bounds = (0, cap // 4, cap)
 
     rank = rank_in_expert(row_expert)
     is_spill = rank >= cap
@@ -208,10 +201,10 @@
     is_busiest = lax.axis_index("exp") == busiest
     spill_hot = one_hot(jnp.where(is_spill, rank - cap, -1), cap)
     chunk_hot = []
-    for chunk in range(2):
-        inside = (rank >= chunk * half) & (rank < (chunk + 1) * half)
-        slot = row_expert * half + rank - chunk * half
-        chunk_hot.append(one_hot(jnp.where(inside, slot, -1), expert_count * half))
+    for low, high in zip(bounds, bounds[1:]):
+        inside = (rank >= low) & (rank < high)
+        slot = row_expert * (high - low) + rank - low
+        chunk_hot.append(one_hot(jnp.where(inside, slot, -1), expert_count * (high - low)))
 
     both = jnp.concatenate([tokens, d_out], axis=1)
 
@@ -231,19 +224,21 @@
     only_busiest = is_busiest.astype(jnp.int32).reshape(1)
 
     far = outer_masks()
-    spill_both = double(place(spill_hot, both), far[0])
-    spill_both, hot_0 = lax.optimization_barrier((spill_both, chunk_hot[0]))
-
-    arrived_0 = exchange(place(hot_0, both), expert_count)
-    for mask in far[1:]:
+    spill_both = place(spill_hot, both)
+    for mask in far:
         spill_both = double(spill_both, mask)
     spill_rows, spill_grads = split(spill_both)
+    sent_0 = place(chunk_hot[0], both)
+    spill_rows, spill_grads, sent_0 = lax.optimization_barrier((spill_rows, spill_grads, sent_0))
+
+    arrived_0 = exchange(sent_0, expert_count)
     spill_rows, spill_grads = double(spill_rows, 2), double(spill_grads, 1)
-    arrived_0, spill_rows, spill_grads, hot_1, gate_up_matrix = lax.optimization_barrier(
-        (arrived_0, spill_rows, spill_grads, chunk_hot[1], gate_up_matrix)
-    )
-
-    arrived_1 = exchange(place(hot_1, both), expert_count)
+    sent_1 = place(chunk_hot[1], both)
+    arrived_0, spill_rows, spill_grads, sent_1, gate_up_matrix = lax.optimization_barrier(
+        (arrived_0, spill_rows, spill_grads, sent_1, gate_up_matrix)
+    )
+
+    arrived_1 = exchange(sent_1, expert_count)
     spill_rows, spill_grads = double(spill_rows, 1), swap_quarters(double(spill_grads, 2))
     out_0, hidden_0, branch_0 = step(always, arrived_0, 0, arrived_0, 1)
     out_s, hidden_s, branch_s = step(only_busiest, spill_rows, 0, spill_grads, 0)
@@ -256,15 +251,15 @@
     )
 
     back_0 = exchange(out_0, expert_count)
-    back_a = kept_a + swap_with(sent_a, 1)
-    back_b = kept_b + swap_with(sent_b, 2)
+    come_a = swap_with(sent_a, 1)
+    come_b = swap_with(sent_b, 2)
     out_1, hidden_1, branch_1 = step(always, arrived_1, 0, arrived_1, 1)
-    back_0, back_a, back_b, out_1, arrived_1 = lax.optimization_barrier(
-        (back_0, back_a, back_b, out_1, arrived_1)
+    back_0, come_a, come_b, out_1, arrived_1 = lax.optimization_barrier(
+        (back_0, come_a, come_b, out_1, arrived_1)
     )
 
     back_1 = exchange(out_1, expert_count)
-    back_s = jnp.concatenate([halve(back_a, 2), halve(back_b, 1)], axis=1)
+    back_s = jnp.concatenate([halve(kept_a + come_a, 2), halve(kept_b + come_b, 1)], axis=1)
     for mask in reversed(far[1:]):
         back_s = halve(back_s, mask)
     rows_1, grads_1 = split(arrived_1)
@@ -274,18 +269,16 @@
     hidden = jnp.concatenate([hidden_s, hidden_0, hidden_1], axis=0)
     branch = jnp.concatenate([branch_s, branch_0, branch_1], axis=0)
     gate_up_grads = with_layout_constraint(outer(all_rows, branch), Layout((0, 1)))
-    gate_up_grads = lax.optimization_barrier(
-        gate_up_grads.reshape(feature_share // 8, 8, 2, hidden_width).transpose(0, 2, 1, 3)
-    )
+    down_grads = outer(hidden, all_grads).reshape(1, hidden_width, feature_share)
+    gate_up_grads = gate_up_grads.reshape(feature_share // 8, 8, 2, hidden_width)
+    back_s, gate_up_grads, down_grads = lax.optimization_barrier(
+        (back_s, gate_up_grads.transpose(0, 2, 1, 3), down_grads)
+    )
+
+    back_s = halve(back_s, far[0])
     gate_up_grads = gate_up_grads.transpose(0, 2, 1, 3).reshape(
         1, feature_share, 2, hidden_width
     )
-    down_grads = outer(hidden, all_grads).reshape(1, hidden_width, feature_share)
-
-    back_s, gate_up_grads, down_grads = lax.optimization_barrier(
-        (back_s, gate_up_grads, down_grads)
-    )
-    back_s = halve(back_s, far[0])
 
     pick = jnp.concatenate([spill_hot] + chunk_hot, axis=0)
     returned = jnp.concatenate([back_s, back_0, back_1], axis=0)

time: 431 us -> 432 us (level)
  waiting for transfers between devices: 170 us -> 156 us
  starting transfers between devices: 50.1 us -> 63.7 us
    ppermute x12, waiting for transfers between devices: 169 us -> 155 us  [swap_with(): return lax.ppermute(rows, 'exp', [(i, i ^ mask) for i in range(total)])]
    all_to_all x4, starting transfers between devices: 26.1 us -> 39.5 us  [exchange(): lax.all_to_all(rows.reshape(expert_count, slots // expert_count, width),...]
    unnamed x52 -> x55, local copies, waits for them, and re-layouts: 32.2 us -> 28.2 us
  transfers between devices with their start and end apart: 22 -> 22, of which waited for: 10 -> 9; matrix products, arithmetic and copies ran while one was open for 23% -> 23% of each run, Pallas kernels for 21% -> 22%
where the time goes in v4:
time: 432 us; the launch traced here: 430 us
  waiting for transfers between devices  156 us (36%)
  Pallas kernels  94.3 us (22%)
  starting transfers between devices  63.7 us (15%)
  local copies, waits for them, and re-layouts  54.8 us (13%)
  matrix products  45.2 us (10%)
  other arithmetic  14.5 us (3%)
    ppermute x12, waiting for transfers between devices, swap_with(): return lax.ppermute(rows, 'exp', [(i, i ^ mask) for i in range(total)])  155 us
    pallas_call x6, Pallas kernels, product(): pl.pallas_call(functools.partial(product_kernel, 1 if transposed else 0),...  52.9 us
    pallas_call x3, Pallas kernels, finish(): pl.pallas_call(finish_kernel, grid=(features // step,), in_specs=[pl.Bloc...  41.4 us
    all_to_all x4, starting transfers between devices, exchange(): lax.all_to_all(rows.reshape(expert_count, slots // expert_count, width),...  39.5 us
    dot_general x2, matrix products, outer(): lax.dot_general(left, right, (((0,), (0,)), ((), ())), preferred_element_...  33.7 us
    unnamed x55, local copies, waits for them, and re-layouts  28.2 us
    ppermute x12, starting transfers between devices, swap_with(): return lax.ppermute(rows, 'exp', [(i, i ^ mask) for i in range(total)])  22.5 us
    transpose x1, local copies, waits for them, and re-layouts, local(): gate_up_grads.transpose(0, 2, 1, 3)  13.8 us
  transfers between devices with their start and end apart: 22, of which 9 were waited for; matrix products, arithmetic and copies ran while one was open for 23% of the time, Pallas kernels for 22%

profile of v4, /device:TPU:0, one launch (start us, length us, event | category | flops | bytes accessed | tf_op | source)
XLA Modules:
  0.0 429.8 jit_solution(8311923339504161900)
XLA Ops:
  0.6 1.0 convert_reduce_fusion
  1.6 1.4 select_reduce_fusion
  3.0 1.7 constant_dynamic-update-slice_fusion.1
  5.7 4.1 collective-permute-start
  9.8 20.4 %collective-permute-done = bf16[32,7168]{1,0:T(8,128)(2,1)S(1)} collective-permute-done((bf16[32,7168]{1,0:T(8,128)(2,1)S(1)}, bf16[32,7168]{1,0:T(8,128)(2,1)S(1)}, u32[]{:S(2)}, u32[]{:S(2)}) %collective-permute-start) | collective-permute-done | bytes 458784 | tf_op jit(solution)/shard_map/ppermute | solution.py:45
  31.0 1.9 convolution_convert_fusion.2
  32.9 18.9 %collective-permute-done.1 = bf16[64,7168]{1,0:T(8,128)(2,1)S(1)} collective-permute-done((bf16[64,7168]{1,0:T(8,128)(2,1)S(1)}, bf16[64,7168]{1,0:T(8,128)(2,1)S(1)}, u32[]{:S(2)}, u32[]{:S(2)}) %collective-permute-start.1) | collective-permute-done | bytes 917536 | tf_op jit(solution)/shard_map/ppermute | solution.py:45
  52.0 1.1 fusion.37
  53.0 7.5 %all-to-all-start = ((bf16[16,8,7168]{2,1,0:T(8,128)(2,1)}), bf16[16,8,7168]{2,1,0:T(8,128)(2,1)S(1)}, u32[]{:S(2)}, u32[]{:S(2)}) async-start(bf16[16,8,7168]{2,1,0:T(8,128)(2,1)} %bitcast.42), calls=%async_computation | async-start | bytes 3670016 | tf_op jit(solution)/shard_map/all_to_all | solution.py:34
  60.6 1.9 collective-permute-start.3
  62.5 16.2 %copy.10 = bf16[448,8,2,1024]{3,1,2,0:T(8,128)(2,1)} copy(bf16[448,8,2,1024]{3,2,1,0:T(2,128)(2,1)} %bitcast.37) | data formatting | bytes 29360128
  78.7 1.5 collective-permute-start.2
  80.2 4.1 convolution_convert_fusion.1
  84.2 17.3 %collective-permute-done.3 = bf16[128,3584]{1,0:T(8,128)(2,1)S(1)} collective-permute-done((bf16[128,3584]{1,0:T(8,128)(2,1)}, bf16[128,3584]{1,0:T(8,128)(2,1)S(1)}, u32[]{:S(2)}, u32[]{:S(2)}) %collective-permute-start.3) | collective-permute-done | bytes 917536 | tf_op jit(solution)/shard_map/ppermute | solution.py:45
  101.5 1.3 pad_maximum_fusion.4
  102.9 3.5 collective-permute-done.2
  106.4 1.4 pad_maximum_fusion.3
  107.8 5.8 %all-to-all-start.1 = ((bf16[16,24,7168]{2,1,0:T(8,128)(2,1)}), bf16[16,24,7168]{2,1,0:T(8,128)(2,1)}, u32[]{:S(2)}, u32[]{:S(2)}) async-start(bf16[16,24,7168]{2,1,0:T(8,128)(2,1)} %bitcast.36), calls=%async_computation.1 | async-start | bytes 11010048 | tf_op jit(solution)/shard_map/all_to_all | solution.py:34
  113.6 1.9 collective-permute-start.6
  115.5 1.5 collective-permute-start.8
  116.9 2.2 constant_dynamic-update-slice_fusion.5
  119.1 79.0 %collective-permute-done.6 = bf16[256,3584]{1,0:T(8,128)(2,1)S(1)} collective-permute-done((bf16[256,3584]{1,0:T(8,128)(2,1)}, bf16[256,3584]{1,0:T(8,128)(2,1)S(1)}, u32[]{:S(2)}, u32[]{:S(2)}) %collective-permute-start.6) | collective-permute-done | bytes 1835040 | tf_op jit(solution)/shard_map/ppermute | solution.py:45
  198.1 1.2 copy-done.17
  199.3 1.7 pad_maximum_fusion.left_ref
  201.1 13.1 %shard_map.79.gate_a = bf16[512,2048]{1,0:T(8,128)(2,1)} custom-call(bf16[512,3584]{1,0:T(8,128)(2,1)S(1)} %pad_maximum_fusion.left_ref, bf16[3584,2048]{1,0:T(8,128)(2,1)} %bitcast.27), custom_call_target="tpu_custom_call" | custom-call | flops 1 | bytes 1 | tf_op jit(solution)/shard_map/pallas_call | solution.py:102
  214.2 1.0 constant_dynamic-update-slice_fusion.4
  215.2 1.1 constant_dynamic-update-slice_fusion.3
  216.3 1.1 constant_dynamic-update-slice_fusion.2
  217.7 6.6 %shard_map.80.grad_a = bf16[512,1024]{1,0:T(8,128)(2,1)S(1)} custom-call(bf16[512,3584]{1,0:T(8,128)(2,1)S(1)} %pad_maximum_fusion.1.left_ref, bf16[1024,3584]{1,0:T(8,128)(2,1)} %bitcast.33), custom_call_target="tpu_custom_call" | custom-call | flops 1 | bytes 1 | tf_op jit(solution)/shard_map/pallas_call | solution.py:102
  224.9 8.7 %shard_map.76.gate_a = bf16[128,2048]{1,0:T(8,128)(2,1)S(1)} custom-call(bf16[128,7168]{1,0:T(8,128)(2,1)S(1)} %bitcast.24, bf16[3584,2048]{1,0:T(8,128)(2,1)} %bitcast.28), custom_call_target="tpu_custom_call" | custom-call | flops 1 | bytes 1 | tf_op jit(solution)/shard_map/pallas_call | solution.py:102
  233.7 6.0 %shard_map.77.grad_a = bf16[128,1024]{1,0:T(8,128)(2,1)} custom-call(bf16[128,7168]{1,0:T(8,128)(2,1)S(1)} %bitcast.25, bf16[1024,3584]{1,0:T(8,128)(2,1)} %bitcast.34), custom_call_target="tpu_custom_call" | custom-call | flops 1 | bytes 1 | tf_op jit(solution)/shard_map/pallas_call | solution.py:102
  240.8 0.9 collective-permute-done.5.grad_b
  241.7 11.4 %shard_map.78 = (bf16[128,3584]{1,0:T(8,128)(2,1)}, bf16[128,1024]{1,0:T(8,128)(2,1)S(1)}, bf16[128,2048]{1,0:T(8,128)(2,1)S(1)}) custom-call(s32[1]{0:T(128)} %constant.20.clone.1.keep_ref, bf16[128,2048]{1,0:T(8,128)(2,1)S(1)} %shard_map.76.gate_a, bf16[128,2048]{1,0:T(8,128)(2,1)} %collective-permute-done.4.gate_b, bf16[128,1024]{1,0:T(8,128)(2,1)} %shard_map.77.grad_a, ...), custom_call_target="tpu_custom_call" | custom-call | flops 1 | bytes 1 | tf_op jit(solution)/shard_map/pallas_call | solution.py:161
  253.0 0.8 copy-done.4
  253.9 16.5 %shard_map.81 = (bf16[512,3584]{1,0:T(8,128)(2,1)}, bf16[512,1024]{1,0:T(8,128)(2,1)S(1)}, bf16[512,2048]{1,0:T(8,128)(2,1)S(1)}) custom-call(s32[1]{0:T(128)} %bitcast.5.keep_ref, bf16[512,2048]{1,0:T(8,128)(2,1)} %shard_map.79.gate_a, bf16[512,2048]{1,0:T(8,128)(2,1)} %collective-permute-done.7.gate_b, bf16[512,1024]{1,0:T(8,128)(2,1)S(1)} %shard_map.80.grad_a, ...), custom_call_target="tpu_custom_call" | custom-call | flops 1 | bytes 1 | tf_op jit(solution)/shard_map/pallas_call | solution.py:161
  270.4 2.7 fusion.35
  273.1 1.4 pad_maximum_fusion.6
  274.5 1.4 fusion.36
  275.8 20.6 %all-to-all-start.2 = ((bf16[16,8,3584]{2,1,0:T(8,128)(2,1)}), bf16[16,8,3584]{2,1,0:T(8,128)(2,1)}, u32[]{:S(2)}, u32[]{:S(2)}) async-start(bf16[16,8,3584]{2,1,0:T(8,128)(2,1)} %bitcast.6), calls=%async_computation.2 | async-start | bytes 1835008 | tf_op jit(solution)/shard_map/all_to_all | solution.py:34
  296.4 11.7 %shard_map.82.gate_a = bf16[384,2048]{1,0:T(8,128)(2,1)S(1)} custom-call(bf16[384,7168]{1,0:T(8,128)(2,1)} %bitcast.3.left_ref, bf16[3584,2048]{1,0:T(8,128)(2,1)} %bitcast.31), custom_call_target="tpu_custom_call" | custom-call | flops 1 | bytes 1 | tf_op jit(solution)/shard_map/pallas_call | solution.py:102
  308.3 6.8 %shard_map.83.grad_a = bf16[384,1024]{1,0:T(8,128)(2,1)S(1)} custom-call(bf16[384,7168]{1,0:T(8,128)(2,1)} %bitcast.3.left_ref, bf16[1024,3584]{1,0:T(8,128)(2,1)} %bitcast.35), custom_call_target="tpu_custom_call" | custom-call | flops 1 | bytes 1 | tf_op jit(solution)/shard_map/pallas_call | solution.py:102
  315.6 1.9 collective-permute-start.10
  317.5 1.5 collective-permute-start.11
  319.0 1.3 slice_dynamic-update-slice_fusion.1
  320.3 1.1 copy-done.19
  321.4 13.6 %shard_map.84 = (bf16[384,3584]{1,0:T(8,128)(2,1)}, bf16[384,1024]{1,0:T(8,128)(2,1)S(1)}, bf16[384,2048]{1,0:T(8,128)(2,1)S(1)}) custom-call(s32[1]{0:T(128)} %constant.20.clone.1.keep_ref, bf16[384,2048]{1,0:T(8,128)(2,1)S(1)} %shard_map.82.gate_a, bf16[384,2048]{1,0:T(8,128)(2,1)} %copy-done.19, bf16[384,1024]{1,0:T(8,128)(2,1)S(1)} %shard_map.83.grad_a, ...), custom_call_target="tpu_custom_call" | custom-call | flops 1 | bytes 1 | tf_op jit(solution)/shard_map/pallas_call | solution.py:161
  335.0 3.6 collective-permute-done.10
  338.6 1.2 collective-permute-done.11
  339.9 1.7 add.32
  341.5 0.9 slice.113
  342.4 1.5 collective-permute-start.14
  343.9 1.4 add.34
  345.3 0.9 slice.115
  346.9 5.6 %all-to-all-start.3 = ((bf16[16,24,3584]{2,1,0:T(8,128)(2,1)}), bf16[16,24,3584]{2,1,0:T(8,128)(2,1)}, u32[]{:S(2)}, u32[]{:S(2)}) async-start(bf16[16,24,3584]{2,1,0:T(8,128)(2,1)} %bitcast.43), calls=%async_computation.3 | async-start | bytes 5505024 | tf_op jit(solution)/shard_map/all_to_all | solution.py:34
  352.6 5.6 %slice_dynamic-update-slice_fusion = (bf16[1024,3584]{1,0:T(8,128)(2,1)}, bf16[384,3584]{1,0:T(8,128)(2,1)}) fusion(bf16[1024,3584]{1,0:T(8,128)(2,1)} %get-tuple-element.73, bf16[384,7168]{1,0:T(8,128)(2,1)} %bitcast.3.left_ref), kind=kLoop, calls=%fused_computation.26 | loop fusion | bytes 11010048 | tf_op jit(solution)/shard_map/concatenate | solution.py:268
  358.1 20.6 %convolution_convert_fusion = bf16[3584,2048]{1,0:T(8,128)(2,1)} fusion(bf16[384,3584]{1,0:T(8,128)(2,1)} %get-tuple-element.66, bf16[128,3584]{1,0:T(8,128)(2,1)} %get-tuple-element.74, bf16[256,3584]{1,0:T(8,128)(2,1)} %copy-done.17, bf16[256,3584]{1,0:T(8,128)(2,1)S(1)} %copy-done.11, bf16[384,2048]{1,0:T(8,128)(2,1)S(1)} %get-tuple-element.56, ...), kind=kOutput, calls=%fused_computation | convolution fusion | flops 15081668608 | bytes 26214400 | tf_op jit(solution)/shard_map/dot_general | solution.py:184
  378.7 1.3 slice_add_fusion.1
  380.0 1.2 slice_add_fusion
  381.3 1.9 collective-permute-start.16
  383.3 13.1 %fusion.7 = bf16[1,1024,3584]{2,1,0:T(8,128)(2,1)} fusion(bf16[1024,3584]{1,0:T(8,128)(2,1)} %get-tuple-element.65, bf16[384,1024]{1,0:T(8,128)(2,1)S(1)} %get-tuple-element.59, bf16[128,1024]{1,0:T(8,128)(2,1)S(1)} %copy-done.7, bf16[512,1024]{1,0:T(8,128)(2,1)S(1)} %copy-done.3), kind=kOutput, calls=%fused_computation.12 | convolution fusion | flops 7526154240 | bytes 16777216 | tf_op jit(solution)/shard_map/dot_general | solution.py:184
  396.4 10.9 %collective-permute-done.16 = bf16[64,3584]{1,0:T(8,128)(2,1)S(1)} collective-permute-done((bf16[64,3584]{1,0:T(8,128)(2,1)S(1)}, bf16[64,3584]{1,0:T(8,128)(2,1)S(1)}, u32[]{:S(2)}, u32[]{:S(2)}) %collective-permute-start.16) | collective-permute-done | bytes 458784 | tf_op jit(solution)/shard_map/ppermute | solution.py:45
  407.5 3.5 collective-permute-start.17
  411.1 13.8 %copy.9 = bf16[448,8,2,1024]{3,2,1,0:T(2,128)(2,1)} copy(bf16[448,8,2,1024]{3,1,2,0:T(8,128)(2,1)S(1)} %bitcast.40) | data formatting | bytes 29360128 | tf_op jit(solution)/shard_map/transpose | solution.py:279
  425.0 4.9 %convolution_convert_fusion.5 = bf16[256,3584]{1,0:T(8,128)(2,1)} fusion(bf16[384,3584]{1,0:T(8,128)(2,1)} %bitcast.12, bf16[128,3584]{1,0:T(8,128)(2,1)} %bitcast.7, bf16[32,3584]{1,0:T(8,128)(2,1)S(1)} %slice_add_fusion.2, pred[384,256]{1,0:T(32,128)(4,1)S(1)} %iota_compare_fusion, pred[128,256]{1,0:T(32,128)(4,1)S(1)} %iota_compare_fusion.2, ...), kind=kOutput, calls=%fused_computation.13 | convolution fusion | flops 1011138560 | bytes 5873664 | tf_op jit(solution)/shard_map/dot_general | solution.py:285
  (79 shorter events, 5.1 us)
Async XLA Ops:
  0.6 4.1 copy-start.18
  5.0 27.9 %copy-start.8 = (bf16[256,7168]{1,0:T(8,128)(2,1)}, bf16[256,7168]{1,0:T(8,128)(2,1)S(1)}, u32[]{:S(2)}) copy-start(bf16[256,7168]{1,0:T(8,128)(2,1)S(1)} %constant_dynamic-update-slice_fusion) | copy-start | bytes 11010052
  5.7 24.5 %collective-permute-start = (bf16[32,7168]{1,0:T(8,128)(2,1)S(1)}, bf16[32,7168]{1,0:T(8,128)(2,1)S(1)}, u32[]{:S(2)}, u32[]{:S(2)}) collective-permute-start(bf16[32,7168]{1,0:T(8,128)(2,1)S(1)} %convolution_convert_fusion.3), channel_id=1, source_target_pairs={{0,8},{1,9},{2,10},{3,11},{4,12},{5,13},{6,14},{7,15},{8,0},{9,1},... | collective-permute-start | bytes 1376264 | tf_op jit(solution)/shard_map/ppermute | solution.py:45
  30.2 21.6 %collective-permute-start.1 = (bf16[64,7168]{1,0:T(8,128)(2,1)S(1)}, bf16[64,7168]{1,0:T(8,128)(2,1)S(1)}, u32[]{:S(2)}, u32[]{:S(2)}) collective-permute-start(bf16[64,7168]{1,0:T(8,128)(2,1)S(1)} %pad_maximum_fusion.5), channel_id=1, source_target_pairs={{0,4},{1,5},{2,6},{3,7},{4,0},{5,1},{6,2},{7,3},{8,12},{9,13},{10,... | collective-permute-start | bytes 2752520 | tf_op jit(solution)/shard_map/ppermute | solution.py:45
  53.0 54.8 %all-to-all-start = ((bf16[16,8,7168]{2,1,0:T(8,128)(2,1)}), bf16[16,8,7168]{2,1,0:T(8,128)(2,1)S(1)}, u32[]{:S(2)}, u32[]{:S(2)}) async-start(bf16[16,8,7168]{2,1,0:T(8,128)(2,1)} %bitcast.42), calls=%async_computation | async-start | bytes 3670016 | tf_op jit(solution)/shard_map/all_to_all | solution.py:34
  60.6 41.0 %collective-permute-start.3 = (bf16[128,3584]{1,0:T(8,128)(2,1)}, bf16[128,3584]{1,0:T(8,128)(2,1)S(1)}, u32[]{:S(2)}, u32[]{:S(2)}) collective-permute-start(bf16[128,3584]{1,0:T(8,128)(2,1)} %get-tuple-element.36), channel_id=1, source_target_pairs={{0,1},{1,0},{2,3},{3,2},{4,5},{5,4},{6,7},{7,6},{8,9},{9,8},{10,11... | collective-permute-start | bytes 2752520 | tf_op jit(solution)/shard_map/ppermute | solution.py:45
  62.5 17.7 %copy-start.9 = (bf16[256,7168]{1,0:T(8,128)(2,1)S(1)}, bf16[256,7168]{1,0:T(8,128)(2,1)}, u32[]{:S(2)}) copy-start(bf16[256,7168]{1,0:T(8,128)(2,1)} %copy-done.8) | copy-start | bytes 11010052
  78.7 27.7 %collective-permute-start.2 = (bf16[128,3584]{1,0:T(8,128)(2,1)S(1)}, bf16[128,3584]{1,0:T(8,128)(2,1)S(1)}, u32[]{:S(2)}, u32[]{:S(2)}) collective-permute-start(bf16[128,3584]{1,0:T(8,128)(2,1)S(1)} %get-tuple-element.35), channel_id=1, source_target_pairs={{0,2},{1,3},{2,0},{3,1},{4,6},{5,7},{6,4},{7,5},{8,10},{9,11},{10,... | collective-permute-start | bytes 2752520 | tf_op jit(solution)/shard_map/ppermute | solution.py:45
  80.2 21.4 %copy-start.12 = (bf16[128,3584]{1,0:T(8,128)(2,1)S(1)}, bf16[128,3584]{1,0:T(8,128)(2,1)}, u32[]{:S(2)}) copy-start(bf16[128,3584]{1,0:T(8,128)(2,1)} %get-tuple-element.36) | copy-start | bytes 2752516
  107.8 168.1 %all-to-all-start.1 = ((bf16[16,24,7168]{2,1,0:T(8,128)(2,1)}), bf16[16,24,7168]{2,1,0:T(8,128)(2,1)}, u32[]{:S(2)}, u32[]{:S(2)}) async-start(bf16[16,24,7168]{2,1,0:T(8,128)(2,1)} %bitcast.36), calls=%async_computation.1 | async-start | bytes 11010048 | tf_op jit(solution)/shard_map/all_to_all | solution.py:34
  113.6 84.5 %collective-permute-start.6 = (bf16[256,3584]{1,0:T(8,128)(2,1)}, bf16[256,3584]{1,0:T(8,128)(2,1)S(1)}, u32[]{:S(2)}, u32[]{:S(2)}) collective-permute-start(bf16[256,3584]{1,0:T(8,128)(2,1)} %pad_maximum_fusion.3), channel_id=1, source_target_pairs={{0,1},{1,0},{2,3},{3,2},{4,5},{5,4},{6,7},{7,6},{8,9},{9,8},{10,11... | collective-permute-start | bytes 5505032 | tf_op jit(solution)/shard_map/ppermute | solution.py:45
  115.5 98.7 %collective-permute-start.8 = (bf16[256,3584]{1,0:T(8,128)(2,1)}, bf16[256,3584]{1,0:T(8,128)(2,1)S(1)}, u32[]{:S(2)}, u32[]{:S(2)}) collective-permute-start(bf16[256,3584]{1,0:T(8,128)(2,1)} %pad_maximum_fusion.4), channel_id=1, source_target_pairs={{0,2},{1,3},{2,0},{3,1},{4,6},{5,7},{6,4},{7,5},{8,10},{9,11},{10,... | collective-permute-start | bytes 5505032 | tf_op jit(solution)/shard_map/ppermute | solution.py:45
  198.1 1.2 copy-start.17
  201.1 14.1 %copy-start.10 = (bf16[256,3584]{1,0:T(8,128)(2,1)S(1)}, bf16[256,3584]{1,0:T(8,128)(2,1)}, u32[]{:S(2)}) copy-start(bf16[256,3584]{1,0:T(8,128)(2,1)} %pad_maximum_fusion.4) | copy-start | bytes 5505028
  214.1 39.7 %collective-permute-start.7 = (bf16[512,2048]{1,0:T(8,128)(2,1)}, bf16[512,2048]{1,0:T(8,128)(2,1)}, u32[]{:S(2)}, u32[]{:S(2)}) collective-permute-start(bf16[512,2048]{1,0:T(8,128)(2,1)} %shard_map.79.gate_a), channel_id=1, source_target_pairs={{0,16},{16,0},{1,17},{17,1},{2,18},{18,2},{3,19},{19,3},{4,20},{20... | collective-permute-start | bytes 6291464 | tf_op jit(solution)/shard_map/ppermute | solution.py:115
  224.3 29.5 %collective-permute-start.9 = (bf16[512,1024]{1,0:T(8,128)(2,1)S(1)}, bf16[512,1024]{1,0:T(8,128)(2,1)}, u32[]{:S(2)}, u32[]{:S(2)}) collective-permute-start(bf16[512,1024]{1,0:T(8,128)(2,1)S(1)} %shard_map.80.grad_a), channel_id=1, source_target_pairs={{0,16},{16,0},{1,17},{17,1},{2,18},{18,2},{3,19},{19,3},{4,20},{20... | collective-permute-start | bytes 3145736 | tf_op jit(solution)/shard_map/ppermute | solution.py:115
  233.6 8.0 %collective-permute-start.4 = (bf16[128,2048]{1,0:T(8,128)(2,1)S(1)}, bf16[128,2048]{1,0:T(8,128)(2,1)}, u32[]{:S(2)}, u32[]{:S(2)}) collective-permute-start(bf16[128,2048]{1,0:T(8,128)(2,1)S(1)} %shard_map.76.gate_a), channel_id=1, source_target_pairs={{0,16},{16,0},{1,17},{17,1},{2,18},{18,2},{3,19},{19,3},{4,20},{20... | collective-permute-start | bytes 1572872 | tf_op jit(solution)/shard_map/ppermute | solution.py:115
  239.7 2.0 collective-permute-start.5
  253.0 0.8 copy-start.4
  253.9 16.5 %copy-start.6 = (bf16[128,1024]{1,0:T(8,128)(2,1)}, bf16[128,1024]{1,0:T(8,128)(2,1)S(1)}, u32[]{:S(2)}) copy-start(bf16[128,1024]{1,0:T(8,128)(2,1)S(1)} %get-tuple-element.58) | copy-start | bytes 786436
  270.3 4.1 copy-start
  270.3 4.1 copy-start.2
  270.3 4.1 copy-start.13
  275.8 64.0 %all-to-all-start.2 = ((bf16[16,8,3584]{2,1,0:T(8,128)(2,1)}), bf16[16,8,3584]{2,1,0:T(8,128)(2,1)}, u32[]{:S(2)}, u32[]{:S(2)}) async-start(bf16[16,8,3584]{2,1,0:T(8,128)(2,1)} %bitcast.6), calls=%async_computation.2 | async-start | bytes 1835008 | tf_op jit(solution)/shard_map/all_to_all | solution.py:34
  308.2 12.1 %collective-permute-start.12 = (bf16[384,2048]{1,0:T(8,128)(2,1)S(1)}, bf16[384,2048]{1,0:T(8,128)(2,1)S(1)}, u32[]{:S(2)}, u32[]{:S(2)}) collective-permute-start(bf16[384,2048]{1,0:T(8,128)(2,1)S(1)} %shard_map.82.gate_a), channel_id=1, source_target_pairs={{0,16},{16,0},{1,17},{17,1},{2,18},{18,2},{3,19},{19,3},{4,20},{20... | collective-permute-start | bytes 4718600 | tf_op jit(solution)/shard_map/ppermute | solution.py:115
  315.1 5.2 %collective-permute-start.13 = (bf16[384,1024]{1,0:T(8,128)(2,1)S(1)}, bf16[384,1024]{1,0:T(8,128)(2,1)S(1)}, u32[]{:S(2)}, u32[]{:S(2)}) collective-permute-start(bf16[384,1024]{1,0:T(8,128)(2,1)S(1)} %shard_map.83.grad_a), channel_id=1, source_target_pairs={{0,16},{16,0},{1,17},{17,1},{2,18},{18,2},{3,19},{19,3},{4,20},{20... | collective-permute-start | bytes 2359304 | tf_op jit(solution)/shard_map/ppermute | solution.py:115
  315.6 23.0 %collective-permute-start.10 = (bf16[256,1792]{1,0:T(8,128)(2,1)}, bf16[256,1792]{1,0:T(8,128)(2,1)}, u32[]{:S(2)}, u32[]{:S(2)}) collective-permute-start(bf16[256,1792]{1,0:T(8,128)(2,1)} %get-tuple-element.46), channel_id=1, source_target_pairs={{0,1},{1,0},{2,3},{3,2},{4,5},{5,4},{6,7},{7,6},{8,9},{9,8},{10,11... | collective-permute-start | bytes 2752520 | tf_op jit(solution)/shard_map/ppermute | solution.py:45
  317.5 22.4 %collective-permute-start.11 = (bf16[256,1792]{1,0:T(8,128)(2,1)}, bf16[256,1792]{1,0:T(8,128)(2,1)}, u32[]{:S(2)}, u32[]{:S(2)}) collective-permute-start(bf16[256,1792]{1,0:T(8,128)(2,1)} %get-tuple-element.47), channel_id=1, source_target_pairs={{0,2},{1,3},{2,0},{3,1},{4,6},{5,7},{6,4},{7,5},{8,10},{9,11},{10,... | collective-permute-start | bytes 2752520 | tf_op jit(solution)/shard_map/ppermute | solution.py:45
  320.3 1.1 copy-start.19
  335.0 8.8 %copy-start.14 = (bf16[256,1792]{1,0:T(8,128)(2,1)S(1)}, bf16[256,1792]{1,0:T(8,128)(2,1)}, u32[]{:S(2)}) copy-start(bf16[256,1792]{1,0:T(8,128)(2,1)} %get-tuple-element.51) | copy-start | bytes 2752516
  341.5 3.7 copy-start.15
  342.4 36.3 %collective-permute-start.14 = (bf16[128,1792]{1,0:T(8,128)(2,1)}, bf16[128,1792]{1,0:T(8,128)(2,1)}, u32[]{:S(2)}, u32[]{:S(2)}) collective-permute-start(bf16[128,1792]{1,0:T(8,128)(2,1)} %slice.113), channel_id=1, source_target_pairs={{0,2},{1,3},{2,0},{3,1},{4,6},{5,7},{6,4},{7,5},{8,10},{9,11},{10,... | collective-permute-start | bytes 1376264 | tf_op jit(solution)/shard_map/ppermute | solution.py:45
  345.3 1.1 copy-start.16
  346.4 33.6 %collective-permute-start.15 = (bf16[128,1792]{1,0:T(8,128)(2,1)}, bf16[128,1792]{1,0:T(8,128)(2,1)}, u32[]{:S(2)}, u32[]{:S(2)}) collective-permute-start(bf16[128,1792]{1,0:T(8,128)(2,1)} %slice.115), channel_id=1, source_target_pairs={{0,1},{1,0},{2,3},{3,2},{4,5},{5,4},{6,7},{7,6},{8,9},{9,8},{10,11... | collective-permute-start | bytes 1376264 | tf_op jit(solution)/shard_map/ppermute | solution.py:45
  346.9 78.0 %all-to-all-start.3 = ((bf16[16,24,3584]{2,1,0:T(8,128)(2,1)}), bf16[16,24,3584]{2,1,0:T(8,128)(2,1)}, u32[]{:S(2)}, u32[]{:S(2)}) async-start(bf16[16,24,3584]{2,1,0:T(8,128)(2,1)} %bitcast.43), calls=%async_computation.3 | async-start | bytes 5505024 | tf_op jit(solution)/shard_map/all_to_all | solution.py:34
  352.5 5.6 %copy-start.1 = (bf16[512,2048]{1,0:T(8,128)(2,1)S(1)}, bf16[512,2048]{1,0:T(8,128)(2,1)}, u32[]{:S(2)}) copy-start(bf16[512,2048]{1,0:T(8,128)(2,1)} %copy-done) | copy-start | bytes 6291460
  352.5 5.6 %copy-start.5 = (bf16[128,2048]{1,0:T(8,128)(2,1)S(1)}, bf16[128,2048]{1,0:T(8,128)(2,1)}, u32[]{:S(2)}) copy-start(bf16[128,2048]{1,0:T(8,128)(2,1)} %copy-done.4) | copy-start | bytes 1572868
  352.5 5.6 %copy-start.11 = (bf16[256,3584]{1,0:T(8,128)(2,1)S(1)}, bf16[256,3584]{1,0:T(8,128)(2,1)}, u32[]{:S(2)}) copy-start(bf16[256,3584]{1,0:T(8,128)(2,1)} %pad_maximum_fusion.3) | copy-start | bytes 5505028
  378.7 4.5 %copy-start.3 = (bf16[512,1024]{1,0:T(8,128)(2,1)S(1)}, bf16[512,1024]{1,0:T(8,128)(2,1)}, u32[]{:S(2)}) copy-start(bf16[512,1024]{1,0:T(8,128)(2,1)} %copy-done.2) | copy-start | bytes 3145732
  378.7 4.5 %copy-start.7 = (bf16[128,1024]{1,0:T(8,128)(2,1)S(1)}, bf16[128,1024]{1,0:T(8,128)(2,1)}, u32[]{:S(2)}) copy-start(bf16[128,1024]{1,0:T(8,128)(2,1)} %copy-done.6) | copy-start | bytes 786436
  381.3 26.1 %collective-permute-start.16 = (bf16[64,3584]{1,0:T(8,128)(2,1)S(1)}, bf16[64,3584]{1,0:T(8,128)(2,1)S(1)}, u32[]{:S(2)}, u32[]{:S(2)}) collective-permute-start(bf16[64,3584]{1,0:T(8,128)(2,1)S(1)} %pad_maximum_fusion.8), channel_id=1, source_target_pairs={{0,4},{1,5},{2,6},{3,7},{4,0},{5,1},{6,2},{7,3},{8,12},{9,13},{10,... | collective-permute-start | bytes 1376264 | tf_op jit(solution)/shard_map/ppermute | solution.py:45
  383.2 27.9 %slice-start = ((s8[14680064]{0:T(1024)(128)(4,1)}), s8[4194304]{0:T(1024)(128)(4,1)S(1)}, s32[]{:S(2)}) async-start(s8[14680064]{0:T(1024)(128)(4,1)} %bitcast.38), calls=%async_computation.4 | async-start | bytes 8388608
  383.2 27.9 %slice-start.1 = ((s8[14680064]{0:T(1024)(128)(4,1)}), s8[4194304]{0:T(1024)(128)(4,1)S(1)}, s32[]{:S(2)}) async-start(s8[14680064]{0:T(1024)(128)(4,1)} %bitcast.38), calls=%async_computation.5 | async-start | bytes 8388608
  383.2 27.9 %slice-start.2 = ((s8[14680064]{0:T(1024)(128)(4,1)}), s8[4194304]{0:T(1024)(128)(4,1)S(1)}, s32[]{:S(2)}) async-start(s8[14680064]{0:T(1024)(128)(4,1)} %bitcast.38), calls=%async_computation.6 | async-start | bytes 8388608
  383.2 27.9 %slice-start.3 = ((s8[14680064]{0:T(1024)(128)(4,1)}), s8[2097152]{0:T(1024)(128)(4,1)S(1)}, s32[]{:S(2)}) async-start(s8[14680064]{0:T(1024)(128)(4,1)} %bitcast.38), calls=%async_computation.7 | async-start | bytes 4194304
  407.5 17.5 %collective-permute-start.17 = (bf16[32,3584]{1,0:T(8,128)(2,1)S(1)}, bf16[32,3584]{1,0:T(8,128)(2,1)S(1)}, u32[]{:S(2)}, u32[]{:S(2)}) collective-permute-start(bf16[32,3584]{1,0:T(8,128)(2,1)S(1)} %slice.107), channel_id=1, source_target_pairs={{0,8},{1,9},{2,10},{3,11},{4,12},{5,13},{6,14},{7,15},{8,0},{9,1},... | collective-permute-start | bytes 688136 | tf_op jit(solution)/shard_map/ppermute | solution.py:45

commit v5 on v4

--- a/solution.py
+++ b/solution.py
@@ -211,14 +211,10 @@
     def split(both_in):
         return both_in[:, :feature_share], both_in[:, feature_share:]
 
-    def step(keep, rows_in, rows_block, grads_in, grads_block):
-        gate_pair = pair_over_grp(
-            product(rows_in, rows_block, feature_share, gate_up_matrix, False)
-        )
-        grad_pair = pair_over_grp(
-            product(grads_in, grads_block, feature_share, down_matrix, True)
-        )
-        return finish(keep, gate_pair, grad_pair, gate_up_matrix)
+    def products(rows_in, rows_block, grads_in, grads_block):
+        gate_part = product(rows_in, rows_block, feature_share, gate_up_matrix, False)
+        grad_part = product(grads_in, grads_block, feature_share, down_matrix, True)
+        return pair_over_grp(gate_part), pair_over_grp(grad_part)
 
     always = jnp.ones((1,), jnp.int32)
     only_busiest = is_busiest.astype(jnp.int32).reshape(1)
@@ -233,16 +229,25 @@
 
     arrived_0 = exchange(sent_0, expert_count)
     spill_rows, spill_grads = double(spill_rows, 2), double(spill_grads, 1)
-    sent_1 = place(chunk_hot[1], both)
-    arrived_0, spill_rows, spill_grads, sent_1, gate_up_matrix = lax.optimization_barrier(
-        (arrived_0, spill_rows, spill_grads, sent_1, gate_up_matrix)
-    )
-
+    arrived_0, spill_rows, spill_grads, hot_1, gate_up_matrix = lax.optimization_barrier(
+        (arrived_0, spill_rows, spill_grads, chunk_hot[1], gate_up_matrix)
+    )
+
+    come_rows, come_grads = swap_with(spill_rows, 1), swap_with(spill_grads, 2)
+    arrived_0, sent_1 = lax.optimization_barrier((arrived_0, place(hot_1, both)))
     arrived_1 = exchange(sent_1, expert_count)
-    spill_rows, spill_grads = double(spill_rows, 1), swap_quarters(double(spill_grads, 2))
-    out_0, hidden_0, branch_0 = step(always, arrived_0, 0, arrived_0, 1)
-    out_s, hidden_s, branch_s = step(only_busiest, spill_rows, 0, spill_grads, 0)
+    out_0, hidden_0, branch_0 = finish(
+        always, *products(arrived_0, 0, arrived_0, 1), gate_up_matrix
+    )
     rows_0, grads_0 = split(arrived_0)
+    come_rows, come_grads, out_0, rows_0, grads_0 = lax.optimization_barrier(
+        (come_rows, come_grads, out_0, rows_0, grads_0)
+    )
+    spill_rows = jnp.concatenate([spill_rows, come_rows], axis=0)
+    spill_grads = swap_quarters(jnp.concatenate([spill_grads, come_grads], axis=0))
+    out_s, hidden_s, branch_s = finish(
+        only_busiest, *products(spill_rows, 0, spill_grads, 0), gate_up_matrix
+    )
     middle = feature_share // 2
     kept_a, sent_a = halves(out_s[:, :middle])
     kept_b, sent_b = halves(swap_quarters(out_s[:, middle:]))
@@ -251,18 +256,25 @@
     )
 
     back_0 = exchange(out_0, expert_count)
-    come_a = swap_with(sent_a, 1)
-    come_b = swap_with(sent_b, 2)
-    out_1, hidden_1, branch_1 = step(always, arrived_1, 0, arrived_1, 1)
-    back_0, come_a, come_b, out_1, arrived_1 = lax.optimization_barrier(
-        (back_0, come_a, come_b, out_1, arrived_1)
-    )
-
-    back_1 = exchange(out_1, expert_count)
-    back_s = jnp.concatenate([halve(kept_a + come_a, 2), halve(kept_b + come_b, 1)], axis=1)
+    come_a, come_b = swap_with(sent_a, 1), swap_with(sent_b, 2)
+    come_a, come_b, gate_pair, grad_pair = lax.optimization_barrier(
+        (come_a, come_b, *products(arrived_1, 0, arrived_1, 1))
+    )
+    kept_a, sent_a = halves(kept_a + come_a)
+    kept_b, sent_b = halves(kept_b + come_b)
+    come_a, come_b = swap_with(sent_a, 2), swap_with(sent_b, 1)
+    out_1, hidden_1, branch_1 = finish(always, gate_pair, grad_pair, gate_up_matrix)
+    come_a, come_b, out_1 = lax.optimization_barrier((come_a, come_b, out_1))
+    back_s = jnp.concatenate([kept_a + come_a, kept_b + come_b], axis=1)
+    back_0, back_s, out_1, arrived_1 = lax.optimization_barrier(
+        (back_0, back_s, out_1, arrived_1)
+    )
+
     for mask in reversed(far[1:]):
         back_s = halve(back_s, mask)
     rows_1, grads_1 = split(arrived_1)
+    out_1, rows_1 = lax.optimization_barrier((out_1, rows_1))
+    back_1 = exchange(out_1, expert_count)
 
     all_rows = jnp.concatenate([spill_rows, rows_0, rows_1], axis=0)
     all_grads = jnp.concatenate([spill_grads, grads_0, grads_1], axis=0)

time: 432 us -> 416 us (0.963)
  waiting for transfers between devices: 156 us -> 146 us
    ppermute x12, waiting for transfers between devices: 155 us -> 144 us  [swap_with(): return lax.ppermute(rows, 'exp', [(i, i ^ mask) for i in range(total)])]
    unnamed x55 -> x61, local copies, waits for them, and re-layouts: 28.2 us -> 27.5 us
  transfers between devices with their start and end apart: 22 -> 22, of which waited for: 9 -> 9; matrix products, arithmetic and copies ran while one was open for 23% -> 21% of each run, Pallas kernels for 22% -> 19%
where the time goes in v5:
time: 416 us; the launch traced here: 415 us
  waiting for transfers between devices  146 us (35%)
  Pallas kernels  92.3 us (22%)
  starting transfers between devices  60.4 us (15%)
  local copies, waits for them, and re-layouts  53.6 us (13%)
  matrix products  48.1 us (12%)
  other arithmetic  12.5 us (3%)
    ppermute x12, waiting for transfers between devices, swap_with(): return lax.ppermute(rows, 'exp', [(i, i ^ mask) for i in range(total)])  144 us
    pallas_call x6, Pallas kernels, product(): pl.pallas_call(functools.partial(product_kernel, 1 if transposed else 0),...  51.1 us
    pallas_call x3, Pallas kernels, finish(): pl.pallas_call(finish_kernel, grid=(features // step,), in_specs=[pl.Bloc...  41.2 us
    all_to_all x4, starting transfers between devices, exchange(): lax.all_to_all(rows.reshape(expert_count, slots // expert_count, width),...  39.3 us
    dot_general x2, matrix products, outer(): lax.dot_general(left, right, (((0,), (0,)), ((), ())), preferred_element_...  34.6 us
    unnamed x61, local copies, waits for them, and re-layouts  27.5 us
    ppermute x12, starting transfers between devices, swap_with(): return lax.ppermute(rows, 'exp', [(i, i ^ mask) for i in range(total)])  19.5 us
    transpose x1, local copies, waits for them, and re-layouts, local(): gate_up_grads.transpose(0, 2, 1, 3)  13.8 us
  transfers between devices with their start and end apart: 22, of which 9 were waited for; matrix products, arithmetic and copies ran while one was open for 21% of the time, Pallas kernels for 19%

profile of v5, /device:TPU:0, one launch (start us, length us, event | category | flops | bytes accessed | tf_op | source)
XLA Modules:
  0.0 414.5 jit_solution(60249862186242195)
XLA Ops:
  0.6 1.0 convert_reduce_fusion
  1.6 1.3 select_reduce_fusion
  3.0 1.7 constant_dynamic-update-slice_fusion.1
  5.0 0.7 convolution_convert_fusion.3
  5.7 4.1 collective-permute-start
  9.8 20.3 %collective-permute-done = bf16[32,7168]{1,0:T(8,128)(2,1)S(1)} collective-permute-done((bf16[32,7168]{1,0:T(8,128)(2,1)S(1)}, bf16[32,7168]{1,0:T(8,128)(2,1)S(1)}, u32[]{:S(2)}, u32[]{:S(2)}) %collective-permute-start) | collective-permute-done | bytes 458784 | tf_op jit(solution)/shard_map/ppermute | solution.py:45
  30.2 0.8 collective-permute-start.1
  31.0 1.9 convolution_convert_fusion.2
  32.9 18.9 %collective-permute-done.1 = bf16[64,7168]{1,0:T(8,128)(2,1)S(1)} collective-permute-done((bf16[64,7168]{1,0:T(8,128)(2,1)S(1)}, bf16[64,7168]{1,0:T(8,128)(2,1)S(1)}, u32[]{:S(2)}, u32[]{:S(2)}) %collective-permute-start.1) | collective-permute-done | bytes 917536 | tf_op jit(solution)/shard_map/ppermute | solution.py:45
  51.9 1.0 fusion.40
  53.0 7.5 %all-to-all-start = ((bf16[16,8,7168]{2,1,0:T(8,128)(2,1)}), bf16[16,8,7168]{2,1,0:T(8,128)(2,1)S(1)}, u32[]{:S(2)}, u32[]{:S(2)}) async-start(bf16[16,8,7168]{2,1,0:T(8,128)(2,1)} %bitcast.43), calls=%async_computation | async-start | bytes 3670016 | tf_op jit(solution)/shard_map/all_to_all | solution.py:34
  60.5 1.9 collective-permute-start.3
  62.4 1.5 collective-permute-start.2
  63.9 16.1 %copy.10 = bf16[448,8,2,1024]{3,1,2,0:T(8,128)(2,1)} copy(bf16[448,8,2,1024]{3,2,1,0:T(2,128)(2,1)} %bitcast.38) | data formatting | bytes 29360128
  80.1 21.4 %collective-permute-done.3 = bf16[128,3584]{1,0:T(8,128)(2,1)S(1)} collective-permute-done((bf16[128,3584]{1,0:T(8,128)(2,1)}, bf16[128,3584]{1,0:T(8,128)(2,1)S(1)}, u32[]{:S(2)}, u32[]{:S(2)}) %collective-permute-start.3) | collective-permute-done | bytes 917536 | tf_op jit(solution)/shard_map/ppermute | solution.py:45
  101.5 1.4 pad_maximum_fusion.4
  102.8 1.4 pad_maximum_fusion.3
  104.2 6.1 %convolution_convert_fusion.1 = bf16[384,7168]{1,0:T(8,128)(2,1)} fusion(bf16[384,256]{1,0:T(8,128)(2,1)S(1)} %fusion.23, bf16[256,7168]{1,0:T(8,128)(2,1)} %copy-done.10), kind=kOutput, calls=%fused_computation.1 | convolution fusion | flops 1412038656 | bytes 9371648 | tf_op jit(solution)/shard_map/dot_general | solution.py:27
  110.3 5.7 %all-to-all-start.1 = ((bf16[16,24,7168]{2,1,0:T(8,128)(2,1)}), bf16[16,24,7168]{2,1,0:T(8,128)(2,1)}, u32[]{:S(2)}, u32[]{:S(2)}) async-start(bf16[16,24,7168]{2,1,0:T(8,128)(2,1)} %bitcast.37), calls=%async_computation.1 | async-start | bytes 11010048 | tf_op jit(solution)/shard_map/all_to_all | solution.py:34
  116.0 1.9 collective-permute-start.4
  117.9 1.5 collective-permute-start.5
  119.4 8.7 %shard_map.76.gate_a = bf16[128,2048]{1,0:T(8,128)(2,1)S(1)} custom-call(bf16[128,7168]{1,0:T(8,128)(2,1)S(1)} %bitcast.25, bf16[3584,2048]{1,0:T(8,128)(2,1)} %bitcast.28), custom_call_target="tpu_custom_call" | custom-call | flops 1 | bytes 1 | tf_op jit(solution)/shard_map/pallas_call | solution.py:102
  128.2 5.3 %shard_map.77.grad_a = bf16[128,1024]{1,0:T(8,128)(2,1)S(1)} custom-call(bf16[128,7168]{1,0:T(8,128)(2,1)S(1)} %bitcast.26, bf16[1024,3584]{1,0:T(8,128)(2,1)} %bitcast.34), custom_call_target="tpu_custom_call" | custom-call | flops 1 | bytes 1 | tf_op jit(solution)/shard_map/pallas_call | solution.py:102
  133.6 0.6 collective-permute-start.7
  134.1 1.3 fusion.39
  135.4 11.2 %shard_map.78 = (bf16[128,3584]{1,0:T(8,128)(2,1)}, bf16[128,1024]{1,0:T(8,128)(2,1)S(1)}, bf16[128,2048]{1,0:T(8,128)(2,1)S(1)}) custom-call(s32[1]{0:T(128)} %constant.20.clone.1.keep_ref, bf16[128,2048]{1,0:T(8,128)(2,1)S(1)} %shard_map.76.gate_a, bf16[128,2048]{1,0:T(8,128)(2,1)S(1)} %collective-permute-done.6.gate_b, ...), custom_call_target="tpu_custom_call" | custom-call | flops 1 | bytes 1 | tf_op jit(solution)/shard_map/pallas_call | solution.py:161
  146.7 0.8 copy-done.8
  147.4 52.4 %collective-permute-done.4 = bf16[256,3584]{1,0:T(8,128)(2,1)S(1)} collective-permute-done((bf16[256,3584]{1,0:T(8,128)(2,1)}, bf16[256,3584]{1,0:T(8,128)(2,1)S(1)}, u32[]{:S(2)}, u32[]{:S(2)}) %collective-permute-start.4) | collective-permute-done | bytes 1835040 | tf_op jit(solution)/shard_map/ppermute | solution.py:45
  199.9 5.4 %collective-permute-done.5 = bf16[256,3584]{1,0:T(8,128)(2,1)S(1)} collective-permute-done((bf16[256,3584]{1,0:T(8,128)(2,1)}, bf16[256,3584]{1,0:T(8,128)(2,1)S(1)}, u32[]{:S(2)}, u32[]{:S(2)}) %collective-permute-start.5) | collective-permute-done | bytes 1835040 | tf_op jit(solution)/shard_map/ppermute | solution.py:45
  205.5 1.2 copy-done.11
  206.7 1.0 constant_dynamic-update-slice_fusion.6
  207.7 11.9 %shard_map.79.gate_a = bf16[512,2048]{1,0:T(8,128)(2,1)S(1)} custom-call(bf16[512,3584]{1,0:T(8,128)(2,1)S(1)} %pad_maximum_fusion.left_ref, bf16[3584,2048]{1,0:T(8,128)(2,1)} %bitcast.30), custom_call_target="tpu_custom_call" | custom-call | flops 1 | bytes 1 | tf_op jit(solution)/shard_map/pallas_call | solution.py:102
  219.7 1.1 constant_dynamic-update-slice_fusion.5
  220.9 1.2 constant_dynamic-update-slice_fusion.4
  222.1 1.2 constant_dynamic-update-slice_fusion.3
  223.5 6.6 %shard_map.80.grad_a = bf16[512,1024]{1,0:T(8,128)(2,1)S(1)} custom-call(bf16[512,3584]{1,0:T(8,128)(2,1)S(1)} %pad_maximum_fusion.1.left_ref, bf16[1024,3584]{1,0:T(8,128)(2,1)} %bitcast.35), custom_call_target="tpu_custom_call" | custom-call | flops 1 | bytes 1 | tf_op jit(solution)/shard_map/pallas_call | solution.py:102
  231.1 1.9 collective-permute-done.9.grad_b
  233.0 16.4 %shard_map.81 = (bf16[512,3584]{1,0:T(8,128)(2,1)}, bf16[512,1024]{1,0:T(8,128)(2,1)S(1)}, bf16[512,2048]{1,0:T(8,128)(2,1)S(1)}) custom-call(s32[1]{0:T(128)} %bitcast.5.keep_ref, bf16[512,2048]{1,0:T(8,128)(2,1)} %copy-done, bf16[512,2048]{1,0:T(8,128)(2,1)} %collective-permute-done.8.gate_b, bf16[512,1024]{1,0:T(8,128)(2,1)S(1)} %shard_map.80.grad_a, ...), custom_call_target="tpu_custom_call" | custom-call | flops 1 | bytes 1 | tf_op jit(solution)/shard_map/pallas_call | solution.py:161
  249.4 2.7 fusion.37
  252.1 1.4 pad_maximum_fusion.6
  253.5 1.4 fusion.38
  254.9 11.7 %shard_map.82.gate_a = bf16[384,2048]{1,0:T(8,128)(2,1)S(1)} custom-call(bf16[384,7168]{1,0:T(8,128)(2,1)} %bitcast.3.left_ref, bf16[3584,2048]{1,0:T(8,128)(2,1)} %bitcast.32), custom_call_target="tpu_custom_call" | custom-call | flops 1 | bytes 1 | tf_op jit(solution)/shard_map/pallas_call | solution.py:102
  266.7 0.4 collective-permute-start.12
  267.1 4.8 %collective-permute-start.10 = (bf16[256,1792]{1,0:T(8,128)(2,1)}, bf16[256,1792]{1,0:T(8,128)(2,1)}, u32[]{:S(2)}, u32[]{:S(2)}) collective-permute-start(bf16[256,1792]{1,0:T(8,128)(2,1)} %get-tuple-element.68), channel_id=1, source_target_pairs={{0,1},{1,0},{2,3},{3,2},{4,5},{5,4},{6,7},{7,6},{8,9},{9,8},{10,11... | collective-permute-start | bytes 2752520 | tf_op jit(solution)/shard_map/ppermute | solution.py:45
  271.9 6.8 %shard_map.83.grad_a = bf16[384,1024]{1,0:T(8,128)(2,1)S(1)} custom-call(bf16[384,7168]{1,0:T(8,128)(2,1)} %bitcast.3.left_ref, bf16[1024,3584]{1,0:T(8,128)(2,1)} %bitcast.36), custom_call_target="tpu_custom_call" | custom-call | flops 1 | bytes 1 | tf_op jit(solution)/shard_map/pallas_call | solution.py:102
  278.7 10.5 %all-to-all-start.2 = ((bf16[16,8,3584]{2,1,0:T(8,128)(2,1)}), bf16[16,8,3584]{2,1,0:T(8,128)(2,1)}, u32[]{:S(2)}, u32[]{:S(2)}) async-start(bf16[16,8,3584]{2,1,0:T(8,128)(2,1)} %bitcast.6), calls=%async_computation.2 | async-start | bytes 1835008 | tf_op jit(solution)/shard_map/all_to_all | solution.py:34
  289.3 4.0 collective-permute-done.10
  293.3 4.9 %collective-permute-done.11 = bf16[256,1792]{1,0:T(8,128)(2,1)} collective-permute-done((bf16[256,1792]{1,0:T(8,128)(2,1)}, bf16[256,1792]{1,0:T(8,128)(2,1)}, u32[]{:S(2)}, u32[]{:S(2)}) %collective-permute-start.11) | collective-permute-done | bytes 917536 | tf_op jit(solution)/shard_map/ppermute | solution.py:45
  298.3 1.7 add.33
  300.1 1.4 add.32
  301.6 1.0 constant_dynamic-update-slice_fusion.2
  302.6 13.6 %shard_map.84 = (bf16[384,3584]{1,0:T(8,128)(2,1)}, bf16[384,1024]{1,0:T(8,128)(2,1)S(1)}, bf16[384,2048]{1,0:T(8,128)(2,1)S(1)}) custom-call(s32[1]{0:T(128)} %constant.20.clone.1.keep_ref, bf16[384,2048]{1,0:T(8,128)(2,1)S(1)} %shard_map.82.gate_a, bf16[384,2048]{1,0:T(8,128)(2,1)} %collective-permute-done.12.gate_b, ...), custom_call_target="tpu_custom_call" | custom-call | flops 1 | bytes 1 | tf_op jit(solution)/shard_map/pallas_call | solution.py:161
  316.2 1.1 copy-done.3
  317.3 0.9 copy-done.6
  318.3 1.0 pad_maximum_fusion.8
  319.3 5.5 %slice_dynamic-update-slice_fusion = (bf16[1024,3584]{1,0:T(8,128)(2,1)}, bf16[384,3584]{1,0:T(8,128)(2,1)}) fusion(bf16[1024,3584]{1,0:T(8,128)(2,1)} %constant_dynamic-update-slice_fusion.2, bf16[384,7168]{1,0:T(8,128)(2,1)} %bitcast.3.left_ref), kind=kLoop, calls=%fused_computation.26 | loop fusion | bytes 11010048 | tf_op jit(solution)/shard_map/concatenate | solution.py:280
  324.9 15.5 %all-to-all-start.3 = ((bf16[16,24,3584]{2,1,0:T(8,128)(2,1)}), bf16[16,24,3584]{2,1,0:T(8,128)(2,1)}, u32[]{:S(2)}, u32[]{:S(2)}) async-start(bf16[16,24,3584]{2,1,0:T(8,128)(2,1)} %bitcast.44), calls=%async_computation.3 | async-start | bytes 5505024 | tf_op jit(solution)/shard_map/all_to_all | solution.py:34
  340.5 21.4 %convolution_convert_fusion = bf16[3584,2048]{1,0:T(8,128)(2,1)} fusion(bf16[384,3584]{1,0:T(8,128)(2,1)} %get-tuple-element.86, bf16[128,3584]{1,0:T(8,128)(2,1)} %get-tuple-element.83, bf16[256,3584]{1,0:T(8,128)(2,1)} %copy-done.19, bf16[256,3584]{1,0:T(8,128)(2,1)} %pad_maximum_fusion.3, bf16[384,2048]{1,0:T(8,128)(2,1)} %copy-done.3, ...), kind=kOutput, calls=%fused_computation | convolution fusion | flops 15081668608 | bytes 26214400 | tf_op jit(solution)/shard_map/dot_general | solution.py:184
  362.0 13.2 %fusion.7 = bf16[1,1024,3584]{2,1,0:T(8,128)(2,1)} fusion(bf16[1024,3584]{1,0:T(8,128)(2,1)} %get-tuple-element.99, bf16[384,1024]{1,0:T(8,128)(2,1)S(1)} %copy-done.7, bf16[128,1024]{1,0:T(8,128)(2,1)S(1)} %get-tuple-element.91, bf16[512,1024]{1,0:T(8,128)(2,1)S(1)} %copy-done.5), kind=kOutput, calls=%fused_computation.12 | convolution fusion | flops 7526154240 | bytes 16777216 | tf_op jit(solution)/shard_map/dot_general | solution.py:184
  375.2 1.1 slice_add_fusion.2
  376.3 2.8 collective-permute-start.17
  379.2 13.8 %copy.9 = bf16[448,8,2,1024]{3,2,1,0:T(2,128)(2,1)} copy(bf16[448,8,2,1024]{3,1,2,0:T(8,128)(2,1)S(1)} %bitcast.41) | data formatting | bytes 29360128 | tf_op jit(solution)/shard_map/transpose | solution.py:291
  393.0 16.6 %collective-permute-done.17 = bf16[32,3584]{1,0:T(8,128)(2,1)S(1)} collective-permute-done((bf16[32,3584]{1,0:T(8,128)(2,1)S(1)}, bf16[32,3584]{1,0:T(8,128)(2,1)S(1)}, u32[]{:S(2)}, u32[]{:S(2)}) %collective-permute-start.17) | collective-permute-done | bytes 229408 | tf_op jit(solution)/shard_map/ppermute | solution.py:45
  409.7 4.9 %convolution_convert_fusion.5 = bf16[256,3584]{1,0:T(8,128)(2,1)} fusion(bf16[384,3584]{1,0:T(8,128)(2,1)} %bitcast.12, bf16[128,3584]{1,0:T(8,128)(2,1)} %bitcast.7, bf16[32,3584]{1,0:T(8,128)(2,1)S(1)} %slice_add_fusion.3, bf16[384,256]{1,0:T(8,128)(2,1)S(1)} %copy-done.22, bf16[128,256]{1,0:T(8,128)(2,1)S(1)} %fusion.30, bf16[32,256]{1,0:T(8,128)(2,1)S(1)} %fusion.32), kind=kOutput, calls=%fused_computation.13 | convolution fusion | flops 1011695616 | bytes 6012928 | tf_op jit(solution)/shard_map/dot_general | solution.py:297
  (87 shorter events, 2.2 us)
Async XLA Ops:
  0.6 4.1 copy-start.20
  4.9 27.9 %copy-start.10 = (bf16[256,7168]{1,0:T(8,128)(2,1)}, bf16[256,7168]{1,0:T(8,128)(2,1)S(1)}, u32[]{:S(2)}) copy-start(bf16[256,7168]{1,0:T(8,128)(2,1)S(1)} %constant_dynamic-update-slice_fusion) | copy-start | bytes 11010052
  5.7 24.5 %collective-permute-start = (bf16[32,7168]{1,0:T(8,128)(2,1)S(1)}, bf16[32,7168]{1,0:T(8,128)(2,1)S(1)}, u32[]{:S(2)}, u32[]{:S(2)}) collective-permute-start(bf16[32,7168]{1,0:T(8,128)(2,1)S(1)} %convolution_convert_fusion.3), channel_id=1, source_target_pairs={{0,8},{1,9},{2,10},{3,11},{4,12},{5,13},{6,14},{7,15},{8,0},{9,1},... | collective-permute-start | bytes 1376264 | tf_op jit(solution)/shard_map/ppermute | solution.py:45
  30.2 21.6 %collective-permute-start.1 = (bf16[64,7168]{1,0:T(8,128)(2,1)S(1)}, bf16[64,7168]{1,0:T(8,128)(2,1)S(1)}, u32[]{:S(2)}, u32[]{:S(2)}) collective-permute-start(bf16[64,7168]{1,0:T(8,128)(2,1)S(1)} %pad_maximum_fusion.5), channel_id=1, source_target_pairs={{0,4},{1,5},{2,6},{3,7},{4,0},{5,1},{6,2},{7,3},{8,12},{9,13},{10,... | collective-permute-start | bytes 2752520 | tf_op jit(solution)/shard_map/ppermute | solution.py:45
  53.0 51.3 %all-to-all-start = ((bf16[16,8,7168]{2,1,0:T(8,128)(2,1)}), bf16[16,8,7168]{2,1,0:T(8,128)(2,1)S(1)}, u32[]{:S(2)}, u32[]{:S(2)}) async-start(bf16[16,8,7168]{2,1,0:T(8,128)(2,1)} %bitcast.43), calls=%async_computation | async-start | bytes 3670016 | tf_op jit(solution)/shard_map/all_to_all | solution.py:34
  60.5 41.0 %collective-permute-start.3 = (bf16[128,3584]{1,0:T(8,128)(2,1)}, bf16[128,3584]{1,0:T(8,128)(2,1)S(1)}, u32[]{:S(2)}, u32[]{:S(2)}) collective-permute-start(bf16[128,3584]{1,0:T(8,128)(2,1)} %get-tuple-element.53), channel_id=1, source_target_pairs={{0,1},{1,0},{2,3},{3,2},{4,5},{5,4},{6,7},{7,6},{8,9},{9,8},{10,11... | collective-permute-start | bytes 2752520 | tf_op jit(solution)/shard_map/ppermute | solution.py:45
  62.4 40.4 %collective-permute-start.2 = (bf16[128,3584]{1,0:T(8,128)(2,1)S(1)}, bf16[128,3584]{1,0:T(8,128)(2,1)S(1)}, u32[]{:S(2)}, u32[]{:S(2)}) collective-permute-start(bf16[128,3584]{1,0:T(8,128)(2,1)S(1)} %get-tuple-element.52), channel_id=1, source_target_pairs={{0,2},{1,3},{2,0},{3,1},{4,6},{5,7},{6,4},{7,5},{8,10},{9,11},{10,... | collective-permute-start | bytes 2752520 | tf_op jit(solution)/shard_map/ppermute | solution.py:45
  63.9 37.6 %copy-start.13 = (bf16[128,3584]{1,0:T(8,128)(2,1)S(1)}, bf16[128,3584]{1,0:T(8,128)(2,1)}, u32[]{:S(2)}) copy-start(bf16[128,3584]{1,0:T(8,128)(2,1)} %get-tuple-element.53) | copy-start | bytes 2752516
  80.1 24.2 %copy-start.21 = (bf16[384,256]{1,0:T(8,128)(2,1)}, bf16[384,256]{1,0:T(8,128)(2,1)S(1)}, u32[]{:S(2)}) copy-start(bf16[384,256]{1,0:T(8,128)(2,1)S(1)} %fusion.23) | copy-start | bytes 589828
  110.3 144.6 %all-to-all-start.1 = ((bf16[16,24,7168]{2,1,0:T(8,128)(2,1)}), bf16[16,24,7168]{2,1,0:T(8,128)(2,1)}, u32[]{:S(2)}, u32[]{:S(2)}) async-start(bf16[16,24,7168]{2,1,0:T(8,128)(2,1)} %bitcast.37), calls=%async_computation.1 | async-start | bytes 11010048 | tf_op jit(solution)/shard_map/all_to_all | solution.py:34
  116.0 83.9 %collective-permute-start.4 = (bf16[256,3584]{1,0:T(8,128)(2,1)}, bf16[256,3584]{1,0:T(8,128)(2,1)S(1)}, u32[]{:S(2)}, u32[]{:S(2)}) collective-permute-start(bf16[256,3584]{1,0:T(8,128)(2,1)} %pad_maximum_fusion.3), channel_id=1, source_target_pairs={{0,1},{1,0},{2,3},{3,2},{4,5},{5,4},{6,7},{7,6},{8,9},{9,8},{10,11... | collective-permute-start | bytes 5505032 | tf_op jit(solution)/shard_map/ppermute | solution.py:45
  117.9 87.3 %collective-permute-start.5 = (bf16[256,3584]{1,0:T(8,128)(2,1)}, bf16[256,3584]{1,0:T(8,128)(2,1)S(1)}, u32[]{:S(2)}, u32[]{:S(2)}) collective-permute-start(bf16[256,3584]{1,0:T(8,128)(2,1)} %pad_maximum_fusion.4), channel_id=1, source_target_pairs={{0,2},{1,3},{2,0},{3,1},{4,6},{5,7},{6,4},{7,5},{8,10},{9,11},{10,... | collective-permute-start | bytes 5505032 | tf_op jit(solution)/shard_map/ppermute | solution.py:45
  128.1 7.3 %collective-permute-start.6 = (bf16[128,2048]{1,0:T(8,128)(2,1)S(1)}, bf16[128,2048]{1,0:T(8,128)(2,1)S(1)}, u32[]{:S(2)}, u32[]{:S(2)}) collective-permute-start(bf16[128,2048]{1,0:T(8,128)(2,1)S(1)} %shard_map.76.gate_a), channel_id=1, source_target_pairs={{0,16},{16,0},{1,17},{17,1},{2,18},{18,2},{3,19},{19,3},{4,20},{20... | collective-permute-start | bytes 1572872 | tf_op jit(solution)/shard_map/ppermute | solution.py:115
  133.6 1.9 collective-permute-start.7
  135.4 69.8 %copy-start.12 = (bf16[256,3584]{1,0:T(8,128)(2,1)S(1)}, bf16[256,3584]{1,0:T(8,128)(2,1)}, u32[]{:S(2)}) copy-start(bf16[256,3584]{1,0:T(8,128)(2,1)} %pad_maximum_fusion.3) | copy-start | bytes 5505028
  146.7 0.8 copy-start.8
  199.9 5.6 %copy-start.19 = (bf16[256,3584]{1,0:T(8,128)(2,1)}, bf16[256,3584]{1,0:T(8,128)(2,1)S(1)}, u32[]{:S(2)}) copy-start(bf16[256,3584]{1,0:T(8,128)(2,1)S(1)} %collective-permute-done.4) | copy-start | bytes 5505028
  205.2 1.5 copy-start.11
  219.6 3.6 copy-start
  219.7 13.3 %collective-permute-start.8 = (bf16[512,2048]{1,0:T(8,128)(2,1)S(1)}, bf16[512,2048]{1,0:T(8,128)(2,1)}, u32[]{:S(2)}, u32[]{:S(2)}) collective-permute-start(bf16[512,2048]{1,0:T(8,128)(2,1)S(1)} %shard_map.79.gate_a), channel_id=1, source_target_pairs={{0,16},{16,0},{1,17},{17,1},{2,18},{18,2},{3,19},{19,3},{4,20},{20... | collective-permute-start | bytes 6291464 | tf_op jit(solution)/shard_map/ppermute | solution.py:115
  230.1 2.9 collective-permute-start.9
  249.3 4.1 copy-start.1
  249.3 4.1 copy-start.4
  249.3 4.1 copy-start.15
  266.7 31.6 %collective-permute-start.12 = (bf16[384,2048]{1,0:T(8,128)(2,1)S(1)}, bf16[384,2048]{1,0:T(8,128)(2,1)}, u32[]{:S(2)}, u32[]{:S(2)}) collective-permute-start(bf16[384,2048]{1,0:T(8,128)(2,1)S(1)} %shard_map.82.gate_a), channel_id=1, source_target_pairs={{0,16},{16,0},{1,17},{17,1},{2,18},{18,2},{3,19},{19,3},{4,20},{20... | collective-permute-start | bytes 4718600 | tf_op jit(solution)/shard_map/ppermute | solution.py:115
  267.1 26.2 %collective-permute-start.10 = (bf16[256,1792]{1,0:T(8,128)(2,1)}, bf16[256,1792]{1,0:T(8,128)(2,1)}, u32[]{:S(2)}, u32[]{:S(2)}) collective-permute-start(bf16[256,1792]{1,0:T(8,128)(2,1)} %get-tuple-element.68), channel_id=1, source_target_pairs={{0,1},{1,0},{2,3},{3,2},{4,5},{5,4},{6,7},{7,6},{8,9},{9,8},{10,11... | collective-permute-start | bytes 2752520 | tf_op jit(solution)/shard_map/ppermute | solution.py:45
  271.9 26.4 %collective-permute-start.11 = (bf16[256,1792]{1,0:T(8,128)(2,1)}, bf16[256,1792]{1,0:T(8,128)(2,1)}, u32[]{:S(2)}, u32[]{:S(2)}) collective-permute-start(bf16[256,1792]{1,0:T(8,128)(2,1)} %get-tuple-element.69), channel_id=1, source_target_pairs={{0,2},{1,3},{2,0},{3,1},{4,6},{5,7},{6,4},{7,5},{8,10},{9,11},{10,... | collective-permute-start | bytes 2752520 | tf_op jit(solution)/shard_map/ppermute | solution.py:45
  278.7 10.7 %collective-permute-start.13 = (bf16[384,1024]{1,0:T(8,128)(2,1)S(1)}, bf16[384,1024]{1,0:T(8,128)(2,1)S(1)}, u32[]{:S(2)}, u32[]{:S(2)}) collective-permute-start(bf16[384,1024]{1,0:T(8,128)(2,1)S(1)} %shard_map.83.grad_a), channel_id=1, source_target_pairs={{0,16},{16,0},{1,17},{17,1},{2,18},{18,2},{3,19},{19,3},{4,20},{20... | collective-permute-start | bytes 2359304 | tf_op jit(solution)/shard_map/ppermute | solution.py:115
  278.7 40.6 %all-to-all-start.2 = ((bf16[16,8,3584]{2,1,0:T(8,128)(2,1)}), bf16[16,8,3584]{2,1,0:T(8,128)(2,1)}, u32[]{:S(2)}, u32[]{:S(2)}) async-start(bf16[16,8,3584]{2,1,0:T(8,128)(2,1)} %bitcast.6), calls=%async_computation.2 | async-start | bytes 1835008 | tf_op jit(solution)/shard_map/all_to_all | solution.py:34
  289.3 10.8 %copy-start.16 = (bf16[256,1792]{1,0:T(8,128)(2,1)S(1)}, bf16[256,1792]{1,0:T(8,128)(2,1)}, u32[]{:S(2)}) copy-start(bf16[256,1792]{1,0:T(8,128)(2,1)} %get-tuple-element.67) | copy-start | bytes 2752516
  289.3 12.3 %copy-start.14 = (bf16[128,3584]{1,0:T(8,128)(2,1)S(1)}, bf16[128,3584]{1,0:T(8,128)(2,1)}, u32[]{:S(2)}) copy-start(bf16[128,3584]{1,0:T(8,128)(2,1)} %get-tuple-element.93) | copy-start | bytes 2752516
  300.0 18.3 %collective-permute-start.15 = (bf16[128,1792]{1,0:T(8,128)(2,1)S(1)}, bf16[128,1792]{1,0:T(8,128)(2,1)S(1)}, u32[]{:S(2)}, u32[]{:S(2)}) collective-permute-start(bf16[128,1792]{1,0:T(8,128)(2,1)S(1)} %slice.112), channel_id=1, source_target_pairs={{0,1},{1,0},{2,3},{3,2},{4,5},{5,4},{6,7},{7,6},{8,9},{9,8},{10,11... | collective-permute-start | bytes 1376264 | tf_op jit(solution)/shard_map/ppermute | solution.py:45
  301.5 16.7 %collective-permute-start.14 = (bf16[128,1792]{1,0:T(8,128)(2,1)S(1)}, bf16[128,1792]{1,0:T(8,128)(2,1)S(1)}, u32[]{:S(2)}, u32[]{:S(2)}) collective-permute-start(bf16[128,1792]{1,0:T(8,128)(2,1)S(1)} %slice.111), channel_id=1, source_target_pairs={{0,2},{1,3},{2,0},{3,1},{4,6},{5,7},{6,4},{7,5},{8,10},{9,11},{10,... | collective-permute-start | bytes 1376264 | tf_op jit(solution)/shard_map/ppermute | solution.py:45
  316.2 1.1 copy-start.3
  317.3 0.9 copy-start.6
  319.3 5.5 %copy-start.17 = (bf16[128,3584]{1,0:T(8,128)(2,1)S(1)}, bf16[128,3584]{1,0:T(8,128)(2,1)}, u32[]{:S(2)}) copy-start(bf16[128,3584]{1,0:T(8,128)(2,1)} %pad_maximum_fusion.8) | copy-start | bytes 2752516
  324.8 15.7 %copy-start.2 = (bf16[512,2048]{1,0:T(8,128)(2,1)S(1)}, bf16[512,2048]{1,0:T(8,128)(2,1)}, u32[]{:S(2)}) copy-start(bf16[512,2048]{1,0:T(8,128)(2,1)} %copy-done.1) | copy-start | bytes 6291460
  324.8 15.7 %copy-start.9 = (bf16[128,2048]{1,0:T(8,128)(2,1)S(1)}, bf16[128,2048]{1,0:T(8,128)(2,1)}, u32[]{:S(2)}) copy-start(bf16[128,2048]{1,0:T(8,128)(2,1)} %copy-done.8) | copy-start | bytes 1572868
  324.9 50.3 %collective-permute-start.16 = (bf16[64,3584]{1,0:T(8,128)(2,1)S(1)}, bf16[64,3584]{1,0:T(8,128)(2,1)}, u32[]{:S(2)}, u32[]{:S(2)}) collective-permute-start(bf16[64,3584]{1,0:T(8,128)(2,1)S(1)} %slice.103), channel_id=1, source_target_pairs={{0,4},{1,5},{2,6},{3,7},{4,0},{5,1},{6,2},{7,3},{8,12},{9,13},{10,... | collective-permute-start | bytes 1376264 | tf_op jit(solution)/shard_map/ppermute | solution.py:45
  324.9 84.7 %all-to-all-start.3 = ((bf16[16,24,3584]{2,1,0:T(8,128)(2,1)}), bf16[16,24,3584]{2,1,0:T(8,128)(2,1)}, u32[]{:S(2)}, u32[]{:S(2)}) async-start(bf16[16,24,3584]{2,1,0:T(8,128)(2,1)} %bitcast.44), calls=%async_computation.3 | async-start | bytes 5505024 | tf_op jit(solution)/shard_map/all_to_all | solution.py:34
  340.5 21.5 %copy-start.5 = (bf16[512,1024]{1,0:T(8,128)(2,1)S(1)}, bf16[512,1024]{1,0:T(8,128)(2,1)}, u32[]{:S(2)}) copy-start(bf16[512,1024]{1,0:T(8,128)(2,1)} %copy-done.4) | copy-start | bytes 3145732
  340.5 21.5 %copy-start.7 = (bf16[384,1024]{1,0:T(8,128)(2,1)S(1)}, bf16[384,1024]{1,0:T(8,128)(2,1)}, u32[]{:S(2)}) copy-start(bf16[384,1024]{1,0:T(8,128)(2,1)} %copy-done.6) | copy-start | bytes 2359300
  362.0 17.2 %slice-start = ((s8[14680064]{0:T(1024)(128)(4,1)}), s8[4194304]{0:T(1024)(128)(4,1)S(1)}, s32[]{:S(2)}) async-start(s8[14680064]{0:T(1024)(128)(4,1)} %bitcast.39), calls=%async_computation.4 | async-start | bytes 8388608
  362.0 13.2 %copy-start.18 = (bf16[128,3584]{1,0:T(8,128)(2,1)S(1)}, bf16[128,3584]{1,0:T(8,128)(2,1)}, u32[]{:S(2)}) copy-start(bf16[128,3584]{1,0:T(8,128)(2,1)} %pad_maximum_fusion.8) | copy-start | bytes 2752516
  362.0 17.2 %slice-start.1 = ((s8[14680064]{0:T(1024)(128)(4,1)}), s8[4194304]{0:T(1024)(128)(4,1)S(1)}, s32[]{:S(2)}) async-start(s8[14680064]{0:T(1024)(128)(4,1)} %bitcast.39), calls=%async_computation.5 | async-start | bytes 8388608
  362.0 17.2 %slice-start.2 = ((s8[14680064]{0:T(1024)(128)(4,1)}), s8[4194304]{0:T(1024)(128)(4,1)S(1)}, s32[]{:S(2)}) async-start(s8[14680064]{0:T(1024)(128)(4,1)} %bitcast.39), calls=%async_computation.6 | async-start | bytes 8388608
  362.0 17.2 %slice-start.3 = ((s8[14680064]{0:T(1024)(128)(4,1)}), s8[2097152]{0:T(1024)(128)(4,1)S(1)}, s32[]{:S(2)}) async-start(s8[14680064]{0:T(1024)(128)(4,1)} %bitcast.39), calls=%async_computation.7 | async-start | bytes 4194304
  376.3 33.3 %collective-permute-start.17 = (bf16[32,3584]{1,0:T(8,128)(2,1)S(1)}, bf16[32,3584]{1,0:T(8,128)(2,1)S(1)}, u32[]{:S(2)}, u32[]{:S(2)}) collective-permute-start(bf16[32,3584]{1,0:T(8,128)(2,1)S(1)} %slice.107), channel_id=1, source_target_pairs={{0,8},{1,9},{2,10},{3,11},{4,12},{5,13},{6,14},{7,15},{8,0},{9,1},... | collective-permute-start | bytes 688136 | tf_op jit(solution)/shard_map/ppermute | solution.py:45
  379.2 30.4 %copy-start.22 = (bf16[384,256]{1,0:T(8,128)(2,1)S(1)}, bf16[384,256]{1,0:T(8,128)(2,1)}, u32[]{:S(2)}) copy-start(bf16[384,256]{1,0:T(8,128)(2,1)} %copy-done.21) | copy-start | bytes 589828

commit v6 on v5

--- a/solution.py
+++ b/solution.py
@@ -193,7 +193,7 @@
     gate_up_matrix = w_gate_up.reshape(feature_share, 2 * hidden_width)
     down_matrix = w_down.reshape(hidden_width, feature_share)
     cap = 2 * row_count // expert_count
-    bounds = (0, cap // 4, cap)
+    bounds = (0, cap // 2, cap)
 
     rank = rank_in_expert(row_expert)
     is_spill = rank >= cap
@@ -228,52 +228,47 @@
     spill_rows, spill_grads, sent_0 = lax.optimization_barrier((spill_rows, spill_grads, sent_0))
 
     arrived_0 = exchange(sent_0, expert_count)
-    spill_rows, spill_grads = double(spill_rows, 2), double(spill_grads, 1)
-    arrived_0, spill_rows, spill_grads, hot_1, gate_up_matrix = lax.optimization_barrier(
-        (arrived_0, spill_rows, spill_grads, chunk_hot[1], gate_up_matrix)
-    )
-
-    come_rows, come_grads = swap_with(spill_rows, 1), swap_with(spill_grads, 2)
-    arrived_0, sent_1 = lax.optimization_barrier((arrived_0, place(hot_1, both)))
+    spill_rows = double(double(spill_rows, 2), 1)
+    spill_grads = swap_quarters(double(double(spill_grads, 1), 2))
+    sent_1 = place(chunk_hot[1], both)
+    arrived_0, spill_rows, spill_grads, sent_1, gate_up_matrix = lax.optimization_barrier(
+        (arrived_0, spill_rows, spill_grads, sent_1, gate_up_matrix)
+    )
+
     arrived_1 = exchange(sent_1, expert_count)
-    out_0, hidden_0, branch_0 = finish(
-        always, *products(arrived_0, 0, arrived_0, 1), gate_up_matrix
-    )
-    rows_0, grads_0 = split(arrived_0)
-    come_rows, come_grads, out_0, rows_0, grads_0 = lax.optimization_barrier(
-        (come_rows, come_grads, out_0, rows_0, grads_0)
-    )
-    spill_rows = jnp.concatenate([spill_rows, come_rows], axis=0)
-    spill_grads = swap_quarters(jnp.concatenate([spill_grads, come_grads], axis=0))
     out_s, hidden_s, branch_s = finish(
         only_busiest, *products(spill_rows, 0, spill_grads, 0), gate_up_matrix
     )
     middle = feature_share // 2
     kept_a, sent_a = halves(out_s[:, :middle])
     kept_b, sent_b = halves(swap_quarters(out_s[:, middle:]))
-    arrived_1, out_0, kept_a, sent_a, kept_b, sent_b = lax.optimization_barrier(
-        (arrived_1, out_0, kept_a, sent_a, kept_b, sent_b)
+    arrived_0, kept_a, sent_a, kept_b, sent_b = lax.optimization_barrier(
+        (arrived_0, kept_a, sent_a, kept_b, sent_b)
+    )
+    come_a, come_b = swap_with(sent_a, 1), swap_with(sent_b, 2)
+    out_0, hidden_0, branch_0 = finish(
+        always, *products(arrived_0, 0, arrived_0, 1), gate_up_matrix
+    )
+    rows_0, grads_0 = split(arrived_0)
+    arrived_1, out_0, come_a, come_b = lax.optimization_barrier(
+        (arrived_1, out_0, come_a, come_b)
     )
 
     back_0 = exchange(out_0, expert_count)
-    come_a, come_b = swap_with(sent_a, 1), swap_with(sent_b, 2)
-    come_a, come_b, gate_pair, grad_pair = lax.optimization_barrier(
-        (come_a, come_b, *products(arrived_1, 0, arrived_1, 1))
-    )
     kept_a, sent_a = halves(kept_a + come_a)
     kept_b, sent_b = halves(kept_b + come_b)
     come_a, come_b = swap_with(sent_a, 2), swap_with(sent_b, 1)
-    out_1, hidden_1, branch_1 = finish(always, gate_pair, grad_pair, gate_up_matrix)
-    come_a, come_b, out_1 = lax.optimization_barrier((come_a, come_b, out_1))
+    out_1, hidden_1, branch_1 = finish(
+        always, *products(arrived_1, 0, arrived_1, 1), gate_up_matrix
+    )
+    back_0, come_a, come_b, out_1, arrived_1 = lax.optimization_barrier(
+        (back_0, come_a, come_b, out_1, arrived_1)
+    )
     back_s = jnp.concatenate([kept_a + come_a, kept_b + come_b], axis=1)
-    back_0, back_s, out_1, arrived_1 = lax.optimization_barrier(
-        (back_0, back_s, out_1, arrived_1)
-    )
 
     for mask in reversed(far[1:]):
         back_s = halve(back_s, mask)
     rows_1, grads_1 = split(arrived_1)
-    out_1, rows_1 = lax.optimization_barrier((out_1, rows_1))
     back_1 = exchange(out_1, expert_count)
 
     all_rows = jnp.concatenate([spill_rows, rows_0, rows_1], axis=0)

time: 416 us -> 403 us (0.969)
  waiting for transfers between devices: 146 us -> 131 us
  local copies, waits for them, and re-layouts: 53.6 us -> 63.4 us
    ppermute x12, waiting for transfers between devices: 144 us -> 127 us  [swap_with(): return lax.ppermute(rows, 'exp', [(i, i ^ mask) for i in range(total)])]
    transpose x1, local copies, waits for them, and re-layouts: 13.8 us -> 27.1 us  [local(): gate_up_grads.transpose(0, 2, 1, 3)]
    slice x2 -> x3, local copies, waits for them, and re-layouts: 2.36 us -> 8.47 us  [split(): return (both_in[:, :feature_share], both_in[:, feature_share:])]
    concatenate x1 -> x0, local copies, waits for them, and re-layouts: 5.48 us -> none  [local(): all_grads = jnp.concatenate([spill_grads, grads_0, grads_1], axis=0)]
    all_to_all x4, starting transfers between devices: 39.3 us -> 34.5 us  [exchange(): lax.all_to_all(rows.reshape(expert_count, slots // expert_count, width),...]
    ppermute x12, starting transfers between devices: 19.5 us -> 23.8 us  [swap_with(): return lax.ppermute(rows, 'exp', [(i, i ^ mask) for i in range(total)])]
    unnamed x61 -> x54, local copies, waits for them, and re-layouts: 27.5 us -> 24.4 us
  transfers between devices with their start and end apart: 22 -> 22, of which waited for: 9 -> 8; matrix products, arithmetic and copies ran while one was open for 21% -> 26% of each run, Pallas kernels for 19% -> 23%
where the time goes in v6:
time: 403 us; the launch traced here: 402 us
  waiting for transfers between devices  131 us (33%)
  Pallas kernels  90.8 us (23%)
  local copies, waits for them, and re-layouts  63.4 us (16%)
  starting transfers between devices  59.2 us (15%)
  matrix products  44.6 us (11%)
  other arithmetic  10.4 us (3%)
    ppermute x12, waiting for transfers between devices, swap_with(): return lax.ppermute(rows, 'exp', [(i, i ^ mask) for i in range(total)])  127 us
    pallas_call x6, Pallas kernels, product(): pl.pallas_call(functools.partial(product_kernel, 1 if transposed else 0),...  51.6 us
    pallas_call x3, Pallas kernels, finish(): pl.pallas_call(finish_kernel, grid=(features // step,), in_specs=[pl.Bloc...  39.2 us
    all_to_all x4, starting transfers between devices, exchange(): lax.all_to_all(rows.reshape(expert_count, slots // expert_count, width),...  34.5 us
    dot_general x2, matrix products, outer(): lax.dot_general(left, right, (((0,), (0,)), ((), ())), preferred_element_...  33 us
    transpose x1, local copies, waits for them, and re-layouts, local(): gate_up_grads.transpose(0, 2, 1, 3)  27.1 us
    unnamed x54, local copies, waits for them, and re-layouts  24.4 us
    ppermute x12, starting transfers between devices, swap_with(): return lax.ppermute(rows, 'exp', [(i, i ^ mask) for i in range(total)])  23.8 us
  transfers between devices with their start and end apart: 22, of which 8 were waited for; matrix products, arithmetic and copies ran while one was open for 26% of the time, Pallas kernels for 23%

profile of v6, /device:TPU:0, one launch (start us, length us, event | category | flops | bytes accessed | tf_op | source)
XLA Modules:
  0.0 401.7 jit_solution(4271230427538111671)
XLA Ops:
  0.7 1.8 constant_dynamic-update-slice_fusion.1
  2.5 0.2 convert_reduce_fusion
  2.7 0.6 select_reduce_fusion
  3.3 0.2 constant_dynamic-update-slice_fusion
  3.5 0.7 convolution_convert_fusion.3
  4.3 4.1 %collective-permute-start = (bf16[32,7168]{1,0:T(8,128)(2,1)S(1)}, bf16[32,7168]{1,0:T(8,128)(2,1)S(1)}, u32[]{:S(2)}, u32[]{:S(2)}) collective-permute-start(bf16[32,7168]{1,0:T(8,128)(2,1)S(1)} %convolution_convert_fusion.3), channel_id=1, source_target_pairs={{0,8},{1,9},{2,10},{3,11},{4,12},{5,13},{6,14},{7,15},{8,0},{9,1},... | collective-permute-start | bytes 1376264 | tf_op jit(solution)/shard_map/ppermute | solution.py:45
  8.4 20.3 %collective-permute-done = bf16[32,7168]{1,0:T(8,128)(2,1)S(1)} collective-permute-done((bf16[32,7168]{1,0:T(8,128)(2,1)S(1)}, bf16[32,7168]{1,0:T(8,128)(2,1)S(1)}, u32[]{:S(2)}, u32[]{:S(2)}) %collective-permute-start) | collective-permute-done | bytes 458784 | tf_op jit(solution)/shard_map/ppermute | solution.py:45
  28.8 0.8 collective-permute-start.1
  29.6 3.0 convolution_convert_fusion.2
  32.5 17.9 %collective-permute-done.1 = bf16[64,7168]{1,0:T(8,128)(2,1)S(1)} collective-permute-done((bf16[64,7168]{1,0:T(8,128)(2,1)S(1)}, bf16[64,7168]{1,0:T(8,128)(2,1)S(1)}, u32[]{:S(2)}, u32[]{:S(2)}) %collective-permute-start.1) | collective-permute-done | bytes 917536 | tf_op jit(solution)/shard_map/ppermute | solution.py:45
  50.6 7.6 %all-to-all-start = ((bf16[16,16,7168]{2,1,0:T(8,128)(2,1)}), bf16[16,16,7168]{2,1,0:T(8,128)(2,1)}, u32[]{:S(2)}, u32[]{:S(2)}) async-start(bf16[16,16,7168]{2,1,0:T(8,128)(2,1)} %bitcast.36), calls=%async_computation | async-start | bytes 7340032 | tf_op jit(solution)/shard_map/all_to_all | solution.py:34
  58.2 1.9 collective-permute-start.2
  60.1 1.5 collective-permute-start.4
  61.6 50.2 %collective-permute-done.2 = bf16[128,3584]{1,0:T(8,128)(2,1)S(1)} collective-permute-done((bf16[128,3584]{1,0:T(8,128)(2,1)S(1)}, bf16[128,3584]{1,0:T(8,128)(2,1)S(1)}, u32[]{:S(2)}, u32[]{:S(2)}) %collective-permute-start.2) | collective-permute-done | bytes 917536 | tf_op jit(solution)/shard_map/ppermute | solution.py:45
  111.9 1.7 collective-permute-start.3
  113.7 2.5 collective-permute-start.5
  116.3 16.2 %copy.10 = bf16[448,8,2,1024]{3,1,2,0:T(8,128)(2,1)} copy(bf16[448,8,2,1024]{3,2,1,0:T(2,128)(2,1)} %bitcast.32) | data formatting | bytes 29360128
  132.5 3.0 convolution_convert_fusion.1
  135.4 27.2 %collective-permute-done.3 = bf16[256,3584]{1,0:T(8,128)(2,1)S(1)} collective-permute-done((bf16[256,3584]{1,0:T(8,128)(2,1)S(1)}, bf16[256,3584]{1,0:T(8,128)(2,1)S(1)}, u32[]{:S(2)}, u32[]{:S(2)}) %collective-permute-start.3) | collective-permute-done | bytes 1835040 | tf_op jit(solution)/shard_map/ppermute | solution.py:45
  162.6 1.9 pad_maximum_fusion.left_ref
  164.7 2.0 pad_maximum_fusion.1.left_ref
  166.7 10.5 %all-to-all-start.1 = ((bf16[16,16,7168]{2,1,0:T(8,128)(2,1)}), bf16[16,16,7168]{2,1,0:T(8,128)(2,1)}, u32[]{:S(2)}, u32[]{:S(2)}) async-start(bf16[16,16,7168]{2,1,0:T(8,128)(2,1)} %bitcast.35), calls=%async_computation.1 | async-start | bytes 7340032 | tf_op jit(solution)/shard_map/all_to_all | solution.py:34
  177.2 2.0 copy-done
  179.2 12.1 %shard_map.76.gate_a = bf16[512,2048]{1,0:T(8,128)(2,1)S(1)} custom-call(bf16[512,3584]{1,0:T(8,128)(2,1)S(1)} %copy-done, bf16[3584,2048]{1,0:T(8,128)(2,1)} %bitcast.23), custom_call_target="tpu_custom_call" | custom-call | flops 1 | bytes 1 | tf_op jit(solution)/shard_map/pallas_call | solution.py:102
  191.4 7.3 %shard_map.77.grad_a = bf16[512,1024]{1,0:T(8,128)(2,1)S(1)} custom-call(bf16[512,3584]{1,0:T(8,128)(2,1)S(1)} %copy-done.2, bf16[1024,3584]{1,0:T(8,128)(2,1)} %bitcast.29), custom_call_target="tpu_custom_call" | custom-call | flops 1 | bytes 1 | tf_op jit(solution)/shard_map/pallas_call | solution.py:102
  199.4 2.1 collective-permute-done.7.grad_b
  201.5 16.4 %shard_map.78 = (bf16[512,3584]{1,0:T(8,128)(2,1)}, bf16[512,1024]{1,0:T(8,128)(2,1)S(1)}, bf16[512,2048]{1,0:T(8,128)(2,1)S(1)}) custom-call(s32[1]{0:T(128)} %bitcast.2.keep_ref, bf16[512,2048]{1,0:T(8,128)(2,1)} %copy-done.4, bf16[512,2048]{1,0:T(8,128)(2,1)} %collective-permute-done.6.gate_b, bf16[512,1024]{1,0:T(8,128)(2,1)S(1)} %shard_map.77.grad_a, ...), custom_call_target="tpu_custom_call" | custom-call | flops 1 | bytes 1 | tf_op jit(solution)/shard_map/pallas_call | solution.py:161
  217.9 2.0 fusion.42
  219.9 1.0 pad_maximum_fusion.6
  221.0 1.0 fusion.43
  222.0 10.3 %shard_map.79.gate_a = bf16[256,2048]{1,0:T(8,128)(2,1)S(1)} custom-call(bf16[256,7168]{1,0:T(8,128)(2,1)} %bitcast.1.left_ref, bf16[3584,2048]{1,0:T(8,128)(2,1)} %bitcast.25), custom_call_target="tpu_custom_call" | custom-call | flops 1 | bytes 1 | tf_op jit(solution)/shard_map/pallas_call | solution.py:102
  232.3 0.2 collective-permute-start.8
  232.5 1.9 collective-permute-start.10
  234.4 1.5 collective-permute-start.11
  235.9 5.8 %shard_map.80.grad_a = bf16[256,1024]{1,0:T(8,128)(2,1)S(1)} custom-call(bf16[256,7168]{1,0:T(8,128)(2,1)} %bitcast.1.left_ref, bf16[1024,3584]{1,0:T(8,128)(2,1)} %bitcast.30), custom_call_target="tpu_custom_call" | custom-call | flops 1 | bytes 1 | tf_op jit(solution)/shard_map/pallas_call | solution.py:102
  241.8 1.9 collective-permute-done.9.grad_b
  243.7 11.4 %shard_map.81 = (bf16[256,3584]{1,0:T(8,128)(2,1)}, bf16[256,1024]{1,0:T(8,128)(2,1)S(1)}, bf16[256,2048]{1,0:T(8,128)(2,1)S(1)}) custom-call(s32[1]{0:T(128)} %constant.20.clone.1.keep_ref, bf16[256,2048]{1,0:T(8,128)(2,1)S(1)} %shard_map.79.gate_a, bf16[256,2048]{1,0:T(8,128)(2,1)S(1)} %collective-permute-done.8.gate_b, ...), custom_call_target="tpu_custom_call" | custom-call | flops 1 | bytes 1 | tf_op jit(solution)/shard_map/pallas_call | solution.py:161
  255.1 0.8 copy-done.9
  255.9 9.3 %collective-permute-done.10 = bf16[256,1792]{1,0:T(8,128)(2,1)S(1)} collective-permute-done((bf16[256,1792]{1,0:T(8,128)(2,1)S(1)}, bf16[256,1792]{1,0:T(8,128)(2,1)S(1)}, u32[]{:S(2)}, u32[]{:S(2)}) %collective-permute-start.10) | collective-permute-done | bytes 917536 | tf_op jit(solution)/shard_map/ppermute | solution.py:45
  265.1 0.9 copy-done.22
  266.1 9.2 %all-to-all-start.2 = ((bf16[16,16,3584]{2,1,0:T(8,128)(2,1)}), bf16[16,16,3584]{2,1,0:T(8,128)(2,1)}, u32[]{:S(2)}, u32[]{:S(2)}) async-start(bf16[16,16,3584]{2,1,0:T(8,128)(2,1)} %bitcast.38), calls=%async_computation.2 | async-start | bytes 3670016 | tf_op jit(solution)/shard_map/all_to_all | solution.py:34
  275.3 10.3 %shard_map.82.gate_a = bf16[256,2048]{1,0:T(8,128)(2,1)S(1)} custom-call(bf16[256,7168]{1,0:T(8,128)(2,1)} %bitcast.5.left_ref, bf16[3584,2048]{1,0:T(8,128)(2,1)} %bitcast.27), custom_call_target="tpu_custom_call" | custom-call | flops 1 | bytes 1 | tf_op jit(solution)/shard_map/pallas_call | solution.py:102
  285.7 5.9 %shard_map.83.grad_a = bf16[256,1024]{1,0:T(8,128)(2,1)S(1)} custom-call(bf16[256,7168]{1,0:T(8,128)(2,1)} %bitcast.5.left_ref, bf16[1024,3584]{1,0:T(8,128)(2,1)} %bitcast.31), custom_call_target="tpu_custom_call" | custom-call | flops 1 | bytes 1 | tf_op jit(solution)/shard_map/pallas_call | solution.py:102
  291.6 0.2 add.29
  291.9 1.9 collective-permute-start.12
  293.8 1.4 add.30
  295.3 1.5 collective-permute-start.13
  296.8 0.5 collective-permute-start.15
  297.3 4.2 %fusion.40 = (bf16[256,3584]{1,0:T(8,128)(2,1)}, bf16[256,3584]{1,0:T(8,128)(2,1)}) fusion(bf16[256,7168]{1,0:T(8,128)(2,1)} %bitcast.1.left_ref), kind=kLoop, calls=%fused_computation.71 | loop fusion | bytes 7340032 | tf_op jit(solution)/shard_map/slice | solution.py:212
  301.6 11.4 %shard_map.84 = (bf16[256,3584]{1,0:T(8,128)(2,1)}, bf16[256,1024]{1,0:T(8,128)(2,1)S(1)}, bf16[256,2048]{1,0:T(8,128)(2,1)S(1)}) custom-call(s32[1]{0:T(128)} %constant.20.clone.1.keep_ref, bf16[256,2048]{1,0:T(8,128)(2,1)S(1)} %shard_map.82.gate_a, bf16[256,2048]{1,0:T(8,128)(2,1)S(1)} %collective-permute-done.14.gate_b, ...), custom_call_target="tpu_custom_call" | custom-call | flops 1 | bytes 1 | tf_op jit(solution)/shard_map/pallas_call | solution.py:161
  313.0 1.0 copy-done.7
  313.9 0.8 copy-done.11
  314.7 0.8 copy-done.24
  315.5 2.5 collective-permute-done.13
  318.1 7.2 %all-to-all-start.3 = ((bf16[16,16,3584]{2,1,0:T(8,128)(2,1)}), bf16[16,16,3584]{2,1,0:T(8,128)(2,1)}, u32[]{:S(2)}, u32[]{:S(2)}) async-start(bf16[16,16,3584]{2,1,0:T(8,128)(2,1)} %bitcast.37), calls=%async_computation.3 | async-start | bytes 3670016 | tf_op jit(solution)/shard_map/all_to_all | solution.py:34
  325.2 1.2 slice_add_fusion
  326.4 1.2 slice_add_fusion.1
  327.7 1.9 collective-permute-start.16
  329.7 4.1 %fusion.41 = (bf16[256,3584]{1,0:T(8,128)(2,1)}, bf16[256,3584]{1,0:T(8,128)(2,1)}) fusion(bf16[256,7168]{1,0:T(8,128)(2,1)} %bitcast.5.left_ref), kind=kLoop, calls=%fused_computation.72 | loop fusion | bytes 7340032 | tf_op jit(solution)/shard_map/slice | solution.py:212
  333.8 21.7 %convolution_convert_fusion = bf16[3584,2048]{1,0:T(8,128)(2,1)} fusion(bf16[256,3584]{1,0:T(8,128)(2,1)} %get-tuple-element.74, bf16[256,3584]{1,0:T(8,128)(2,1)} %get-tuple-element.72, bf16[512,3584]{1,0:T(8,128)(2,1)S(1)} %copy-done.1, bf16[256,2048]{1,0:T(8,128)(2,1)S(1)} %copy-done.8, bf16[256,2048]{1,0:T(8,128)(2,1)S(1)} %get-tuple-element.61, ...), kind=kOutput, calls=%fused_computation | convolution fusion | flops 15074328576 | bytes 26214400 | tf_op jit(solution)/shard_map/dot_general | solution.py:184
  355.5 11.3 %fusion.10 = bf16[1,1024,3584]{2,1,0:T(8,128)(2,1)} fusion(bf16[256,3584]{1,0:T(8,128)(2,1)} %get-tuple-element.73, bf16[256,3584]{1,0:T(8,128)(2,1)S(1)} %copy-done.20, bf16[512,3584]{1,0:T(8,128)(2,1)S(1)} %copy-done.3, bf16[256,1024]{1,0:T(8,128)(2,1)S(1)} %copy-done.12, bf16[256,1024]{1,0:T(8,128)(2,1)S(1)} %copy-done.10, ...), kind=kOutput, calls=%fused_computation.15 | convolution fusion | flops 7548174336 | bytes 16777216 | tf_op jit(solution)/shard_map/dot_general | solution.py:184
  367.0 2.6 collective-permute-start.17
  369.7 27.1 %copy.9 = bf16[448,8,2,1024]{3,2,1,0:T(2,128)(2,1)} copy(bf16[448,8,2,1024]{3,1,2,0:T(8,128)(2,1)} %bitcast.33) | data formatting | bytes 29360128 | tf_op jit(solution)/shard_map/transpose | solution.py:286
  396.8 4.9 %convolution_convert_fusion.5 = bf16[256,3584]{1,0:T(8,128)(2,1)} fusion(bf16[256,3584]{1,0:T(8,128)(2,1)} %bitcast.12, bf16[256,3584]{1,0:T(8,128)(2,1)} %bitcast.7, bf16[32,3584]{1,0:T(8,128)(2,1)S(1)} %slice_add_fusion.2, pred[256,256]{1,0:T(32,128)(4,1)S(1)} %get-tuple-element.89, pred[256,256]{1,0:T(32,128)(4,1)S(1)} %get-tuple-element.90, ...), kind=kOutput, calls=%fused_computation.16 | convolution fusion | flops 1011138560 | bytes 5873664 | tf_op jit(solution)/shard_map/dot_general | solution.py:292
  (78 shorter events, 1.3 us)
Async XLA Ops:
  0.6 1.9 copy-start.25
  0.6 2.7 copy-start.21
  3.5 29.0 %copy-start.13 = (bf16[256,7168]{1,0:T(8,128)(2,1)}, bf16[256,7168]{1,0:T(8,128)(2,1)S(1)}, u32[]{:S(2)}) copy-start(bf16[256,7168]{1,0:T(8,128)(2,1)S(1)} %constant_dynamic-update-slice_fusion) | copy-start | bytes 11010052
  4.3 24.5 %collective-permute-start = (bf16[32,7168]{1,0:T(8,128)(2,1)S(1)}, bf16[32,7168]{1,0:T(8,128)(2,1)S(1)}, u32[]{:S(2)}, u32[]{:S(2)}) collective-permute-start(bf16[32,7168]{1,0:T(8,128)(2,1)S(1)} %convolution_convert_fusion.3), channel_id=1, source_target_pairs={{0,8},{1,9},{2,10},{3,11},{4,12},{5,13},{6,14},{7,15},{8,0},{9,1},... | collective-permute-start | bytes 1376264 | tf_op jit(solution)/shard_map/ppermute | solution.py:45
  28.8 21.6 %collective-permute-start.1 = (bf16[64,7168]{1,0:T(8,128)(2,1)S(1)}, bf16[64,7168]{1,0:T(8,128)(2,1)S(1)}, u32[]{:S(2)}, u32[]{:S(2)}) collective-permute-start(bf16[64,7168]{1,0:T(8,128)(2,1)S(1)} %pad_maximum_fusion.5), channel_id=1, source_target_pairs={{0,4},{1,5},{2,6},{3,7},{4,0},{5,1},{6,2},{7,3},{8,12},{9,13},{10,... | collective-permute-start | bytes 2752520 | tf_op jit(solution)/shard_map/ppermute | solution.py:45
  50.6 116.0 %all-to-all-start = ((bf16[16,16,7168]{2,1,0:T(8,128)(2,1)}), bf16[16,16,7168]{2,1,0:T(8,128)(2,1)}, u32[]{:S(2)}, u32[]{:S(2)}) async-start(bf16[16,16,7168]{2,1,0:T(8,128)(2,1)} %bitcast.36), calls=%async_computation | async-start | bytes 7340032 | tf_op jit(solution)/shard_map/all_to_all | solution.py:34
  58.2 53.6 %collective-permute-start.2 = (bf16[128,3584]{1,0:T(8,128)(2,1)S(1)}, bf16[128,3584]{1,0:T(8,128)(2,1)S(1)}, u32[]{:S(2)}, u32[]{:S(2)}) collective-permute-start(bf16[128,3584]{1,0:T(8,128)(2,1)S(1)} %get-tuple-element.38), channel_id=1, source_target_pairs={{0,2},{1,3},{2,0},{3,1},{4,6},{5,7},{6,4},{7,5},{8,10},{9,11},{10,... | collective-permute-start | bytes 2752520 | tf_op jit(solution)/shard_map/ppermute | solution.py:45
  60.1 53.5 %collective-permute-start.4 = (bf16[128,3584]{1,0:T(8,128)(2,1)S(1)}, bf16[128,3584]{1,0:T(8,128)(2,1)S(1)}, u32[]{:S(2)}, u32[]{:S(2)}) collective-permute-start(bf16[128,3584]{1,0:T(8,128)(2,1)S(1)} %get-tuple-element.39), channel_id=1, source_target_pairs={{0,1},{1,0},{2,3},{3,2},{4,5},{5,4},{6,7},{7,6},{8,9},{9,8},{10,11... | collective-permute-start | bytes 2752520 | tf_op jit(solution)/shard_map/ppermute | solution.py:45
  111.9 50.7 %collective-permute-start.3 = (bf16[256,3584]{1,0:T(8,128)(2,1)S(1)}, bf16[256,3584]{1,0:T(8,128)(2,1)S(1)}, u32[]{:S(2)}, u32[]{:S(2)}) collective-permute-start(bf16[256,3584]{1,0:T(8,128)(2,1)S(1)} %pad_maximum_fusion.3), channel_id=1, source_target_pairs={{0,1},{1,0},{2,3},{3,2},{4,5},{5,4},{6,7},{7,6},{8,9},{9,8},{10,11... | collective-permute-start | bytes 5505032 | tf_op jit(solution)/shard_map/ppermute | solution.py:45
  113.7 50.8 %collective-permute-start.5 = (bf16[256,3584]{1,0:T(8,128)(2,1)S(1)}, bf16[256,3584]{1,0:T(8,128)(2,1)S(1)}, u32[]{:S(2)}, u32[]{:S(2)}) collective-permute-start(bf16[256,3584]{1,0:T(8,128)(2,1)S(1)} %pad_maximum_fusion.4), channel_id=1, source_target_pairs={{0,2},{1,3},{2,0},{3,1},{4,6},{5,7},{6,4},{7,5},{8,10},{9,11},{10,... | collective-permute-start | bytes 5505032 | tf_op jit(solution)/shard_map/ppermute | solution.py:45
  116.3 16.2 %copy-start.14 = (bf16[256,7168]{1,0:T(8,128)(2,1)S(1)}, bf16[256,7168]{1,0:T(8,128)(2,1)}, u32[]{:S(2)}) copy-start(bf16[256,7168]{1,0:T(8,128)(2,1)} %copy-done.13) | copy-start | bytes 11010052
  166.7 99.4 %all-to-all-start.1 = ((bf16[16,16,7168]{2,1,0:T(8,128)(2,1)}), bf16[16,16,7168]{2,1,0:T(8,128)(2,1)}, u32[]{:S(2)}, u32[]{:S(2)}) async-start(bf16[16,16,7168]{2,1,0:T(8,128)(2,1)} %bitcast.35), calls=%async_computation.1 | async-start | bytes 7340032 | tf_op jit(solution)/shard_map/all_to_all | solution.py:34
  177.2 2.0 copy-start
  179.2 12.2 %copy-start.2 = (bf16[512,3584]{1,0:T(8,128)(2,1)S(1)}, bf16[512,3584]{1,0:T(8,128)(2,1)}, u32[]{:S(2)}) copy-start(bf16[512,3584]{1,0:T(8,128)(2,1)} %pad_maximum_fusion.1.left_ref) | copy-start | bytes 11010052
  191.3 7.4 %copy-start.4 = (bf16[512,2048]{1,0:T(8,128)(2,1)}, bf16[512,2048]{1,0:T(8,128)(2,1)S(1)}, u32[]{:S(2)}) copy-start(bf16[512,2048]{1,0:T(8,128)(2,1)S(1)} %shard_map.76.gate_a) | copy-start | bytes 6291460
  191.3 10.2 %collective-permute-start.6 = (bf16[512,2048]{1,0:T(8,128)(2,1)S(1)}, bf16[512,2048]{1,0:T(8,128)(2,1)}, u32[]{:S(2)}, u32[]{:S(2)}) collective-permute-start(bf16[512,2048]{1,0:T(8,128)(2,1)S(1)} %shard_map.76.gate_a), channel_id=1, source_target_pairs={{0,16},{16,0},{1,17},{17,1},{2,18},{18,2},{3,19},{19,3},{4,20},{20... | collective-permute-start | bytes 6291464 | tf_op jit(solution)/shard_map/ppermute | solution.py:115
  198.7 2.9 collective-permute-start.7
  217.9 3.0 copy-start.5
  217.9 3.0 copy-start.15
  232.3 11.3 %collective-permute-start.8 = (bf16[256,2048]{1,0:T(8,128)(2,1)S(1)}, bf16[256,2048]{1,0:T(8,128)(2,1)S(1)}, u32[]{:S(2)}, u32[]{:S(2)}) collective-permute-start(bf16[256,2048]{1,0:T(8,128)(2,1)S(1)} %shard_map.79.gate_a), channel_id=1, source_target_pairs={{0,16},{16,0},{1,17},{17,1},{2,18},{18,2},{3,19},{19,3},{4,20},{20... | collective-permute-start | bytes 3145736 | tf_op jit(solution)/shard_map/ppermute | solution.py:115
  232.5 32.6 %collective-permute-start.10 = (bf16[256,1792]{1,0:T(8,128)(2,1)S(1)}, bf16[256,1792]{1,0:T(8,128)(2,1)S(1)}, u32[]{:S(2)}, u32[]{:S(2)}) collective-permute-start(bf16[256,1792]{1,0:T(8,128)(2,1)S(1)} %get-tuple-element.49), channel_id=1, source_target_pairs={{0,1},{1,0},{2,3},{3,2},{4,5},{5,4},{6,7},{7,6},{8,9},{9,8},{10,11... | collective-permute-start | bytes 2752520 | tf_op jit(solution)/shard_map/ppermute | solution.py:45
  234.4 31.6 %collective-permute-start.11 = (bf16[256,1792]{1,0:T(8,128)(2,1)S(1)}, bf16[256,1792]{1,0:T(8,128)(2,1)}, u32[]{:S(2)}, u32[]{:S(2)}) collective-permute-start(bf16[256,1792]{1,0:T(8,128)(2,1)S(1)} %get-tuple-element.50), channel_id=1, source_target_pairs={{0,2},{1,3},{2,0},{3,1},{4,6},{5,7},{6,4},{7,5},{8,10},{9,11},{10,... | collective-permute-start | bytes 2752520 | tf_op jit(solution)/shard_map/ppermute | solution.py:45
  241.7 2.0 collective-permute-start.9
  255.1 0.8 copy-start.9
  265.1 0.9 copy-start.22
  266.1 52.0 %all-to-all-start.2 = ((bf16[16,16,3584]{2,1,0:T(8,128)(2,1)}), bf16[16,16,3584]{2,1,0:T(8,128)(2,1)}, u32[]{:S(2)}, u32[]{:S(2)}) async-start(bf16[16,16,3584]{2,1,0:T(8,128)(2,1)} %bitcast.38), calls=%async_computation.2 | async-start | bytes 3670016 | tf_op jit(solution)/shard_map/all_to_all | solution.py:34
  285.6 5.9 %copy-start.17 = (bf16[256,1792]{1,0:T(8,128)(2,1)S(1)}, bf16[256,1792]{1,0:T(8,128)(2,1)}, u32[]{:S(2)}) copy-start(bf16[256,1792]{1,0:T(8,128)(2,1)} %get-tuple-element.45) | copy-start | bytes 2752516
  285.7 5.9 %copy-start.23 = (bf16[256,1792]{1,0:T(8,128)(2,1)S(1)}, bf16[256,1792]{1,0:T(8,128)(2,1)}, u32[]{:S(2)}) copy-start(bf16[256,1792]{1,0:T(8,128)(2,1)} %copy-done.22) | copy-start | bytes 2752516
  291.6 2.2 copy-start.16
  291.8 3.4 copy-start.18
  291.9 22.9 %collective-permute-start.12 = (bf16[128,1792]{1,0:T(8,128)(2,1)S(1)}, bf16[128,1792]{1,0:T(8,128)(2,1)S(1)}, u32[]{:S(2)}, u32[]{:S(2)}) collective-permute-start(bf16[128,1792]{1,0:T(8,128)(2,1)S(1)} %slice.105), channel_id=1, source_target_pairs={{0,2},{1,3},{2,0},{3,1},{4,6},{5,7},{6,4},{7,5},{8,10},{9,11},{10,... | collective-permute-start | bytes 1376264 | tf_op jit(solution)/shard_map/ppermute | solution.py:45
  295.2 6.3 %copy-start.19 = (bf16[256,1792]{1,0:T(8,128)(2,1)}, bf16[256,1792]{1,0:T(8,128)(2,1)S(1)}, u32[]{:S(2)}) copy-start(bf16[256,1792]{1,0:T(8,128)(2,1)S(1)} %add.30) | copy-start | bytes 2752516
  295.3 22.8 %collective-permute-start.13 = (bf16[128,1792]{1,0:T(8,128)(2,1)S(1)}, bf16[128,1792]{1,0:T(8,128)(2,1)}, u32[]{:S(2)}, u32[]{:S(2)}) collective-permute-start(bf16[128,1792]{1,0:T(8,128)(2,1)S(1)} %slice.106), channel_id=1, source_target_pairs={{0,1},{1,0},{2,3},{3,2},{4,5},{5,4},{6,7},{7,6},{8,9},{9,8},{10,11... | collective-permute-start | bytes 1376264 | tf_op jit(solution)/shard_map/ppermute | solution.py:45
  296.8 4.7 %collective-permute-start.14 = (bf16[256,2048]{1,0:T(8,128)(2,1)S(1)}, bf16[256,2048]{1,0:T(8,128)(2,1)S(1)}, u32[]{:S(2)}, u32[]{:S(2)}) collective-permute-start(bf16[256,2048]{1,0:T(8,128)(2,1)S(1)} %shard_map.82.gate_a), channel_id=1, source_target_pairs={{0,16},{16,0},{1,17},{17,1},{2,18},{18,2},{3,19},{19,3},{4,20},{20... | collective-permute-start | bytes 3145736 | tf_op jit(solution)/shard_map/ppermute | solution.py:115
  296.8 4.7 %collective-permute-start.15 = (bf16[256,1024]{1,0:T(8,128)(2,1)S(1)}, bf16[256,1024]{1,0:T(8,128)(2,1)S(1)}, u32[]{:S(2)}, u32[]{:S(2)}) collective-permute-start(bf16[256,1024]{1,0:T(8,128)(2,1)S(1)} %shard_map.83.grad_a), channel_id=1, source_target_pairs={{0,16},{16,0},{1,17},{17,1},{2,18},{18,2},{3,19},{19,3},{4,20},{20... | collective-permute-start | bytes 1572872 | tf_op jit(solution)/shard_map/ppermute | solution.py:115
  313.0 1.0 copy-start.7
  313.9 0.8 copy-start.11
  314.7 0.8 copy-start.24
  318.1 78.7 %all-to-all-start.3 = ((bf16[16,16,3584]{2,1,0:T(8,128)(2,1)}), bf16[16,16,3584]{2,1,0:T(8,128)(2,1)}, u32[]{:S(2)}, u32[]{:S(2)}) async-start(bf16[16,16,3584]{2,1,0:T(8,128)(2,1)} %bitcast.37), calls=%async_computation.3 | async-start | bytes 3670016 | tf_op jit(solution)/shard_map/all_to_all | solution.py:34
  327.7 6.1 %copy-start.1 = (bf16[512,3584]{1,0:T(8,128)(2,1)S(1)}, bf16[512,3584]{1,0:T(8,128)(2,1)}, u32[]{:S(2)}) copy-start(bf16[512,3584]{1,0:T(8,128)(2,1)} %pad_maximum_fusion.left_ref) | copy-start | bytes 11010052
  327.7 6.1 %copy-start.8 = (bf16[256,2048]{1,0:T(8,128)(2,1)S(1)}, bf16[256,2048]{1,0:T(8,128)(2,1)}, u32[]{:S(2)}) copy-start(bf16[256,2048]{1,0:T(8,128)(2,1)} %copy-done.7) | copy-start | bytes 3145732
  327.7 39.2 %collective-permute-start.16 = (bf16[64,3584]{1,0:T(8,128)(2,1)S(1)}, bf16[64,3584]{1,0:T(8,128)(2,1)S(1)}, u32[]{:S(2)}, u32[]{:S(2)}) collective-permute-start(bf16[64,3584]{1,0:T(8,128)(2,1)S(1)} %pad_maximum_fusion.8), channel_id=1, source_target_pairs={{0,4},{1,5},{2,6},{3,7},{4,0},{5,1},{6,2},{7,3},{8,12},{9,13},{10,... | collective-permute-start | bytes 1376264 | tf_op jit(solution)/shard_map/ppermute | solution.py:45
  333.8 21.7 %copy-start.3 = (bf16[512,3584]{1,0:T(8,128)(2,1)S(1)}, bf16[512,3584]{1,0:T(8,128)(2,1)}, u32[]{:S(2)}) copy-start(bf16[512,3584]{1,0:T(8,128)(2,1)} %pad_maximum_fusion.1.left_ref) | copy-start | bytes 11010052
  333.8 21.7 %copy-start.6 = (bf16[512,1024]{1,0:T(8,128)(2,1)S(1)}, bf16[512,1024]{1,0:T(8,128)(2,1)}, u32[]{:S(2)}) copy-start(bf16[512,1024]{1,0:T(8,128)(2,1)} %copy-done.5) | copy-start | bytes 3145732
  333.8 21.7 %copy-start.10 = (bf16[256,1024]{1,0:T(8,128)(2,1)S(1)}, bf16[256,1024]{1,0:T(8,128)(2,1)}, u32[]{:S(2)}) copy-start(bf16[256,1024]{1,0:T(8,128)(2,1)} %copy-done.9) | copy-start | bytes 1572868
  333.8 21.7 %copy-start.12 = (bf16[256,1024]{1,0:T(8,128)(2,1)S(1)}, bf16[256,1024]{1,0:T(8,128)(2,1)}, u32[]{:S(2)}) copy-start(bf16[256,1024]{1,0:T(8,128)(2,1)} %copy-done.11) | copy-start | bytes 1572868
  333.8 21.7 %copy-start.20 = (bf16[256,3584]{1,0:T(8,128)(2,1)S(1)}, bf16[256,3584]{1,0:T(8,128)(2,1)}, u32[]{:S(2)}) copy-start(bf16[256,3584]{1,0:T(8,128)(2,1)} %get-tuple-element.71) | copy-start | bytes 5505028
  367.0 29.7 %collective-permute-start.17 = (bf16[32,3584]{1,0:T(8,128)(2,1)S(1)}, bf16[32,3584]{1,0:T(8,128)(2,1)S(1)}, u32[]{:S(2)}, u32[]{:S(2)}) collective-permute-start(bf16[32,3584]{1,0:T(8,128)(2,1)S(1)} %slice.99), channel_id=1, source_target_pairs={{0,8},{1,9},{2,10},{3,11},{4,12},{5,13},{6,14},{7,15},{8,0},{9,1},... | collective-permute-start | bytes 688136 | tf_op jit(solution)/shard_map/ppermute | solution.py:45

commit v7 on v6

--- a/solution.py
+++ b/solution.py
@@ -220,7 +220,7 @@
     only_busiest = is_busiest.astype(jnp.int32).reshape(1)
 
     far = outer_masks()
-    spill_both = place(spill_hot, both)
+    spill_both = jnp.concatenate([place(spill_hot, tokens), place(spill_hot, d_out)], axis=1)
     for mask in far:
         spill_both = double(spill_both, mask)
     spill_rows, spill_grads = split(spill_both)
@@ -250,8 +250,8 @@
         always, *products(arrived_0, 0, arrived_0, 1), gate_up_matrix
     )
     rows_0, grads_0 = split(arrived_0)
-    arrived_1, out_0, come_a, come_b = lax.optimization_barrier(
-        (arrived_1, out_0, come_a, come_b)
+    arrived_1, out_0, come_a, come_b, rows_0, grads_0 = lax.optimization_barrier(
+        (arrived_1, out_0, come_a, come_b, rows_0, grads_0)
     )
 
     back_0 = exchange(out_0, expert_count)
@@ -271,15 +271,16 @@
     rows_1, grads_1 = split(arrived_1)
     back_1 = exchange(out_1, expert_count)
 
+    hidden = jnp.concatenate([hidden_s, hidden_0, hidden_1], axis=0)
+    all_grads = jnp.concatenate([spill_grads, grads_0, grads_1], axis=0)
+    down_grads = outer(hidden, all_grads).reshape(1, hidden_width, feature_share)
+    down_grads, spill_rows = lax.optimization_barrier((down_grads, spill_rows))
     all_rows = jnp.concatenate([spill_rows, rows_0, rows_1], axis=0)
-    all_grads = jnp.concatenate([spill_grads, grads_0, grads_1], axis=0)
-    hidden = jnp.concatenate([hidden_s, hidden_0, hidden_1], axis=0)
     branch = jnp.concatenate([branch_s, branch_0, branch_1], axis=0)
     gate_up_grads = with_layout_constraint(outer(all_rows, branch), Layout((0, 1)))
-    down_grads = outer(hidden, all_grads).reshape(1, hidden_width, feature_share)
     gate_up_grads = gate_up_grads.reshape(feature_share // 8, 8, 2, hidden_width)
-    back_s, gate_up_grads, down_grads = lax.optimization_barrier(
-        (back_s, gate_up_grads.transpose(0, 2, 1, 3), down_grads)
+    back_s, gate_up_grads = lax.optimization_barrier(
+        (back_s, gate_up_grads.transpose(0, 2, 1, 3))
     )
 
     back_s = halve(back_s, far[0])

time: 403 us -> 411 us (1.020)
  waiting for transfers between devices: 131 us -> 136 us
    ppermute x12, waiting for transfers between devices: 127 us -> 134 us  [swap_with(): return lax.ppermute(rows, 'exp', [(i, i ^ mask) for i in range(total)])]
    dot_general x3 -> x4, matrix products: 6.66 us -> 9.88 us  [place(): lax.dot_general(one_hot_rows, rows, (((1,), (0,)), ((), ())), preferred_e...]
    unnamed x54 -> x56, local copies, waits for them, and re-layouts: 24.4 us -> 23.6 us
  transfers between devices with their start and end apart: 22 -> 22, of which waited for: 8 -> 7; matrix products, arithmetic and copies ran while one was open for 26% -> 26% of each run, Pallas kernels for 23% -> 22%
where the time goes in v7:
time: 411 us; the launch traced here: 410 us
  waiting for transfers between devices  136 us (33%)
  Pallas kernels  90.8 us (22%)
  local copies, waits for them, and re-layouts  62.4 us (15%)
  starting transfers between devices  57.4 us (14%)
  matrix products  47.8 us (12%)
  other arithmetic  13.8 us (3%)
    ppermute x12, waiting for transfers between devices, swap_with(): return lax.ppermute(rows, 'exp', [(i, i ^ mask) for i in range(total)])  134 us
    pallas_call x6, Pallas kernels, product(): pl.pallas_call(functools.partial(product_kernel, 1 if transposed else 0),...  51.6 us
    pallas_call x3, Pallas kernels, finish(): pl.pallas_call(finish_kernel, grid=(features // step,), in_specs=[pl.Bloc...  39.1 us
    dot_general x2, matrix products, outer(): lax.dot_general(left, right, (((0,), (0,)), ((), ())), preferred_element_...  33 us
    all_to_all x4, starting transfers between devices, exchange(): lax.all_to_all(rows.reshape(expert_count, slots // expert_count, width),...  32.3 us
    transpose x1, local copies, waits for them, and re-layouts, local(): gate_up_grads.transpose(0, 2, 1, 3)  27.1 us
    ppermute x12, starting transfers between devices, swap_with(): return lax.ppermute(rows, 'exp', [(i, i ^ mask) for i in range(total)])  23.9 us
    unnamed x56, local copies, waits for them, and re-layouts  23.6 us
  transfers between devices with their start and end apart: 22, of which 7 were waited for; matrix products, arithmetic and copies ran while one was open for 26% of the time, Pallas kernels for 22%

profile of v7, /device:TPU:0, one launch (start us, length us, event | category | flops | bytes accessed | tf_op | source)
XLA Modules:
  0.0 409.8 jit_solution(12335604098092906549)
XLA Ops:
  0.6 1.0 convert_reduce_fusion
  1.6 1.3 select_reduce_fusion
  3.0 1.9 convolution_convert_fusion.5
  4.9 1.9 convolution_convert_fusion.6
  6.8 4.1 %collective-permute-start = (bf16[32,7168]{1,0:T(8,128)(2,1)S(1)}, bf16[32,7168]{1,0:T(8,128)(2,1)S(1)}, u32[]{:S(2)}, u32[]{:S(2)}) collective-permute-start(bf16[32,7168]{1,0:T(8,128)(2,1)S(1)} %pad_maximum_fusion.9), channel_id=1, source_target_pairs={{0,8},{1,9},{2,10},{3,11},{4,12},{5,13},{6,14},{7,15},{8,0},{9,1},... | collective-permute-start | bytes 1376264 | tf_op jit(solution)/shard_map/ppermute | solution.py:45
  10.9 20.4 %collective-permute-done = bf16[32,7168]{1,0:T(8,128)(2,1)S(1)} collective-permute-done((bf16[32,7168]{1,0:T(8,128)(2,1)S(1)}, bf16[32,7168]{1,0:T(8,128)(2,1)S(1)}, u32[]{:S(2)}, u32[]{:S(2)}) %collective-permute-start) | collective-permute-done | bytes 458784 | tf_op jit(solution)/shard_map/ppermute | solution.py:45
  31.4 0.8 collective-permute-start.1
  32.6 3.1 convolution_convert_fusion.2
  35.7 17.3 %collective-permute-done.1 = bf16[64,7168]{1,0:T(8,128)(2,1)S(1)} collective-permute-done((bf16[64,7168]{1,0:T(8,128)(2,1)S(1)}, bf16[64,7168]{1,0:T(8,128)(2,1)S(1)}, u32[]{:S(2)}, u32[]{:S(2)}) %collective-permute-start.1) | collective-permute-done | bytes 917536 | tf_op jit(solution)/shard_map/ppermute | solution.py:45
  53.2 7.6 %all-to-all-start = ((bf16[16,16,7168]{2,1,0:T(8,128)(2,1)}), bf16[16,16,7168]{2,1,0:T(8,128)(2,1)}, u32[]{:S(2)}, u32[]{:S(2)}) async-start(bf16[16,16,7168]{2,1,0:T(8,128)(2,1)} %bitcast.37), calls=%async_computation | async-start | bytes 7340032 | tf_op jit(solution)/shard_map/all_to_all | solution.py:34
  60.8 1.9 collective-permute-start.2
  62.7 1.5 collective-permute-start.4
  64.2 50.2 %collective-permute-done.2 = bf16[128,3584]{1,0:T(8,128)(2,1)S(1)} collective-permute-done((bf16[128,3584]{1,0:T(8,128)(2,1)S(1)}, bf16[128,3584]{1,0:T(8,128)(2,1)S(1)}, u32[]{:S(2)}, u32[]{:S(2)}) %collective-permute-start.2) | collective-permute-done | bytes 917536 | tf_op jit(solution)/shard_map/ppermute | solution.py:45
  114.5 1.7 collective-permute-start.3
  116.3 2.5 collective-permute-start.5
  118.9 16.2 %copy.10 = bf16[448,8,2,1024]{3,1,2,0:T(8,128)(2,1)} copy(bf16[448,8,2,1024]{3,2,1,0:T(2,128)(2,1)} %bitcast.33) | data formatting | bytes 29360128
  135.1 3.0 convolution_convert_fusion.1
  138.0 27.2 %collective-permute-done.3 = bf16[256,3584]{1,0:T(8,128)(2,1)S(1)} collective-permute-done((bf16[256,3584]{1,0:T(8,128)(2,1)S(1)}, bf16[256,3584]{1,0:T(8,128)(2,1)S(1)}, u32[]{:S(2)}, u32[]{:S(2)}) %collective-permute-start.3) | collective-permute-done | bytes 1835040 | tf_op jit(solution)/shard_map/ppermute | solution.py:45
  165.2 1.9 pad_maximum_fusion.left_ref
  167.3 2.0 pad_maximum_fusion.1.left_ref
  169.2 10.5 %all-to-all-start.1 = ((bf16[16,16,7168]{2,1,0:T(8,128)(2,1)}), bf16[16,16,7168]{2,1,0:T(8,128)(2,1)}, u32[]{:S(2)}, u32[]{:S(2)}) async-start(bf16[16,16,7168]{2,1,0:T(8,128)(2,1)} %bitcast.36), calls=%async_computation.1 | async-start | bytes 7340032 | tf_op jit(solution)/shard_map/all_to_all | solution.py:34
  179.8 2.0 copy-done
  181.8 12.1 %shard_map.76.gate_a = bf16[512,2048]{1,0:T(8,128)(2,1)S(1)} custom-call(bf16[512,3584]{1,0:T(8,128)(2,1)S(1)} %copy-done, bf16[3584,2048]{1,0:T(8,128)(2,1)} %bitcast.24), custom_call_target="tpu_custom_call" | custom-call | flops 1 | bytes 1 | tf_op jit(solution)/shard_map/pallas_call | solution.py:102
  194.0 7.3 %shard_map.77.grad_a = bf16[512,1024]{1,0:T(8,128)(2,1)S(1)} custom-call(bf16[512,3584]{1,0:T(8,128)(2,1)S(1)} %copy-done.2, bf16[1024,3584]{1,0:T(8,128)(2,1)} %bitcast.30), custom_call_target="tpu_custom_call" | custom-call | flops 1 | bytes 1 | tf_op jit(solution)/shard_map/pallas_call | solution.py:102
  202.0 2.1 collective-permute-done.7.grad_b
  204.1 16.4 %shard_map.78 = (bf16[512,3584]{1,0:T(8,128)(2,1)}, bf16[512,1024]{1,0:T(8,128)(2,1)S(1)}, bf16[512,2048]{1,0:T(8,128)(2,1)S(1)}) custom-call(s32[1]{0:T(128)} %bitcast.2.keep_ref, bf16[512,2048]{1,0:T(8,128)(2,1)} %copy-done.4, bf16[512,2048]{1,0:T(8,128)(2,1)} %collective-permute-done.6.gate_b, bf16[512,1024]{1,0:T(8,128)(2,1)S(1)} %shard_map.77.grad_a, ...), custom_call_target="tpu_custom_call" | custom-call | flops 1 | bytes 1 | tf_op jit(solution)/shard_map/pallas_call | solution.py:161
  220.5 2.0 fusion.44
  222.5 1.0 pad_maximum_fusion.6
  223.6 1.1 fusion.45
  224.6 10.3 %shard_map.79.gate_a = bf16[256,2048]{1,0:T(8,128)(2,1)S(1)} custom-call(bf16[256,7168]{1,0:T(8,128)(2,1)} %bitcast.1.left_ref, bf16[3584,2048]{1,0:T(8,128)(2,1)} %bitcast.26), custom_call_target="tpu_custom_call" | custom-call | flops 1 | bytes 1 | tf_op jit(solution)/shard_map/pallas_call | solution.py:102
  234.9 5.8 %shard_map.80.grad_a = bf16[256,1024]{1,0:T(8,128)(2,1)S(1)} custom-call(bf16[256,7168]{1,0:T(8,128)(2,1)} %bitcast.1.left_ref, bf16[1024,3584]{1,0:T(8,128)(2,1)} %bitcast.31), custom_call_target="tpu_custom_call" | custom-call | flops 1 | bytes 1 | tf_op jit(solution)/shard_map/pallas_call | solution.py:102
  241.0 0.4 collective-permute-start.9
  241.3 1.9 collective-permute-start.10
  243.2 1.5 collective-permute-start.11
  244.7 4.1 fusion.43
  248.8 11.4 %shard_map.81 = (bf16[256,3584]{1,0:T(8,128)(2,1)}, bf16[256,1024]{1,0:T(8,128)(2,1)S(1)}, bf16[256,2048]{1,0:T(8,128)(2,1)S(1)}) custom-call(s32[1]{0:T(128)} %constant.20.clone.1.keep_ref, bf16[256,2048]{1,0:T(8,128)(2,1)S(1)} %shard_map.79.gate_a, bf16[256,2048]{1,0:T(8,128)(2,1)S(1)} %collective-permute-done.8.gate_b, ...), custom_call_target="tpu_custom_call" | custom-call | flops 1 | bytes 1 | tf_op jit(solution)/shard_map/pallas_call | solution.py:161
  260.2 0.8 copy-done.9
  261.0 12.2 %collective-permute-done.10 = bf16[256,1792]{1,0:T(8,128)(2,1)S(1)} collective-permute-done((bf16[256,1792]{1,0:T(8,128)(2,1)S(1)}, bf16[256,1792]{1,0:T(8,128)(2,1)S(1)}, u32[]{:S(2)}, u32[]{:S(2)}) %collective-permute-start.10) | collective-permute-done | bytes 917536 | tf_op jit(solution)/shard_map/ppermute | solution.py:45
  273.1 0.9 copy-done.24
  274.1 7.1 %all-to-all-start.2 = ((bf16[16,16,3584]{2,1,0:T(8,128)(2,1)}), bf16[16,16,3584]{2,1,0:T(8,128)(2,1)}, u32[]{:S(2)}, u32[]{:S(2)}) async-start(bf16[16,16,3584]{2,1,0:T(8,128)(2,1)} %bitcast.39), calls=%async_computation.2 | async-start | bytes 3670016 | tf_op jit(solution)/shard_map/all_to_all | solution.py:34
  281.2 10.3 %shard_map.82.gate_a = bf16[256,2048]{1,0:T(8,128)(2,1)S(1)} custom-call(bf16[256,7168]{1,0:T(8,128)(2,1)} %bitcast.5.left_ref, bf16[3584,2048]{1,0:T(8,128)(2,1)} %bitcast.28), custom_call_target="tpu_custom_call" | custom-call | flops 1 | bytes 1 | tf_op jit(solution)/shard_map/pallas_call | solution.py:102
  291.6 5.9 %shard_map.83.grad_a = bf16[256,1024]{1,0:T(8,128)(2,1)S(1)} custom-call(bf16[256,7168]{1,0:T(8,128)(2,1)} %bitcast.5.left_ref, bf16[1024,3584]{1,0:T(8,128)(2,1)} %bitcast.32), custom_call_target="tpu_custom_call" | custom-call | flops 1 | bytes 1 | tf_op jit(solution)/shard_map/pallas_call | solution.py:102
  297.5 0.4 collective-permute-start.15
  298.2 1.9 collective-permute-start.12
  300.2 1.4 add.30
  301.6 1.5 collective-permute-start.13
  303.2 11.4 %shard_map.84 = (bf16[256,3584]{1,0:T(8,128)(2,1)}, bf16[256,1024]{1,0:T(8,128)(2,1)S(1)}, bf16[256,2048]{1,0:T(8,128)(2,1)S(1)}) custom-call(s32[1]{0:T(128)} %constant.20.clone.1.keep_ref, bf16[256,2048]{1,0:T(8,128)(2,1)S(1)} %shard_map.82.gate_a, bf16[256,2048]{1,0:T(8,128)(2,1)S(1)} %collective-permute-done.14.gate_b, ...), custom_call_target="tpu_custom_call" | custom-call | flops 1 | bytes 1 | tf_op jit(solution)/shard_map/pallas_call | solution.py:161
  314.5 1.0 copy-done.7
  315.5 0.8 copy-done.11
  316.3 0.8 copy-done.26
  317.1 6.5 %collective-permute-done.13 = bf16[128,1792]{1,0:T(8,128)(2,1)} collective-permute-done((bf16[128,1792]{1,0:T(8,128)(2,1)S(1)}, bf16[128,1792]{1,0:T(8,128)(2,1)}, u32[]{:S(2)}, u32[]{:S(2)}) %collective-permute-start.13) | collective-permute-done | bytes 458784 | tf_op jit(solution)/shard_map/ppermute | solution.py:45
  323.6 7.0 %all-to-all-start.3 = ((bf16[16,16,3584]{2,1,0:T(8,128)(2,1)}), bf16[16,16,3584]{2,1,0:T(8,128)(2,1)}, u32[]{:S(2)}, u32[]{:S(2)}) async-start(bf16[16,16,3584]{2,1,0:T(8,128)(2,1)} %bitcast.38), calls=%async_computation.3 | async-start | bytes 3670016 | tf_op jit(solution)/shard_map/all_to_all | solution.py:34
  330.6 1.2 slice_add_fusion
  331.8 1.2 slice_add_fusion.1
  333.0 0.8 copy-done.17
  333.8 0.8 pad_maximum_fusion.8
  334.6 1.9 collective-permute-start.16
  336.6 4.1 %fusion.42 = (bf16[256,3584]{1,0:T(8,128)(2,1)}, bf16[256,3584]{1,0:T(8,128)(2,1)}) fusion(bf16[256,7168]{1,0:T(8,128)(2,1)} %bitcast.5.left_ref), kind=kLoop, calls=%fused_computation.75 | loop fusion | bytes 7340032 | tf_op jit(solution)/shard_map/slice | solution.py:212
  340.7 11.6 %fusion.10 = bf16[1,1024,3584]{2,1,0:T(8,128)(2,1)} fusion(bf16[256,3584]{1,0:T(8,128)(2,1)} %get-tuple-element.77, bf16[256,3584]{1,0:T(8,128)(2,1)} %get-tuple-element.65, bf16[512,3584]{1,0:T(8,128)(2,1)S(1)} %copy-done.3, bf16[256,1024]{1,0:T(8,128)(2,1)S(1)} %copy-done.12, bf16[256,1024]{1,0:T(8,128)(2,1)S(1)} %copy-done.10, ...), kind=kOutput, calls=%fused_computation.14 | convolution fusion | flops 7548174336 | bytes 16777216 | tf_op jit(solution)/shard_map/dot_general | solution.py:184
  352.4 21.4 %convolution_convert_fusion = bf16[3584,2048]{1,0:T(8,128)(2,1)} fusion(bf16[256,3584]{1,0:T(8,128)(2,1)} %get-tuple-element.78, bf16[256,3584]{1,0:T(8,128)(2,1)} %get-tuple-element.68, bf16[512,3584]{1,0:T(8,128)(2,1)S(1)} %copy-done.1, bf16[256,2048]{1,0:T(8,128)(2,1)S(1)} %copy-done.8, bf16[256,2048]{1,0:T(8,128)(2,1)S(1)} %get-tuple-element.70, ...), kind=kOutput, calls=%fused_computation | convolution fusion | flops 15074328576 | bytes 26214400 | tf_op jit(solution)/shard_map/dot_general | solution.py:184
  373.8 1.1 fusion.34
  375.0 2.7 collective-permute-start.17
  377.7 27.1 %copy.9 = bf16[448,8,2,1024]{3,2,1,0:T(2,128)(2,1)} copy(bf16[448,8,2,1024]{3,1,2,0:T(8,128)(2,1)} %bitcast.35) | data formatting | bytes 29360128 | tf_op jit(solution)/shard_map/transpose | solution.py:287
  404.9 4.9 %convolution_convert_fusion.4 = bf16[256,3584]{1,0:T(8,128)(2,1)} fusion(bf16[256,3584]{1,0:T(8,128)(2,1)} %bitcast.12, bf16[256,3584]{1,0:T(8,128)(2,1)} %bitcast.7, bf16[32,3584]{1,0:T(8,128)(2,1)S(1)} %slice_add_fusion.2, pred[256,256]{1,0:T(32,128)(4,1)S(1)} %get-tuple-element.95, pred[256,256]{1,0:T(32,128)(4,1)S(1)} %get-tuple-element.96, ...), kind=kOutput, calls=%fused_computation.15 | convolution fusion | flops 1011138560 | bytes 5873664 | tf_op jit(solution)/shard_map/dot_general | solution.py:293
  (82 shorter events, 2.1 us)
Async XLA Ops:
  0.6 31.5 %copy-start.15 = (bf16[256,3584]{1,0:T(8,128)(2,1)S(1)}, bf16[256,3584]{1,0:T(8,128)(2,1)}, u32[]{:S(2)}) copy-start(bf16[256,3584]{1,0:T(8,128)(2,1)} %param.5) | copy-start | bytes 5505028
  6.8 25.6 %copy-start.16 = (bf16[256,3584]{1,0:T(8,128)(2,1)S(1)}, bf16[256,3584]{1,0:T(8,128)(2,1)}, u32[]{:S(2)}) copy-start(bf16[256,3584]{1,0:T(8,128)(2,1)} %param.6) | copy-start | bytes 5505028
  6.8 24.5 %collective-permute-start = (bf16[32,7168]{1,0:T(8,128)(2,1)S(1)}, bf16[32,7168]{1,0:T(8,128)(2,1)S(1)}, u32[]{:S(2)}, u32[]{:S(2)}) collective-permute-start(bf16[32,7168]{1,0:T(8,128)(2,1)S(1)} %pad_maximum_fusion.9), channel_id=1, source_target_pairs={{0,8},{1,9},{2,10},{3,11},{4,12},{5,13},{6,14},{7,15},{8,0},{9,1},... | collective-permute-start | bytes 1376264 | tf_op jit(solution)/shard_map/ppermute | solution.py:45
  31.4 21.6 %collective-permute-start.1 = (bf16[64,7168]{1,0:T(8,128)(2,1)S(1)}, bf16[64,7168]{1,0:T(8,128)(2,1)S(1)}, u32[]{:S(2)}, u32[]{:S(2)}) collective-permute-start(bf16[64,7168]{1,0:T(8,128)(2,1)S(1)} %pad_maximum_fusion.5), channel_id=1, source_target_pairs={{0,4},{1,5},{2,6},{3,7},{4,0},{5,1},{6,2},{7,3},{8,12},{9,13},{10,... | collective-permute-start | bytes 2752520 | tf_op jit(solution)/shard_map/ppermute | solution.py:45
  32.6 3.1 copy-start.13
  53.2 116.0 %all-to-all-start = ((bf16[16,16,7168]{2,1,0:T(8,128)(2,1)}), bf16[16,16,7168]{2,1,0:T(8,128)(2,1)}, u32[]{:S(2)}, u32[]{:S(2)}) async-start(bf16[16,16,7168]{2,1,0:T(8,128)(2,1)} %bitcast.37), calls=%async_computation | async-start | bytes 7340032 | tf_op jit(solution)/shard_map/all_to_all | solution.py:34
  60.8 53.6 %collective-permute-start.2 = (bf16[128,3584]{1,0:T(8,128)(2,1)S(1)}, bf16[128,3584]{1,0:T(8,128)(2,1)S(1)}, u32[]{:S(2)}, u32[]{:S(2)}) collective-permute-start(bf16[128,3584]{1,0:T(8,128)(2,1)S(1)} %get-tuple-element.41), channel_id=1, source_target_pairs={{0,2},{1,3},{2,0},{3,1},{4,6},{5,7},{6,4},{7,5},{8,10},{9,11},{10,... | collective-permute-start | bytes 2752520 | tf_op jit(solution)/shard_map/ppermute | solution.py:45
  62.7 53.5 %collective-permute-start.4 = (bf16[128,3584]{1,0:T(8,128)(2,1)S(1)}, bf16[128,3584]{1,0:T(8,128)(2,1)S(1)}, u32[]{:S(2)}, u32[]{:S(2)}) collective-permute-start(bf16[128,3584]{1,0:T(8,128)(2,1)S(1)} %get-tuple-element.42), channel_id=1, source_target_pairs={{0,1},{1,0},{2,3},{3,2},{4,5},{5,4},{6,7},{7,6},{8,9},{9,8},{10,11... | collective-permute-start | bytes 2752520 | tf_op jit(solution)/shard_map/ppermute | solution.py:45
  114.5 50.7 %collective-permute-start.3 = (bf16[256,3584]{1,0:T(8,128)(2,1)S(1)}, bf16[256,3584]{1,0:T(8,128)(2,1)S(1)}, u32[]{:S(2)}, u32[]{:S(2)}) collective-permute-start(bf16[256,3584]{1,0:T(8,128)(2,1)S(1)} %pad_maximum_fusion.3), channel_id=1, source_target_pairs={{0,1},{1,0},{2,3},{3,2},{4,5},{5,4},{6,7},{7,6},{8,9},{9,8},{10,11... | collective-permute-start | bytes 5505032 | tf_op jit(solution)/shard_map/ppermute | solution.py:45
  116.3 50.9 %collective-permute-start.5 = (bf16[256,3584]{1,0:T(8,128)(2,1)S(1)}, bf16[256,3584]{1,0:T(8,128)(2,1)S(1)}, u32[]{:S(2)}, u32[]{:S(2)}) collective-permute-start(bf16[256,3584]{1,0:T(8,128)(2,1)S(1)} %pad_maximum_fusion.4), channel_id=1, source_target_pairs={{0,2},{1,3},{2,0},{3,1},{4,6},{5,7},{6,4},{7,5},{8,10},{9,11},{10,... | collective-permute-start | bytes 5505032 | tf_op jit(solution)/shard_map/ppermute | solution.py:45
  118.9 16.2 %copy-start.14 = (bf16[256,7168]{1,0:T(8,128)(2,1)S(1)}, bf16[256,7168]{1,0:T(8,128)(2,1)}, u32[]{:S(2)}) copy-start(bf16[256,7168]{1,0:T(8,128)(2,1)} %copy-done.13) | copy-start | bytes 11010052
  169.2 104.8 %all-to-all-start.1 = ((bf16[16,16,7168]{2,1,0:T(8,128)(2,1)}), bf16[16,16,7168]{2,1,0:T(8,128)(2,1)}, u32[]{:S(2)}, u32[]{:S(2)}) async-start(bf16[16,16,7168]{2,1,0:T(8,128)(2,1)} %bitcast.36), calls=%async_computation.1 | async-start | bytes 7340032 | tf_op jit(solution)/shard_map/all_to_all | solution.py:34
  179.8 2.0 copy-start
  181.8 12.2 %copy-start.2 = (bf16[512,3584]{1,0:T(8,128)(2,1)S(1)}, bf16[512,3584]{1,0:T(8,128)(2,1)}, u32[]{:S(2)}) copy-start(bf16[512,3584]{1,0:T(8,128)(2,1)} %pad_maximum_fusion.1.left_ref) | copy-start | bytes 11010052
  193.9 7.4 %copy-start.4 = (bf16[512,2048]{1,0:T(8,128)(2,1)}, bf16[512,2048]{1,0:T(8,128)(2,1)S(1)}, u32[]{:S(2)}) copy-start(bf16[512,2048]{1,0:T(8,128)(2,1)S(1)} %shard_map.76.gate_a) | copy-start | bytes 6291460
  193.9 10.2 %collective-permute-start.6 = (bf16[512,2048]{1,0:T(8,128)(2,1)S(1)}, bf16[512,2048]{1,0:T(8,128)(2,1)}, u32[]{:S(2)}, u32[]{:S(2)}) collective-permute-start(bf16[512,2048]{1,0:T(8,128)(2,1)S(1)} %shard_map.76.gate_a), channel_id=1, source_target_pairs={{0,16},{16,0},{1,17},{17,1},{2,18},{18,2},{3,19},{19,3},{4,20},{20... | collective-permute-start | bytes 6291464 | tf_op jit(solution)/shard_map/ppermute | solution.py:115
  201.3 2.9 collective-permute-start.7
  220.5 3.0 copy-start.5
  220.5 3.0 copy-start.19
  240.8 8.0 %collective-permute-start.8 = (bf16[256,2048]{1,0:T(8,128)(2,1)S(1)}, bf16[256,2048]{1,0:T(8,128)(2,1)S(1)}, u32[]{:S(2)}, u32[]{:S(2)}) collective-permute-start(bf16[256,2048]{1,0:T(8,128)(2,1)S(1)} %shard_map.79.gate_a), channel_id=1, source_target_pairs={{0,16},{16,0},{1,17},{17,1},{2,18},{18,2},{3,19},{19,3},{4,20},{20... | collective-permute-start | bytes 3145736 | tf_op jit(solution)/shard_map/ppermute | solution.py:115
  241.0 7.8 %collective-permute-start.9 = (bf16[256,1024]{1,0:T(8,128)(2,1)S(1)}, bf16[256,1024]{1,0:T(8,128)(2,1)S(1)}, u32[]{:S(2)}, u32[]{:S(2)}) collective-permute-start(bf16[256,1024]{1,0:T(8,128)(2,1)S(1)} %shard_map.80.grad_a), channel_id=1, source_target_pairs={{0,16},{16,0},{1,17},{17,1},{2,18},{18,2},{3,19},{19,3},{4,20},{20... | collective-permute-start | bytes 1572872 | tf_op jit(solution)/shard_map/ppermute | solution.py:115
  241.3 31.8 %collective-permute-start.10 = (bf16[256,1792]{1,0:T(8,128)(2,1)S(1)}, bf16[256,1792]{1,0:T(8,128)(2,1)S(1)}, u32[]{:S(2)}, u32[]{:S(2)}) collective-permute-start(bf16[256,1792]{1,0:T(8,128)(2,1)S(1)} %get-tuple-element.52), channel_id=1, source_target_pairs={{0,1},{1,0},{2,3},{3,2},{4,5},{5,4},{6,7},{7,6},{8,9},{9,8},{10,11... | collective-permute-start | bytes 2752520 | tf_op jit(solution)/shard_map/ppermute | solution.py:45
  243.2 30.9 %collective-permute-start.11 = (bf16[256,1792]{1,0:T(8,128)(2,1)S(1)}, bf16[256,1792]{1,0:T(8,128)(2,1)}, u32[]{:S(2)}, u32[]{:S(2)}) collective-permute-start(bf16[256,1792]{1,0:T(8,128)(2,1)S(1)} %get-tuple-element.53), channel_id=1, source_target_pairs={{0,2},{1,3},{2,0},{3,1},{4,6},{5,7},{6,4},{7,5},{8,10},{9,11},{10,... | collective-permute-start | bytes 2752520 | tf_op jit(solution)/shard_map/ppermute | solution.py:45
  260.2 0.8 copy-start.9
  273.1 0.9 copy-start.24
  274.1 49.5 %all-to-all-start.2 = ((bf16[16,16,3584]{2,1,0:T(8,128)(2,1)}), bf16[16,16,3584]{2,1,0:T(8,128)(2,1)}, u32[]{:S(2)}, u32[]{:S(2)}) async-start(bf16[16,16,3584]{2,1,0:T(8,128)(2,1)} %bitcast.39), calls=%async_computation.2 | async-start | bytes 3670016 | tf_op jit(solution)/shard_map/all_to_all | solution.py:34
  291.5 6.5 %copy-start.21 = (bf16[256,1792]{1,0:T(8,128)(2,1)S(1)}, bf16[256,1792]{1,0:T(8,128)(2,1)}, u32[]{:S(2)}) copy-start(bf16[256,1792]{1,0:T(8,128)(2,1)} %get-tuple-element.48) | copy-start | bytes 2752516
  291.5 6.4 %copy-start.25 = (bf16[256,1792]{1,0:T(8,128)(2,1)S(1)}, bf16[256,1792]{1,0:T(8,128)(2,1)}, u32[]{:S(2)}) copy-start(bf16[256,1792]{1,0:T(8,128)(2,1)} %copy-done.24) | copy-start | bytes 2752516
  291.5 11.6 %collective-permute-start.14 = (bf16[256,2048]{1,0:T(8,128)(2,1)S(1)}, bf16[256,2048]{1,0:T(8,128)(2,1)S(1)}, u32[]{:S(2)}, u32[]{:S(2)}) collective-permute-start(bf16[256,2048]{1,0:T(8,128)(2,1)S(1)} %shard_map.82.gate_a), channel_id=1, source_target_pairs={{0,16},{16,0},{1,17},{17,1},{2,18},{18,2},{3,19},{19,3},{4,20},{20... | collective-permute-start | bytes 3145736 | tf_op jit(solution)/shard_map/ppermute | solution.py:115
  297.5 2.6 copy-start.20
  297.5 5.6 %collective-permute-start.15 = (bf16[256,1024]{1,0:T(8,128)(2,1)S(1)}, bf16[256,1024]{1,0:T(8,128)(2,1)S(1)}, u32[]{:S(2)}, u32[]{:S(2)}) collective-permute-start(bf16[256,1024]{1,0:T(8,128)(2,1)S(1)} %shard_map.83.grad_a), channel_id=1, source_target_pairs={{0,16},{16,0},{1,17},{17,1},{2,18},{18,2},{3,19},{19,3},{4,20},{20... | collective-permute-start | bytes 1572872 | tf_op jit(solution)/shard_map/ppermute | solution.py:115
  298.2 5.0 %copy-start.22 = (bf16[256,1792]{1,0:T(8,128)(2,1)}, bf16[256,1792]{1,0:T(8,128)(2,1)S(1)}, u32[]{:S(2)}) copy-start(bf16[256,1792]{1,0:T(8,128)(2,1)S(1)} %add.29) | copy-start | bytes 2752516
  298.2 18.1 %collective-permute-start.12 = (bf16[128,1792]{1,0:T(8,128)(2,1)S(1)}, bf16[128,1792]{1,0:T(8,128)(2,1)S(1)}, u32[]{:S(2)}, u32[]{:S(2)}) collective-permute-start(bf16[128,1792]{1,0:T(8,128)(2,1)S(1)} %slice.105), channel_id=1, source_target_pairs={{0,2},{1,3},{2,0},{3,1},{4,6},{5,7},{6,4},{7,5},{8,10},{9,11},{10,... | collective-permute-start | bytes 1376264 | tf_op jit(solution)/shard_map/ppermute | solution.py:45
  301.6 13.0 %copy-start.23 = (bf16[256,1792]{1,0:T(8,128)(2,1)}, bf16[256,1792]{1,0:T(8,128)(2,1)S(1)}, u32[]{:S(2)}) copy-start(bf16[256,1792]{1,0:T(8,128)(2,1)S(1)} %add.30) | copy-start | bytes 2752516
  301.6 22.0 %collective-permute-start.13 = (bf16[128,1792]{1,0:T(8,128)(2,1)S(1)}, bf16[128,1792]{1,0:T(8,128)(2,1)}, u32[]{:S(2)}, u32[]{:S(2)}) collective-permute-start(bf16[128,1792]{1,0:T(8,128)(2,1)S(1)} %slice.106), channel_id=1, source_target_pairs={{0,1},{1,0},{2,3},{3,2},{4,5},{5,4},{6,7},{7,6},{8,9},{9,8},{10,11... | collective-permute-start | bytes 1376264 | tf_op jit(solution)/shard_map/ppermute | solution.py:45
  314.5 1.0 copy-start.7
  315.5 0.8 copy-start.11
  316.3 0.8 copy-start.26
  323.6 81.3 %all-to-all-start.3 = ((bf16[16,16,3584]{2,1,0:T(8,128)(2,1)}), bf16[16,16,3584]{2,1,0:T(8,128)(2,1)}, u32[]{:S(2)}, u32[]{:S(2)}) async-start(bf16[16,16,3584]{2,1,0:T(8,128)(2,1)} %bitcast.38), calls=%async_computation.3 | async-start | bytes 3670016 | tf_op jit(solution)/shard_map/all_to_all | solution.py:34
  333.0 0.8 copy-start.17
  334.6 6.1 %copy-start.3 = (bf16[512,3584]{1,0:T(8,128)(2,1)S(1)}, bf16[512,3584]{1,0:T(8,128)(2,1)}, u32[]{:S(2)}) copy-start(bf16[512,3584]{1,0:T(8,128)(2,1)} %pad_maximum_fusion.1.left_ref) | copy-start | bytes 11010052
  334.6 6.1 %copy-start.6 = (bf16[512,1024]{1,0:T(8,128)(2,1)S(1)}, bf16[512,1024]{1,0:T(8,128)(2,1)}, u32[]{:S(2)}) copy-start(bf16[512,1024]{1,0:T(8,128)(2,1)} %copy-done.5) | copy-start | bytes 3145732
  334.6 6.1 %copy-start.10 = (bf16[256,1024]{1,0:T(8,128)(2,1)S(1)}, bf16[256,1024]{1,0:T(8,128)(2,1)}, u32[]{:S(2)}) copy-start(bf16[256,1024]{1,0:T(8,128)(2,1)} %copy-done.9) | copy-start | bytes 1572868
  334.6 6.1 %copy-start.12 = (bf16[256,1024]{1,0:T(8,128)(2,1)S(1)}, bf16[256,1024]{1,0:T(8,128)(2,1)}, u32[]{:S(2)}) copy-start(bf16[256,1024]{1,0:T(8,128)(2,1)} %copy-done.11) | copy-start | bytes 1572868
  334.6 39.2 %collective-permute-start.16 = (bf16[64,3584]{1,0:T(8,128)(2,1)}, bf16[64,3584]{1,0:T(8,128)(2,1)}, u32[]{:S(2)}, u32[]{:S(2)}) collective-permute-start(bf16[64,3584]{1,0:T(8,128)(2,1)} %pad_maximum_fusion.8), channel_id=1, source_target_pairs={{0,4},{1,5},{2,6},{3,7},{4,0},{5,1},{6,2},{7,3},{8,12},{9,13},{10,... | collective-permute-start | bytes 1376264 | tf_op jit(solution)/shard_map/ppermute | solution.py:45
  340.7 11.6 %copy-start.1 = (bf16[512,3584]{1,0:T(8,128)(2,1)S(1)}, bf16[512,3584]{1,0:T(8,128)(2,1)}, u32[]{:S(2)}) copy-start(bf16[512,3584]{1,0:T(8,128)(2,1)} %pad_maximum_fusion.left_ref) | copy-start | bytes 11010052
  340.7 11.6 %copy-start.8 = (bf16[256,2048]{1,0:T(8,128)(2,1)S(1)}, bf16[256,2048]{1,0:T(8,128)(2,1)}, u32[]{:S(2)}) copy-start(bf16[256,2048]{1,0:T(8,128)(2,1)} %copy-done.7) | copy-start | bytes 3145732
  352.4 21.4 %copy-start.18 = (bf16[128,1792]{1,0:T(8,128)(2,1)S(1)}, bf16[128,1792]{1,0:T(8,128)(2,1)}, u32[]{:S(2)}) copy-start(bf16[128,1792]{1,0:T(8,128)(2,1)} %copy-done.17) | copy-start | bytes 1376260
  375.0 29.9 %collective-permute-start.17 = (bf16[32,3584]{1,0:T(8,128)(2,1)S(1)}, bf16[32,3584]{1,0:T(8,128)(2,1)S(1)}, u32[]{:S(2)}, u32[]{:S(2)}) collective-permute-start(bf16[32,3584]{1,0:T(8,128)(2,1)S(1)} %slice.99), channel_id=1, source_target_pairs={{0,8},{1,9},{2,10},{3,11},{4,12},{5,13},{6,14},{7,15},{8,0},{9,1},... | collective-permute-start | bytes 688136 | tf_op jit(solution)/shard_map/ppermute | solution.py:45

commit v8 on v6

--- a/solution.py
+++ b/solution.py
@@ -180,6 +180,42 @@
     )(keep, *gate_pair, *grad_pair, matrix)
 
 
+def outer_kernel(count, *refs):
+    out_ref = refs[-1]
+    total = dot_f32(refs[0][...], refs[count][...], 0, 0)
+    for left_ref, right_ref in zip(refs[1:count], refs[count + 1 : -1]):
+        total += dot_f32(left_ref[...], right_ref[...], 0, 0)
+    out_ref[...] = total.astype(out_ref.dtype)
+
+
+def outer_of_pieces(lefts, rights, shares, share):
+    width = lefts[0].shape[1]
+    step = block_of(share, 512)
+    steps = share // step
+    rows = sum(left.shape[0] for left in lefts)
+
+    def columns(part):
+        return lambda j: (0, part * steps + j)
+
+    return pl.pallas_call(
+        functools.partial(outer_kernel, len(lefts)),
+        grid=(steps,),
+        in_specs=[pl.BlockSpec(left.shape, lambda j: (0, 0)) for left in lefts]
+        + [
+            pl.BlockSpec((right.shape[0], step), columns(part))
+            for right, part in zip(rights, shares)
+        ],
+        out_specs=pl.BlockSpec((width, step), lambda j: (0, j)),
+        out_shape=jax.ShapeDtypeStruct((width, share), jnp.bfloat16),
+        compiler_params=pltpu.CompilerParams(vmem_limit_bytes=VMEM_BYTES // 2),
+        cost_estimate=pl.CostEstimate(
+            flops=2 * rows * width * share,
+            bytes_accessed=2 * (rows * (width + share) + width * share),
+            transcendentals=0,
+        ),
+    )(*lefts, *rights)
+
+
 def outer(left, right):
     return lax.dot_general(
         left, right, (((0,), (0,)), ((), ())), preferred_element_type=jnp.float32
@@ -249,18 +285,17 @@
     out_0, hidden_0, branch_0 = finish(
         always, *products(arrived_0, 0, arrived_0, 1), gate_up_matrix
     )
-    rows_0, grads_0 = split(arrived_0)
-    arrived_1, out_0, come_a, come_b = lax.optimization_barrier(
-        (arrived_1, out_0, come_a, come_b)
-    )
+    rows_0, _ = split(arrived_0)
+    arrived_1, out_0, rows_0 = lax.optimization_barrier((arrived_1, out_0, rows_0))
 
     back_0 = exchange(out_0, expert_count)
+    come_a, come_b, gate_pair, grad_pair = lax.optimization_barrier(
+        (come_a, come_b, *products(arrived_1, 0, arrived_1, 1))
+    )
     kept_a, sent_a = halves(kept_a + come_a)
     kept_b, sent_b = halves(kept_b + come_b)
     come_a, come_b = swap_with(sent_a, 2), swap_with(sent_b, 1)
-    out_1, hidden_1, branch_1 = finish(
-        always, *products(arrived_1, 0, arrived_1, 1), gate_up_matrix
-    )
+    out_1, hidden_1, branch_1 = finish(always, gate_pair, grad_pair, gate_up_matrix)
     back_0, come_a, come_b, out_1, arrived_1 = lax.optimization_barrier(
         (back_0, come_a, come_b, out_1, arrived_1)
     )
@@ -268,15 +303,18 @@
 
     for mask in reversed(far[1:]):
         back_s = halve(back_s, mask)
-    rows_1, grads_1 = split(arrived_1)
+    rows_1, _ = split(arrived_1)
     back_1 = exchange(out_1, expert_count)
 
     all_rows = jnp.concatenate([spill_rows, rows_0, rows_1], axis=0)
-    all_grads = jnp.concatenate([spill_grads, grads_0, grads_1], axis=0)
-    hidden = jnp.concatenate([hidden_s, hidden_0, hidden_1], axis=0)
     branch = jnp.concatenate([branch_s, branch_0, branch_1], axis=0)
     gate_up_grads = with_layout_constraint(outer(all_rows, branch), Layout((0, 1)))
-    down_grads = outer(hidden, all_grads).reshape(1, hidden_width, feature_share)
+    down_grads = outer_of_pieces(
+        (hidden_s, hidden_0, hidden_1),
+        (spill_grads, arrived_0, arrived_1),
+        (0, 1, 1),
+        feature_share,
+    ).reshape(1, hidden_width, feature_share)
     gate_up_grads = gate_up_grads.reshape(feature_share // 8, 8, 2, hidden_width)
     back_s, gate_up_grads, down_grads = lax.optimization_barrier(
         (back_s, gate_up_grads.transpose(0, 2, 1, 3), down_grads)

time: 403 us -> 400 us (level)
  local copies, waits for them, and re-layouts: 63.4 us -> 47 us
  waiting for transfers between devices: 131 us -> 146 us
  matrix products: 44.6 us -> 32.4 us
  Pallas kernels: 90.8 us -> 103 us
    ppermute x12, waiting for transfers between devices: 127 us -> 144 us  [swap_with(): return lax.ppermute(rows, 'exp', [(i, i ^ mask) for i in range(total)])]
    transpose x1, local copies, waits for them, and re-layouts: 27.1 us -> 13.8 us  [local(): gate_up_grads.transpose(0, 2, 1, 3)]
    pallas_call x0 -> x1, Pallas kernels: none -> 12.6 us  [outer_of_pieces(): pl.pallas_call(functools.partial(outer_kernel, len(lefts)), grid=(steps,)...]
    dot_general x2 -> x1, matrix products: 33 us -> 20.8 us  [outer(): lax.dot_general(left, right, (((0,), (0,)), ((), ())), preferred_element_...]
    unnamed x54 -> x62, local copies, waits for them, and re-layouts: 24.4 us -> 23.5 us
  transfers between devices with their start and end apart: 22 -> 22, of which waited for: 8 -> 6; matrix products, arithmetic and copies ran while one was open for 26% -> 19% of each run, Pallas kernels for 23% -> 26%
where the time goes in v8:
time: 400 us; the launch traced here: 399 us
  waiting for transfers between devices  146 us (36%)
  Pallas kernels  103 us (26%)
  starting transfers between devices  57.9 us (14%)
  local copies, waits for them, and re-layouts  47 us (12%)
  matrix products  32.4 us (8%)
  other arithmetic  10.5 us (3%)
    ppermute x12, waiting for transfers between devices, swap_with(): return lax.ppermute(rows, 'exp', [(i, i ^ mask) for i in range(total)])  144 us
    pallas_call x6, Pallas kernels, product(): pl.pallas_call(functools.partial(product_kernel, 1 if transposed else 0),...  51.6 us
    pallas_call x3, Pallas kernels, finish(): pl.pallas_call(finish_kernel, grid=(features // step,), in_specs=[pl.Bloc...  39.2 us
    all_to_all x4, starting transfers between devices, exchange(): lax.all_to_all(rows.reshape(expert_count, slots // expert_count, width),...  34 us
    unnamed x62, local copies, waits for them, and re-layouts  23.5 us
    ppermute x12, starting transfers between devices, swap_with(): return lax.ppermute(rows, 'exp', [(i, i ^ mask) for i in range(total)])  22.9 us
    dot_general x1, matrix products, outer(): lax.dot_general(left, right, (((0,), (0,)), ((), ())), preferred_element_...  20.8 us
    transpose x1, local copies, waits for them, and re-layouts, local(): gate_up_grads.transpose(0, 2, 1, 3)  13.8 us
  transfers between devices with their start and end apart: 22, of which 6 were waited for; matrix products, arithmetic and copies ran while one was open for 19% of the time, Pallas kernels for 26%

profile of v8, /device:TPU:0, one launch (start us, length us, event | category | flops | bytes accessed | tf_op | source)
XLA Modules:
  0.0 398.6 jit_solution(9462739258275753387)
XLA Ops:
  0.7 1.8 constant_dynamic-update-slice_fusion.1
  2.5 0.2 convert_reduce_fusion
  2.7 0.6 select_reduce_fusion
  3.3 0.2 constant_dynamic-update-slice_fusion
  3.5 0.7 convolution_convert_fusion.3
  4.3 4.1 %collective-permute-start = (bf16[32,7168]{1,0:T(8,128)(2,1)S(1)}, bf16[32,7168]{1,0:T(8,128)(2,1)S(1)}, u32[]{:S(2)}, u32[]{:S(2)}) collective-permute-start(bf16[32,7168]{1,0:T(8,128)(2,1)S(1)} %convolution_convert_fusion.3), channel_id=1, source_target_pairs={{0,8},{1,9},{2,10},{3,11},{4,12},{5,13},{6,14},{7,15},{8,0},{9,1},... | collective-permute-start | bytes 1376264 | tf_op jit(solution)/shard_map/ppermute | solution.py:45
  8.4 20.3 %collective-permute-done = bf16[32,7168]{1,0:T(8,128)(2,1)S(1)} collective-permute-done((bf16[32,7168]{1,0:T(8,128)(2,1)S(1)}, bf16[32,7168]{1,0:T(8,128)(2,1)S(1)}, u32[]{:S(2)}, u32[]{:S(2)}) %collective-permute-start) | collective-permute-done | bytes 458784 | tf_op jit(solution)/shard_map/ppermute | solution.py:45
  28.8 0.8 collective-permute-start.1
  29.6 3.0 convolution_convert_fusion.2
  32.5 17.8 %collective-permute-done.1 = bf16[64,7168]{1,0:T(8,128)(2,1)S(1)} collective-permute-done((bf16[64,7168]{1,0:T(8,128)(2,1)S(1)}, bf16[64,7168]{1,0:T(8,128)(2,1)S(1)}, u32[]{:S(2)}, u32[]{:S(2)}) %collective-permute-start.1) | collective-permute-done | bytes 917536 | tf_op jit(solution)/shard_map/ppermute | solution.py:45
  50.4 0.1 pad_maximum_fusion.2
  50.5 0.1 fusion.29
  50.6 7.6 %all-to-all-start = ((bf16[16,16,7168]{2,1,0:T(8,128)(2,1)}), bf16[16,16,7168]{2,1,0:T(8,128)(2,1)}, u32[]{:S(2)}, u32[]{:S(2)}) async-start(bf16[16,16,7168]{2,1,0:T(8,128)(2,1)} %bitcast.37), calls=%async_computation | async-start | bytes 7340032 | tf_op jit(solution)/shard_map/all_to_all | solution.py:34
  58.2 1.9 collective-permute-start.2
  60.1 1.5 collective-permute-start.4
  61.6 50.2 %collective-permute-done.2 = bf16[128,3584]{1,0:T(8,128)(2,1)S(1)} collective-permute-done((bf16[128,3584]{1,0:T(8,128)(2,1)S(1)}, bf16[128,3584]{1,0:T(8,128)(2,1)S(1)}, u32[]{:S(2)}, u32[]{:S(2)}) %collective-permute-start.2) | collective-permute-done | bytes 917536 | tf_op jit(solution)/shard_map/ppermute | solution.py:45
  111.9 1.7 collective-permute-start.3
  113.7 2.5 collective-permute-start.5
  116.3 16.2 %copy.10 = bf16[448,8,2,1024]{3,1,2,0:T(8,128)(2,1)} copy(bf16[448,8,2,1024]{3,2,1,0:T(2,128)(2,1)} %bitcast.31) | data formatting | bytes 29360128
  132.5 3.0 convolution_convert_fusion.1
  135.4 27.2 %collective-permute-done.3 = bf16[256,3584]{1,0:T(8,128)(2,1)S(1)} collective-permute-done((bf16[256,3584]{1,0:T(8,128)(2,1)S(1)}, bf16[256,3584]{1,0:T(8,128)(2,1)S(1)}, u32[]{:S(2)}, u32[]{:S(2)}) %collective-permute-start.3) | collective-permute-done | bytes 1835040 | tf_op jit(solution)/shard_map/ppermute | solution.py:45
  162.6 2.0 pad_maximum_fusion.left_ref
  164.6 0.1 fusion.28
  164.8 2.0 pad_maximum_fusion.1.left_ref.refs_3_
  166.8 10.5 %all-to-all-start.1 = ((bf16[16,16,7168]{2,1,0:T(8,128)(2,1)}), bf16[16,16,7168]{2,1,0:T(8,128)(2,1)}, u32[]{:S(2)}, u32[]{:S(2)}) async-start(bf16[16,16,7168]{2,1,0:T(8,128)(2,1)} %bitcast.36), calls=%async_computation.1 | async-start | bytes 7340032 | tf_op jit(solution)/shard_map/all_to_all | solution.py:34
  177.3 2.0 copy-done
  179.3 12.1 %shard_map.76.gate_a = bf16[512,2048]{1,0:T(8,128)(2,1)S(1)} custom-call(bf16[512,3584]{1,0:T(8,128)(2,1)S(1)} %copy-done, bf16[3584,2048]{1,0:T(8,128)(2,1)} %bitcast.22), custom_call_target="tpu_custom_call" | custom-call | flops 1 | bytes 1 | tf_op jit(solution)/shard_map/pallas_call | solution.py:102
  191.5 7.2 %shard_map.77.grad_a = bf16[512,1024]{1,0:T(8,128)(2,1)S(1)} custom-call(bf16[512,3584]{1,0:T(8,128)(2,1)S(1)} %copy-done.2, bf16[1024,3584]{1,0:T(8,128)(2,1)} %bitcast.28), custom_call_target="tpu_custom_call" | custom-call | flops 1 | bytes 1 | tf_op jit(solution)/shard_map/pallas_call | solution.py:102
  199.5 2.1 collective-permute-done.7.grad_b
  201.6 16.4 %shard_map.78 = (bf16[512,3584]{1,0:T(8,128)(2,1)}, bf16[512,1024]{1,0:T(8,128)(2,1)S(1)}, bf16[512,2048]{1,0:T(8,128)(2,1)S(1)}) custom-call(s32[1]{0:T(128)} %bitcast.2.keep_ref, bf16[512,2048]{1,0:T(8,128)(2,1)} %copy-done.4, bf16[512,2048]{1,0:T(8,128)(2,1)} %collective-permute-done.6.gate_b, bf16[512,1024]{1,0:T(8,128)(2,1)S(1)} %shard_map.77.grad_a, ...), custom_call_target="tpu_custom_call" | custom-call | flops 1 | bytes 1 | tf_op jit(solution)/shard_map/pallas_call | solution.py:161
  218.0 2.0 fusion.26
  220.0 1.4 pad_maximum_fusion.6
  221.4 1.4 fusion.27
  222.7 10.3 %shard_map.79.gate_a = bf16[256,2048]{1,0:T(8,128)(2,1)S(1)} custom-call(bf16[256,7168]{1,0:T(8,128)(2,1)} %bitcast.1.left_ref.refs_4_, bf16[3584,2048]{1,0:T(8,128)(2,1)} %bitcast.24), custom_call_target="tpu_custom_call" | custom-call | flops 1 | bytes 1 | tf_op jit(solution)/shard_map/pallas_call | solution.py:102
  233.1 0.2 collective-permute-start.10
  233.3 5.8 %shard_map.80.grad_a = bf16[256,1024]{1,0:T(8,128)(2,1)S(1)} custom-call(bf16[256,7168]{1,0:T(8,128)(2,1)} %bitcast.1.left_ref.refs_4_, bf16[1024,3584]{1,0:T(8,128)(2,1)} %bitcast.29), custom_call_target="tpu_custom_call" | custom-call | flops 1 | bytes 1 | tf_op jit(solution)/shard_map/pallas_call | solution.py:102
  239.0 0.4 collective-permute-start.11
  239.5 2.9 slice.82
  242.4 11.4 %shard_map.81 = (bf16[256,3584]{1,0:T(8,128)(2,1)}, bf16[256,1024]{1,0:T(8,128)(2,1)S(1)}, bf16[256,2048]{1,0:T(8,128)(2,1)S(1)}) custom-call(s32[1]{0:T(128)} %constant.20.clone.1.keep_ref, bf16[256,2048]{1,0:T(8,128)(2,1)S(1)} %shard_map.79.gate_a, bf16[256,2048]{1,0:T(8,128)(2,1)S(1)} %collective-permute-done.10.gate_b, ...), custom_call_target="tpu_custom_call" | custom-call | flops 1 | bytes 1 | tf_op jit(solution)/shard_map/pallas_call | solution.py:161
  253.8 0.8 copy-done.9
  254.7 11.1 %all-to-all-start.2 = ((bf16[16,16,3584]{2,1,0:T(8,128)(2,1)}), bf16[16,16,3584]{2,1,0:T(8,128)(2,1)}, u32[]{:S(2)}, u32[]{:S(2)}) async-start(bf16[16,16,3584]{2,1,0:T(8,128)(2,1)} %bitcast.38), calls=%async_computation.2 | async-start | bytes 3670016 | tf_op jit(solution)/shard_map/all_to_all | solution.py:34
  265.7 10.4 %shard_map.82.gate_a = bf16[256,2048]{1,0:T(8,128)(2,1)S(1)} custom-call(bf16[256,7168]{1,0:T(8,128)(2,1)} %bitcast.5.left_ref.refs_5_, bf16[3584,2048]{1,0:T(8,128)(2,1)} %bitcast.26), custom_call_target="tpu_custom_call" | custom-call | flops 1 | bytes 1 | tf_op jit(solution)/shard_map/pallas_call | solution.py:102
  276.3 1.9 collective-permute-start.8
  278.2 1.5 collective-permute-start.9
  279.7 5.8 %shard_map.83.grad_a = bf16[256,1024]{1,0:T(8,128)(2,1)S(1)} custom-call(bf16[256,7168]{1,0:T(8,128)(2,1)} %bitcast.5.left_ref.refs_5_, bf16[1024,3584]{1,0:T(8,128)(2,1)} %bitcast.30), custom_call_target="tpu_custom_call" | custom-call | flops 1 | bytes 1 | tf_op jit(solution)/shard_map/pallas_call | solution.py:102
  285.6 27.9 %collective-permute-done.8 = bf16[256,1792]{1,0:T(8,128)(2,1)S(1)} collective-permute-done((bf16[256,1792]{1,0:T(8,128)(2,1)S(1)}, bf16[256,1792]{1,0:T(8,128)(2,1)S(1)}, u32[]{:S(2)}, u32[]{:S(2)}) %collective-permute-start.8) | collective-permute-done | bytes 917536 | tf_op jit(solution)/shard_map/ppermute | solution.py:45
  313.5 0.2 add.29
  313.8 1.2 collective-permute-start.14
  315.0 0.2 add.30
  315.3 1.5 collective-permute-start.15
  316.8 11.4 %shard_map.84 = (bf16[256,3584]{1,0:T(8,128)(2,1)}, bf16[256,1024]{1,0:T(8,128)(2,1)S(1)}, bf16[256,2048]{1,0:T(8,128)(2,1)S(1)}) custom-call(s32[1]{0:T(128)} %constant.20.clone.1.keep_ref, bf16[256,2048]{1,0:T(8,128)(2,1)S(1)} %shard_map.82.gate_a, bf16[256,2048]{1,0:T(8,128)(2,1)S(1)} %collective-permute-done.12.gate_b, ...), custom_call_target="tpu_custom_call" | custom-call | flops 1 | bytes 1 | tf_op jit(solution)/shard_map/pallas_call | solution.py:161
  328.1 1.0 copy-done.7
  329.1 0.8 copy-done.11
  329.9 0.8 copy-done.24
  330.7 4.9 %all-to-all-start.3 = ((bf16[16,16,3584]{2,1,0:T(8,128)(2,1)}), bf16[16,16,3584]{2,1,0:T(8,128)(2,1)}, u32[]{:S(2)}, u32[]{:S(2)}) async-start(bf16[16,16,3584]{2,1,0:T(8,128)(2,1)} %bitcast.39), calls=%async_computation.3 | async-start | bytes 3670016 | tf_op jit(solution)/shard_map/all_to_all | solution.py:34
  335.6 1.4 slice_add_fusion
  336.9 1.9 slice_add_fusion.1
  338.9 1.9 collective-permute-start.16
  340.8 2.8 slice.89
  343.7 20.8 %convolution_convert_fusion = bf16[3584,2048]{1,0:T(8,128)(2,1)} fusion(bf16[256,3584]{1,0:T(8,128)(2,1)} %slice.89, bf16[256,3584]{1,0:T(8,128)(2,1)S(1)} %copy-done.21, bf16[512,3584]{1,0:T(8,128)(2,1)S(1)} %copy-done.1, bf16[256,2048]{1,0:T(8,128)(2,1)S(1)} %copy-done.8, bf16[256,2048]{1,0:T(8,128)(2,1)S(1)} %get-tuple-element.71, ...), kind=kOutput, calls=%fused_computation | convolution fusion | flops 15074328576 | bytes 26214400 | tf_op jit(solution)/shard_map/dot_general | solution.py:220
  364.5 12.6 %shard_map.85 = bf16[1024,3584]{1,0:T(8,128)(2,1)} custom-call(bf16[512,1024]{1,0:T(8,128)(2,1)S(1)} %copy-done.6, bf16[256,1024]{1,0:T(8,128)(2,1)S(1)} %copy-done.10, bf16[256,1024]{1,0:T(8,128)(2,1)S(1)} %copy-done.12, bf16[512,3584]{1,0:T(8,128)(2,1)S(1)} %copy-done.3, bf16[256,7168]{1,0:T(8,128)(2,1)} %bitcast.1.left_ref.refs_4_, ...), custom_call_target="tpu_custom_call" | custom-call | flops 7516192768 | bytes 16777216 | tf_op jit(solution)/shard_map/pallas_call | solution.py:200
  377.3 2.4 collective-permute-start.17
  379.8 13.8 %copy.9 = bf16[448,8,2,1024]{3,2,1,0:T(2,128)(2,1)} copy(bf16[448,8,2,1024]{3,1,2,0:T(8,128)(2,1)S(1)} %bitcast.34) | data formatting | bytes 29360128 | tf_op jit(solution)/shard_map/transpose | solution.py:324
  393.7 4.9 %convolution_convert_fusion.4 = bf16[256,3584]{1,0:T(8,128)(2,1)} fusion(bf16[256,3584]{1,0:T(8,128)(2,1)} %bitcast.12, bf16[256,3584]{1,0:T(8,128)(2,1)} %bitcast.7, bf16[32,3584]{1,0:T(8,128)(2,1)S(1)} %slice_add_fusion.2, pred[256,256]{1,0:T(32,128)(4,1)S(1)} %get-tuple-element.95, pred[256,256]{1,0:T(32,128)(4,1)S(1)} %get-tuple-element.96, ...), kind=kOutput, calls=%fused_computation.9 | convolution fusion | flops 1011138560 | bytes 5873664 | tf_op jit(solution)/shard_map/dot_general | solution.py:330
  (87 shorter events, 1.1 us)
Async XLA Ops:
  0.6 1.9 copy-start.25
  0.6 2.7 copy-start.20
  3.5 29.0 %copy-start.13 = (bf16[256,7168]{1,0:T(8,128)(2,1)}, bf16[256,7168]{1,0:T(8,128)(2,1)S(1)}, u32[]{:S(2)}) copy-start(bf16[256,7168]{1,0:T(8,128)(2,1)S(1)} %constant_dynamic-update-slice_fusion) | copy-start | bytes 11010052
  4.3 24.5 %collective-permute-start = (bf16[32,7168]{1,0:T(8,128)(2,1)S(1)}, bf16[32,7168]{1,0:T(8,128)(2,1)S(1)}, u32[]{:S(2)}, u32[]{:S(2)}) collective-permute-start(bf16[32,7168]{1,0:T(8,128)(2,1)S(1)} %convolution_convert_fusion.3), channel_id=1, source_target_pairs={{0,8},{1,9},{2,10},{3,11},{4,12},{5,13},{6,14},{7,15},{8,0},{9,1},... | collective-permute-start | bytes 1376264 | tf_op jit(solution)/shard_map/ppermute | solution.py:45
  28.8 21.6 %collective-permute-start.1 = (bf16[64,7168]{1,0:T(8,128)(2,1)S(1)}, bf16[64,7168]{1,0:T(8,128)(2,1)S(1)}, u32[]{:S(2)}, u32[]{:S(2)}) collective-permute-start(bf16[64,7168]{1,0:T(8,128)(2,1)S(1)} %pad_maximum_fusion.5), channel_id=1, source_target_pairs={{0,4},{1,5},{2,6},{3,7},{4,0},{5,1},{6,2},{7,3},{8,12},{9,13},{10,... | collective-permute-start | bytes 2752520 | tf_op jit(solution)/shard_map/ppermute | solution.py:45
  50.6 116.1 %all-to-all-start = ((bf16[16,16,7168]{2,1,0:T(8,128)(2,1)}), bf16[16,16,7168]{2,1,0:T(8,128)(2,1)}, u32[]{:S(2)}, u32[]{:S(2)}) async-start(bf16[16,16,7168]{2,1,0:T(8,128)(2,1)} %bitcast.37), calls=%async_computation | async-start | bytes 7340032 | tf_op jit(solution)/shard_map/all_to_all | solution.py:34
  58.2 53.6 %collective-permute-start.2 = (bf16[128,3584]{1,0:T(8,128)(2,1)S(1)}, bf16[128,3584]{1,0:T(8,128)(2,1)S(1)}, u32[]{:S(2)}, u32[]{:S(2)}) collective-permute-start(bf16[128,3584]{1,0:T(8,128)(2,1)S(1)} %get-tuple-element.43), channel_id=1, source_target_pairs={{0,2},{1,3},{2,0},{3,1},{4,6},{5,7},{6,4},{7,5},{8,10},{9,11},{10,... | collective-permute-start | bytes 2752520 | tf_op jit(solution)/shard_map/ppermute | solution.py:45
  60.1 53.5 %collective-permute-start.4 = (bf16[128,3584]{1,0:T(8,128)(2,1)S(1)}, bf16[128,3584]{1,0:T(8,128)(2,1)S(1)}, u32[]{:S(2)}, u32[]{:S(2)}) collective-permute-start(bf16[128,3584]{1,0:T(8,128)(2,1)S(1)} %get-tuple-element.44), channel_id=1, source_target_pairs={{0,1},{1,0},{2,3},{3,2},{4,5},{5,4},{6,7},{7,6},{8,9},{9,8},{10,11... | collective-permute-start | bytes 2752520 | tf_op jit(solution)/shard_map/ppermute | solution.py:45
  111.9 50.7 %collective-permute-start.3 = (bf16[256,3584]{1,0:T(8,128)(2,1)S(1)}, bf16[256,3584]{1,0:T(8,128)(2,1)S(1)}, u32[]{:S(2)}, u32[]{:S(2)}) collective-permute-start(bf16[256,3584]{1,0:T(8,128)(2,1)S(1)} %pad_maximum_fusion.3), channel_id=1, source_target_pairs={{0,1},{1,0},{2,3},{3,2},{4,5},{5,4},{6,7},{7,6},{8,9},{9,8},{10,11... | collective-permute-start | bytes 5505032 | tf_op jit(solution)/shard_map/ppermute | solution.py:45
  113.7 50.9 %collective-permute-start.5 = (bf16[256,3584]{1,0:T(8,128)(2,1)S(1)}, bf16[256,3584]{1,0:T(8,128)(2,1)S(1)}, u32[]{:S(2)}, u32[]{:S(2)}) collective-permute-start(bf16[256,3584]{1,0:T(8,128)(2,1)S(1)} %pad_maximum_fusion.4), channel_id=1, source_target_pairs={{0,2},{1,3},{2,0},{3,1},{4,6},{5,7},{6,4},{7,5},{8,10},{9,11},{10,... | collective-permute-start | bytes 5505032 | tf_op jit(solution)/shard_map/ppermute | solution.py:45
  116.3 16.2 %copy-start.14 = (bf16[256,7168]{1,0:T(8,128)(2,1)S(1)}, bf16[256,7168]{1,0:T(8,128)(2,1)}, u32[]{:S(2)}) copy-start(bf16[256,7168]{1,0:T(8,128)(2,1)} %copy-done.13) | copy-start | bytes 11010052
  166.8 87.9 %all-to-all-start.1 = ((bf16[16,16,7168]{2,1,0:T(8,128)(2,1)}), bf16[16,16,7168]{2,1,0:T(8,128)(2,1)}, u32[]{:S(2)}, u32[]{:S(2)}) async-start(bf16[16,16,7168]{2,1,0:T(8,128)(2,1)} %bitcast.36), calls=%async_computation.1 | async-start | bytes 7340032 | tf_op jit(solution)/shard_map/all_to_all | solution.py:34
  177.3 2.0 copy-start
  179.3 12.2 %copy-start.2 = (bf16[512,3584]{1,0:T(8,128)(2,1)S(1)}, bf16[512,3584]{1,0:T(8,128)(2,1)}, u32[]{:S(2)}) copy-start(bf16[512,3584]{1,0:T(8,128)(2,1)} %pad_maximum_fusion.1.left_ref.refs_3_) | copy-start | bytes 11010052
  191.4 7.4 %copy-start.4 = (bf16[512,2048]{1,0:T(8,128)(2,1)}, bf16[512,2048]{1,0:T(8,128)(2,1)S(1)}, u32[]{:S(2)}) copy-start(bf16[512,2048]{1,0:T(8,128)(2,1)S(1)} %shard_map.76.gate_a) | copy-start | bytes 6291460
  191.4 10.2 %collective-permute-start.6 = (bf16[512,2048]{1,0:T(8,128)(2,1)S(1)}, bf16[512,2048]{1,0:T(8,128)(2,1)}, u32[]{:S(2)}, u32[]{:S(2)}) collective-permute-start(bf16[512,2048]{1,0:T(8,128)(2,1)S(1)} %shard_map.76.gate_a), channel_id=1, source_target_pairs={{0,16},{16,0},{1,17},{17,1},{2,18},{18,2},{3,19},{19,3},{4,20},{20... | collective-permute-start | bytes 6291464 | tf_op jit(solution)/shard_map/ppermute | solution.py:115
  198.8 2.9 collective-permute-start.7
  218.0 3.4 copy-start.5
  218.0 3.4 copy-start.15
  233.1 9.3 %collective-permute-start.10 = (bf16[256,2048]{1,0:T(8,128)(2,1)S(1)}, bf16[256,2048]{1,0:T(8,128)(2,1)S(1)}, u32[]{:S(2)}, u32[]{:S(2)}) collective-permute-start(bf16[256,2048]{1,0:T(8,128)(2,1)S(1)} %shard_map.79.gate_a), channel_id=1, source_target_pairs={{0,16},{16,0},{1,17},{17,1},{2,18},{18,2},{3,19},{19,3},{4,20},{20... | collective-permute-start | bytes 3145736 | tf_op jit(solution)/shard_map/ppermute | solution.py:115
  239.0 3.3 collective-permute-start.11
  253.8 0.8 copy-start.9
  254.7 76.0 %all-to-all-start.2 = ((bf16[16,16,3584]{2,1,0:T(8,128)(2,1)}), bf16[16,16,3584]{2,1,0:T(8,128)(2,1)}, u32[]{:S(2)}, u32[]{:S(2)}) async-start(bf16[16,16,3584]{2,1,0:T(8,128)(2,1)} %bitcast.38), calls=%async_computation.2 | async-start | bytes 3670016 | tf_op jit(solution)/shard_map/all_to_all | solution.py:34
  265.7 10.6 %copy-start.23 = (bf16[256,1792]{1,0:T(8,128)(2,1)S(1)}, bf16[256,1792]{1,0:T(8,128)(2,1)}, u32[]{:S(2)}) copy-start(bf16[256,1792]{1,0:T(8,128)(2,1)} %get-tuple-element.51) | copy-start | bytes 2752516
  265.7 12.5 %copy-start.22 = (bf16[256,1792]{1,0:T(8,128)(2,1)S(1)}, bf16[256,1792]{1,0:T(8,128)(2,1)}, u32[]{:S(2)}) copy-start(bf16[256,1792]{1,0:T(8,128)(2,1)} %get-tuple-element.52) | copy-start | bytes 2752516
  276.2 37.3 %copy-start.17 = (bf16[256,1792]{1,0:T(8,128)(2,1)S(1)}, bf16[256,1792]{1,0:T(8,128)(2,1)}, u32[]{:S(2)}) copy-start(bf16[256,1792]{1,0:T(8,128)(2,1)} %get-tuple-element.50) | copy-start | bytes 2752516
  276.2 37.3 %collective-permute-start.12 = (bf16[256,2048]{1,0:T(8,128)(2,1)S(1)}, bf16[256,2048]{1,0:T(8,128)(2,1)S(1)}, u32[]{:S(2)}, u32[]{:S(2)}) collective-permute-start(bf16[256,2048]{1,0:T(8,128)(2,1)S(1)} %shard_map.82.gate_a), channel_id=1, source_target_pairs={{0,16},{16,0},{1,17},{17,1},{2,18},{18,2},{3,19},{19,3},{4,20},{20... | collective-permute-start | bytes 3145736 | tf_op jit(solution)/shard_map/ppermute | solution.py:115
  276.3 37.2 %collective-permute-start.8 = (bf16[256,1792]{1,0:T(8,128)(2,1)S(1)}, bf16[256,1792]{1,0:T(8,128)(2,1)S(1)}, u32[]{:S(2)}, u32[]{:S(2)}) collective-permute-start(bf16[256,1792]{1,0:T(8,128)(2,1)S(1)} %copy-done.23), channel_id=1, source_target_pairs={{0,1},{1,0},{2,3},{3,2},{4,5},{5,4},{6,7},{7,6},{8,9},{9,8},{10,11... | collective-permute-start | bytes 2752520 | tf_op jit(solution)/shard_map/ppermute | solution.py:45
  278.2 35.3 %collective-permute-start.9 = (bf16[256,1792]{1,0:T(8,128)(2,1)S(1)}, bf16[256,1792]{1,0:T(8,128)(2,1)S(1)}, u32[]{:S(2)}, u32[]{:S(2)}) collective-permute-start(bf16[256,1792]{1,0:T(8,128)(2,1)S(1)} %copy-done.22), channel_id=1, source_target_pairs={{0,2},{1,3},{2,0},{3,1},{4,6},{5,7},{6,4},{7,5},{8,10},{9,11},{10,... | collective-permute-start | bytes 2752520 | tf_op jit(solution)/shard_map/ppermute | solution.py:45
  285.5 29.5 %copy-start.16 = (bf16[256,1792]{1,0:T(8,128)(2,1)S(1)}, bf16[256,1792]{1,0:T(8,128)(2,1)}, u32[]{:S(2)}) copy-start(bf16[256,1792]{1,0:T(8,128)(2,1)} %get-tuple-element.59) | copy-start | bytes 2752516
  285.5 28.0 %collective-permute-start.13 = (bf16[256,1024]{1,0:T(8,128)(2,1)S(1)}, bf16[256,1024]{1,0:T(8,128)(2,1)S(1)}, u32[]{:S(2)}, u32[]{:S(2)}) collective-permute-start(bf16[256,1024]{1,0:T(8,128)(2,1)S(1)} %shard_map.83.grad_a), channel_id=1, source_target_pairs={{0,16},{16,0},{1,17},{17,1},{2,18},{18,2},{3,19},{19,3},{4,20},{20... | collective-permute-start | bytes 1572872 | tf_op jit(solution)/shard_map/ppermute | solution.py:115
  313.8 1.5 copy-start.18
  313.8 16.1 %collective-permute-start.14 = (bf16[128,1792]{1,0:T(8,128)(2,1)S(1)}, bf16[128,1792]{1,0:T(8,128)(2,1)S(1)}, u32[]{:S(2)}, u32[]{:S(2)}) collective-permute-start(bf16[128,1792]{1,0:T(8,128)(2,1)S(1)} %slice.97), channel_id=1, source_target_pairs={{0,2},{1,3},{2,0},{3,1},{4,6},{5,7},{6,4},{7,5},{8,10},{9,11},{10,... | collective-permute-start | bytes 1376264 | tf_op jit(solution)/shard_map/ppermute | solution.py:45
  315.2 12.9 %copy-start.19 = (bf16[256,1792]{1,0:T(8,128)(2,1)}, bf16[256,1792]{1,0:T(8,128)(2,1)S(1)}, u32[]{:S(2)}) copy-start(bf16[256,1792]{1,0:T(8,128)(2,1)S(1)} %add.30) | copy-start | bytes 2752516
  315.3 15.4 %collective-permute-start.15 = (bf16[128,1792]{1,0:T(8,128)(2,1)S(1)}, bf16[128,1792]{1,0:T(8,128)(2,1)}, u32[]{:S(2)}, u32[]{:S(2)}) collective-permute-start(bf16[128,1792]{1,0:T(8,128)(2,1)S(1)} %slice.98), channel_id=1, source_target_pairs={{0,1},{1,0},{2,3},{3,2},{4,5},{5,4},{6,7},{7,6},{8,9},{9,8},{10,11... | collective-permute-start | bytes 1376264 | tf_op jit(solution)/shard_map/ppermute | solution.py:45
  328.1 1.0 copy-start.7
  329.1 0.8 copy-start.11
  329.9 0.8 copy-start.24
  330.7 63.0 %all-to-all-start.3 = ((bf16[16,16,3584]{2,1,0:T(8,128)(2,1)}), bf16[16,16,3584]{2,1,0:T(8,128)(2,1)}, u32[]{:S(2)}, u32[]{:S(2)}) async-start(bf16[16,16,3584]{2,1,0:T(8,128)(2,1)} %bitcast.39), calls=%async_computation.3 | async-start | bytes 3670016 | tf_op jit(solution)/shard_map/all_to_all | solution.py:34
  335.6 8.1 %copy-start.1 = (bf16[512,3584]{1,0:T(8,128)(2,1)S(1)}, bf16[512,3584]{1,0:T(8,128)(2,1)}, u32[]{:S(2)}) copy-start(bf16[512,3584]{1,0:T(8,128)(2,1)} %pad_maximum_fusion.left_ref) | copy-start | bytes 11010052
  335.6 8.1 %copy-start.8 = (bf16[256,2048]{1,0:T(8,128)(2,1)S(1)}, bf16[256,2048]{1,0:T(8,128)(2,1)}, u32[]{:S(2)}) copy-start(bf16[256,2048]{1,0:T(8,128)(2,1)} %copy-done.7) | copy-start | bytes 3145732
  335.6 8.1 %copy-start.21 = (bf16[256,3584]{1,0:T(8,128)(2,1)S(1)}, bf16[256,3584]{1,0:T(8,128)(2,1)}, u32[]{:S(2)}) copy-start(bf16[256,3584]{1,0:T(8,128)(2,1)} %slice.82) | copy-start | bytes 5505028
  338.9 38.3 %collective-permute-start.16 = (bf16[64,3584]{1,0:T(8,128)(2,1)S(1)}, bf16[64,3584]{1,0:T(8,128)(2,1)S(1)}, u32[]{:S(2)}, u32[]{:S(2)}) collective-permute-start(bf16[64,3584]{1,0:T(8,128)(2,1)S(1)} %pad_maximum_fusion.8), channel_id=1, source_target_pairs={{0,4},{1,5},{2,6},{3,7},{4,0},{5,1},{6,2},{7,3},{8,12},{9,13},{10,... | collective-permute-start | bytes 1376264 | tf_op jit(solution)/shard_map/ppermute | solution.py:45
  343.7 20.8 %copy-start.3 = (bf16[512,3584]{1,0:T(8,128)(2,1)S(1)}, bf16[512,3584]{1,0:T(8,128)(2,1)}, u32[]{:S(2)}) copy-start(bf16[512,3584]{1,0:T(8,128)(2,1)} %pad_maximum_fusion.1.left_ref.refs_3_) | copy-start | bytes 11010052
  343.7 20.8 %copy-start.6 = (bf16[512,1024]{1,0:T(8,128)(2,1)S(1)}, bf16[512,1024]{1,0:T(8,128)(2,1)}, u32[]{:S(2)}) copy-start(bf16[512,1024]{1,0:T(8,128)(2,1)} %copy-done.5) | copy-start | bytes 3145732
  343.7 20.8 %copy-start.10 = (bf16[256,1024]{1,0:T(8,128)(2,1)S(1)}, bf16[256,1024]{1,0:T(8,128)(2,1)}, u32[]{:S(2)}) copy-start(bf16[256,1024]{1,0:T(8,128)(2,1)} %copy-done.9) | copy-start | bytes 1572868
  343.7 20.8 %copy-start.12 = (bf16[256,1024]{1,0:T(8,128)(2,1)S(1)}, bf16[256,1024]{1,0:T(8,128)(2,1)}, u32[]{:S(2)}) copy-start(bf16[256,1024]{1,0:T(8,128)(2,1)} %copy-done.11) | copy-start | bytes 1572868
  364.5 15.3 %slice-start = ((s8[14680064]{0:T(1024)(128)(4,1)}), s8[4194304]{0:T(1024)(128)(4,1)S(1)}, s32[]{:S(2)}) async-start(s8[14680064]{0:T(1024)(128)(4,1)} %bitcast.32), calls=%async_computation.4 | async-start | bytes 8388608
  364.5 15.3 %slice-start.1 = ((s8[14680064]{0:T(1024)(128)(4,1)}), s8[4194304]{0:T(1024)(128)(4,1)S(1)}, s32[]{:S(2)}) async-start(s8[14680064]{0:T(1024)(128)(4,1)} %bitcast.32), calls=%async_computation.5 | async-start | bytes 8388608
  364.5 15.3 %slice-start.2 = ((s8[14680064]{0:T(1024)(128)(4,1)}), s8[4194304]{0:T(1024)(128)(4,1)S(1)}, s32[]{:S(2)}) async-start(s8[14680064]{0:T(1024)(128)(4,1)} %bitcast.32), calls=%async_computation.6 | async-start | bytes 8388608
  364.5 15.3 %slice-start.3 = ((s8[14680064]{0:T(1024)(128)(4,1)}), s8[2097152]{0:T(1024)(128)(4,1)S(1)}, s32[]{:S(2)}) async-start(s8[14680064]{0:T(1024)(128)(4,1)} %bitcast.32), calls=%async_computation.7 | async-start | bytes 4194304
  377.3 16.4 %collective-permute-start.17 = (bf16[32,3584]{1,0:T(8,128)(2,1)S(1)}, bf16[32,3584]{1,0:T(8,128)(2,1)S(1)}, u32[]{:S(2)}, u32[]{:S(2)}) collective-permute-start(bf16[32,3584]{1,0:T(8,128)(2,1)S(1)} %slice.91), channel_id=1, source_target_pairs={{0,8},{1,9},{2,10},{3,11},{4,12},{5,13},{6,14},{7,15},{8,0},{9,1},... | collective-permute-start | bytes 688136 | tf_op jit(solution)/shard_map/ppermute | solution.py:45

commit v9 on v8

--- a/solution.py
+++ b/solution.py
@@ -286,16 +286,17 @@
         always, *products(arrived_0, 0, arrived_0, 1), gate_up_matrix
     )
     rows_0, _ = split(arrived_0)
-    arrived_1, out_0, rows_0 = lax.optimization_barrier((arrived_1, out_0, rows_0))
+    arrived_1, out_0, come_a, come_b, rows_0 = lax.optimization_barrier(
+        (arrived_1, out_0, come_a, come_b, rows_0)
+    )
 
     back_0 = exchange(out_0, expert_count)
-    come_a, come_b, gate_pair, grad_pair = lax.optimization_barrier(
-        (come_a, come_b, *products(arrived_1, 0, arrived_1, 1))
-    )
     kept_a, sent_a = halves(kept_a + come_a)
     kept_b, sent_b = halves(kept_b + come_b)
     come_a, come_b = swap_with(sent_a, 2), swap_with(sent_b, 1)
-    out_1, hidden_1, branch_1 = finish(always, gate_pair, grad_pair, gate_up_matrix)
+    out_1, hidden_1, branch_1 = finish(
+        always, *products(arrived_1, 0, arrived_1, 1), gate_up_matrix
+    )
     back_0, come_a, come_b, out_1, arrived_1 = lax.optimization_barrier(
         (back_0, come_a, come_b, out_1, arrived_1)
     )

time: 400 us -> 390 us (0.975)
  waiting for transfers between devices: 146 us -> 133 us
    ppermute x12, waiting for transfers between devices: 144 us -> 131 us  [swap_with(): return lax.ppermute(rows, 'exp', [(i, i ^ mask) for i in range(total)])]
  transfers between devices with their start and end apart: 22 -> 22, of which waited for: 6 -> 8; matrix products, arithmetic and copies ran while one was open for 19% -> 20% of each run, Pallas kernels for 26% -> 27%
where the time goes in v9:
time: 390 us; the launch traced here: 389 us
  waiting for transfers between devices  133 us (34%)
  Pallas kernels  103 us (26%)
  starting transfers between devices  59.3 us (15%)
  local copies, waits for them, and re-layouts  47.6 us (12%)
  matrix products  32.4 us (8%)
  other arithmetic  11.4 us (3%)
    ppermute x12, waiting for transfers between devices, swap_with(): return lax.ppermute(rows, 'exp', [(i, i ^ mask) for i in range(total)])  131 us
    pallas_call x6, Pallas kernels, product(): pl.pallas_call(functools.partial(product_kernel, 1 if transposed else 0),...  51.6 us
    pallas_call x3, Pallas kernels, finish(): pl.pallas_call(finish_kernel, grid=(features // step,), in_specs=[pl.Bloc...  39.2 us
    all_to_all x4, starting transfers between devices, exchange(): lax.all_to_all(rows.reshape(expert_count, slots // expert_count, width),...  34.6 us
    unnamed x62, local copies, waits for them, and re-layouts  24.5 us
    ppermute x12, starting transfers between devices, swap_with(): return lax.ppermute(rows, 'exp', [(i, i ^ mask) for i in range(total)])  23.8 us
    dot_general x1, matrix products, outer(): lax.dot_general(left, right, (((0,), (0,)), ((), ())), preferred_element_...  20.8 us
    transpose x1, local copies, waits for them, and re-layouts, local(): gate_up_grads.transpose(0, 2, 1, 3)  13.8 us
  transfers between devices with their start and end apart: 22, of which 8 were waited for; matrix products, arithmetic and copies ran while one was open for 20% of the time, Pallas kernels for 27%

profile of v9, /device:TPU:0, one launch (start us, length us, event | category | flops | bytes accessed | tf_op | source)
XLA Modules:
  0.0 388.8 jit_solution(17152070407952273655)
XLA Ops:
  0.7 1.8 constant_dynamic-update-slice_fusion.1
  2.5 0.2 convert_reduce_fusion
  2.7 0.6 select_reduce_fusion
  3.3 0.2 constant_dynamic-update-slice_fusion
  3.5 0.7 convolution_convert_fusion.3
  4.3 4.1 %collective-permute-start = (bf16[32,7168]{1,0:T(8,128)(2,1)S(1)}, bf16[32,7168]{1,0:T(8,128)(2,1)S(1)}, u32[]{:S(2)}, u32[]{:S(2)}) collective-permute-start(bf16[32,7168]{1,0:T(8,128)(2,1)S(1)} %convolution_convert_fusion.3), channel_id=1, source_target_pairs={{0,8},{1,9},{2,10},{3,11},{4,12},{5,13},{6,14},{7,15},{8,0},{9,1},... | collective-permute-start | bytes 1376264 | tf_op jit(solution)/shard_map/ppermute | solution.py:45
  8.4 20.3 %collective-permute-done = bf16[32,7168]{1,0:T(8,128)(2,1)S(1)} collective-permute-done((bf16[32,7168]{1,0:T(8,128)(2,1)S(1)}, bf16[32,7168]{1,0:T(8,128)(2,1)S(1)}, u32[]{:S(2)}, u32[]{:S(2)}) %collective-permute-start) | collective-permute-done | bytes 458784 | tf_op jit(solution)/shard_map/ppermute | solution.py:45
  28.8 0.8 collective-permute-start.1
  29.6 3.0 convolution_convert_fusion.2
  32.5 17.8 %collective-permute-done.1 = bf16[64,7168]{1,0:T(8,128)(2,1)S(1)} collective-permute-done((bf16[64,7168]{1,0:T(8,128)(2,1)S(1)}, bf16[64,7168]{1,0:T(8,128)(2,1)S(1)}, u32[]{:S(2)}, u32[]{:S(2)}) %collective-permute-start.1) | collective-permute-done | bytes 917536 | tf_op jit(solution)/shard_map/ppermute | solution.py:45
  50.6 7.6 %all-to-all-start = ((bf16[16,16,7168]{2,1,0:T(8,128)(2,1)}), bf16[16,16,7168]{2,1,0:T(8,128)(2,1)}, u32[]{:S(2)}, u32[]{:S(2)}) async-start(bf16[16,16,7168]{2,1,0:T(8,128)(2,1)} %bitcast.37), calls=%async_computation | async-start | bytes 7340032 | tf_op jit(solution)/shard_map/all_to_all | solution.py:34
  58.2 1.9 collective-permute-start.2
  60.1 1.5 collective-permute-start.4
  61.6 50.2 %collective-permute-done.2 = bf16[128,3584]{1,0:T(8,128)(2,1)S(1)} collective-permute-done((bf16[128,3584]{1,0:T(8,128)(2,1)S(1)}, bf16[128,3584]{1,0:T(8,128)(2,1)S(1)}, u32[]{:S(2)}, u32[]{:S(2)}) %collective-permute-start.2) | collective-permute-done | bytes 917536 | tf_op jit(solution)/shard_map/ppermute | solution.py:45
  111.9 1.7 collective-permute-start.3
  113.7 2.5 collective-permute-start.5
  116.3 16.2 %copy.10 = bf16[448,8,2,1024]{3,1,2,0:T(8,128)(2,1)} copy(bf16[448,8,2,1024]{3,2,1,0:T(2,128)(2,1)} %bitcast.31) | data formatting | bytes 29360128
  132.5 3.0 convolution_convert_fusion.1
  135.4 27.2 %collective-permute-done.3 = bf16[256,3584]{1,0:T(8,128)(2,1)S(1)} collective-permute-done((bf16[256,3584]{1,0:T(8,128)(2,1)S(1)}, bf16[256,3584]{1,0:T(8,128)(2,1)S(1)}, u32[]{:S(2)}, u32[]{:S(2)}) %collective-permute-start.3) | collective-permute-done | bytes 1835040 | tf_op jit(solution)/shard_map/ppermute | solution.py:45
  162.6 2.0 pad_maximum_fusion.left_ref
  164.8 2.0 pad_maximum_fusion.1.left_ref.refs_3_
  166.8 10.5 %all-to-all-start.1 = ((bf16[16,16,7168]{2,1,0:T(8,128)(2,1)}), bf16[16,16,7168]{2,1,0:T(8,128)(2,1)}, u32[]{:S(2)}, u32[]{:S(2)}) async-start(bf16[16,16,7168]{2,1,0:T(8,128)(2,1)} %bitcast.36), calls=%async_computation.1 | async-start | bytes 7340032 | tf_op jit(solution)/shard_map/all_to_all | solution.py:34
  177.3 2.0 copy-done
  179.3 12.1 %shard_map.76.gate_a = bf16[512,2048]{1,0:T(8,128)(2,1)S(1)} custom-call(bf16[512,3584]{1,0:T(8,128)(2,1)S(1)} %copy-done, bf16[3584,2048]{1,0:T(8,128)(2,1)} %bitcast.22), custom_call_target="tpu_custom_call" | custom-call | flops 1 | bytes 1 | tf_op jit(solution)/shard_map/pallas_call | solution.py:102
  191.5 7.2 %shard_map.77.grad_a = bf16[512,1024]{1,0:T(8,128)(2,1)S(1)} custom-call(bf16[512,3584]{1,0:T(8,128)(2,1)S(1)} %copy-done.2, bf16[1024,3584]{1,0:T(8,128)(2,1)} %bitcast.28), custom_call_target="tpu_custom_call" | custom-call | flops 1 | bytes 1 | tf_op jit(solution)/shard_map/pallas_call | solution.py:102
  199.5 2.1 collective-permute-done.7.grad_b
  201.6 16.4 %shard_map.78 = (bf16[512,3584]{1,0:T(8,128)(2,1)}, bf16[512,1024]{1,0:T(8,128)(2,1)S(1)}, bf16[512,2048]{1,0:T(8,128)(2,1)S(1)}) custom-call(s32[1]{0:T(128)} %bitcast.2.keep_ref, bf16[512,2048]{1,0:T(8,128)(2,1)} %copy-done.4, bf16[512,2048]{1,0:T(8,128)(2,1)} %collective-permute-done.6.gate_b, bf16[512,1024]{1,0:T(8,128)(2,1)S(1)} %shard_map.77.grad_a, ...), custom_call_target="tpu_custom_call" | custom-call | flops 1 | bytes 1 | tf_op jit(solution)/shard_map/pallas_call | solution.py:161
  218.0 2.0 fusion.26
  220.0 1.0 pad_maximum_fusion.6
  221.0 1.1 fusion.27
  222.1 10.3 %shard_map.79.gate_a = bf16[256,2048]{1,0:T(8,128)(2,1)S(1)} custom-call(bf16[256,7168]{1,0:T(8,128)(2,1)} %bitcast.1.left_ref.refs_4_, bf16[3584,2048]{1,0:T(8,128)(2,1)} %bitcast.24), custom_call_target="tpu_custom_call" | custom-call | flops 1 | bytes 1 | tf_op jit(solution)/shard_map/pallas_call | solution.py:102
  232.4 0.2 collective-permute-start.8
  232.6 1.9 collective-permute-start.10
  234.5 1.4 collective-permute-start.11
  236.0 5.8 %shard_map.80.grad_a = bf16[256,1024]{1,0:T(8,128)(2,1)S(1)} custom-call(bf16[256,7168]{1,0:T(8,128)(2,1)} %bitcast.1.left_ref.refs_4_, bf16[1024,3584]{1,0:T(8,128)(2,1)} %bitcast.29), custom_call_target="tpu_custom_call" | custom-call | flops 1 | bytes 1 | tf_op jit(solution)/shard_map/pallas_call | solution.py:102
  241.8 2.9 slice.82
  244.7 11.4 %shard_map.81 = (bf16[256,3584]{1,0:T(8,128)(2,1)}, bf16[256,1024]{1,0:T(8,128)(2,1)S(1)}, bf16[256,2048]{1,0:T(8,128)(2,1)S(1)}) custom-call(s32[1]{0:T(128)} %constant.20.clone.1.keep_ref, bf16[256,2048]{1,0:T(8,128)(2,1)S(1)} %shard_map.79.gate_a, bf16[256,2048]{1,0:T(8,128)(2,1)S(1)} %collective-permute-done.8.gate_b, ...), custom_call_target="tpu_custom_call" | custom-call | flops 1 | bytes 1 | tf_op jit(solution)/shard_map/pallas_call | solution.py:161
  256.2 0.8 copy-done.9
  257.0 8.2 %collective-permute-done.10 = bf16[256,1792]{1,0:T(8,128)(2,1)S(1)} collective-permute-done((bf16[256,1792]{1,0:T(8,128)(2,1)S(1)}, bf16[256,1792]{1,0:T(8,128)(2,1)S(1)}, u32[]{:S(2)}, u32[]{:S(2)}) %collective-permute-start.10) | collective-permute-done | bytes 917536 | tf_op jit(solution)/shard_map/ppermute | solution.py:45
  265.2 0.9 copy-done.22
  266.2 9.2 %all-to-all-start.2 = ((bf16[16,16,3584]{2,1,0:T(8,128)(2,1)}), bf16[16,16,3584]{2,1,0:T(8,128)(2,1)}, u32[]{:S(2)}, u32[]{:S(2)}) async-start(bf16[16,16,3584]{2,1,0:T(8,128)(2,1)} %bitcast.39), calls=%async_computation.2 | async-start | bytes 3670016 | tf_op jit(solution)/shard_map/all_to_all | solution.py:34
  275.4 10.3 %shard_map.82.gate_a = bf16[256,2048]{1,0:T(8,128)(2,1)S(1)} custom-call(bf16[256,7168]{1,0:T(8,128)(2,1)} %bitcast.5.left_ref.refs_5_, bf16[3584,2048]{1,0:T(8,128)(2,1)} %bitcast.26), custom_call_target="tpu_custom_call" | custom-call | flops 1 | bytes 1 | tf_op jit(solution)/shard_map/pallas_call | solution.py:102
  285.9 5.9 %shard_map.83.grad_a = bf16[256,1024]{1,0:T(8,128)(2,1)S(1)} custom-call(bf16[256,7168]{1,0:T(8,128)(2,1)} %bitcast.5.left_ref.refs_5_, bf16[1024,3584]{1,0:T(8,128)(2,1)} %bitcast.30), custom_call_target="tpu_custom_call" | custom-call | flops 1 | bytes 1 | tf_op jit(solution)/shard_map/pallas_call | solution.py:102
  291.8 0.4 collective-permute-start.15
  292.2 0.2 add.29
  292.5 1.9 collective-permute-start.12
  294.4 1.4 add.30
  295.9 1.5 collective-permute-start.13
  297.4 11.4 %shard_map.84 = (bf16[256,3584]{1,0:T(8,128)(2,1)}, bf16[256,1024]{1,0:T(8,128)(2,1)S(1)}, bf16[256,2048]{1,0:T(8,128)(2,1)S(1)}) custom-call(s32[1]{0:T(128)} %constant.20.clone.1.keep_ref, bf16[256,2048]{1,0:T(8,128)(2,1)S(1)} %shard_map.82.gate_a, bf16[256,2048]{1,0:T(8,128)(2,1)S(1)} %collective-permute-done.14.gate_b, ...), custom_call_target="tpu_custom_call" | custom-call | flops 1 | bytes 1 | tf_op jit(solution)/shard_map/pallas_call | solution.py:161
  308.8 1.0 copy-done.7
  309.8 0.8 copy-done.11
  310.6 0.8 copy-done.24
  311.3 6.8 %collective-permute-done.13 = bf16[128,1792]{1,0:T(8,128)(2,1)} collective-permute-done((bf16[128,1792]{1,0:T(8,128)(2,1)S(1)}, bf16[128,1792]{1,0:T(8,128)(2,1)}, u32[]{:S(2)}, u32[]{:S(2)}) %collective-permute-start.13) | collective-permute-done | bytes 458784 | tf_op jit(solution)/shard_map/ppermute | solution.py:45
  318.2 7.3 %all-to-all-start.3 = ((bf16[16,16,3584]{2,1,0:T(8,128)(2,1)}), bf16[16,16,3584]{2,1,0:T(8,128)(2,1)}, u32[]{:S(2)}, u32[]{:S(2)}) async-start(bf16[16,16,3584]{2,1,0:T(8,128)(2,1)} %bitcast.38), calls=%async_computation.3 | async-start | bytes 3670016 | tf_op jit(solution)/shard_map/all_to_all | solution.py:34
  325.5 1.4 slice_add_fusion
  326.8 1.9 slice_add_fusion.1
  328.8 1.9 collective-permute-start.16
  330.7 2.8 slice.89
  333.6 20.8 %convolution_convert_fusion = bf16[3584,2048]{1,0:T(8,128)(2,1)} fusion(bf16[256,3584]{1,0:T(8,128)(2,1)} %slice.89, bf16[256,3584]{1,0:T(8,128)(2,1)S(1)} %copy-done.21, bf16[512,3584]{1,0:T(8,128)(2,1)S(1)} %copy-done.1, bf16[256,2048]{1,0:T(8,128)(2,1)S(1)} %copy-done.8, bf16[256,2048]{1,0:T(8,128)(2,1)S(1)} %get-tuple-element.63, ...), kind=kOutput, calls=%fused_computation | convolution fusion | flops 15074328576 | bytes 26214400 | tf_op jit(solution)/shard_map/dot_general | solution.py:220
  354.4 12.6 %shard_map.85 = bf16[1024,3584]{1,0:T(8,128)(2,1)} custom-call(bf16[512,1024]{1,0:T(8,128)(2,1)S(1)} %copy-done.6, bf16[256,1024]{1,0:T(8,128)(2,1)S(1)} %copy-done.10, bf16[256,1024]{1,0:T(8,128)(2,1)S(1)} %copy-done.12, bf16[512,3584]{1,0:T(8,128)(2,1)S(1)} %copy-done.3, bf16[256,7168]{1,0:T(8,128)(2,1)} %bitcast.1.left_ref.refs_4_, ...), custom_call_target="tpu_custom_call" | custom-call | flops 7516192768 | bytes 16777216 | tf_op jit(solution)/shard_map/pallas_call | solution.py:200
  367.0 0.1 collective-permute-done.16
  367.3 2.6 collective-permute-start.17
  370.0 13.8 %copy.9 = bf16[448,8,2,1024]{3,2,1,0:T(2,128)(2,1)} copy(bf16[448,8,2,1024]{3,1,2,0:T(8,128)(2,1)S(1)} %bitcast.34) | data formatting | bytes 29360128 | tf_op jit(solution)/shard_map/transpose | solution.py:325
  383.9 4.9 %convolution_convert_fusion.4 = bf16[256,3584]{1,0:T(8,128)(2,1)} fusion(bf16[256,3584]{1,0:T(8,128)(2,1)} %bitcast.12, bf16[256,3584]{1,0:T(8,128)(2,1)} %bitcast.7, bf16[32,3584]{1,0:T(8,128)(2,1)S(1)} %slice_add_fusion.2, pred[256,256]{1,0:T(32,128)(4,1)S(1)} %get-tuple-element.87, pred[256,256]{1,0:T(32,128)(4,1)S(1)} %get-tuple-element.88, ...), kind=kOutput, calls=%fused_computation.9 | convolution fusion | flops 1011138560 | bytes 5873664 | tf_op jit(solution)/shard_map/dot_general | solution.py:331
  (87 shorter events, 1.4 us)
Async XLA Ops:
  0.6 1.9 copy-start.25
  0.6 2.7 copy-start.20
  3.5 29.0 %copy-start.13 = (bf16[256,7168]{1,0:T(8,128)(2,1)}, bf16[256,7168]{1,0:T(8,128)(2,1)S(1)}, u32[]{:S(2)}) copy-start(bf16[256,7168]{1,0:T(8,128)(2,1)S(1)} %constant_dynamic-update-slice_fusion) | copy-start | bytes 11010052
  4.3 24.5 %collective-permute-start = (bf16[32,7168]{1,0:T(8,128)(2,1)S(1)}, bf16[32,7168]{1,0:T(8,128)(2,1)S(1)}, u32[]{:S(2)}, u32[]{:S(2)}) collective-permute-start(bf16[32,7168]{1,0:T(8,128)(2,1)S(1)} %convolution_convert_fusion.3), channel_id=1, source_target_pairs={{0,8},{1,9},{2,10},{3,11},{4,12},{5,13},{6,14},{7,15},{8,0},{9,1},... | collective-permute-start | bytes 1376264 | tf_op jit(solution)/shard_map/ppermute | solution.py:45
  28.8 21.6 %collective-permute-start.1 = (bf16[64,7168]{1,0:T(8,128)(2,1)S(1)}, bf16[64,7168]{1,0:T(8,128)(2,1)S(1)}, u32[]{:S(2)}, u32[]{:S(2)}) collective-permute-start(bf16[64,7168]{1,0:T(8,128)(2,1)S(1)} %pad_maximum_fusion.5), channel_id=1, source_target_pairs={{0,4},{1,5},{2,6},{3,7},{4,0},{5,1},{6,2},{7,3},{8,12},{9,13},{10,... | collective-permute-start | bytes 2752520 | tf_op jit(solution)/shard_map/ppermute | solution.py:45
  50.6 116.1 %all-to-all-start = ((bf16[16,16,7168]{2,1,0:T(8,128)(2,1)}), bf16[16,16,7168]{2,1,0:T(8,128)(2,1)}, u32[]{:S(2)}, u32[]{:S(2)}) async-start(bf16[16,16,7168]{2,1,0:T(8,128)(2,1)} %bitcast.37), calls=%async_computation | async-start | bytes 7340032 | tf_op jit(solution)/shard_map/all_to_all | solution.py:34
  58.2 53.6 %collective-permute-start.2 = (bf16[128,3584]{1,0:T(8,128)(2,1)S(1)}, bf16[128,3584]{1,0:T(8,128)(2,1)S(1)}, u32[]{:S(2)}, u32[]{:S(2)}) collective-permute-start(bf16[128,3584]{1,0:T(8,128)(2,1)S(1)} %get-tuple-element.39), channel_id=1, source_target_pairs={{0,2},{1,3},{2,0},{3,1},{4,6},{5,7},{6,4},{7,5},{8,10},{9,11},{10,... | collective-permute-start | bytes 2752520 | tf_op jit(solution)/shard_map/ppermute | solution.py:45
  60.1 53.5 %collective-permute-start.4 = (bf16[128,3584]{1,0:T(8,128)(2,1)S(1)}, bf16[128,3584]{1,0:T(8,128)(2,1)S(1)}, u32[]{:S(2)}, u32[]{:S(2)}) collective-permute-start(bf16[128,3584]{1,0:T(8,128)(2,1)S(1)} %get-tuple-element.40), channel_id=1, source_target_pairs={{0,1},{1,0},{2,3},{3,2},{4,5},{5,4},{6,7},{7,6},{8,9},{9,8},{10,11... | collective-permute-start | bytes 2752520 | tf_op jit(solution)/shard_map/ppermute | solution.py:45
  111.9 50.7 %collective-permute-start.3 = (bf16[256,3584]{1,0:T(8,128)(2,1)S(1)}, bf16[256,3584]{1,0:T(8,128)(2,1)S(1)}, u32[]{:S(2)}, u32[]{:S(2)}) collective-permute-start(bf16[256,3584]{1,0:T(8,128)(2,1)S(1)} %pad_maximum_fusion.3), channel_id=1, source_target_pairs={{0,1},{1,0},{2,3},{3,2},{4,5},{5,4},{6,7},{7,6},{8,9},{9,8},{10,11... | collective-permute-start | bytes 5505032 | tf_op jit(solution)/shard_map/ppermute | solution.py:45
  113.7 50.9 %collective-permute-start.5 = (bf16[256,3584]{1,0:T(8,128)(2,1)S(1)}, bf16[256,3584]{1,0:T(8,128)(2,1)S(1)}, u32[]{:S(2)}, u32[]{:S(2)}) collective-permute-start(bf16[256,3584]{1,0:T(8,128)(2,1)S(1)} %pad_maximum_fusion.4), channel_id=1, source_target_pairs={{0,2},{1,3},{2,0},{3,1},{4,6},{5,7},{6,4},{7,5},{8,10},{9,11},{10,... | collective-permute-start | bytes 5505032 | tf_op jit(solution)/shard_map/ppermute | solution.py:45
  116.3 16.2 %copy-start.14 = (bf16[256,7168]{1,0:T(8,128)(2,1)S(1)}, bf16[256,7168]{1,0:T(8,128)(2,1)}, u32[]{:S(2)}) copy-start(bf16[256,7168]{1,0:T(8,128)(2,1)} %copy-done.13) | copy-start | bytes 11010052
  166.8 99.4 %all-to-all-start.1 = ((bf16[16,16,7168]{2,1,0:T(8,128)(2,1)}), bf16[16,16,7168]{2,1,0:T(8,128)(2,1)}, u32[]{:S(2)}, u32[]{:S(2)}) async-start(bf16[16,16,7168]{2,1,0:T(8,128)(2,1)} %bitcast.36), calls=%async_computation.1 | async-start | bytes 7340032 | tf_op jit(solution)/shard_map/all_to_all | solution.py:34
  177.3 2.0 copy-start
  179.3 12.2 %copy-start.2 = (bf16[512,3584]{1,0:T(8,128)(2,1)S(1)}, bf16[512,3584]{1,0:T(8,128)(2,1)}, u32[]{:S(2)}) copy-start(bf16[512,3584]{1,0:T(8,128)(2,1)} %pad_maximum_fusion.1.left_ref.refs_3_) | copy-start | bytes 11010052
  191.4 7.4 %copy-start.4 = (bf16[512,2048]{1,0:T(8,128)(2,1)}, bf16[512,2048]{1,0:T(8,128)(2,1)S(1)}, u32[]{:S(2)}) copy-start(bf16[512,2048]{1,0:T(8,128)(2,1)S(1)} %shard_map.76.gate_a) | copy-start | bytes 6291460
  191.4 10.2 %collective-permute-start.6 = (bf16[512,2048]{1,0:T(8,128)(2,1)S(1)}, bf16[512,2048]{1,0:T(8,128)(2,1)}, u32[]{:S(2)}, u32[]{:S(2)}) collective-permute-start(bf16[512,2048]{1,0:T(8,128)(2,1)S(1)} %shard_map.76.gate_a), channel_id=1, source_target_pairs={{0,16},{16,0},{1,17},{17,1},{2,18},{18,2},{3,19},{19,3},{4,20},{20... | collective-permute-start | bytes 6291464 | tf_op jit(solution)/shard_map/ppermute | solution.py:115
  198.8 2.9 collective-permute-start.7
  218.0 3.0 copy-start.5
  218.0 3.0 copy-start.15
  232.4 12.3 %collective-permute-start.8 = (bf16[256,2048]{1,0:T(8,128)(2,1)S(1)}, bf16[256,2048]{1,0:T(8,128)(2,1)S(1)}, u32[]{:S(2)}, u32[]{:S(2)}) collective-permute-start(bf16[256,2048]{1,0:T(8,128)(2,1)S(1)} %shard_map.79.gate_a), channel_id=1, source_target_pairs={{0,16},{16,0},{1,17},{17,1},{2,18},{18,2},{3,19},{19,3},{4,20},{20... | collective-permute-start | bytes 3145736 | tf_op jit(solution)/shard_map/ppermute | solution.py:115
  232.6 32.6 %collective-permute-start.10 = (bf16[256,1792]{1,0:T(8,128)(2,1)S(1)}, bf16[256,1792]{1,0:T(8,128)(2,1)S(1)}, u32[]{:S(2)}, u32[]{:S(2)}) collective-permute-start(bf16[256,1792]{1,0:T(8,128)(2,1)S(1)} %get-tuple-element.50), channel_id=1, source_target_pairs={{0,1},{1,0},{2,3},{3,2},{4,5},{5,4},{6,7},{7,6},{8,9},{9,8},{10,11... | collective-permute-start | bytes 2752520 | tf_op jit(solution)/shard_map/ppermute | solution.py:45
  234.5 31.6 %collective-permute-start.11 = (bf16[256,1792]{1,0:T(8,128)(2,1)S(1)}, bf16[256,1792]{1,0:T(8,128)(2,1)}, u32[]{:S(2)}, u32[]{:S(2)}) collective-permute-start(bf16[256,1792]{1,0:T(8,128)(2,1)S(1)} %get-tuple-element.51), channel_id=1, source_target_pairs={{0,2},{1,3},{2,0},{3,1},{4,6},{5,7},{6,4},{7,5},{8,10},{9,11},{10,... | collective-permute-start | bytes 2752520 | tf_op jit(solution)/shard_map/ppermute | solution.py:45
  241.8 3.0 collective-permute-start.9
  256.2 0.8 copy-start.9
  265.2 0.9 copy-start.22
  266.2 52.0 %all-to-all-start.2 = ((bf16[16,16,3584]{2,1,0:T(8,128)(2,1)}), bf16[16,16,3584]{2,1,0:T(8,128)(2,1)}, u32[]{:S(2)}, u32[]{:S(2)}) async-start(bf16[16,16,3584]{2,1,0:T(8,128)(2,1)} %bitcast.39), calls=%async_computation.2 | async-start | bytes 3670016 | tf_op jit(solution)/shard_map/all_to_all | solution.py:34
  285.8 6.5 %copy-start.17 = (bf16[256,1792]{1,0:T(8,128)(2,1)S(1)}, bf16[256,1792]{1,0:T(8,128)(2,1)}, u32[]{:S(2)}) copy-start(bf16[256,1792]{1,0:T(8,128)(2,1)} %get-tuple-element.46) | copy-start | bytes 2752516
  285.8 6.4 %copy-start.23 = (bf16[256,1792]{1,0:T(8,128)(2,1)S(1)}, bf16[256,1792]{1,0:T(8,128)(2,1)}, u32[]{:S(2)}) copy-start(bf16[256,1792]{1,0:T(8,128)(2,1)} %copy-done.22) | copy-start | bytes 2752516
  285.8 11.6 %collective-permute-start.14 = (bf16[256,2048]{1,0:T(8,128)(2,1)S(1)}, bf16[256,2048]{1,0:T(8,128)(2,1)S(1)}, u32[]{:S(2)}, u32[]{:S(2)}) collective-permute-start(bf16[256,2048]{1,0:T(8,128)(2,1)S(1)} %shard_map.82.gate_a), channel_id=1, source_target_pairs={{0,16},{16,0},{1,17},{17,1},{2,18},{18,2},{3,19},{19,3},{4,20},{20... | collective-permute-start | bytes 3145736 | tf_op jit(solution)/shard_map/ppermute | solution.py:115
  291.8 2.7 copy-start.16
  291.8 5.6 %collective-permute-start.15 = (bf16[256,1024]{1,0:T(8,128)(2,1)S(1)}, bf16[256,1024]{1,0:T(8,128)(2,1)S(1)}, u32[]{:S(2)}, u32[]{:S(2)}) collective-permute-start(bf16[256,1024]{1,0:T(8,128)(2,1)S(1)} %shard_map.83.grad_a), channel_id=1, source_target_pairs={{0,16},{16,0},{1,17},{17,1},{2,18},{18,2},{3,19},{19,3},{4,20},{20... | collective-permute-start | bytes 1572872 | tf_op jit(solution)/shard_map/ppermute | solution.py:115
  292.4 5.0 %copy-start.18 = (bf16[256,1792]{1,0:T(8,128)(2,1)}, bf16[256,1792]{1,0:T(8,128)(2,1)S(1)}, u32[]{:S(2)}) copy-start(bf16[256,1792]{1,0:T(8,128)(2,1)S(1)} %add.29) | copy-start | bytes 2752516
  292.5 18.1 %collective-permute-start.12 = (bf16[128,1792]{1,0:T(8,128)(2,1)S(1)}, bf16[128,1792]{1,0:T(8,128)(2,1)S(1)}, u32[]{:S(2)}, u32[]{:S(2)}) collective-permute-start(bf16[128,1792]{1,0:T(8,128)(2,1)S(1)} %slice.97), channel_id=1, source_target_pairs={{0,2},{1,3},{2,0},{3,1},{4,6},{5,7},{6,4},{7,5},{8,10},{9,11},{10,... | collective-permute-start | bytes 1376264 | tf_op jit(solution)/shard_map/ppermute | solution.py:45
  295.8 13.0 %copy-start.19 = (bf16[256,1792]{1,0:T(8,128)(2,1)}, bf16[256,1792]{1,0:T(8,128)(2,1)S(1)}, u32[]{:S(2)}) copy-start(bf16[256,1792]{1,0:T(8,128)(2,1)S(1)} %add.30) | copy-start | bytes 2752516
  295.9 22.3 %collective-permute-start.13 = (bf16[128,1792]{1,0:T(8,128)(2,1)S(1)}, bf16[128,1792]{1,0:T(8,128)(2,1)}, u32[]{:S(2)}, u32[]{:S(2)}) collective-permute-start(bf16[128,1792]{1,0:T(8,128)(2,1)S(1)} %slice.98), channel_id=1, source_target_pairs={{0,1},{1,0},{2,3},{3,2},{4,5},{5,4},{6,7},{7,6},{8,9},{9,8},{10,11... | collective-permute-start | bytes 1376264 | tf_op jit(solution)/shard_map/ppermute | solution.py:45
  308.8 1.0 copy-start.7
  309.8 0.8 copy-start.11
  310.6 0.8 copy-start.24
  318.2 65.7 %all-to-all-start.3 = ((bf16[16,16,3584]{2,1,0:T(8,128)(2,1)}), bf16[16,16,3584]{2,1,0:T(8,128)(2,1)}, u32[]{:S(2)}, u32[]{:S(2)}) async-start(bf16[16,16,3584]{2,1,0:T(8,128)(2,1)} %bitcast.38), calls=%async_computation.3 | async-start | bytes 3670016 | tf_op jit(solution)/shard_map/all_to_all | solution.py:34
  325.5 8.1 %copy-start.1 = (bf16[512,3584]{1,0:T(8,128)(2,1)S(1)}, bf16[512,3584]{1,0:T(8,128)(2,1)}, u32[]{:S(2)}) copy-start(bf16[512,3584]{1,0:T(8,128)(2,1)} %pad_maximum_fusion.left_ref) | copy-start | bytes 11010052
  325.5 8.1 %copy-start.8 = (bf16[256,2048]{1,0:T(8,128)(2,1)S(1)}, bf16[256,2048]{1,0:T(8,128)(2,1)}, u32[]{:S(2)}) copy-start(bf16[256,2048]{1,0:T(8,128)(2,1)} %copy-done.7) | copy-start | bytes 3145732
  325.5 8.1 %copy-start.21 = (bf16[256,3584]{1,0:T(8,128)(2,1)S(1)}, bf16[256,3584]{1,0:T(8,128)(2,1)}, u32[]{:S(2)}) copy-start(bf16[256,3584]{1,0:T(8,128)(2,1)} %slice.82) | copy-start | bytes 5505028
  328.8 38.4 %collective-permute-start.16 = (bf16[64,3584]{1,0:T(8,128)(2,1)S(1)}, bf16[64,3584]{1,0:T(8,128)(2,1)S(1)}, u32[]{:S(2)}, u32[]{:S(2)}) collective-permute-start(bf16[64,3584]{1,0:T(8,128)(2,1)S(1)} %pad_maximum_fusion.8), channel_id=1, source_target_pairs={{0,4},{1,5},{2,6},{3,7},{4,0},{5,1},{6,2},{7,3},{8,12},{9,13},{10,... | collective-permute-start | bytes 1376264 | tf_op jit(solution)/shard_map/ppermute | solution.py:45
  333.6 20.8 %copy-start.3 = (bf16[512,3584]{1,0:T(8,128)(2,1)S(1)}, bf16[512,3584]{1,0:T(8,128)(2,1)}, u32[]{:S(2)}) copy-start(bf16[512,3584]{1,0:T(8,128)(2,1)} %pad_maximum_fusion.1.left_ref.refs_3_) | copy-start | bytes 11010052
  333.6 20.8 %copy-start.6 = (bf16[512,1024]{1,0:T(8,128)(2,1)S(1)}, bf16[512,1024]{1,0:T(8,128)(2,1)}, u32[]{:S(2)}) copy-start(bf16[512,1024]{1,0:T(8,128)(2,1)} %copy-done.5) | copy-start | bytes 3145732
  333.6 20.8 %copy-start.10 = (bf16[256,1024]{1,0:T(8,128)(2,1)S(1)}, bf16[256,1024]{1,0:T(8,128)(2,1)}, u32[]{:S(2)}) copy-start(bf16[256,1024]{1,0:T(8,128)(2,1)} %copy-done.9) | copy-start | bytes 1572868
  333.6 20.8 %copy-start.12 = (bf16[256,1024]{1,0:T(8,128)(2,1)S(1)}, bf16[256,1024]{1,0:T(8,128)(2,1)}, u32[]{:S(2)}) copy-start(bf16[256,1024]{1,0:T(8,128)(2,1)} %copy-done.11) | copy-start | bytes 1572868
  354.4 15.6 %slice-start = ((s8[14680064]{0:T(1024)(128)(4,1)}), s8[4194304]{0:T(1024)(128)(4,1)S(1)}, s32[]{:S(2)}) async-start(s8[14680064]{0:T(1024)(128)(4,1)} %bitcast.32), calls=%async_computation.4 | async-start | bytes 8388608
  354.4 15.6 %slice-start.1 = ((s8[14680064]{0:T(1024)(128)(4,1)}), s8[4194304]{0:T(1024)(128)(4,1)S(1)}, s32[]{:S(2)}) async-start(s8[14680064]{0:T(1024)(128)(4,1)} %bitcast.32), calls=%async_computation.5 | async-start | bytes 8388608
  354.4 15.6 %slice-start.2 = ((s8[14680064]{0:T(1024)(128)(4,1)}), s8[4194304]{0:T(1024)(128)(4,1)S(1)}, s32[]{:S(2)}) async-start(s8[14680064]{0:T(1024)(128)(4,1)} %bitcast.32), calls=%async_computation.6 | async-start | bytes 8388608
  354.4 15.6 %slice-start.3 = ((s8[14680064]{0:T(1024)(128)(4,1)}), s8[2097152]{0:T(1024)(128)(4,1)S(1)}, s32[]{:S(2)}) async-start(s8[14680064]{0:T(1024)(128)(4,1)} %bitcast.32), calls=%async_computation.7 | async-start | bytes 4194304
  367.3 16.5 %collective-permute-start.17 = (bf16[32,3584]{1,0:T(8,128)(2,1)S(1)}, bf16[32,3584]{1,0:T(8,128)(2,1)S(1)}, u32[]{:S(2)}, u32[]{:S(2)}) collective-permute-start(bf16[32,3584]{1,0:T(8,128)(2,1)S(1)} %slice.91), channel_id=1, source_target_pairs={{0,8},{1,9},{2,10},{3,11},{4,12},{5,13},{6,14},{7,15},{8,0},{9,1},... | collective-permute-start | bytes 688136 | tf_op jit(solution)/shard_map/ppermute | solution.py:45

commit v10 on v9

--- a/solution.py
+++ b/solution.py
@@ -87,24 +87,36 @@
     )
 
 
-def product_kernel(right_dim, left_ref, right_ref, out_ref):
-    out_ref[...] = dot_f32(left_ref[...], right_ref[...], 1, right_dim).astype(out_ref.dtype)
-
-
-def product(left, column_block, depth, right, transposed):
+def product_kernel(right_dim, steps, left_ref, right_ref, *out_refs):
+    for piece, out_ref in enumerate(out_refs):
+
+        @pl.when(pl.program_id(0) // steps == piece)
+        def _():
+            out_ref[...] = dot_f32(left_ref[...], right_ref[...], 1, right_dim).astype(
+                out_ref.dtype
+            )
+
+
+def product(left, column_block, depth, right, transposed, pieces):
     height = left.shape[0]
     width = right.shape[0] if transposed else right.shape[1]
-    step = block_of(width, 256)
+    share = width // pieces
+    step = block_of(share, 256)
+    steps = share // step
     if transposed:
         right_spec = pl.BlockSpec((step, depth), lambda j: (j, 0))
     else:
         right_spec = pl.BlockSpec((depth, step), lambda j: (0, j))
+
+    def place_of(piece):
+        return lambda j: (0, jnp.clip(j - piece * steps, 0, steps - 1))
+
     return pl.pallas_call(
-        functools.partial(product_kernel, 1 if transposed else 0),
+        functools.partial(product_kernel, 1 if transposed else 0, steps),
         grid=(width // step,),
         in_specs=[pl.BlockSpec((height, depth), lambda j: (0, column_block)), right_spec],
-        out_specs=pl.BlockSpec((height, step), lambda j: (0, j)),
-        out_shape=jax.ShapeDtypeStruct((height, width), jnp.bfloat16),
+        out_specs=[pl.BlockSpec((height, step), place_of(piece)) for piece in range(pieces)],
+        out_shape=[jax.ShapeDtypeStruct((height, share), jnp.bfloat16)] * pieces,
         compiler_params=pltpu.CompilerParams(vmem_limit_bytes=VMEM_BYTES),
         cost_estimate=SMALL_COST,
     )(left, right)
@@ -117,7 +129,17 @@
 
 
 def finish_kernel(
-    keep_ref, gate_a, gate_b, grad_a, grad_b, matrix_ref, out_ref, hidden_ref, branch_ref
+    keep_ref,
+    gate_a,
+    gate_b,
+    up_a,
+    up_b,
+    grad_a,
+    grad_b,
+    matrix_ref,
+    out_ref,
+    hidden_ref,
+    branch_ref,
 ):
     height, width = hidden_ref.shape
 
@@ -130,14 +152,12 @@
         def _(i):
             here = pl.ds(pl.multiple_of(i * step, step), step)
 
-            def total(one, two, columns):
-                return one[here, columns].astype(jnp.float32) + two[here, columns].astype(
-                    jnp.float32
-                )
-
-            gate_value = total(gate_a, gate_b, pl.ds(0, width))
-            upward = total(gate_a, gate_b, pl.ds(width, width))
-            hidden_grads = total(grad_a, grad_b, pl.ds(0, width))
+            def total(one, two):
+                return one[here, :].astype(jnp.float32) + two[here, :].astype(jnp.float32)
+
+            gate_value = total(gate_a, gate_b)
+            upward = total(up_a, up_b)
+            hidden_grads = total(grad_a, grad_b)
             sigmoid_value = jax.nn.sigmoid(gate_value)
             activated = gate_value * sigmoid_value
             gate_slope = sigmoid_value * (1.0 + gate_value * (1.0 - sigmoid_value))
@@ -152,7 +172,7 @@
     out_ref[...] = dot_f32(branch_ref[...], matrix_ref[...], 1, 1).astype(out_ref.dtype)
 
 
-def finish(keep, gate_pair, grad_pair, matrix):
+def finish(keep, gate_pair, up_pair, grad_pair, matrix):
     height, width = grad_pair[0].shape
     features = matrix.shape[0]
     step = block_of(features, 512)
@@ -163,10 +183,9 @@
         grid=(features // step,),
         in_specs=[
             pl.BlockSpec(memory_space=pltpu.SMEM),
-            whole(2 * width),
-            whole(2 * width),
-            whole(width),
-            whole(width),
+        ]
+        + [whole(width)] * 6
+        + [
             pl.BlockSpec((step, 2 * width), lambda j: (j, 0)),
         ],
         out_specs=[
@@ -177,7 +196,7 @@
         out_shape=[shape(features), shape(width), shape(2 * width)],
         compiler_params=pltpu.CompilerParams(vmem_limit_bytes=VMEM_BYTES),
         cost_estimate=SMALL_COST,
-    )(keep, *gate_pair, *grad_pair, matrix)
+    )(keep, *gate_pair, *up_pair, *grad_pair, matrix)
 
 
 def outer_kernel(count, *refs):
@@ -248,9 +267,9 @@
         return both_in[:, :feature_share], both_in[:, feature_share:]
 
     def products(rows_in, rows_block, grads_in, grads_block):
-        gate_part = product(rows_in, rows_block, feature_share, gate_up_matrix, False)
-        grad_part = product(grads_in, grads_block, feature_share, down_matrix, True)
-        return pair_over_grp(gate_part), pair_over_grp(grad_part)
+        parts = product(rows_in, rows_block, feature_share, gate_up_matrix, False, 2)
+        parts += product(grads_in, grads_block, feature_share, down_matrix, True, 1)
+        return [pair_over_grp(part) for part in parts]
 
     always = jnp.ones((1,), jnp.int32)
     only_busiest = is_busiest.astype(jnp.int32).reshape(1)

time: 390 us -> 389 us (level)
  starting transfers between devices: 59.3 us -> 65.1 us
  local copies, waits for them, and re-layouts: 47.6 us -> 43.6 us
    all_to_all x4, starting transfers between devices: 34.6 us -> 39.1 us  [exchange(): lax.all_to_all(rows.reshape(expert_count, slots // expert_count, width),...]
    unnamed x62 -> x46, local copies, waits for them, and re-layouts: 24.5 us -> 22.7 us
  transfers between devices with their start and end apart: 22 -> 25, of which waited for: 8 -> 9; matrix products, arithmetic and copies ran while one was open for 20% -> 19% of each run, Pallas kernels for 27% -> 27%
where the time goes in v10:
time: 389 us; the launch traced here: 387 us
  waiting for transfers between devices  132 us (34%)
  Pallas kernels  103 us (26%)
  starting transfers between devices  65.1 us (17%)
  local copies, waits for them, and re-layouts  43.6 us (11%)
  matrix products  31.4 us (8%)
  other arithmetic  10.3 us (3%)
    ppermute x12, waiting for transfers between devices, swap_with(): return lax.ppermute(rows, 'exp', [(i, i ^ mask) for i in range(total)])  130 us
    pallas_call x6, Pallas kernels, product(): pl.pallas_call(functools.partial(product_kernel, 1 if transposed else 0,...  51.3 us
    pallas_call x3, Pallas kernels, finish(): pl.pallas_call(finish_kernel, grid=(features // step,), in_specs=[pl.Bloc...  39.2 us
    all_to_all x4, starting transfers between devices, exchange(): lax.all_to_all(rows.reshape(expert_count, slots // expert_count, width),...  39.1 us
    ppermute x12, starting transfers between devices, swap_with(): return lax.ppermute(rows, 'exp', [(i, i ^ mask) for i in range(total)])  23.8 us
    unnamed x46, local copies, waits for them, and re-layouts  22.7 us
    dot_general x1, matrix products, outer(): lax.dot_general(left, right, (((0,), (0,)), ((), ())), preferred_element_...  19.8 us
    transpose x1, local copies, waits for them, and re-layouts, local(): gate_up_grads.transpose(0, 2, 1, 3)  13.8 us
  transfers between devices with their start and end apart: 25, of which 9 were waited for; matrix products, arithmetic and copies ran while one was open for 19% of the time, Pallas kernels for 27%

profile of v10, /device:TPU:0, one launch (start us, length us, event | category | flops | bytes accessed | tf_op | source)
XLA Modules:
  0.0 387.1 jit_solution(8558542473063366733)
XLA Ops:
  0.7 1.8 constant_dynamic-update-slice_fusion.1
  2.5 0.2 convert_reduce_fusion
  2.7 0.7 select_reduce_fusion
  3.4 0.2 constant_dynamic-update-slice_fusion
  3.6 0.7 convolution_convert_fusion.3
  4.3 4.1 %collective-permute-start = (bf16[32,7168]{1,0:T(8,128)(2,1)S(1)}, bf16[32,7168]{1,0:T(8,128)(2,1)S(1)}, u32[]{:S(2)}, u32[]{:S(2)}) collective-permute-start(bf16[32,7168]{1,0:T(8,128)(2,1)S(1)} %convolution_convert_fusion.3), channel_id=1, source_target_pairs={{0,8},{1,9},{2,10},{3,11},{4,12},{5,13},{6,14},{7,15},{8,0},{9,1},... | collective-permute-start | bytes 1376264 | tf_op jit(solution)/shard_map/ppermute | solution.py:45
  8.4 20.3 %collective-permute-done = bf16[32,7168]{1,0:T(8,128)(2,1)S(1)} collective-permute-done((bf16[32,7168]{1,0:T(8,128)(2,1)S(1)}, bf16[32,7168]{1,0:T(8,128)(2,1)S(1)}, u32[]{:S(2)}, u32[]{:S(2)}) %collective-permute-start) | collective-permute-done | bytes 458784 | tf_op jit(solution)/shard_map/ppermute | solution.py:45
  28.8 0.8 collective-permute-start.1
  29.6 3.0 convolution_convert_fusion.2
  32.6 17.8 %collective-permute-done.1 = bf16[64,7168]{1,0:T(8,128)(2,1)S(1)} collective-permute-done((bf16[64,7168]{1,0:T(8,128)(2,1)S(1)}, bf16[64,7168]{1,0:T(8,128)(2,1)S(1)}, u32[]{:S(2)}, u32[]{:S(2)}) %collective-permute-start.1) | collective-permute-done | bytes 917536 | tf_op jit(solution)/shard_map/ppermute | solution.py:45
  50.7 7.6 %all-to-all-start = ((bf16[16,16,7168]{2,1,0:T(8,128)(2,1)}), bf16[16,16,7168]{2,1,0:T(8,128)(2,1)}, u32[]{:S(2)}, u32[]{:S(2)}) async-start(bf16[16,16,7168]{2,1,0:T(8,128)(2,1)} %bitcast.37), calls=%async_computation | async-start | bytes 7340032 | tf_op jit(solution)/shard_map/all_to_all | solution.py:34
  58.3 1.9 collective-permute-start.2
  60.1 1.5 collective-permute-start.4
  61.6 50.2 %collective-permute-done.2 = bf16[128,3584]{1,0:T(8,128)(2,1)S(1)} collective-permute-done((bf16[128,3584]{1,0:T(8,128)(2,1)S(1)}, bf16[128,3584]{1,0:T(8,128)(2,1)S(1)}, u32[]{:S(2)}, u32[]{:S(2)}) %collective-permute-start.2) | collective-permute-done | bytes 917536 | tf_op jit(solution)/shard_map/ppermute | solution.py:45
  111.9 1.7 collective-permute-start.3
  113.7 2.5 collective-permute-start.5
  116.3 16.2 %copy.10 = bf16[448,8,2,1024]{3,1,2,0:T(8,128)(2,1)} copy(bf16[448,8,2,1024]{3,2,1,0:T(2,128)(2,1)} %bitcast.31) | data formatting | bytes 29360128
  132.5 3.0 convolution_convert_fusion.1
  135.5 27.2 %collective-permute-done.3 = bf16[256,3584]{1,0:T(8,128)(2,1)S(1)} collective-permute-done((bf16[256,3584]{1,0:T(8,128)(2,1)S(1)}, bf16[256,3584]{1,0:T(8,128)(2,1)S(1)}, u32[]{:S(2)}, u32[]{:S(2)}) %collective-permute-start.3) | collective-permute-done | bytes 1835040 | tf_op jit(solution)/shard_map/ppermute | solution.py:45
  162.7 2.0 pad_maximum_fusion.left_ref
  164.8 2.0 pad_maximum_fusion.1.left_ref.refs_3_
  166.8 10.5 %all-to-all-start.1 = ((bf16[16,16,7168]{2,1,0:T(8,128)(2,1)}), bf16[16,16,7168]{2,1,0:T(8,128)(2,1)}, u32[]{:S(2)}, u32[]{:S(2)}) async-start(bf16[16,16,7168]{2,1,0:T(8,128)(2,1)} %bitcast.36), calls=%async_computation.1 | async-start | bytes 7340032 | tf_op jit(solution)/shard_map/all_to_all | solution.py:34
  177.4 2.0 copy-done.2
  179.4 12.2 %shard_map.76 = (bf16[512,1024]{1,0:T(8,128)(2,1)S(1)}, bf16[512,1024]{1,0:T(8,128)(2,1)S(1)}) custom-call(bf16[512,3584]{1,0:T(8,128)(2,1)S(1)} %copy-done.2, bf16[3584,2048]{1,0:T(8,128)(2,1)} %bitcast.22), custom_call_target="tpu_custom_call" | custom-call | flops 1 | bytes 1 | tf_op jit(solution)/shard_map/pallas_call | solution.py:114
  191.7 0.5 collective-permute-start.7
  192.2 6.7 %shard_map.77.grad_a = bf16[512,1024]{1,0:T(8,128)(2,1)S(1)} custom-call(bf16[512,3584]{1,0:T(8,128)(2,1)S(1)} %copy-done, bf16[1024,3584]{1,0:T(8,128)(2,1)} %bitcast.28), custom_call_target="tpu_custom_call" | custom-call | flops 1 | bytes 1 | tf_op jit(solution)/shard_map/pallas_call | solution.py:114
  199.7 2.1 collective-permute-done.8.grad_b
  201.7 16.4 %shard_map.78 = (bf16[512,3584]{1,0:T(8,128)(2,1)}, bf16[512,1024]{1,0:T(8,128)(2,1)S(1)}, bf16[512,2048]{1,0:T(8,128)(2,1)}) custom-call(s32[1]{0:T(128)} %bitcast.2.keep_ref, bf16[512,1024]{1,0:T(8,128)(2,1)S(1)} %get-tuple-element.50.gate_a, bf16[512,1024]{1,0:T(8,128)(2,1)} %collective-permute-done.6.gate_b, ...), custom_call_target="tpu_custom_call" | custom-call | flops 1 | bytes 1 | tf_op jit(solution)/shard_map/pallas_call | solution.py:181
  218.2 2.0 fusion.26
  220.3 0.8 copy-done.9
  221.3 1.9 collective-permute-start.12
  223.2 1.5 collective-permute-start.13
  224.7 10.4 %shard_map.79 = (bf16[256,1024]{1,0:T(8,128)(2,1)S(1)}, bf16[256,1024]{1,0:T(8,128)(2,1)S(1)}) custom-call(bf16[256,7168]{1,0:T(8,128)(2,1)} %bitcast.1.left_ref.refs_4_, bf16[3584,2048]{1,0:T(8,128)(2,1)} %bitcast.24), custom_call_target="tpu_custom_call" | custom-call | flops 1 | bytes 1 | tf_op jit(solution)/shard_map/pallas_call | solution.py:114
  235.2 0.5 collective-permute-start.10
  235.7 5.8 %shard_map.80.grad_a = bf16[256,1024]{1,0:T(8,128)(2,1)S(1)} custom-call(bf16[256,7168]{1,0:T(8,128)(2,1)} %bitcast.1.left_ref.refs_4_, bf16[1024,3584]{1,0:T(8,128)(2,1)} %bitcast.29), custom_call_target="tpu_custom_call" | custom-call | flops 1 | bytes 1 | tf_op jit(solution)/shard_map/pallas_call | solution.py:114
  241.5 0.2 collective-permute-start.11
  241.6 2.9 slice.82
  244.5 11.4 %shard_map.81 = (bf16[256,3584]{1,0:T(8,128)(2,1)}, bf16[256,1024]{1,0:T(8,128)(2,1)S(1)}, bf16[256,2048]{1,0:T(8,128)(2,1)S(1)}) custom-call(s32[1]{0:T(128)} %constant.20.clone.1.keep_ref, bf16[256,1024]{1,0:T(8,128)(2,1)S(1)} %get-tuple-element.57.gate_a, bf16[256,1024]{1,0:T(8,128)(2,1)S(1)} %collective-permute-done.9.gate_b, ...), custom_call_target="tpu_custom_call" | custom-call | flops 1 | bytes 1 | tf_op jit(solution)/shard_map/pallas_call | solution.py:181
  255.9 3.3 collective-permute-done.12
  259.2 0.9 copy-done.14
  260.2 13.6 %all-to-all-start.2 = ((bf16[16,16,3584]{2,1,0:T(8,128)(2,1)}), bf16[16,16,3584]{2,1,0:T(8,128)(2,1)}, u32[]{:S(2)}, u32[]{:S(2)}) async-start(bf16[16,16,3584]{2,1,0:T(8,128)(2,1)} %bitcast.38), calls=%async_computation.2 | async-start | bytes 3670016 | tf_op jit(solution)/shard_map/all_to_all | solution.py:34
  273.8 10.4 %shard_map.82 = (bf16[256,1024]{1,0:T(8,128)(2,1)S(1)}, bf16[256,1024]{1,0:T(8,128)(2,1)S(1)}) custom-call(bf16[256,7168]{1,0:T(8,128)(2,1)} %bitcast.5.left_ref.refs_5_, bf16[3584,2048]{1,0:T(8,128)(2,1)} %bitcast.26), custom_call_target="tpu_custom_call" | custom-call | flops 1 | bytes 1 | tf_op jit(solution)/shard_map/pallas_call | solution.py:114
  284.4 0.5 collective-permute-start.17
  284.9 5.8 %shard_map.83.grad_a = bf16[256,1024]{1,0:T(8,128)(2,1)S(1)} custom-call(bf16[256,7168]{1,0:T(8,128)(2,1)} %bitcast.5.left_ref.refs_5_, bf16[1024,3584]{1,0:T(8,128)(2,1)} %bitcast.30), custom_call_target="tpu_custom_call" | custom-call | flops 1 | bytes 1 | tf_op jit(solution)/shard_map/pallas_call | solution.py:114
  290.7 0.2 collective-permute-start.18
  290.9 0.2 add.29
  291.2 1.9 collective-permute-start.14
  293.1 1.4 add.30
  294.5 1.5 collective-permute-start.15
  296.1 11.4 %shard_map.84 = (bf16[256,3584]{1,0:T(8,128)(2,1)}, bf16[256,1024]{1,0:T(8,128)(2,1)S(1)}, bf16[256,2048]{1,0:T(8,128)(2,1)S(1)}) custom-call(s32[1]{0:T(128)} %constant.20.clone.1.keep_ref, bf16[256,1024]{1,0:T(8,128)(2,1)S(1)} %get-tuple-element.67.gate_a, bf16[256,1024]{1,0:T(8,128)(2,1)S(1)} %collective-permute-done.16.gate_b, ...), custom_call_target="tpu_custom_call" | custom-call | flops 1 | bytes 1 | tf_op jit(solution)/shard_map/pallas_call | solution.py:181
  307.5 0.6 collective-permute-done.14
  308.1 0.8 copy-done.16
  308.9 7.7 %collective-permute-done.15 = bf16[128,1792]{1,0:T(8,128)(2,1)} collective-permute-done((bf16[128,1792]{1,0:T(8,128)(2,1)S(1)}, bf16[128,1792]{1,0:T(8,128)(2,1)}, u32[]{:S(2)}, u32[]{:S(2)}) %collective-permute-start.15) | collective-permute-done | bytes 458784 | tf_op jit(solution)/shard_map/ppermute | solution.py:45
  316.6 7.3 %all-to-all-start.3 = ((bf16[16,16,3584]{2,1,0:T(8,128)(2,1)}), bf16[16,16,3584]{2,1,0:T(8,128)(2,1)}, u32[]{:S(2)}, u32[]{:S(2)}) async-start(bf16[16,16,3584]{2,1,0:T(8,128)(2,1)} %bitcast.39), calls=%async_computation.3 | async-start | bytes 3670016 | tf_op jit(solution)/shard_map/all_to_all | solution.py:34
  323.9 1.4 slice_add_fusion
  325.2 1.7 slice_add_fusion.1
  327.0 1.9 collective-permute-start.19
  329.0 1.6 slice.89
  330.6 19.8 %convolution_convert_fusion = bf16[3584,2048]{1,0:T(8,128)(2,1)} fusion(bf16[256,3584]{1,0:T(8,128)(2,1)S(1)} %slice.89, bf16[256,3584]{1,0:T(8,128)(2,1)S(1)} %copy-done.13, bf16[512,3584]{1,0:T(8,128)(2,1)S(1)} %copy-done.3, bf16[256,2048]{1,0:T(8,128)(2,1)S(1)} %get-tuple-element.76, bf16[256,2048]{1,0:T(8,128)(2,1)S(1)} %get-tuple-element.75, ...), kind=kOutput, calls=%fused_computation | convolution fusion | flops 15074328576 | bytes 26214400 | tf_op jit(solution)/shard_map/dot_general | solution.py:239
  350.5 12.5 %shard_map.85 = bf16[1024,3584]{1,0:T(8,128)(2,1)} custom-call(bf16[512,1024]{1,0:T(8,128)(2,1)S(1)} %copy-done.6, bf16[256,1024]{1,0:T(8,128)(2,1)S(1)} %get-tuple-element.78.refs_1_, bf16[256,1024]{1,0:T(8,128)(2,1)S(1)} %get-tuple-element.79.refs_2_, bf16[512,3584]{1,0:T(8,128)(2,1)S(1)} %copy-done.1, bf16[256,7168]{1,0:T(8,128)(2,1)} %bitcast.1.left_ref.refs_4_, ...), custom_call_target="tpu_custom_call" | custom-call | flops 7516192768 | bytes 16777216 | tf_op jit(solution)/shard_map/pallas_call | solution.py:219
  363.0 2.6 collective-permute-done.19
  365.7 2.6 collective-permute-start.20
  368.4 13.8 %copy.9 = bf16[448,8,2,1024]{3,2,1,0:T(2,128)(2,1)} copy(bf16[448,8,2,1024]{3,1,2,0:T(8,128)(2,1)S(1)} %bitcast.34) | data formatting | bytes 29360128 | tf_op jit(solution)/shard_map/transpose | solution.py:344
  382.2 4.9 %convolution_convert_fusion.4 = bf16[256,3584]{1,0:T(8,128)(2,1)} fusion(bf16[256,3584]{1,0:T(8,128)(2,1)} %bitcast.12, bf16[256,3584]{1,0:T(8,128)(2,1)} %bitcast.7, bf16[32,3584]{1,0:T(8,128)(2,1)S(1)} %slice_add_fusion.2, pred[256,256]{1,0:T(32,128)(4,1)S(1)} %get-tuple-element.99, pred[256,256]{1,0:T(32,128)(4,1)S(1)} %get-tuple-element.100, ...), kind=kOutput, calls=%fused_computation.9 | convolution fusion | flops 1011138560 | bytes 5873664 | tf_op jit(solution)/shard_map/dot_general | solution.py:350
  (77 shorter events, 1.7 us)
Async XLA Ops:
  0.6 1.9 copy-start.17
  0.6 2.7 copy-start.12
  3.6 29.0 %copy-start.7 = (bf16[256,7168]{1,0:T(8,128)(2,1)}, bf16[256,7168]{1,0:T(8,128)(2,1)S(1)}, u32[]{:S(2)}) copy-start(bf16[256,7168]{1,0:T(8,128)(2,1)S(1)} %constant_dynamic-update-slice_fusion) | copy-start | bytes 11010052
  4.3 24.5 %collective-permute-start = (bf16[32,7168]{1,0:T(8,128)(2,1)S(1)}, bf16[32,7168]{1,0:T(8,128)(2,1)S(1)}, u32[]{:S(2)}, u32[]{:S(2)}) collective-permute-start(bf16[32,7168]{1,0:T(8,128)(2,1)S(1)} %convolution_convert_fusion.3), channel_id=1, source_target_pairs={{0,8},{1,9},{2,10},{3,11},{4,12},{5,13},{6,14},{7,15},{8,0},{9,1},... | collective-permute-start | bytes 1376264 | tf_op jit(solution)/shard_map/ppermute | solution.py:45
  28.8 21.6 %collective-permute-start.1 = (bf16[64,7168]{1,0:T(8,128)(2,1)S(1)}, bf16[64,7168]{1,0:T(8,128)(2,1)S(1)}, u32[]{:S(2)}, u32[]{:S(2)}) collective-permute-start(bf16[64,7168]{1,0:T(8,128)(2,1)S(1)} %pad_maximum_fusion.5), channel_id=1, source_target_pairs={{0,4},{1,5},{2,6},{3,7},{4,0},{5,1},{6,2},{7,3},{8,12},{9,13},{10,... | collective-permute-start | bytes 2752520 | tf_op jit(solution)/shard_map/ppermute | solution.py:45
  50.7 116.1 %all-to-all-start = ((bf16[16,16,7168]{2,1,0:T(8,128)(2,1)}), bf16[16,16,7168]{2,1,0:T(8,128)(2,1)}, u32[]{:S(2)}, u32[]{:S(2)}) async-start(bf16[16,16,7168]{2,1,0:T(8,128)(2,1)} %bitcast.37), calls=%async_computation | async-start | bytes 7340032 | tf_op jit(solution)/shard_map/all_to_all | solution.py:34
  58.3 53.6 %collective-permute-start.2 = (bf16[128,3584]{1,0:T(8,128)(2,1)S(1)}, bf16[128,3584]{1,0:T(8,128)(2,1)S(1)}, u32[]{:S(2)}, u32[]{:S(2)}) collective-permute-start(bf16[128,3584]{1,0:T(8,128)(2,1)S(1)} %get-tuple-element.45), channel_id=1, source_target_pairs={{0,2},{1,3},{2,0},{3,1},{4,6},{5,7},{6,4},{7,5},{8,10},{9,11},{10,... | collective-permute-start | bytes 2752520 | tf_op jit(solution)/shard_map/ppermute | solution.py:45
  60.1 53.5 %collective-permute-start.4 = (bf16[128,3584]{1,0:T(8,128)(2,1)S(1)}, bf16[128,3584]{1,0:T(8,128)(2,1)S(1)}, u32[]{:S(2)}, u32[]{:S(2)}) collective-permute-start(bf16[128,3584]{1,0:T(8,128)(2,1)S(1)} %get-tuple-element.46), channel_id=1, source_target_pairs={{0,1},{1,0},{2,3},{3,2},{4,5},{5,4},{6,7},{7,6},{8,9},{9,8},{10,11... | collective-permute-start | bytes 2752520 | tf_op jit(solution)/shard_map/ppermute | solution.py:45
  111.9 50.7 %collective-permute-start.3 = (bf16[256,3584]{1,0:T(8,128)(2,1)S(1)}, bf16[256,3584]{1,0:T(8,128)(2,1)S(1)}, u32[]{:S(2)}, u32[]{:S(2)}) collective-permute-start(bf16[256,3584]{1,0:T(8,128)(2,1)S(1)} %pad_maximum_fusion.3), channel_id=1, source_target_pairs={{0,1},{1,0},{2,3},{3,2},{4,5},{5,4},{6,7},{7,6},{8,9},{9,8},{10,11... | collective-permute-start | bytes 5505032 | tf_op jit(solution)/shard_map/ppermute | solution.py:45
  113.7 50.9 %collective-permute-start.5 = (bf16[256,3584]{1,0:T(8,128)(2,1)S(1)}, bf16[256,3584]{1,0:T(8,128)(2,1)S(1)}, u32[]{:S(2)}, u32[]{:S(2)}) collective-permute-start(bf16[256,3584]{1,0:T(8,128)(2,1)S(1)} %pad_maximum_fusion.4), channel_id=1, source_target_pairs={{0,2},{1,3},{2,0},{3,1},{4,6},{5,7},{6,4},{7,5},{8,10},{9,11},{10,... | collective-permute-start | bytes 5505032 | tf_op jit(solution)/shard_map/ppermute | solution.py:45
  116.3 16.2 %copy-start.8 = (bf16[256,7168]{1,0:T(8,128)(2,1)S(1)}, bf16[256,7168]{1,0:T(8,128)(2,1)}, u32[]{:S(2)}) copy-start(bf16[256,7168]{1,0:T(8,128)(2,1)} %copy-done.7) | copy-start | bytes 11010052
  166.8 93.4 %all-to-all-start.1 = ((bf16[16,16,7168]{2,1,0:T(8,128)(2,1)}), bf16[16,16,7168]{2,1,0:T(8,128)(2,1)}, u32[]{:S(2)}, u32[]{:S(2)}) async-start(bf16[16,16,7168]{2,1,0:T(8,128)(2,1)} %bitcast.36), calls=%async_computation.1 | async-start | bytes 7340032 | tf_op jit(solution)/shard_map/all_to_all | solution.py:34
  177.4 2.0 copy-start.2
  179.4 12.8 %copy-start = (bf16[512,3584]{1,0:T(8,128)(2,1)S(1)}, bf16[512,3584]{1,0:T(8,128)(2,1)}, u32[]{:S(2)}) copy-start(bf16[512,3584]{1,0:T(8,128)(2,1)} %pad_maximum_fusion.1.left_ref.refs_3_) | copy-start | bytes 11010052
  191.6 8.0 %collective-permute-start.6 = (bf16[512,1024]{1,0:T(8,128)(2,1)S(1)}, bf16[512,1024]{1,0:T(8,128)(2,1)}, u32[]{:S(2)}, u32[]{:S(2)}) collective-permute-start(bf16[512,1024]{1,0:T(8,128)(2,1)S(1)} %get-tuple-element.50.gate_a), channel_id=1, source_target_pairs={{0,16},{16,0},{1,17},{17,1},{2,18},{18,2},{3,19},{19,3},{4,20},{20... | collective-permute-start | bytes 3145736 | tf_op jit(solution)/shard_map/ppermute | solution.py:127
  191.7 7.9 %collective-permute-start.7 = (bf16[512,1024]{1,0:T(8,128)(2,1)S(1)}, bf16[512,1024]{1,0:T(8,128)(2,1)}, u32[]{:S(2)}, u32[]{:S(2)}) collective-permute-start(bf16[512,1024]{1,0:T(8,128)(2,1)S(1)} %get-tuple-element.51.up_a), channel_id=1, source_target_pairs={{0,16},{16,0},{1,17},{17,1},{2,18},{18,2},{3,19},{19,3},{4,20},{20... | collective-permute-start | bytes 3145736 | tf_op jit(solution)/shard_map/ppermute | solution.py:127
  198.9 2.9 copy-start.4
  198.9 2.9 collective-permute-start.8
  218.2 2.1 copy-start.5
  218.2 3.0 copy-start.9
  221.3 38.0 %collective-permute-start.12 = (bf16[256,1792]{1,0:T(8,128)(2,1)S(1)}, bf16[256,1792]{1,0:T(8,128)(2,1)S(1)}, u32[]{:S(2)}, u32[]{:S(2)}) collective-permute-start(bf16[256,1792]{1,0:T(8,128)(2,1)S(1)} %get-tuple-element.60), channel_id=1, source_target_pairs={{0,1},{1,0},{2,3},{3,2},{4,5},{5,4},{6,7},{7,6},{8,9},{9,8},{10,11... | collective-permute-start | bytes 2752520 | tf_op jit(solution)/shard_map/ppermute | solution.py:45
  223.2 37.0 %collective-permute-start.13 = (bf16[256,1792]{1,0:T(8,128)(2,1)S(1)}, bf16[256,1792]{1,0:T(8,128)(2,1)}, u32[]{:S(2)}, u32[]{:S(2)}) collective-permute-start(bf16[256,1792]{1,0:T(8,128)(2,1)S(1)} %get-tuple-element.61), channel_id=1, source_target_pairs={{0,2},{1,3},{2,0},{3,1},{4,6},{5,7},{6,4},{7,5},{8,10},{9,11},{10,... | collective-permute-start | bytes 2752520 | tf_op jit(solution)/shard_map/ppermute | solution.py:45
  235.1 9.4 %collective-permute-start.9 = (bf16[256,1024]{1,0:T(8,128)(2,1)S(1)}, bf16[256,1024]{1,0:T(8,128)(2,1)S(1)}, u32[]{:S(2)}, u32[]{:S(2)}) collective-permute-start(bf16[256,1024]{1,0:T(8,128)(2,1)S(1)} %get-tuple-element.57.gate_a), channel_id=1, source_target_pairs={{0,16},{16,0},{1,17},{17,1},{2,18},{18,2},{3,19},{19,3},{4,20},{20... | collective-permute-start | bytes 1572872 | tf_op jit(solution)/shard_map/ppermute | solution.py:127
  235.2 9.3 %collective-permute-start.10 = (bf16[256,1024]{1,0:T(8,128)(2,1)S(1)}, bf16[256,1024]{1,0:T(8,128)(2,1)S(1)}, u32[]{:S(2)}, u32[]{:S(2)}) collective-permute-start(bf16[256,1024]{1,0:T(8,128)(2,1)S(1)} %get-tuple-element.58.up_a), channel_id=1, source_target_pairs={{0,16},{16,0},{1,17},{17,1},{2,18},{18,2},{3,19},{19,3},{4,20},{20... | collective-permute-start | bytes 1572872 | tf_op jit(solution)/shard_map/ppermute | solution.py:127
  241.5 3.0 collective-permute-start.11
  259.2 0.9 copy-start.14
  260.2 56.4 %all-to-all-start.2 = ((bf16[16,16,3584]{2,1,0:T(8,128)(2,1)}), bf16[16,16,3584]{2,1,0:T(8,128)(2,1)}, u32[]{:S(2)}, u32[]{:S(2)}) async-start(bf16[16,16,3584]{2,1,0:T(8,128)(2,1)} %bitcast.38), calls=%async_computation.2 | async-start | bytes 3670016 | tf_op jit(solution)/shard_map/all_to_all | solution.py:34
  284.3 11.8 %collective-permute-start.16 = (bf16[256,1024]{1,0:T(8,128)(2,1)S(1)}, bf16[256,1024]{1,0:T(8,128)(2,1)S(1)}, u32[]{:S(2)}, u32[]{:S(2)}) collective-permute-start(bf16[256,1024]{1,0:T(8,128)(2,1)S(1)} %get-tuple-element.67.gate_a), channel_id=1, source_target_pairs={{0,16},{16,0},{1,17},{17,1},{2,18},{18,2},{3,19},{19,3},{4,20},{20... | collective-permute-start | bytes 1572872 | tf_op jit(solution)/shard_map/ppermute | solution.py:127
  284.4 6.5 %copy-start.15 = (bf16[256,1792]{1,0:T(8,128)(2,1)S(1)}, bf16[256,1792]{1,0:T(8,128)(2,1)}, u32[]{:S(2)}) copy-start(bf16[256,1792]{1,0:T(8,128)(2,1)} %copy-done.14) | copy-start | bytes 2752516
  284.4 11.7 %collective-permute-start.17 = (bf16[256,1024]{1,0:T(8,128)(2,1)S(1)}, bf16[256,1024]{1,0:T(8,128)(2,1)S(1)}, u32[]{:S(2)}, u32[]{:S(2)}) collective-permute-start(bf16[256,1024]{1,0:T(8,128)(2,1)S(1)} %get-tuple-element.68.up_a), channel_id=1, source_target_pairs={{0,16},{16,0},{1,17},{17,1},{2,18},{18,2},{3,19},{19,3},{4,20},{20... | collective-permute-start | bytes 1572872 | tf_op jit(solution)/shard_map/ppermute | solution.py:127
  290.7 5.4 %collective-permute-start.18 = (bf16[256,1024]{1,0:T(8,128)(2,1)S(1)}, bf16[256,1024]{1,0:T(8,128)(2,1)S(1)}, u32[]{:S(2)}, u32[]{:S(2)}) collective-permute-start(bf16[256,1024]{1,0:T(8,128)(2,1)S(1)} %shard_map.83.grad_a), channel_id=1, source_target_pairs={{0,16},{16,0},{1,17},{17,1},{2,18},{18,2},{3,19},{19,3},{4,20},{20... | collective-permute-start | bytes 1572872 | tf_op jit(solution)/shard_map/ppermute | solution.py:127
  291.1 5.0 %copy-start.10 = (bf16[256,1792]{1,0:T(8,128)(2,1)}, bf16[256,1792]{1,0:T(8,128)(2,1)S(1)}, u32[]{:S(2)}) copy-start(bf16[256,1792]{1,0:T(8,128)(2,1)S(1)} %add.29) | copy-start | bytes 2752516
  291.2 16.9 %collective-permute-start.14 = (bf16[128,1792]{1,0:T(8,128)(2,1)S(1)}, bf16[128,1792]{1,0:T(8,128)(2,1)S(1)}, u32[]{:S(2)}, u32[]{:S(2)}) collective-permute-start(bf16[128,1792]{1,0:T(8,128)(2,1)S(1)} %slice.97), channel_id=1, source_target_pairs={{0,2},{1,3},{2,0},{3,1},{4,6},{5,7},{6,4},{7,5},{8,10},{9,11},{10,... | collective-permute-start | bytes 1376264 | tf_op jit(solution)/shard_map/ppermute | solution.py:45
  294.5 13.0 %copy-start.11 = (bf16[256,1792]{1,0:T(8,128)(2,1)}, bf16[256,1792]{1,0:T(8,128)(2,1)S(1)}, u32[]{:S(2)}) copy-start(bf16[256,1792]{1,0:T(8,128)(2,1)S(1)} %add.30) | copy-start | bytes 2752516
  294.5 22.0 %collective-permute-start.15 = (bf16[128,1792]{1,0:T(8,128)(2,1)S(1)}, bf16[128,1792]{1,0:T(8,128)(2,1)}, u32[]{:S(2)}, u32[]{:S(2)}) collective-permute-start(bf16[128,1792]{1,0:T(8,128)(2,1)S(1)} %slice.98), channel_id=1, source_target_pairs={{0,1},{1,0},{2,3},{3,2},{4,5},{5,4},{6,7},{7,6},{8,9},{9,8},{10,11... | collective-permute-start | bytes 1376264 | tf_op jit(solution)/shard_map/ppermute | solution.py:45
  308.1 0.8 copy-start.16
  316.6 65.7 %all-to-all-start.3 = ((bf16[16,16,3584]{2,1,0:T(8,128)(2,1)}), bf16[16,16,3584]{2,1,0:T(8,128)(2,1)}, u32[]{:S(2)}, u32[]{:S(2)}) async-start(bf16[16,16,3584]{2,1,0:T(8,128)(2,1)} %bitcast.39), calls=%async_computation.3 | async-start | bytes 3670016 | tf_op jit(solution)/shard_map/all_to_all | solution.py:34
  323.9 6.7 %copy-start.3 = (bf16[512,3584]{1,0:T(8,128)(2,1)S(1)}, bf16[512,3584]{1,0:T(8,128)(2,1)}, u32[]{:S(2)}) copy-start(bf16[512,3584]{1,0:T(8,128)(2,1)} %pad_maximum_fusion.left_ref) | copy-start | bytes 11010052
  323.9 6.7 %copy-start.13 = (bf16[256,3584]{1,0:T(8,128)(2,1)S(1)}, bf16[256,3584]{1,0:T(8,128)(2,1)}, u32[]{:S(2)}) copy-start(bf16[256,3584]{1,0:T(8,128)(2,1)} %slice.82) | copy-start | bytes 5505028
  327.0 38.5 %collective-permute-start.19 = (bf16[64,3584]{1,0:T(8,128)(2,1)S(1)}, bf16[64,3584]{1,0:T(8,128)(2,1)S(1)}, u32[]{:S(2)}, u32[]{:S(2)}) collective-permute-start(bf16[64,3584]{1,0:T(8,128)(2,1)S(1)} %pad_maximum_fusion.8), channel_id=1, source_target_pairs={{0,4},{1,5},{2,6},{3,7},{4,0},{5,1},{6,2},{7,3},{8,12},{9,13},{10,... | collective-permute-start | bytes 1376264 | tf_op jit(solution)/shard_map/ppermute | solution.py:45
  330.6 19.8 %copy-start.1 = (bf16[512,3584]{1,0:T(8,128)(2,1)S(1)}, bf16[512,3584]{1,0:T(8,128)(2,1)}, u32[]{:S(2)}) copy-start(bf16[512,3584]{1,0:T(8,128)(2,1)} %pad_maximum_fusion.1.left_ref.refs_3_) | copy-start | bytes 11010052
  330.6 19.8 %copy-start.6 = (bf16[512,1024]{1,0:T(8,128)(2,1)S(1)}, bf16[512,1024]{1,0:T(8,128)(2,1)}, u32[]{:S(2)}) copy-start(bf16[512,1024]{1,0:T(8,128)(2,1)} %copy-done.5) | copy-start | bytes 3145732
  350.4 17.9 %slice-start = ((s8[14680064]{0:T(1024)(128)(4,1)}), s8[4194304]{0:T(1024)(128)(4,1)S(1)}, s32[]{:S(2)}) async-start(s8[14680064]{0:T(1024)(128)(4,1)} %bitcast.32), calls=%async_computation.4 | async-start | bytes 8388608
  350.5 17.9 %slice-start.1 = ((s8[14680064]{0:T(1024)(128)(4,1)}), s8[4194304]{0:T(1024)(128)(4,1)S(1)}, s32[]{:S(2)}) async-start(s8[14680064]{0:T(1024)(128)(4,1)} %bitcast.32), calls=%async_computation.5 | async-start | bytes 8388608
  350.5 17.9 %slice-start.2 = ((s8[14680064]{0:T(1024)(128)(4,1)}), s8[4194304]{0:T(1024)(128)(4,1)S(1)}, s32[]{:S(2)}) async-start(s8[14680064]{0:T(1024)(128)(4,1)} %bitcast.32), calls=%async_computation.6 | async-start | bytes 8388608
  350.5 17.9 %slice-start.3 = ((s8[14680064]{0:T(1024)(128)(4,1)}), s8[2097152]{0:T(1024)(128)(4,1)S(1)}, s32[]{:S(2)}) async-start(s8[14680064]{0:T(1024)(128)(4,1)} %bitcast.32), calls=%async_computation.7 | async-start | bytes 4194304
  365.7 16.5 %collective-permute-start.20 = (bf16[32,3584]{1,0:T(8,128)(2,1)S(1)}, bf16[32,3584]{1,0:T(8,128)(2,1)S(1)}, u32[]{:S(2)}, u32[]{:S(2)}) collective-permute-start(bf16[32,3584]{1,0:T(8,128)(2,1)S(1)} %slice.91), channel_id=1, source_target_pairs={{0,8},{1,9},{2,10},{3,11},{4,12},{5,13},{6,14},{7,15},{8,0},{9,1},... | collective-permute-start | bytes 688136 | tf_op jit(solution)/shard_map/ppermute | solution.py:45

commit v11 on v10

--- a/solution.py
+++ b/solution.py
@@ -128,20 +128,11 @@
     return lax.psum(part, "grp"), jnp.zeros_like(part)
 
 
-def finish_kernel(
-    keep_ref,
-    gate_a,
-    gate_b,
-    up_a,
-    up_b,
-    grad_a,
-    grad_b,
-    matrix_ref,
-    out_ref,
-    hidden_ref,
-    branch_ref,
-):
+def finish_kernel(pieces, keep_ref, *refs):
+    pairs = [(refs[2 * i], refs[2 * i + 1]) for i in range(3 * pieces)]
+    matrix_ref, out_ref, hidden_ref, branch_ref = refs[6 * pieces :]
     height, width = hidden_ref.shape
+    share = width // pieces
 
     @pl.when(pl.program_id(0) == 0)
     def _():
@@ -152,39 +143,44 @@
         def _(i):
             here = pl.ds(pl.multiple_of(i * step, step), step)
 
-            def total(one, two):
+            def total(pair):
+                one, two = pair
                 return one[here, :].astype(jnp.float32) + two[here, :].astype(jnp.float32)
 
-            gate_value = total(gate_a, gate_b)
-            upward = total(up_a, up_b)
-            hidden_grads = total(grad_a, grad_b)
-            sigmoid_value = jax.nn.sigmoid(gate_value)
-            activated = gate_value * sigmoid_value
-            gate_slope = sigmoid_value * (1.0 + gate_value * (1.0 - sigmoid_value))
-
-            def put(ref, columns, value):
-                ref[here, columns] = jnp.where(keep, value, 0.0).astype(ref.dtype)
-
-            put(hidden_ref, pl.ds(0, width), activated * upward)
-            put(branch_ref, pl.ds(0, width), hidden_grads * upward * gate_slope)
-            put(branch_ref, pl.ds(width, width), hidden_grads * activated)
+            def put(ref, first, value):
+                kept = jnp.where(keep, value, 0.0).astype(ref.dtype)
+                ref[here, pl.ds(first, share)] = kept
+
+            for piece in range(pieces):
+                gate_value = total(pairs[piece])
+                upward = total(pairs[pieces + piece])
+                hidden_grads = total(pairs[2 * pieces + piece])
+                sigmoid_value = jax.nn.sigmoid(gate_value)
+                activated = gate_value * sigmoid_value
+                gate_slope = sigmoid_value * (1.0 + gate_value * (1.0 - sigmoid_value))
+                first = piece * share
+                put(hidden_ref, first, activated * upward)
+                put(branch_ref, first, hidden_grads * upward * gate_slope)
+                put(branch_ref, width + first, hidden_grads * activated)
 
     out_ref[...] = dot_f32(branch_ref[...], matrix_ref[...], 1, 1).astype(out_ref.dtype)
 
 
-def finish(keep, gate_pair, up_pair, grad_pair, matrix):
-    height, width = grad_pair[0].shape
+def finish(keep, pairs, matrix):
+    pieces = len(pairs) // 3
+    height, share = pairs[0][0].shape
+    width = pieces * share
     features = matrix.shape[0]
     step = block_of(features, 512)
     whole = lambda columns: pl.BlockSpec((height, columns), lambda j: (0, 0))
     shape = lambda columns: jax.ShapeDtypeStruct((height, columns), jnp.bfloat16)
     return pl.pallas_call(
-        finish_kernel,
+        functools.partial(finish_kernel, pieces),
         grid=(features // step,),
         in_specs=[
             pl.BlockSpec(memory_space=pltpu.SMEM),
         ]
-        + [whole(width)] * 6
+        + [whole(share)] * (6 * pieces)
         + [
             pl.BlockSpec((step, 2 * width), lambda j: (j, 0)),
         ],
@@ -196,7 +192,7 @@
         out_shape=[shape(features), shape(width), shape(2 * width)],
         compiler_params=pltpu.CompilerParams(vmem_limit_bytes=VMEM_BYTES),
         cost_estimate=SMALL_COST,
-    )(keep, *gate_pair, *up_pair, *grad_pair, matrix)
+    )(keep, *[part for pair in pairs for part in pair], matrix)
 
 
 def outer_kernel(count, *refs):
@@ -266,9 +262,9 @@
     def split(both_in):
         return both_in[:, :feature_share], both_in[:, feature_share:]
 
-    def products(rows_in, rows_block, grads_in, grads_block):
-        parts = product(rows_in, rows_block, feature_share, gate_up_matrix, False, 2)
-        parts += product(grads_in, grads_block, feature_share, down_matrix, True, 1)
+    def products(rows_in, rows_block, grads_in, grads_block, pieces):
+        parts = product(rows_in, rows_block, feature_share, gate_up_matrix, False, 2 * pieces)
+        parts += product(grads_in, grads_block, feature_share, down_matrix, True, pieces)
         return [pair_over_grp(part) for part in parts]
 
     always = jnp.ones((1,), jnp.int32)
@@ -292,7 +288,7 @@
 
     arrived_1 = exchange(sent_1, expert_count)
     out_s, hidden_s, branch_s = finish(
-        only_busiest, *products(spill_rows, 0, spill_grads, 0), gate_up_matrix
+        only_busiest, products(spill_rows, 0, spill_grads, 0, 1), gate_up_matrix
     )
     middle = feature_share // 2
     kept_a, sent_a = halves(out_s[:, :middle])
@@ -302,7 +298,7 @@
     )
     come_a, come_b = swap_with(sent_a, 1), swap_with(sent_b, 2)
     out_0, hidden_0, branch_0 = finish(
-        always, *products(arrived_0, 0, arrived_0, 1), gate_up_matrix
+        always, products(arrived_0, 0, arrived_0, 1, 1), gate_up_matrix
     )
     rows_0, _ = split(arrived_0)
     arrived_1, out_0, come_a, come_b, rows_0 = lax.optimization_barrier(
@@ -314,7 +310,7 @@
     kept_b, sent_b = halves(kept_b + come_b)
     come_a, come_b = swap_with(sent_a, 2), swap_with(sent_b, 1)
     out_1, hidden_1, branch_1 = finish(
-        always, *products(arrived_1, 0, arrived_1, 1), gate_up_matrix
+        always, products(arrived_1, 0, arrived_1, 1, 2), gate_up_matrix
     )
     back_0, come_a, come_b, out_1, arrived_1 = lax.optimization_barrier(
         (back_0, come_a, come_b, out_1, arrived_1)

time: 389 us -> 399 us (1.026)
  local copies, waits for them, and re-layouts: 43.6 us -> 56.8 us
    transpose x1, local copies, waits for them, and re-layouts: 13.8 us -> 27.1 us  [local(): gate_up_grads.transpose(0, 2, 1, 3)]
    unnamed x46 -> x38, local copies, waits for them, and re-layouts: 22.7 us -> 22.6 us
  transfers between devices with their start and end apart: 25 -> 28, of which waited for: 9 -> 11; matrix products, arithmetic and copies ran while one was open for 19% -> 21% of each run, Pallas kernels for 27% -> 26%
where the time goes in v11:
time: 399 us; the launch traced here: 397 us
  waiting for transfers between devices  130 us (33%)
  Pallas kernels  102 us (26%)
  starting transfers between devices  64.7 us (16%)
  local copies, waits for them, and re-layouts  56.8 us (14%)
  matrix products  31.5 us (8%)
  other arithmetic  10.3 us (3%)
    ppermute x12, waiting for transfers between devices, swap_with(): return lax.ppermute(rows, 'exp', [(i, i ^ mask) for i in range(total)])  126 us
    pallas_call x6, Pallas kernels, product(): pl.pallas_call(functools.partial(product_kernel, 1 if transposed else 0,...  51.6 us
    pallas_call x3, Pallas kernels, finish(): pl.pallas_call(functools.partial(finish_kernel, pieces), grid=(features /...  39.3 us
    all_to_all x4, starting transfers between devices, exchange(): lax.all_to_all(rows.reshape(expert_count, slots // expert_count, width),...  38.1 us
    transpose x1, local copies, waits for them, and re-layouts, local(): gate_up_grads.transpose(0, 2, 1, 3)  27.1 us
    ppermute x12, starting transfers between devices, swap_with(): return lax.ppermute(rows, 'exp', [(i, i ^ mask) for i in range(total)])  23.9 us
    unnamed x38, local copies, waits for them, and re-layouts  22.6 us
    dot_general x1, matrix products, outer(): lax.dot_general(left, right, (((0,), (0,)), ((), ())), preferred_element_...  19.9 us
  transfers between devices with their start and end apart: 28, of which 11 were waited for; matrix products, arithmetic and copies ran while one was open for 21% of the time, Pallas kernels for 26%

profile of v11, /device:TPU:0, one launch (start us, length us, event | category | flops | bytes accessed | tf_op | source)
XLA Modules:
  0.0 397.2 jit_solution(18038182435564705095)
XLA Ops:
  0.7 1.8 constant_dynamic-update-slice_fusion.1
  2.7 0.7 select_reduce_fusion
  3.4 0.2 constant_dynamic-update-slice_fusion
  3.6 0.7 convolution_convert_fusion.3
  4.3 4.1 %collective-permute-start = (bf16[32,7168]{1,0:T(8,128)(2,1)S(1)}, bf16[32,7168]{1,0:T(8,128)(2,1)S(1)}, u32[]{:S(2)}, u32[]{:S(2)}) collective-permute-start(bf16[32,7168]{1,0:T(8,128)(2,1)S(1)} %convolution_convert_fusion.3), channel_id=1, source_target_pairs={{0,8},{1,9},{2,10},{3,11},{4,12},{5,13},{6,14},{7,15},{8,0},{9,1},... | collective-permute-start | bytes 1376264 | tf_op jit(solution)/shard_map/ppermute | solution.py:45
  8.4 20.4 %collective-permute-done = bf16[32,7168]{1,0:T(8,128)(2,1)S(1)} collective-permute-done((bf16[32,7168]{1,0:T(8,128)(2,1)S(1)}, bf16[32,7168]{1,0:T(8,128)(2,1)S(1)}, u32[]{:S(2)}, u32[]{:S(2)}) %collective-permute-start) | collective-permute-done | bytes 458784 | tf_op jit(solution)/shard_map/ppermute | solution.py:45
  28.8 0.8 collective-permute-start.1
  29.6 3.0 convolution_convert_fusion.2
  32.6 17.8 %collective-permute-done.1 = bf16[64,7168]{1,0:T(8,128)(2,1)S(1)} collective-permute-done((bf16[64,7168]{1,0:T(8,128)(2,1)S(1)}, bf16[64,7168]{1,0:T(8,128)(2,1)S(1)}, u32[]{:S(2)}, u32[]{:S(2)}) %collective-permute-start.1) | collective-permute-done | bytes 917536 | tf_op jit(solution)/shard_map/ppermute | solution.py:45
  50.7 7.6 %all-to-all-start = ((bf16[16,16,7168]{2,1,0:T(8,128)(2,1)}), bf16[16,16,7168]{2,1,0:T(8,128)(2,1)}, u32[]{:S(2)}, u32[]{:S(2)}) async-start(bf16[16,16,7168]{2,1,0:T(8,128)(2,1)} %bitcast.35), calls=%async_computation | async-start | bytes 7340032 | tf_op jit(solution)/shard_map/all_to_all | solution.py:34
  58.3 1.9 collective-permute-start.2
  60.2 1.5 collective-permute-start.4
  61.6 50.2 %collective-permute-done.2 = bf16[128,3584]{1,0:T(8,128)(2,1)S(1)} collective-permute-done((bf16[128,3584]{1,0:T(8,128)(2,1)S(1)}, bf16[128,3584]{1,0:T(8,128)(2,1)S(1)}, u32[]{:S(2)}, u32[]{:S(2)}) %collective-permute-start.2) | collective-permute-done | bytes 917536 | tf_op jit(solution)/shard_map/ppermute | solution.py:45
  112.0 1.7 collective-permute-start.3
  113.8 2.5 collective-permute-start.5
  116.3 16.2 %copy.10 = bf16[448,8,2,1024]{3,1,2,0:T(8,128)(2,1)} copy(bf16[448,8,2,1024]{3,2,1,0:T(2,128)(2,1)} %bitcast.31) | data formatting | bytes 29360128
  132.5 3.0 convolution_convert_fusion.1
  135.5 27.2 %collective-permute-done.3 = bf16[256,3584]{1,0:T(8,128)(2,1)S(1)} collective-permute-done((bf16[256,3584]{1,0:T(8,128)(2,1)S(1)}, bf16[256,3584]{1,0:T(8,128)(2,1)S(1)}, u32[]{:S(2)}, u32[]{:S(2)}) %collective-permute-start.3) | collective-permute-done | bytes 1835040 | tf_op jit(solution)/shard_map/ppermute | solution.py:45
  162.7 1.9 pad_maximum_fusion.left_ref
  164.7 2.0 pad_maximum_fusion.1.left_ref.refs_3_
  166.7 10.5 %all-to-all-start.1 = ((bf16[16,16,7168]{2,1,0:T(8,128)(2,1)}), bf16[16,16,7168]{2,1,0:T(8,128)(2,1)}, u32[]{:S(2)}, u32[]{:S(2)}) async-start(bf16[16,16,7168]{2,1,0:T(8,128)(2,1)} %bitcast.34), calls=%async_computation.1 | async-start | bytes 7340032 | tf_op jit(solution)/shard_map/all_to_all | solution.py:34
  177.3 2.0 copy-done.2
  179.3 12.2 %shard_map.76 = (bf16[512,1024]{1,0:T(8,128)(2,1)S(1)}, bf16[512,1024]{1,0:T(8,128)(2,1)S(1)}) custom-call(bf16[512,3584]{1,0:T(8,128)(2,1)S(1)} %copy-done.2, bf16[3584,2048]{1,0:T(8,128)(2,1)} %bitcast.22), custom_call_target="tpu_custom_call" | custom-call | flops 1 | bytes 1 | tf_op jit(solution)/shard_map/pallas_call | solution.py:114
  191.6 0.5 collective-permute-start.7
  192.1 6.7 %shard_map.77.refs_4_ = bf16[512,1024]{1,0:T(8,128)(2,1)S(1)} custom-call(bf16[512,3584]{1,0:T(8,128)(2,1)S(1)} %copy-done, bf16[1024,3584]{1,0:T(8,128)(2,1)} %bitcast.28), custom_call_target="tpu_custom_call" | custom-call | flops 1 | bytes 1 | tf_op jit(solution)/shard_map/pallas_call | solution.py:114
  199.6 2.1 collective-permute-done.8.refs_5_
  201.7 16.4 %shard_map.78 = (bf16[512,3584]{1,0:T(8,128)(2,1)}, bf16[512,1024]{1,0:T(8,128)(2,1)S(1)}, bf16[512,2048]{1,0:T(8,128)(2,1)}) custom-call(s32[1]{0:T(128)} %bitcast.2.keep_ref, bf16[512,1024]{1,0:T(8,128)(2,1)S(1)} %get-tuple-element.54.refs_0_, bf16[512,1024]{1,0:T(8,128)(2,1)} %collective-permute-done.6.refs_1_, ...), custom_call_target="tpu_custom_call" | custom-call | flops 1 | bytes 1 | tf_op jit(solution)/shard_map/pallas_call | solution.py:177
  218.1 2.0 fusion.26
  220.2 0.8 copy-done.9
  221.2 1.9 collective-permute-start.12
  223.1 1.4 collective-permute-start.13
  224.6 10.4 %shard_map.79 = (bf16[256,1024]{1,0:T(8,128)(2,1)S(1)}, bf16[256,1024]{1,0:T(8,128)(2,1)S(1)}) custom-call(bf16[256,7168]{1,0:T(8,128)(2,1)} %bitcast.1.left_ref.refs_4_, bf16[3584,2048]{1,0:T(8,128)(2,1)} %bitcast.24), custom_call_target="tpu_custom_call" | custom-call | flops 1 | bytes 1 | tf_op jit(solution)/shard_map/pallas_call | solution.py:114
  235.1 0.5 collective-permute-start.10
  235.6 5.8 %shard_map.80.refs_4_ = bf16[256,1024]{1,0:T(8,128)(2,1)S(1)} custom-call(bf16[256,7168]{1,0:T(8,128)(2,1)} %bitcast.1.left_ref.refs_4_, bf16[1024,3584]{1,0:T(8,128)(2,1)} %bitcast.29), custom_call_target="tpu_custom_call" | custom-call | flops 1 | bytes 1 | tf_op jit(solution)/shard_map/pallas_call | solution.py:114
  241.5 2.9 slice.82
  244.4 11.4 %shard_map.81 = (bf16[256,3584]{1,0:T(8,128)(2,1)}, bf16[256,1024]{1,0:T(8,128)(2,1)S(1)}, bf16[256,2048]{1,0:T(8,128)(2,1)S(1)}) custom-call(s32[1]{0:T(128)} %constant.20.clone.1.keep_ref, bf16[256,1024]{1,0:T(8,128)(2,1)S(1)} %get-tuple-element.61.refs_0_, bf16[256,1024]{1,0:T(8,128)(2,1)S(1)} %collective-permute-done.9.refs_1_, ...), custom_call_target="tpu_custom_call" | custom-call | flops 1 | bytes 1 | tf_op jit(solution)/shard_map/pallas_call | solution.py:177
  255.8 3.3 collective-permute-done.12
  259.2 0.9 copy-done.14
  260.1 13.6 %all-to-all-start.2 = ((bf16[16,16,3584]{2,1,0:T(8,128)(2,1)}), bf16[16,16,3584]{2,1,0:T(8,128)(2,1)}, u32[]{:S(2)}, u32[]{:S(2)}) async-start(bf16[16,16,3584]{2,1,0:T(8,128)(2,1)} %bitcast.36), calls=%async_computation.2 | async-start | bytes 3670016 | tf_op jit(solution)/shard_map/all_to_all | solution.py:34
  273.7 10.7 %shard_map.82 = (bf16[256,512]{1,0:T(8,128)(2,1)S(1)}, bf16[256,512]{1,0:T(8,128)(2,1)S(1)}, bf16[256,512]{1,0:T(8,128)(2,1)S(1)}, bf16[256,512]{1,0:T(8,128)(2,1)S(1)}) custom-call(bf16[256,7168]{1,0:T(8,128)(2,1)} %bitcast.5.left_ref.refs_5_, bf16[3584,2048]{1,0:T(8,128)(2,1)} %bitcast.26), custom_call_target="tpu_custom_call" | custom-call | flops 1 | bytes 1 | tf_op jit(solution)/shard_map/pallas_call | solution.py:114
  284.5 0.5 collective-permute-start.17
  285.1 0.2 add.29
  285.3 1.9 collective-permute-start.14
  287.3 1.4 add.30
  288.7 1.5 collective-permute-start.15
  290.3 5.9 %shard_map.83 = (bf16[256,512]{1,0:T(8,128)(2,1)S(1)}, bf16[256,512]{1,0:T(8,128)(2,1)S(1)}) custom-call(bf16[256,7168]{1,0:T(8,128)(2,1)} %bitcast.5.left_ref.refs_5_, bf16[1024,3584]{1,0:T(8,128)(2,1)} %bitcast.30), custom_call_target="tpu_custom_call" | custom-call | flops 1 | bytes 1 | tf_op jit(solution)/shard_map/pallas_call | solution.py:114
  296.2 0.5 collective-permute-start.20
  296.8 0.9 collective-permute-done.19.refs_7_
  297.7 0.4 collective-permute-done.20.refs_9_
  298.1 0.4 collective-permute-done.21.refs_11_
  298.5 11.4 %shard_map.84 = (bf16[256,3584]{1,0:T(8,128)(2,1)}, bf16[256,1024]{1,0:T(8,128)(2,1)S(1)}, bf16[256,2048]{1,0:T(8,128)(2,1)S(1)}) custom-call(s32[1]{0:T(128)} %constant.20.clone.1.keep_ref, bf16[256,512]{1,0:T(8,128)(2,1)S(1)} %get-tuple-element.71.refs_0_, bf16[256,512]{1,0:T(8,128)(2,1)S(1)} %collective-permute-done.16.refs_1_, ...), custom_call_target="tpu_custom_call" | custom-call | flops 1 | bytes 1 | tf_op jit(solution)/shard_map/pallas_call | solution.py:177
  309.9 0.8 copy-done.16
  310.7 4.5 %collective-permute-done.15 = bf16[128,1792]{1,0:T(8,128)(2,1)} collective-permute-done((bf16[128,1792]{1,0:T(8,128)(2,1)S(1)}, bf16[128,1792]{1,0:T(8,128)(2,1)}, u32[]{:S(2)}, u32[]{:S(2)}) %collective-permute-start.15) | collective-permute-done | bytes 458784 | tf_op jit(solution)/shard_map/ppermute | solution.py:45
  315.2 6.3 %all-to-all-start.3 = ((bf16[16,16,3584]{2,1,0:T(8,128)(2,1)}), bf16[16,16,3584]{2,1,0:T(8,128)(2,1)}, u32[]{:S(2)}, u32[]{:S(2)}) async-start(bf16[16,16,3584]{2,1,0:T(8,128)(2,1)} %bitcast.37), calls=%async_computation.3 | async-start | bytes 3670016 | tf_op jit(solution)/shard_map/all_to_all | solution.py:34
  321.5 1.4 slice_add_fusion
  322.9 1.7 slice_add_fusion.1
  324.7 1.9 collective-permute-start.22
  326.6 1.6 slice.89
  328.3 19.9 %convolution_convert_fusion = bf16[3584,2048]{1,0:T(8,128)(2,1)} fusion(bf16[256,3584]{1,0:T(8,128)(2,1)S(1)} %slice.89, bf16[256,3584]{1,0:T(8,128)(2,1)S(1)} %copy-done.13, bf16[512,3584]{1,0:T(8,128)(2,1)S(1)} %copy-done.3, bf16[256,2048]{1,0:T(8,128)(2,1)S(1)} %get-tuple-element.84, bf16[256,2048]{1,0:T(8,128)(2,1)S(1)} %get-tuple-element.83, ...), kind=kOutput, calls=%fused_computation | convolution fusion | flops 15074328576 | bytes 26214400 | tf_op jit(solution)/shard_map/dot_general | solution.py:235
  348.2 11.5 %shard_map.85 = bf16[1024,3584]{1,0:T(8,128)(2,1)} custom-call(bf16[512,1024]{1,0:T(8,128)(2,1)S(1)} %copy-done.6, bf16[256,1024]{1,0:T(8,128)(2,1)S(1)} %get-tuple-element.86.refs_1_, bf16[256,1024]{1,0:T(8,128)(2,1)S(1)} %get-tuple-element.87.refs_2_, bf16[512,3584]{1,0:T(8,128)(2,1)S(1)} %copy-done.1, bf16[256,7168]{1,0:T(8,128)(2,1)} %bitcast.1.left_ref.refs_4_, ...), custom_call_target="tpu_custom_call" | custom-call | flops 7516192768 | bytes 16777216 | tf_op jit(solution)/shard_map/pallas_call | solution.py:215
  359.6 2.7 collective-permute-done.22
  362.4 2.6 collective-permute-start.23
  365.2 27.1 %copy.9 = bf16[448,8,2,1024]{3,2,1,0:T(2,128)(2,1)} copy(bf16[448,8,2,1024]{3,1,2,0:T(8,128)(2,1)} %bitcast.32) | data formatting | bytes 29360128 | tf_op jit(solution)/shard_map/transpose | solution.py:340
  392.3 4.9 %convolution_convert_fusion.4 = bf16[256,3584]{1,0:T(8,128)(2,1)} fusion(bf16[256,3584]{1,0:T(8,128)(2,1)} %bitcast.12, bf16[256,3584]{1,0:T(8,128)(2,1)} %bitcast.7, bf16[32,3584]{1,0:T(8,128)(2,1)S(1)} %slice_add_fusion.2, pred[256,256]{1,0:T(32,128)(4,1)S(1)} %get-tuple-element.107, pred[256,256]{1,0:T(32,128)(4,1)S(1)} %get-tuple-element.108, ...), kind=kOutput, calls=%fused_computation.9 | convolution fusion | flops 1011138560 | bytes 5873664 | tf_op jit(solution)/shard_map/dot_general | solution.py:346
  (74 shorter events, 2.3 us)
Async XLA Ops:
  0.6 1.9 copy-start.17
  0.6 2.7 copy-start.12
  3.6 29.1 %copy-start.7 = (bf16[256,7168]{1,0:T(8,128)(2,1)}, bf16[256,7168]{1,0:T(8,128)(2,1)S(1)}, u32[]{:S(2)}) copy-start(bf16[256,7168]{1,0:T(8,128)(2,1)S(1)} %constant_dynamic-update-slice_fusion) | copy-start | bytes 11010052
  4.3 24.5 %collective-permute-start = (bf16[32,7168]{1,0:T(8,128)(2,1)S(1)}, bf16[32,7168]{1,0:T(8,128)(2,1)S(1)}, u32[]{:S(2)}, u32[]{:S(2)}) collective-permute-start(bf16[32,7168]{1,0:T(8,128)(2,1)S(1)} %convolution_convert_fusion.3), channel_id=1, source_target_pairs={{0,8},{1,9},{2,10},{3,11},{4,12},{5,13},{6,14},{7,15},{8,0},{9,1},... | collective-permute-start | bytes 1376264 | tf_op jit(solution)/shard_map/ppermute | solution.py:45
  28.8 21.6 %collective-permute-start.1 = (bf16[64,7168]{1,0:T(8,128)(2,1)S(1)}, bf16[64,7168]{1,0:T(8,128)(2,1)S(1)}, u32[]{:S(2)}, u32[]{:S(2)}) collective-permute-start(bf16[64,7168]{1,0:T(8,128)(2,1)S(1)} %pad_maximum_fusion.5), channel_id=1, source_target_pairs={{0,4},{1,5},{2,6},{3,7},{4,0},{5,1},{6,2},{7,3},{8,12},{9,13},{10,... | collective-permute-start | bytes 2752520 | tf_op jit(solution)/shard_map/ppermute | solution.py:45
  50.7 116.0 %all-to-all-start = ((bf16[16,16,7168]{2,1,0:T(8,128)(2,1)}), bf16[16,16,7168]{2,1,0:T(8,128)(2,1)}, u32[]{:S(2)}, u32[]{:S(2)}) async-start(bf16[16,16,7168]{2,1,0:T(8,128)(2,1)} %bitcast.35), calls=%async_computation | async-start | bytes 7340032 | tf_op jit(solution)/shard_map/all_to_all | solution.py:34
  58.3 53.6 %collective-permute-start.2 = (bf16[128,3584]{1,0:T(8,128)(2,1)S(1)}, bf16[128,3584]{1,0:T(8,128)(2,1)S(1)}, u32[]{:S(2)}, u32[]{:S(2)}) collective-permute-start(bf16[128,3584]{1,0:T(8,128)(2,1)S(1)} %get-tuple-element.49), channel_id=1, source_target_pairs={{0,2},{1,3},{2,0},{3,1},{4,6},{5,7},{6,4},{7,5},{8,10},{9,11},{10,... | collective-permute-start | bytes 2752520 | tf_op jit(solution)/shard_map/ppermute | solution.py:45
  60.2 53.5 %collective-permute-start.4 = (bf16[128,3584]{1,0:T(8,128)(2,1)S(1)}, bf16[128,3584]{1,0:T(8,128)(2,1)S(1)}, u32[]{:S(2)}, u32[]{:S(2)}) collective-permute-start(bf16[128,3584]{1,0:T(8,128)(2,1)S(1)} %get-tuple-element.50), channel_id=1, source_target_pairs={{0,1},{1,0},{2,3},{3,2},{4,5},{5,4},{6,7},{7,6},{8,9},{9,8},{10,11... | collective-permute-start | bytes 2752520 | tf_op jit(solution)/shard_map/ppermute | solution.py:45
  112.0 50.7 %collective-permute-start.3 = (bf16[256,3584]{1,0:T(8,128)(2,1)S(1)}, bf16[256,3584]{1,0:T(8,128)(2,1)S(1)}, u32[]{:S(2)}, u32[]{:S(2)}) collective-permute-start(bf16[256,3584]{1,0:T(8,128)(2,1)S(1)} %pad_maximum_fusion.3), channel_id=1, source_target_pairs={{0,1},{1,0},{2,3},{3,2},{4,5},{5,4},{6,7},{7,6},{8,9},{9,8},{10,11... | collective-permute-start | bytes 5505032 | tf_op jit(solution)/shard_map/ppermute | solution.py:45
  113.8 50.8 %collective-permute-start.5 = (bf16[256,3584]{1,0:T(8,128)(2,1)S(1)}, bf16[256,3584]{1,0:T(8,128)(2,1)S(1)}, u32[]{:S(2)}, u32[]{:S(2)}) collective-permute-start(bf16[256,3584]{1,0:T(8,128)(2,1)S(1)} %pad_maximum_fusion.4), channel_id=1, source_target_pairs={{0,2},{1,3},{2,0},{3,1},{4,6},{5,7},{6,4},{7,5},{8,10},{9,11},{10,... | collective-permute-start | bytes 5505032 | tf_op jit(solution)/shard_map/ppermute | solution.py:45
  116.3 16.2 %copy-start.8 = (bf16[256,7168]{1,0:T(8,128)(2,1)S(1)}, bf16[256,7168]{1,0:T(8,128)(2,1)}, u32[]{:S(2)}) copy-start(bf16[256,7168]{1,0:T(8,128)(2,1)} %copy-done.7) | copy-start | bytes 11010052
  166.7 93.4 %all-to-all-start.1 = ((bf16[16,16,7168]{2,1,0:T(8,128)(2,1)}), bf16[16,16,7168]{2,1,0:T(8,128)(2,1)}, u32[]{:S(2)}, u32[]{:S(2)}) async-start(bf16[16,16,7168]{2,1,0:T(8,128)(2,1)} %bitcast.34), calls=%async_computation.1 | async-start | bytes 7340032 | tf_op jit(solution)/shard_map/all_to_all | solution.py:34
  177.3 2.0 copy-start.2
  179.3 12.8 %copy-start = (bf16[512,3584]{1,0:T(8,128)(2,1)S(1)}, bf16[512,3584]{1,0:T(8,128)(2,1)}, u32[]{:S(2)}) copy-start(bf16[512,3584]{1,0:T(8,128)(2,1)} %pad_maximum_fusion.1.left_ref.refs_3_) | copy-start | bytes 11010052
  191.5 8.0 %collective-permute-start.6 = (bf16[512,1024]{1,0:T(8,128)(2,1)S(1)}, bf16[512,1024]{1,0:T(8,128)(2,1)}, u32[]{:S(2)}, u32[]{:S(2)}) collective-permute-start(bf16[512,1024]{1,0:T(8,128)(2,1)S(1)} %get-tuple-element.54.refs_0_), channel_id=1, source_target_pairs={{0,16},{16,0},{1,17},{17,1},{2,18},{18,2},{3,19},{19,3},{4,20},{20... | collective-permute-start | bytes 3145736 | tf_op jit(solution)/shard_map/ppermute | solution.py:127
  191.6 8.0 %collective-permute-start.7 = (bf16[512,1024]{1,0:T(8,128)(2,1)S(1)}, bf16[512,1024]{1,0:T(8,128)(2,1)}, u32[]{:S(2)}, u32[]{:S(2)}) collective-permute-start(bf16[512,1024]{1,0:T(8,128)(2,1)S(1)} %get-tuple-element.55.refs_2_), channel_id=1, source_target_pairs={{0,16},{16,0},{1,17},{17,1},{2,18},{18,2},{3,19},{19,3},{4,20},{20... | collective-permute-start | bytes 3145736 | tf_op jit(solution)/shard_map/ppermute | solution.py:127
  198.8 2.9 copy-start.4
  198.8 2.9 collective-permute-start.8
  218.1 2.1 copy-start.5
  218.1 3.0 copy-start.9
  221.2 38.0 %collective-permute-start.12 = (bf16[256,1792]{1,0:T(8,128)(2,1)S(1)}, bf16[256,1792]{1,0:T(8,128)(2,1)S(1)}, u32[]{:S(2)}, u32[]{:S(2)}) collective-permute-start(bf16[256,1792]{1,0:T(8,128)(2,1)S(1)} %get-tuple-element.64), channel_id=1, source_target_pairs={{0,1},{1,0},{2,3},{3,2},{4,5},{5,4},{6,7},{7,6},{8,9},{9,8},{10,11... | collective-permute-start | bytes 2752520 | tf_op jit(solution)/shard_map/ppermute | solution.py:45
  223.1 37.0 %collective-permute-start.13 = (bf16[256,1792]{1,0:T(8,128)(2,1)S(1)}, bf16[256,1792]{1,0:T(8,128)(2,1)}, u32[]{:S(2)}, u32[]{:S(2)}) collective-permute-start(bf16[256,1792]{1,0:T(8,128)(2,1)S(1)} %get-tuple-element.65), channel_id=1, source_target_pairs={{0,2},{1,3},{2,0},{3,1},{4,6},{5,7},{6,4},{7,5},{8,10},{9,11},{10,... | collective-permute-start | bytes 2752520 | tf_op jit(solution)/shard_map/ppermute | solution.py:45
  235.0 9.4 %collective-permute-start.9 = (bf16[256,1024]{1,0:T(8,128)(2,1)S(1)}, bf16[256,1024]{1,0:T(8,128)(2,1)S(1)}, u32[]{:S(2)}, u32[]{:S(2)}) collective-permute-start(bf16[256,1024]{1,0:T(8,128)(2,1)S(1)} %get-tuple-element.61.refs_0_), channel_id=1, source_target_pairs={{0,16},{16,0},{1,17},{17,1},{2,18},{18,2},{3,19},{19,3},{4,20},{20... | collective-permute-start | bytes 1572872 | tf_op jit(solution)/shard_map/ppermute | solution.py:127
  235.1 9.3 %collective-permute-start.10 = (bf16[256,1024]{1,0:T(8,128)(2,1)S(1)}, bf16[256,1024]{1,0:T(8,128)(2,1)S(1)}, u32[]{:S(2)}, u32[]{:S(2)}) collective-permute-start(bf16[256,1024]{1,0:T(8,128)(2,1)S(1)} %get-tuple-element.62.refs_2_), channel_id=1, source_target_pairs={{0,16},{16,0},{1,17},{17,1},{2,18},{18,2},{3,19},{19,3},{4,20},{20... | collective-permute-start | bytes 1572872 | tf_op jit(solution)/shard_map/ppermute | solution.py:127
  241.4 3.0 collective-permute-start.11
  259.2 0.9 copy-start.14
  260.1 55.1 %all-to-all-start.2 = ((bf16[16,16,3584]{2,1,0:T(8,128)(2,1)}), bf16[16,16,3584]{2,1,0:T(8,128)(2,1)}, u32[]{:S(2)}, u32[]{:S(2)}) async-start(bf16[16,16,3584]{2,1,0:T(8,128)(2,1)} %bitcast.36), calls=%async_computation.2 | async-start | bytes 3670016 | tf_op jit(solution)/shard_map/all_to_all | solution.py:34
  273.7 11.3 %copy-start.15 = (bf16[256,1792]{1,0:T(8,128)(2,1)S(1)}, bf16[256,1792]{1,0:T(8,128)(2,1)}, u32[]{:S(2)}) copy-start(bf16[256,1792]{1,0:T(8,128)(2,1)} %copy-done.14) | copy-start | bytes 2752516
  284.4 11.7 %collective-permute-start.16 = (bf16[256,512]{1,0:T(8,128)(2,1)S(1)}, bf16[256,512]{1,0:T(8,128)(2,1)S(1)}, u32[]{:S(2)}, u32[]{:S(2)}) collective-permute-start(bf16[256,512]{1,0:T(8,128)(2,1)S(1)} %get-tuple-element.71.refs_0_), channel_id=1, source_target_pairs={{0,16},{16,0},{1,17},{17,1},{2,18},{18,2},{3,19},{19,3},{4,20},{20... | collective-permute-start | bytes 786440 | tf_op jit(solution)/shard_map/ppermute | solution.py:127
  284.5 11.7 %collective-permute-start.17 = (bf16[256,512]{1,0:T(8,128)(2,1)S(1)}, bf16[256,512]{1,0:T(8,128)(2,1)S(1)}, u32[]{:S(2)}, u32[]{:S(2)}) collective-permute-start(bf16[256,512]{1,0:T(8,128)(2,1)S(1)} %get-tuple-element.72.refs_2_), channel_id=1, source_target_pairs={{0,16},{16,0},{1,17},{17,1},{2,18},{18,2},{3,19},{19,3},{4,20},{20... | collective-permute-start | bytes 786440 | tf_op jit(solution)/shard_map/ppermute | solution.py:127
  285.0 11.7 %collective-permute-start.18 = (bf16[256,512]{1,0:T(8,128)(2,1)S(1)}, bf16[256,512]{1,0:T(8,128)(2,1)S(1)}, u32[]{:S(2)}, u32[]{:S(2)}) collective-permute-start(bf16[256,512]{1,0:T(8,128)(2,1)S(1)} %get-tuple-element.73.refs_4_), channel_id=1, source_target_pairs={{0,16},{16,0},{1,17},{17,1},{2,18},{18,2},{3,19},{19,3},{4,20},{20... | collective-permute-start | bytes 786440 | tf_op jit(solution)/shard_map/ppermute | solution.py:127
  285.3 3.4 copy-start.10
  285.3 24.6 %collective-permute-start.14 = (bf16[128,1792]{1,0:T(8,128)(2,1)S(1)}, bf16[128,1792]{1,0:T(8,128)(2,1)S(1)}, u32[]{:S(2)}, u32[]{:S(2)}) collective-permute-start(bf16[128,1792]{1,0:T(8,128)(2,1)S(1)} %slice.97), channel_id=1, source_target_pairs={{0,2},{1,3},{2,0},{3,1},{4,6},{5,7},{6,4},{7,5},{8,10},{9,11},{10,... | collective-permute-start | bytes 1376264 | tf_op jit(solution)/shard_map/ppermute | solution.py:45
  288.7 7.5 %copy-start.11 = (bf16[256,1792]{1,0:T(8,128)(2,1)}, bf16[256,1792]{1,0:T(8,128)(2,1)S(1)}, u32[]{:S(2)}) copy-start(bf16[256,1792]{1,0:T(8,128)(2,1)S(1)} %add.30) | copy-start | bytes 2752516
  288.7 26.5 %collective-permute-start.15 = (bf16[128,1792]{1,0:T(8,128)(2,1)S(1)}, bf16[128,1792]{1,0:T(8,128)(2,1)}, u32[]{:S(2)}, u32[]{:S(2)}) collective-permute-start(bf16[128,1792]{1,0:T(8,128)(2,1)S(1)} %slice.98), channel_id=1, source_target_pairs={{0,1},{1,0},{2,3},{3,2},{4,5},{5,4},{6,7},{7,6},{8,9},{9,8},{10,11... | collective-permute-start | bytes 1376264 | tf_op jit(solution)/shard_map/ppermute | solution.py:45
  296.1 1.6 collective-permute-start.19
  296.2 1.9 collective-permute-start.20
  296.7 1.8 collective-permute-start.21
  309.9 0.8 copy-start.16
  315.2 77.1 %all-to-all-start.3 = ((bf16[16,16,3584]{2,1,0:T(8,128)(2,1)}), bf16[16,16,3584]{2,1,0:T(8,128)(2,1)}, u32[]{:S(2)}, u32[]{:S(2)}) async-start(bf16[16,16,3584]{2,1,0:T(8,128)(2,1)} %bitcast.37), calls=%async_computation.3 | async-start | bytes 3670016 | tf_op jit(solution)/shard_map/all_to_all | solution.py:34
  321.5 6.7 %copy-start.3 = (bf16[512,3584]{1,0:T(8,128)(2,1)S(1)}, bf16[512,3584]{1,0:T(8,128)(2,1)}, u32[]{:S(2)}) copy-start(bf16[512,3584]{1,0:T(8,128)(2,1)} %pad_maximum_fusion.left_ref) | copy-start | bytes 11010052
  321.5 6.7 %copy-start.13 = (bf16[256,3584]{1,0:T(8,128)(2,1)S(1)}, bf16[256,3584]{1,0:T(8,128)(2,1)}, u32[]{:S(2)}) copy-start(bf16[256,3584]{1,0:T(8,128)(2,1)} %slice.82) | copy-start | bytes 5505028
  324.7 37.6 %collective-permute-start.22 = (bf16[64,3584]{1,0:T(8,128)(2,1)S(1)}, bf16[64,3584]{1,0:T(8,128)(2,1)S(1)}, u32[]{:S(2)}, u32[]{:S(2)}) collective-permute-start(bf16[64,3584]{1,0:T(8,128)(2,1)S(1)} %pad_maximum_fusion.8), channel_id=1, source_target_pairs={{0,4},{1,5},{2,6},{3,7},{4,0},{5,1},{6,2},{7,3},{8,12},{9,13},{10,... | collective-permute-start | bytes 1376264 | tf_op jit(solution)/shard_map/ppermute | solution.py:45
  328.3 19.9 %copy-start.1 = (bf16[512,3584]{1,0:T(8,128)(2,1)S(1)}, bf16[512,3584]{1,0:T(8,128)(2,1)}, u32[]{:S(2)}) copy-start(bf16[512,3584]{1,0:T(8,128)(2,1)} %pad_maximum_fusion.1.left_ref.refs_3_) | copy-start | bytes 11010052
  328.3 19.9 %copy-start.6 = (bf16[512,1024]{1,0:T(8,128)(2,1)S(1)}, bf16[512,1024]{1,0:T(8,128)(2,1)}, u32[]{:S(2)}) copy-start(bf16[512,1024]{1,0:T(8,128)(2,1)} %copy-done.5) | copy-start | bytes 3145732
  362.4 29.8 %collective-permute-start.23 = (bf16[32,3584]{1,0:T(8,128)(2,1)S(1)}, bf16[32,3584]{1,0:T(8,128)(2,1)S(1)}, u32[]{:S(2)}, u32[]{:S(2)}) collective-permute-start(bf16[32,3584]{1,0:T(8,128)(2,1)S(1)} %slice.91), channel_id=1, source_target_pairs={{0,8},{1,9},{2,10},{3,11},{4,12},{5,13},{6,14},{7,15},{8,0},{9,1},... | collective-permute-start | bytes 688136 | tf_op jit(solution)/shard_map/ppermute | solution.py:45
